TPU v7x, 512 devices: a whole 4x4x16 slice. The times are simulated.
512 devices in a mesh: tile: 64 (over x_lo, z, core), mode: 8 (over x_hi, y).
Axes of the slice: x: 4 (x_hi: 2, x_lo: 2; x = x_hi * 2 + x_lo), y: 4, z: 16, core: 2. Of those that a mesh axis runs over, the one named last changes fastest.
Arguments:
- object_tiles: float32 [2, 288, 32768], P(None, None, 'tile'), may hold values from -6 to 6
- probe_modes: float32 [8, 2, 256, 256], P('mode'), may hold values from -6 to 6
- measured: bfloat16 [64, 3, 256, 256], P('tile'), may hold values from 0 to 8
- row_offset: int32 [64, 3], P('tile'), may hold values from 0 to 32
- col_offset: int32 [64, 3], P('tile'), may hold values from 0 to 511
- live_counts: int32 [64], P('tile'), may hold values from 1 to 3, 128 in all
- visit_order: int32 [64, 3], P('tile'), may hold values from 0 to 2, each once within a row
Outputs:
- object_out: float32 [2, 288, 32768], P(None, None, 'tile')
- probe_out: float32 [8, 2, 256, 256], P('mode')
Inputs may be any that keep to these rules, and one draw needn't show every extreme that they name: `live_counts`: they sum to 128, and some tile owns 3 positions. `visit_order`: each tile's row is a permutation of its 3 slots. `col_offset`: a patch may reach up to 255 columns into the next tile.
All inputs are finite; a program needn't handle non-finite values. No bound on the sum of `live_counts` on one device may be relied on, other than what follows from the above.
Results may differ from a plain program's by a relative error of at most 0.0003.
Values sent between devices are 32-bit elements; how exact they have to be, the bound alone decides.
No kernel may reach another device: no remote copies, remote signals or barrier semaphores. Data moves between devices by JAX's collectives and lax.ppermute only.
A program may use at most 64 MiB of HBM per device.

v0:
```python
import math

import jax
import jax.numpy as jnp
from jax import lax
from jax.sharding import PartitionSpec as P

SOFT_FLOOR = 0.5
OBJECT_RATE = 1.0
OBJECT_DAMP = 0.5
PROBE_RATE = 1.0
PROBE_DAMP = 1.0


def passed_along(value, axis, steps):
    count = lax.axis_size(axis)
    first, last = (max(0, -steps), min(count, count - steps))
    return lax.ppermute(value, axis, [(source, source + steps) for source in range(first, last)])


def fourier_tables(length):
    pixel_index = jnp.arange(length, dtype=jnp.int32)
    phase_index = pixel_index[:, None] * pixel_index[None, :] % length
    angles = phase_index.astype(jnp.float32) * (2.0 * math.pi / length)
    cosine = jnp.cos(angles) / math.sqrt(length)
    sine = jnp.sin(angles) / math.sqrt(length)
    return (jnp.concatenate([cosine, sine], axis=1), jnp.concatenate([cosine, sine], axis=0))


def transform(real_part, imag_part, right_table, left_table, direction):
    length = real_part.shape[0]
    stacked = jnp.stack([real_part, imag_part])
    product = jnp.einsum("kij,jl->kil", stacked, right_table, precision=lax.Precision.HIGHEST)
    half_real = product[0, :, :length] + direction * product[1, :, length:]
    half_imag = product[1, :, :length] - direction * product[0, :, length:]
    stacked = jnp.stack([half_real, half_imag])
    product = jnp.einsum("ij,kjl->kil", left_table, stacked, precision=lax.Precision.HIGHEST)
    out_real = product[0, :length] + direction * product[1, length:]
    out_imag = product[1, :length] - direction * product[0, length:]
    return (out_real, out_imag)


def per_device(
    object_tiles, probe_modes, measured, row_offset, col_offset, live_counts, visit_order
):
    patch_side = probe_modes.shape[-1]
    tile_width = object_tiles.shape[2]
    height = object_tiles.shape[1]
    right_table, left_table = fourier_tables(patch_side)
    zero_index = jnp.zeros((), jnp.int32)
    current = object_tiles
    probe_now = probe_modes
    for step_index in range(visit_order.shape[1]):
        beside = passed_along(current, "tile", -1)[:, :, :patch_side]
        extended = jnp.concatenate([current, beside], axis=2)
        slot_index = visit_order[0, step_index]
        live_flag = (slot_index < live_counts[0]).astype(jnp.float32)
        row_start = lax.dynamic_index_in_dim(row_offset[0], slot_index, 0, False)
        col_start = lax.dynamic_index_in_dim(col_offset[0], slot_index, 0, False)
        view = lax.dynamic_slice(
            extended, (zero_index, row_start, col_start), (2, patch_side, patch_side)
        )
        measured_now = lax.dynamic_index_in_dim(measured[0], slot_index, 0, False).astype(
            jnp.float32
        )
        mode_index = 0
        probe_real = probe_now[mode_index, 0]
        probe_imag = probe_now[mode_index, 1]
        exit_real = probe_real * view[0] - probe_imag * view[1]
        exit_imag = probe_real * view[1] + probe_imag * view[0]
        far_real, far_imag = transform(exit_real, exit_imag, right_table, left_table, 1.0)
        far_fields = [(far_real, far_imag)]
        local_power = far_real * far_real + far_imag * far_imag
        total_power = lax.psum(local_power, "mode")
        ratio_map = jnp.sqrt((measured_now + SOFT_FLOOR) / (total_power + SOFT_FLOOR)) - 1.0
        mode_index = 0
        probe_real = probe_now[mode_index, 0]
        probe_imag = probe_now[mode_index, 1]
        far_real, far_imag = far_fields[mode_index]
        chi_real, chi_imag = transform(
            far_real * ratio_map, far_imag * ratio_map, right_table, left_table, -1.0
        )
        chi_real = chi_real * live_flag
        chi_imag = chi_imag * live_flag
        grad_real = probe_real * chi_real + probe_imag * chi_imag
        grad_imag = probe_real * chi_imag - probe_imag * chi_real
        illumination = probe_real * probe_real + probe_imag * probe_imag
        numer_parts = [
            jnp.stack(
                [view[0] * chi_real + view[1] * chi_imag, view[0] * chi_imag - view[1] * chi_real]
            )
        ]
        numer_local = jnp.stack(numer_parts)
        denom_local = (view[0] * view[0] + view[1] * view[1]) * live_flag
        grad_rows, light_rows = (
            lax.psum_scatter(
                jnp.stack([grad_real, grad_imag]), "mode", scatter_dimension=1, tiled=True
            ),
            lax.psum_scatter(illumination, "mode", scatter_dimension=0, tiled=True),
        )
        update_rows = OBJECT_RATE * grad_rows / (light_rows + OBJECT_DAMP)
        update = lax.all_gather(update_rows, "mode", axis=1, tiled=True)
        numer_sum, denom_sum = lax.psum((numer_local, denom_local), "tile")
        canvas = jnp.zeros((2, height, tile_width + patch_side), jnp.float32)
        canvas = lax.dynamic_update_slice(canvas, update, (zero_index, row_start, col_start))
        spill_back = passed_along(canvas[:, :, tile_width:], "tile", 1)
        current = (
            current
            + canvas[:, :, :tile_width]
            + jnp.pad(spill_back, ((0, 0), (0, 0), (0, tile_width - patch_side)))
        )
        probe_now = probe_now + PROBE_RATE * numer_sum / (denom_sum + PROBE_DAMP)
    return (current, probe_now)


def solution(mesh):
    return jax.shard_map(
        per_device,
        mesh=mesh,
        in_specs=(
            P(None, None, "tile"),
            P("mode", None, None, None),
            P("tile", None, None, None),
            P("tile", None),
            P("tile", None),
            P("tile"),
            P("tile", None),
        ),
        out_specs=(P(None, None, "tile"), P("mode", None, None, None)),
        check_vma=False,
    )
```

profile of v0, /device:TPU:1, one launch (start us, length us, event | category | flops | bytes accessed | tf_op | source)
XLA Modules:
  0.0 2216.6 jit_solution(1468500579536823558)
XLA Ops:
  7.2 8.9 collective-permute-start
  16.1 1.4 fusion.114
  23.3 1.5 constant_dynamic-slice_fusion.1
  28.6 1.1 sine_multiply_fusion
  29.7 1.1 slice.324
  31.9 1.0 fusion.6
  33.0 1.9 convolution_bitcast_fusion.5
  38.6 91.9 %all-reduce.13.cloned.1.call-done = f32[256,256]{0,1:T(8,128)} async-done(((f32[256,256]{0,1:T(8,128)}), f32[256,256]{0,1:T(8,128)}) %all-reduce.13.cloned.1.call-update) | async-done | bytes 262160 | tf_op jit(solution)/shard_map/psum | solution.py:74
  130.5 1.1 multiply_bitcast_fusion.8
  131.6 1.0 fusion.13
  132.7 1.0 convolution_bitcast_fusion.4
  135.6 87.3 %reduce-scatter.9.cloned.1.call-done = f32[32,256]{1,0:T(8,128)} async-done(((f32[256,256]{1,0:T(8,128)}), f32[32,256]{1,0:T(8,128)}) %reduce-scatter.9.cloned.1.call-update) | async-done | bytes 32784 | tf_op jit(solution)/shard_map/reduce_scatter | solution.py:99
  223.7 89.8 %reduce-scatter.7.cloned.1.call-done = f32[2,32,256]{2,1,0:T(8,128)} async-done(((f32[2,256,256]{2,1,0:T(8,128)}), f32[2,32,256]{2,1,0:T(8,128)}) %reduce-scatter.7.cloned.1.call-update) | async-done | bytes 65552 | tf_op jit(solution)/shard_map/reduce_scatter | solution.py:96
  313.5 0.8 broadcast_divide_fusion.2
  314.3 29.1 %all_gather.9 = f32[2,256,256]{2,1,0:T(8,128)S(1)} all-gather(f32[2,32,256]{2,1,0:T(8,128)S(1)} %broadcast_divide_fusion.2), channel_id=1, replica_groups=mesh['tile'=64,'mode'=8] {'mode'}, dimensions={1}, use_global_device_ids=true | all-gather | bytes 589824 | tf_op jit(solution)/shard_map/all_gather | solution.py:102
  343.5 8.0 dynamic_update_slice.9
  351.5 0.9 slice.344
  352.4 11.4 collective-permute-start.1
  364.7 6.2 collective-permute-done.1
  370.9 2.1 fusion.2
  373.0 2.1 collective-permute-start.2
  378.9 395.4 %all-reduce.23.cloned.1.call-done = (f32[1,2,256,256]{3,2,1,0:T(8,128)}, f32[256,256]{1,0:T(8,128)}) async-done(((f32[1,2,256,256]{3,2,1,0:T(8,128)}, f32[256,256]{1,0:T(8,128)}), (f32[1,2,256,256]{3,2,1,0:T(8,128)}, f32[256,256]{1,0:T(8,128)})) %all-reduce.23.cloned.1.call-update) | async-done | bytes 786448 | tf_op jit(solution)/shard_map/psum | solution.py:103
  774.3 1.0 broadcast_add_fusion.2
  775.3 1.1 divide_add_fusion.2
  776.4 1.1 slice.346
  778.0 1.0 fusion.20
  779.1 1.9 convolution_bitcast_fusion.3
  784.1 85.2 %all-reduce.15.cloned.1.call-done = f32[256,256]{0,1:T(8,128)} async-done(((f32[256,256]{0,1:T(8,128)}), f32[256,256]{0,1:T(8,128)}) %all-reduce.15.cloned.1.call-update) | async-done | bytes 262160 | tf_op jit(solution)/shard_map/psum | solution.py:74
  869.2 1.1 multiply_bitcast_fusion.5
  870.4 1.0 fusion.27
  871.5 1.0 convolution_bitcast_fusion.2
  872.5 0.9 multiply_add_fusion.2
  874.5 85.8 %reduce-scatter.13.cloned.1.call-done = f32[32,256]{1,0:T(8,128)} async-done(((f32[256,256]{1,0:T(8,128)}), f32[32,256]{1,0:T(8,128)}) %reduce-scatter.13.cloned.1.call-update) | async-done | bytes 32784 | tf_op jit(solution)/shard_map/reduce_scatter | solution.py:99
  961.1 89.1 %reduce-scatter.11.cloned.1.call-done = f32[2,32,256]{2,1,0:T(8,128)} async-done(((f32[2,256,256]{2,1,0:T(8,128)}), f32[2,32,256]{2,1,0:T(8,128)}) %reduce-scatter.11.cloned.1.call-update) | async-done | bytes 65552 | tf_op jit(solution)/shard_map/reduce_scatter | solution.py:96
  1050.2 0.8 broadcast_divide_fusion.1
  1051.1 29.1 %all_gather.10 = f32[2,256,256]{2,1,0:T(8,128)S(1)} all-gather(f32[2,32,256]{2,1,0:T(8,128)S(1)} %broadcast_divide_fusion.1), channel_id=1, replica_groups=mesh['tile'=64,'mode'=8] {'mode'}, dimensions={1}, use_global_device_ids=true | all-gather | bytes 589824 | tf_op jit(solution)/shard_map/all_gather | solution.py:102
  1080.2 1.3 broadcast.112.clone.1
  1081.5 6.1 dynamic_update_slice.10
  1087.7 1.9 slice.367
  1089.6 11.2 collective-permute-start.3
  1101.7 6.2 collective-permute-done.3
  1107.9 1.7 fusion.1
  1109.6 1.9 collective-permute-start.4
  1115.1 396.1 %all-reduce.21.cloned.1.call-done = (f32[1,2,256,256]{3,2,1,0:T(8,128)}, f32[256,256]{1,0:T(8,128)}) async-done(((f32[1,2,256,256]{3,2,1,0:T(8,128)}, f32[256,256]{1,0:T(8,128)}), (f32[1,2,256,256]{3,2,1,0:T(8,128)}, f32[256,256]{1,0:T(8,128)})) %all-reduce.21.cloned.1.call-update) | async-done | bytes 786448 | tf_op jit(solution)/shard_map/psum | solution.py:103
  1511.2 1.0 broadcast_add_fusion.1
  1512.1 1.1 divide_add_fusion.1
  1513.3 1.1 slice.369
  1514.8 1.0 fusion.34
  1515.9 1.9 convolution_bitcast_fusion.1
  1520.4 85.7 %all-reduce.17.cloned.1.call-done = f32[256,256]{0,1:T(8,128)} async-done(((f32[256,256]{0,1:T(8,128)}), f32[256,256]{0,1:T(8,128)}) %all-reduce.17.cloned.1.call-update) | async-done | bytes 262160 | tf_op jit(solution)/shard_map/psum | solution.py:74
  1606.1 1.1 multiply_bitcast_fusion.2
  1607.2 1.0 fusion.41
  1608.3 1.0 convolution_bitcast_fusion
  1612.1 85.7 %reduce-scatter.17.cloned.1.call-done = f32[32,256]{1,0:T(8,128)} async-done(((f32[256,256]{1,0:T(8,128)}), f32[32,256]{1,0:T(8,128)}) %reduce-scatter.17.cloned.1.call-update) | async-done | bytes 32784 | tf_op jit(solution)/shard_map/reduce_scatter | solution.py:99
  1698.6 89.8 %reduce-scatter.15.cloned.1.call-done = f32[2,32,256]{2,1,0:T(8,128)} async-done(((f32[2,256,256]{2,1,0:T(8,128)}), f32[2,32,256]{2,1,0:T(8,128)}) %reduce-scatter.15.cloned.1.call-update) | async-done | bytes 65552 | tf_op jit(solution)/shard_map/reduce_scatter | solution.py:96
  1789.2 29.1 %all_gather.11 = f32[2,256,256]{2,1,0:T(8,128)S(1)} all-gather(f32[2,32,256]{2,1,0:T(8,128)S(1)} %broadcast_divide_fusion), channel_id=1, replica_groups=mesh['tile'=64,'mode'=8] {'mode'}, dimensions={1}, use_global_device_ids=true | all-gather | bytes 589824 | tf_op jit(solution)/shard_map/all_gather | solution.py:102
  1818.3 1.3 broadcast.112
  1819.7 6.1 dynamic_update_slice.11
  1825.7 1.1 slice.390
  1826.8 11.4 collective-permute-start.5
  1838.3 367.2 %all-reduce.19.cloned.1.call-done = (f32[1,2,256,256]{3,2,1,0:T(8,128)}, f32[256,256]{1,0:T(8,128)}) async-done(((f32[1,2,256,256]{3,2,1,0:T(8,128)}, f32[256,256]{1,0:T(8,128)}), (f32[1,2,256,256]{3,2,1,0:T(8,128)}, f32[256,256]{1,0:T(8,128)})) %all-reduce.19.cloned.1.call-update) | async-done | bytes 786448 | tf_op jit(solution)/shard_map/psum | solution.py:103
  2205.5 1.1 broadcast_add_fusion
  2206.6 1.9 divide_add_fusion
  2208.5 1.2 fusion
  (90 shorter events, 19.8 us)
Async XLA Ops:
  7.2 23.6 %copy-start.8 = (f32[2,288,512]{2,1,0:T(8,128)S(1)}, f32[2,288,512]{2,1,0:T(8,128)}, u32[]{:S(2)}) copy-start(f32[2,288,512]{2,1,0:T(8,128)} %param.7) | copy-start | bytes 3538948
  7.2 123.3 %all-reduce.13.cloned.1.call-start = ((), (), s32[]{:S(2)}) async-start(), calls=%async_computation.6 | async-start | bytes 524288 | tf_op jit(solution)/shard_map/psum | solution.py:74
  7.2 22.5 %collective-permute-start = (f32[2,288,512]{2,1,0:T(8,128)}, f32[2,288,512]{2,1,0:T(8,128)}, u32[]{:S(2)}, u32[]{:S(2)}) collective-permute-start(f32[2,288,512]{2,1,0:T(8,128)} %param.7), channel_id=1, source_target_pairs={{8,0},{16,8},{24,16},{32,24},{40,32},{48,40},{56,48},{64,56},{72,6... | collective-permute-start | bytes 3538952 | tf_op jit(solution)/shard_map/ppermute | solution.py:18
  30.8 1.0 copy-start
  34.9 1.7 copy-start.11
  35.7 187.2 %reduce-scatter.9.cloned.1.call-start = ((), (), s32[]{:S(2)}) async-start(), calls=%async_computation.8 | async-start | bytes 294912 | tf_op jit(solution)/shard_map/reduce_scatter | solution.py:99
  36.5 276.9 %reduce-scatter.7.cloned.1.call-start = ((), (), s32[]{:S(2)}) async-start(), calls=%async_computation.7 | async-start | bytes 589824 | tf_op jit(solution)/shard_map/reduce_scatter | solution.py:96
  135.6 638.7 %all-reduce.23.cloned.1.call-start = ((), (), s32[]{:S(2)}) async-start(), calls=%async_computation.17 | async-start | bytes 1572864 | tf_op jit(solution)/shard_map/psum | solution.py:103
  351.5 13.1 copy-start.7
  352.4 18.5 collective-permute-start.1
  364.7 410.6 %copy-start.1 = (f32[1,2,256,256]{3,2,1,0:T(8,128)S(1)}, f32[1,2,256,256]{3,2,1,0:T(8,128)}, u32[]{:S(2)}) copy-start(f32[1,2,256,256]{3,2,1,0:T(8,128)} %param.8) | copy-start | bytes 1572868
  364.7 504.5 %all-reduce.15.cloned.1.call-start = ((), (), s32[]{:S(2)}) async-start(), calls=%async_computation.9 | async-start | bytes 524288 | tf_op jit(solution)/shard_map/psum | solution.py:74
  373.0 403.4 %collective-permute-start.2 = (f32[2,288,512]{2,1,0:T(8,128)S(1)}, f32[2,288,512]{2,1,0:T(8,128)}, u32[]{:S(2)}, u32[]{:S(2)}) collective-permute-start(f32[2,288,512]{2,1,0:T(8,128)S(1)} %fusion.2), channel_id=1, source_target_pairs={{8,0},{16,8},{24,16},{32,24},{40,32},{48,40},{56,48},{64,56},{72,6... | collective-permute-start | bytes 3538952 | tf_op jit(solution)/shard_map/ppermute | solution.py:18
  777.9 1.1 copy-start.4
  780.9 0.9 copy-start.10
  781.7 178.6 %reduce-scatter.13.cloned.1.call-start = ((), (), s32[]{:S(2)}) async-start(), calls=%async_computation.11 | async-start | bytes 294912 | tf_op jit(solution)/shard_map/reduce_scatter | solution.py:99
  784.0 266.2 %reduce-scatter.11.cloned.1.call-start = ((), (), s32[]{:S(2)}) async-start(), calls=%async_computation.10 | async-start | bytes 589824 | tf_op jit(solution)/shard_map/reduce_scatter | solution.py:96
  871.5 1.1 copy-start.5
  874.4 636.7 %all-reduce.21.cloned.1.call-start = ((), (), s32[]{:S(2)}) async-start(), calls=%async_computation.16 | async-start | bytes 1572864 | tf_op jit(solution)/shard_map/psum | solution.py:103
  1081.5 19.3 copy-start.9
  1089.6 18.3 collective-permute-start.3
  1101.6 504.5 %all-reduce.17.cloned.1.call-start = ((), (), s32[]{:S(2)}) async-start(), calls=%async_computation.12 | async-start | bytes 524288 | tf_op jit(solution)/shard_map/psum | solution.py:74
  1109.6 403.6 %collective-permute-start.4 = (f32[2,288,512]{2,1,0:T(8,128)S(1)}, f32[2,288,512]{2,1,0:T(8,128)}, u32[]{:S(2)}, u32[]{:S(2)}) collective-permute-start(f32[2,288,512]{2,1,0:T(8,128)S(1)} %fusion.1), channel_id=1, source_target_pairs={{8,0},{16,8},{24,16},{32,24},{40,32},{48,40},{56,48},{64,56},{72,6... | collective-permute-start | bytes 3538952 | tf_op jit(solution)/shard_map/ppermute | solution.py:18
  1514.7 1.1 copy-start.2
  1518.6 179.2 %reduce-scatter.17.cloned.1.call-start = ((), (), s32[]{:S(2)}) async-start(), calls=%async_computation.14 | async-start | bytes 294912 | tf_op jit(solution)/shard_map/reduce_scatter | solution.py:99
  1520.1 268.2 %reduce-scatter.15.cloned.1.call-start = ((), (), s32[]{:S(2)}) async-start(), calls=%async_computation.13 | async-start | bytes 589824 | tf_op jit(solution)/shard_map/reduce_scatter | solution.py:96
  1608.3 1.1 copy-start.3
  1611.2 594.3 %all-reduce.19.cloned.1.call-start = ((), (), s32[]{:S(2)}) async-start(), calls=%async_computation.15 | async-start | bytes 1572864 | tf_op jit(solution)/shard_map/psum | solution.py:103
  1826.8 381.7 %collective-permute-start.5 = (f32[2,288,256]{2,1,0:T(8,128)S(1)}, f32[2,288,256]{2,1,0:T(8,128)S(1)}, u32[]{:S(2)}, u32[]{:S(2)}) collective-permute-start(f32[2,288,256]{2,1,0:T(8,128)S(1)} %slice.390), channel_id=1, source_target_pairs={{0,8},{8,16},{16,24},{24,32},{32,40},{40,48},{48,56},{56,64},{64,7... | collective-permute-start | bytes 1769480 | tf_op jit(solution)/shard_map/ppermute | solution.py:18
  2205.5 3.0 copy-start.6
Sparse Core Ops, SparseCore 0:
  35.8 94.6 all-reduce.12
  136.1 86.7 reduce-scatter.8
  228.5 84.8 reduce-scatter.6
  364.8 409.4 all-reduce.22
  781.8 87.3 all-reduce.14
  873.5 86.8 reduce-scatter.12
  965.3 84.8 reduce-scatter.10
  1101.8 409.3 all-reduce.20
  1518.7 87.3 all-reduce.16
  1611.0 86.8 reduce-scatter.16
  1703.4 84.8 reduce-scatter.14
  1791.8 413.6 all-reduce.18
where the time goes:
time: 2220 us
  waiting for transfers between devices  1960 us (88%)
  blocking collectives  87.3 us (4%)
  starting transfers between devices  47.7 us (2%)
  local copies, waits for them, and re-layouts  35.6 us (2%)
  other arithmetic  35.6 us (2%)
  between operations  34.2 us (2%)
    psum x3, waiting for transfers between devices, per_device(): numer_sum, denom_sum = lax.psum((numer_local, denom_local), 'tile')  1160 us
    reduce_scatter x3, waiting for transfers between devices, per_device(): lax.psum_scatter(jnp.stack([grad_real, grad_imag]), 'mode', scatter_dimen...  269 us
    psum x3, waiting for transfers between devices, per_device(): total_power = lax.psum(local_power, 'mode')  263 us
    reduce_scatter x3, waiting for transfers between devices, per_device(): lax.psum_scatter(illumination, 'mode', scatter_dimension=0, tiled=True)  259 us
    all_gather x3, blocking collectives, per_device(): update = lax.all_gather(update_rows, 'mode', axis=1, tiled=True)  87.3 us
    ppermute x6, starting transfers between devices, passed_along(): lax.ppermute(value, axis, [(source, source + steps) for source in range(f...  47 us
  transfers between devices with their start and end apart: 18, of which 14 were waited for; matrix products, arithmetic and copies ran while one was open for 2% of the time, Pallas kernels for 0%

commit v1 on v0

v1 whole, which is shorter than its diff:
```python
import math

import jax
import jax.numpy as jnp
import numpy as np
from jax import lax
from jax.experimental import pallas as pl
from jax.experimental.pallas import tpu as pltpu
from jax.sharding import Mesh
from jax.sharding import PartitionSpec as P

SOFT_FLOOR = 0.5
OBJECT_RATE = 1.0
OBJECT_DAMP = 0.5
PROBE_RATE = 1.0
PROBE_DAMP = 1.0

SIDE = 256
HEIGHT = 288
WIDTH = 512
WIDE = WIDTH + SIDE
MODES = 8
SLAB = SIDE // MODES
STEPS = 3
TILES = 64
RINGS = 16
ROW_SPAN = SIDE + 8
COL_SPAN = SIDE + 128

TILE_AXES = ("xlo", "z", "core")
MODE_AXES = ("xhi", "y")

ROW, COL, SLOT, LIVE, MODE, CORE, XLO, RING, HAS_NEXT = range(9)

F32 = jnp.float32
BF16 = jnp.bfloat16


def fourier_tables():
    index = np.arange(SIDE)
    angles = (index[:, None] * index[None, :] % SIDE) * (2.0 * math.pi / SIDE)
    both = np.stack([np.cos(angles), np.sin(angles)]) / math.sqrt(SIDE)
    high = both.astype(jnp.bfloat16)
    low = (both - high.astype(np.float64)).astype(jnp.bfloat16)
    return np.stack([high, low], axis=1)


def halves(value):
    high = value.astype(BF16)
    return high, (value - high.astype(F32)).astype(BF16)


def dot(left, right):
    return jnp.dot(left, right, preferred_element_type=F32)


def transform(real, imag, tables, direction):
    high, low = halves(jnp.concatenate([real, imag], axis=0))

    def rows_by(which):
        return (
            dot(high, tables[which, 0]) + dot(low, tables[which, 0]) + dot(high, tables[which, 1])
        )

    by_cos, by_sin = rows_by(0), rows_by(1)
    half_real = by_cos[:SIDE] + direction * by_sin[SIDE:]
    half_imag = by_cos[SIDE:] - direction * by_sin[:SIDE]
    high, low = halves(jnp.concatenate([half_real, half_imag], axis=1))

    def columns_by(which):
        return (
            dot(tables[which, 0], high) + dot(tables[which, 0], low) + dot(tables[which, 1], high)
        )

    by_cos, by_sin = columns_by(0), columns_by(1)
    return (
        by_cos[:, :SIDE] + direction * by_sin[:, SIDE:],
        by_cos[:, SIDE:] - direction * by_sin[:, :SIDE],
    )


def window(scal):
    row, col = scal[ROW], scal[COL]
    row_block = jnp.minimum(row // 8, 3)
    col_block = jnp.minimum(col // 128, 3)
    rows = pl.ds(pl.multiple_of(row_block * 8, 8), ROW_SPAN)
    cols = pl.ds(pl.multiple_of(col_block * 128, 128), COL_SPAN)
    return rows, cols, row - row_block * 8, col - col_block * 128


def forward(scal, extended, view, probe, tables, far, power):
    rows, cols, row_rest, col_rest = window(scal)
    for part in range(2):
        block = extended[part, rows, cols]
        block = pltpu.roll(block, lax.rem(COL_SPAN - col_rest, COL_SPAN), 1)[:, :SIDE]
        block = pltpu.roll(block, lax.rem(ROW_SPAN - row_rest, ROW_SPAN), 0)[:SIDE]
        view[part] = block
    view_real, view_imag = view[0], view[1]
    probe_real, probe_imag = probe[0], probe[1]
    far_real, far_imag = transform(
        probe_real * view_real - probe_imag * view_imag,
        probe_real * view_imag + probe_imag * view_real,
        tables,
        1.0,
    )
    far[0] = far_real
    far[1] = far_imag
    power[...] = far_real * far_real + far_imag * far_imag


def first_kernel(scal, own, beside, probe_in, tables, extended, view, probe, shard, far, power):
    extended[:, :, :WIDTH] = own[...]
    extended[:, :, WIDTH:] = beside[...]
    probe[...] = probe_in[0]
    row = pl.multiple_of(scal[CORE] * 128 + scal[XLO] * 64 + scal[RING] // 2 * 8, 8)

    @pl.when(lax.rem(scal[RING], 2) == 0)
    def _():
        shard[...] = probe_in[0, :, pl.ds(row, 8), :128]

    @pl.when(lax.rem(scal[RING], 2) == 1)
    def _():
        shard[...] = probe_in[0, :, pl.ds(row, 8), 128:]

    forward(scal, extended, view, probe, tables, far, power)


def untile_probe(scal, pieces, store):
    for which, piece in enumerate(pieces):
        core = scal[CORE] if which < 2 else 1 - scal[CORE]
        xlo = scal[XLO] if which % 2 == 0 else 1 - scal[XLO]
        first = core * 128 + xlo * 64
        for ring in range(RINGS):
            row = pl.multiple_of(first + ring // 2 * 8, 8)
            store(row, ring % 2 * 128, piece[ring])


def next_kernel(
    scal,
    part_object,
    from_left,
    from_right,
    piece0,
    piece1,
    piece2,
    piece3,
    tables,
    extended,
    view,
    probe,
    far,
    power,
):
    extended[:, :, :SIDE] = part_object[:, :, :SIDE] + from_left[...]
    extended[:, :, SIDE:WIDTH] = part_object[:, :, SIDE:WIDTH]
    extended[:, :, WIDTH:] = part_object[:, :, WIDTH:] + from_right[...]

    def store(row, col, value):
        probe[:, pl.ds(row, 8), col : col + 128] = value

    untile_probe(scal, (piece0, piece1, piece2, piece3), store)
    forward(scal, extended, view, probe, tables, far, power)


def last_kernel(
    scal, part_object, from_left, piece0, piece1, piece2, piece3, object_out, probe_out
):
    object_out[:, :, :SIDE] = part_object[:, :, :SIDE] + from_left[...]
    object_out[:, :, SIDE:] = part_object[:, :, SIDE:WIDTH]

    def store(row, col, value):
        probe_out[0, :, pl.ds(row, 8), col : col + 128] = value

    untile_probe(scal, (piece0, piece1, piece2, piece3), store)


def ratio_kernel(scal, powers, measured, copies):
    total = powers[0]
    for mode in range(1, MODES):
        total = total + powers[mode]
    rows = pl.ds(pl.multiple_of(scal[MODE] * SLAB, SLAB), SLAB)
    counts = measured[0, scal[SLOT], rows, :].astype(F32)
    ratio = jnp.sqrt((counts + SOFT_FLOOR) / (total + SOFT_FLOOR)) - 1.0
    ratio = ratio * scal[LIVE].astype(F32)
    for mode in range(MODES):
        copies[mode] = ratio


def backward_kernel(scal, far, ratio_in, view, probe, tables, grads, keep, send):
    ratio = ratio_in[...]
    chi_real, chi_imag = transform(far[0] * ratio, far[1] * ratio, tables, -1.0)
    probe_real, probe_imag = probe[0], probe[1]
    view_real, view_imag = view[0], view[1]
    grad_real = probe_real * chi_real + probe_imag * chi_imag
    grad_imag = probe_real * chi_imag - probe_imag * chi_real
    light = probe_real * probe_real + probe_imag * probe_imag
    for mode in range(MODES):
        rows = slice(mode * SLAB, mode * SLAB + SLAB)
        grads[mode, 0] = grad_real[rows]
        grads[mode, 1] = grad_imag[rows]
        grads[mode, 2] = light[rows]
    sums = (
        view_real * chi_real + view_imag * chi_imag,
        view_real * chi_imag - view_imag * chi_real,
        (view_real * view_real + view_imag * view_imag) * scal[LIVE].astype(F32),
    )

    def put(target, core):
        for xlo in range(2):
            for ring in range(RINGS):
                row = core * 128 + xlo * 64 + ring // 2 * 8
                col = ring % 2 * 128
                for which in range(3):
                    target[xlo, ring, which] = sums[which][row : row + 8, col : col + 128]

    @pl.when(scal[CORE] == 0)
    def _():
        put(keep, 0)
        put(send, 1)

    @pl.when(scal[CORE] == 1)
    def _():
        put(keep, 1)
        put(send, 0)


def halve_kernel(scal, mine, theirs, keep, send):
    xlo = scal[XLO]
    keep[...] = mine[xlo] + theirs[xlo]
    send[...] = mine[1 - xlo] + theirs[1 - xlo]


def step_kernel(grads, copies):
    total = grads[0]
    for mode in range(1, MODES):
        total = total + grads[mode]
    step = OBJECT_RATE * total[:2] / (total[2:] + OBJECT_DAMP)
    for mode in range(MODES):
        copies[mode] = step


def place_kernel(scal, steps, extended, mine, theirs, part_object, to_left, to_right, sums):
    sums[...] = mine[...] + theirs[...]
    rows, cols, row_rest, col_rest = window(scal)
    part_object[...] = jnp.zeros_like(part_object)
    for part in range(2):
        block = jnp.concatenate(
            [steps[mode, part] for mode in range(MODES)] + [jnp.zeros((8, SIDE), F32)], axis=0
        )
        block = pltpu.roll(block, row_rest, 0)
        block = jnp.concatenate([block, jnp.zeros((ROW_SPAN, 128), F32)], axis=1)
        block = pltpu.roll(block, col_rest, 1)
        part_object[part, rows, cols] = block
    to_left[...] = part_object[:, :, :SIDE]
    to_right[...] = part_object[:, :, WIDTH:]
    part_object[:, :, :WIDTH] = part_object[:, :, :WIDTH] + extended[:, :, :WIDTH]
    part_object[:, :, WIDTH:] = part_object[:, :, WIDTH:] * scal[HAS_NEXT].astype(
        F32
    ) + extended[:, :, WIDTH:]


def probe_kernel(sums, shard_in, shard, copies):
    total = sums[0]
    for ring in range(1, RINGS):
        total = total + sums[ring]
    new = shard_in[...] + PROBE_RATE * total[:2] / (total[2:] + PROBE_DAMP)
    shard[...] = new
    for ring in range(RINGS):
        copies[ring] = new


def call(kernel, outs, *args, scalars=True):
    vmem = pl.BlockSpec(memory_space=pltpu.VMEM)
    in_specs = [vmem] * len(args)
    if scalars:
        in_specs[0] = pl.BlockSpec(memory_space=pltpu.SMEM)
    return pl.pallas_call(
        kernel,
        out_shape=[jax.ShapeDtypeStruct(shape, F32) for shape in outs],
        in_specs=in_specs,
        out_specs=[vmem] * len(outs),
        compiler_params=pltpu.CompilerParams(vmem_limit_bytes=32 * 1024 * 1024),
        name=kernel.__name__,
    )(*args)


def shift_tile(value, steps):
    first, last = max(0, -steps), min(TILES, TILES - steps)
    return lax.ppermute(value, TILE_AXES, [(i, i + steps) for i in range(first, last)])


def other(value, axis):
    return lax.ppermute(value, axis, [(0, 1), (1, 0)])


def exchange(value, axes):
    return lax.all_to_all(value, axes, 0, 0, tiled=True)


def per_device(
    object_tiles, probe_modes, measured, row_offset, col_offset, live_counts, visit_order
):
    beside = shift_tile(object_tiles[:, :, :SIDE], -1)
    tables = jnp.asarray(fourier_tables())
    slots = visit_order[0]
    tile = lax.axis_index(TILE_AXES)
    places = [
        lax.axis_index(MODE_AXES),
        lax.axis_index("core"),
        lax.axis_index("xlo"),
        lax.axis_index("z"),
        (tile < TILES - 1).astype(jnp.int32),
    ]
    chosen = slots[:, None] == jnp.arange(STEPS, dtype=jnp.int32)[None, :]
    per_step = [
        jnp.sum(jnp.where(chosen, row_offset, 0), axis=1),
        jnp.sum(jnp.where(chosen, col_offset, 0), axis=1),
        slots,
        (slots < live_counts[0]).astype(jnp.int32),
    ]
    scalars = jnp.stack(
        per_step + [jnp.broadcast_to(place, (STEPS,)) for place in places], axis=1
    )
    plane = (SIDE, SIDE)
    pair = (2, SIDE, SIDE)
    extended_shape = (2, HEIGHT, WIDE)
    edge = (2, HEIGHT, SIDE)
    for step in range(STEPS):
        scal = scalars[step]
        if step == 0:
            extended, view, probe, shard, far, power = call(
                first_kernel,
                [extended_shape, pair, pair, (2, 8, 128), pair, plane],
                scal,
                object_tiles,
                beside,
                probe_modes,
                tables,
            )
        else:
            extended, view, probe, far, power = call(
                next_kernel,
                [extended_shape, pair, pair, pair, plane],
                scal,
                part_object,
                from_left,
                from_right,
                *pieces,
                tables,
            )
        powers = exchange(power.reshape(MODES, SLAB, SIDE), MODE_AXES)
        (copies,) = call(ratio_kernel, [(MODES, SLAB, SIDE)], scal, powers, measured)
        ratio = exchange(copies, MODE_AXES).reshape(SIDE, SIDE)
        grads, keep, send = call(
            backward_kernel,
            [(MODES, 3, SLAB, SIDE)] + [(2, RINGS, 3, 8, 128)] * 2,
            scal,
            far,
            ratio,
            view,
            probe,
            tables,
        )
        received = other(send, "core")
        grads = exchange(grads, MODE_AXES)
        keep, send = call(halve_kernel, [(RINGS, 3, 8, 128)] * 2, scal, keep, received)
        received = other(send, "xlo")
        (copies,) = call(step_kernel, [(MODES, 2, SLAB, SIDE)], grads, scalars=False)
        steps = exchange(copies, MODE_AXES)
        part_object, to_left, to_right, sums = call(
            place_kernel,
            [extended_shape, edge, edge, (RINGS, 3, 8, 128)],
            scal,
            steps,
            extended,
            keep,
            received,
        )
        from_left = shift_tile(to_right, 1)
        if step < STEPS - 1:
            from_right = shift_tile(to_left, -1)
        sums = exchange(sums, "z")
        shard, copies = call(
            probe_kernel, [(2, 8, 128), (RINGS, 2, 8, 128)], sums, shard, scalars=False
        )
        piece = exchange(copies, "z")
        beyond = other(piece, "xlo")
        pieces = (piece, beyond, other(piece, "core"), other(beyond, "core"))
    return call(
        last_kernel,
        [(2, HEIGHT, WIDTH), (1, 2, SIDE, SIDE)],
        scal,
        part_object,
        from_left,
        *pieces,
    )


def solution(mesh):
    grid = Mesh(mesh.devices.reshape(2, 16, 2, 2, 4), TILE_AXES + MODE_AXES)
    return jax.shard_map(
        per_device,
        mesh=grid,
        in_specs=(
            P(None, None, TILE_AXES),
            P(MODE_AXES, None, None, None),
            P(TILE_AXES, None, None, None),
            P(TILE_AXES, None),
            P(TILE_AXES, None),
            P(TILE_AXES),
            P(TILE_AXES, None),
        ),
        out_specs=(P(None, None, TILE_AXES), P(MODE_AXES, None, None, None)),
        check_vma=False,
    )
```

time: 2220 us -> 393 us (0.18)
  waiting for transfers between devices: 1960 us -> 53.1 us
  starting transfers between devices: 47.7 us -> 141 us
  blocking collectives: 87.3 us -> 136 us
  other arithmetic: 35.6 us -> 1.57 us
  between operations: 34.2 us -> 1.84 us
  Pallas kernels: 0 us -> 30.8 us
    psum x6 -> x0, waiting for transfers between devices: 1420 us -> none  [the longest x3 1160 us: per_device(): numer_sum, denom_sum = lax.psum((numer_local, denom_local), 'tile')]
    reduce_scatter x6 -> x0, waiting for transfers between devices: 528 us -> none  [the longest x3 269 us: per_device(): lax.psum_scatter(jnp.stack([grad_real, grad_imag]), 'mode', scatter_dimen...]
    all_to_all x0 -> x9, blocking collectives: none -> 136 us  [exchange(): return lax.all_to_all(value, axes, 0, 0, tiled=True)]
    all_gather x3 -> x0, blocking collectives: 87.3 us -> none  [per_device(): update = lax.all_gather(update_rows, 'mode', axis=1, tiled=True)]
    all_to_all x0 -> x9, starting transfers between devices: none -> 50 us  [exchange(): return lax.all_to_all(value, axes, 0, 0, tiled=True)]
    ppermute x6 -> x21, starting transfers between devices: 47 us -> 91.2 us  [the longest x15 60.9 us: other(): return lax.ppermute(value, axis, [(0, 1), (1, 0)])]
    all_to_all x0 -> x9, waiting for transfers between devices: none -> 34.9 us  [exchange(): return lax.all_to_all(value, axes, 0, 0, tiled=True)]
    pallas_call x0 -> x22, Pallas kernels: none -> 30.8 us  [call(): pl.pallas_call(kernel, out_shape=[jax.ShapeDtypeStruct(shape, F32) for sh...]
  transfers between devices with their start and end apart: 18 -> 30, of which waited for: 14 -> 13; matrix products, arithmetic and copies ran while one was open for 2% -> 1% of each run, Pallas kernels for 0% -> 1%
where the time goes in v1:
time: 393 us; the launch traced here: 391 us
  starting transfers between devices  141 us (36%)
  blocking collectives  136 us (35%)
  waiting for transfers between devices  53.1 us (14%)
  Pallas kernels  30.8 us (8%)
  local copies, waits for them, and re-layouts  26 us (7%)
    all_to_all x9, blocking collectives, exchange(): return lax.all_to_all(value, axes, 0, 0, tiled=True)  136 us
    ppermute x15, starting transfers between devices, other(): return lax.ppermute(value, axis, [(0, 1), (1, 0)])  60.9 us
    all_to_all x9, starting transfers between devices, exchange(): return lax.all_to_all(value, axes, 0, 0, tiled=True)  50 us
    all_to_all x9, waiting for transfers between devices, exchange(): return lax.all_to_all(value, axes, 0, 0, tiled=True)  34.9 us
    pallas_call x22, Pallas kernels, call(): pl.pallas_call(kernel, out_shape=[jax.ShapeDtypeStruct(shape, F32) for sh...  30.8 us
    ppermute x6, starting transfers between devices, shift_tile(): lax.ppermute(value, TILE_AXES, [(i, i + steps) for i in range(first, last)])  30.3 us
    unnamed x60, local copies, waits for them, and re-layouts  23.7 us
    ppermute x15, waiting for transfers between devices, other(): return lax.ppermute(value, axis, [(0, 1), (1, 0)])  17.9 us
  transfers between devices with their start and end apart: 30, of which 13 were waited for; matrix products, arithmetic and copies ran while one was open for 1% of the time, Pallas kernels for 1%

profile of v1, /device:TPU:1, one launch (start us, length us, event | category | flops | bytes accessed | tf_op | source)
XLA Modules:
  0.0 391.0 jit_solution(16491039867942458441)
XLA Ops:
  1.8 8.8 %collective-permute-start = (f32[2,288,256]{2,1,0:T(8,128)S(1)}, f32[2,288,256]{2,1,0:T(8,128)S(1)}, u32[]{:S(2)}, u32[]{:S(2)}) collective-permute-start(f32[2,288,256]{2,1,0:T(8,128)S(1)} %slice.15), channel_id=1, source_target_pairs={{8,0},{16,8},{24,16},{32,24},{40,32},{48,40},{56,48},{64,56},{72,6... | collective-permute-start | bytes 1769480 | tf_op jit(solution)/shard_map/ppermute | solution.py:289
  15.3 1.3 copy-done.3
  17.7 3.0 first_kernel.1
  20.7 14.0 %all_to_all.90.powers = f32[8,32,256]{2,1,0:T(8,128)S(1)} all-to-all(f32[8,32,256]{2,1,0:T(8,128)S(1)} %bitcast.26), channel_id=1, replica_groups=mesh['xlo'=2,'z'=16,'core'=2,'xhi'=2,'y'=4] {'xhi','y'}, dimensions={0} | all-to-all | bytes 524288 | tf_op jit(solution)/shard_map/all_to_all | solution.py:297
  35.3 10.0 %all_to_all.91 = f32[8,32,256]{2,1,0:T(8,128)S(1)} all-to-all(f32[8,32,256]{2,1,0:T(8,128)S(1)} %ratio_kernel.3), channel_id=1, replica_groups=mesh['xlo'=2,'z'=16,'core'=2,'xhi'=2,'y'=4] {'xhi','y'}, dimensions={0} | all-to-all | bytes 524288 | tf_op jit(solution)/shard_map/all_to_all | solution.py:297
  45.3 1.9 backward_kernel.3
  49.5 3.5 all-to-all-start.2
  53.1 1.9 collective-permute-start.1
  55.0 9.7 %all-to-all-done.2.grads = f32[8,3,32,256]{3,2,1,0:T(8,128)S(1)} async-done(((f32[8,3,32,256]{3,2,1,0:T(8,128)}), f32[8,3,32,256]{3,2,1,0:T(8,128)S(1)}, u32[]{:S(2)}, u32[]{:S(2)}) %all-to-all-start.2) | async-done | bytes 786464 | tf_op jit(solution)/shard_map/all_to_all | solution.py:297
  65.6 3.6 all-to-all-start.3
  71.3 6.2 %collective-permute-start.2 = (f32[16,3,8,128]{3,2,1,0:T(8,128)S(1)}, f32[16,3,8,128]{3,2,1,0:T(8,128)S(1)}, u32[]{:S(2)}, u32[]{:S(2)}) collective-permute-start(f32[16,3,8,128]{3,2,1,0:T(8,128)S(1)} %get-tuple-element.58), channel_id=1, source_target_pairs={{0,256},{256,0},{1,257},{257,1},{2,258},{258,2},{3,259},{259,3},{4... | collective-permute-start | bytes 589832 | tf_op jit(solution)/shard_map/ppermute | solution.py:293
  77.5 3.2 collective-permute-done.2.theirs
  82.3 1.2 place_kernel.3
  83.5 1.2 copy-done.8
  85.6 28.7 %all_to_all.92.sums = f32[16,3,8,128]{3,2,1,0:T(8,128)S(1)} all-to-all(f32[16,3,8,128]{3,2,1,0:T(8,128)S(1)} %get-tuple-element.62), channel_id=1, replica_groups=mesh['xlo'=2,'z'=16,'core'=2,'xhi'=2,'y'=4] {'z'}, dimensions={0} | all-to-all | bytes 393216 | tf_op jit(solution)/shard_map/all_to_all | solution.py:297
  115.0 8.7 %all-to-all-start.5 = ((f32[16,2,8,128]{3,2,1,0:T(8,128)}), f32[16,2,8,128]{3,2,1,0:T(8,128)S(1)}, u32[]{:S(2)}, u32[]{:S(2)}) async-start(f32[16,2,8,128]{3,2,1,0:T(8,128)} %get-tuple-element.64), calls=%async_computation.5 | async-start | bytes 262144 | tf_op jit(solution)/shard_map/all_to_all | solution.py:297
  123.7 4.6 %collective-permute-start.3 = (f32[2,288,256]{2,1,0:T(8,128)}, f32[2,288,256]{2,1,0:T(8,128)S(1)}, u32[]{:S(2)}, u32[]{:S(2)}) collective-permute-start(f32[2,288,256]{2,1,0:T(8,128)} %copy-done.25), channel_id=1, source_target_pairs={{0,8},{8,16},{16,24},{24,32},{32,40},{40,48},{48,56},{56,64},{64,7... | collective-permute-start | bytes 1769480 | tf_op jit(solution)/shard_map/ppermute | solution.py:289
  128.3 1.9 collective-permute-start.4
  130.3 5.4 %all-to-all-done.5.piece0 = f32[16,2,8,128]{3,2,1,0:T(8,128)S(1)} async-done(((f32[16,2,8,128]{3,2,1,0:T(8,128)}), f32[16,2,8,128]{3,2,1,0:T(8,128)S(1)}, u32[]{:S(2)}, u32[]{:S(2)}) %all-to-all-start.5) | async-done | bytes 131104 | tf_op jit(solution)/shard_map/all_to_all | solution.py:297
  135.7 1.9 collective-permute-start.5
  137.6 6.3 %collective-permute-start.6 = (f32[16,2,8,128]{3,2,1,0:T(8,128)S(1)}, f32[16,2,8,128]{3,2,1,0:T(8,128)S(1)}, u32[]{:S(2)}, u32[]{:S(2)}) collective-permute-start(f32[16,2,8,128]{3,2,1,0:T(8,128)S(1)} %all-to-all-done.5.piece0), channel_id=1, source_target_pairs={{0,8},{8,0},{1,9},{9,1},{2,10},{10,2},{3,11},{11,3},{4,12},{12,4},... | collective-permute-start | bytes 393224 | tf_op jit(solution)/shard_map/ppermute | solution.py:293
  143.9 4.1 %collective-permute-start.7 = (f32[16,2,8,128]{3,2,1,0:T(8,128)S(1)}, f32[16,2,8,128]{3,2,1,0:T(8,128)S(1)}, u32[]{:S(2)}, u32[]{:S(2)}) collective-permute-start(f32[16,2,8,128]{3,2,1,0:T(8,128)S(1)} %collective-permute-done.5.piece1), channel_id=1, source_target_pairs={{0,8},{8,0},{1,9},{9,1},{2,10},{10,2},{3,11},{11,3},{4,12},{12,4},... | collective-permute-start | bytes 393224 | tf_op jit(solution)/shard_map/ppermute | solution.py:293
  149.0 1.5 copy-done.9
  151.5 3.0 next_kernel.2
  154.5 14.1 %all_to_all.93.powers = f32[8,32,256]{2,1,0:T(8,128)S(1)} all-to-all(f32[8,32,256]{2,1,0:T(8,128)S(1)} %bitcast.24), channel_id=1, replica_groups=mesh['xlo'=2,'z'=16,'core'=2,'xhi'=2,'y'=4] {'xhi','y'}, dimensions={0} | all-to-all | bytes 524288 | tf_op jit(solution)/shard_map/all_to_all | solution.py:297
  169.2 10.9 %all_to_all.94 = f32[8,32,256]{2,1,0:T(8,128)S(1)} all-to-all(f32[8,32,256]{2,1,0:T(8,128)S(1)} %ratio_kernel.4), channel_id=1, replica_groups=mesh['xlo'=2,'z'=16,'core'=2,'xhi'=2,'y'=4] {'xhi','y'}, dimensions={0} | all-to-all | bytes 524288 | tf_op jit(solution)/shard_map/all_to_all | solution.py:297
  180.1 1.9 backward_kernel.4
  184.4 3.5 all-to-all-start.8
  188.0 4.4 %collective-permute-start.8 = (f32[2,16,3,8,128]{4,3,2,1,0:T(8,128)}, f32[2,16,3,8,128]{4,3,2,1,0:T(8,128)}, u32[]{:S(2)}, u32[]{:S(2)}) collective-permute-start(f32[2,16,3,8,128]{4,3,2,1,0:T(8,128)} %copy-done.29), channel_id=1, source_target_pairs={{0,8},{8,0},{1,9},{9,1},{2,10},{10,2},{3,11},{11,3},{4,12},{12,4},... | collective-permute-start | bytes 1179656 | tf_op jit(solution)/shard_map/ppermute | solution.py:293
  192.4 5.4 %all-to-all-done.8.grads = f32[8,3,32,256]{3,2,1,0:T(8,128)S(1)} async-done(((f32[8,3,32,256]{3,2,1,0:T(8,128)}), f32[8,3,32,256]{3,2,1,0:T(8,128)S(1)}, u32[]{:S(2)}, u32[]{:S(2)}) %all-to-all-start.8) | async-done | bytes 786464 | tf_op jit(solution)/shard_map/all_to_all | solution.py:297
  198.6 6.7 %all-to-all-start.9 = ((f32[8,2,32,256]{3,2,1,0:T(8,128)}), f32[8,2,32,256]{3,2,1,0:T(8,128)S(1)}, u32[]{:S(2)}, u32[]{:S(2)}) async-start(f32[8,2,32,256]{3,2,1,0:T(8,128)} %step_kernel.4), calls=%async_computation.9 | async-start | bytes 1048576 | tf_op jit(solution)/shard_map/all_to_all | solution.py:297
  207.4 2.2 collective-permute-start.9
  209.6 5.9 %collective-permute-done.9.theirs = f32[16,3,8,128]{3,2,1,0:T(8,128)S(1)} collective-permute-done((f32[16,3,8,128]{3,2,1,0:T(8,128)S(1)}, f32[16,3,8,128]{3,2,1,0:T(8,128)S(1)}, u32[]{:S(2)}, u32[]{:S(2)}) %collective-permute-start.9) | collective-permute-done | bytes 196640 | tf_op jit(solution)/shard_map/ppermute | solution.py:293
  217.1 1.2 place_kernel.4
  218.3 1.2 copy-done.6
  220.4 16.6 %all_to_all.95.sums = f32[16,3,8,128]{3,2,1,0:T(8,128)S(1)} all-to-all(f32[16,3,8,128]{3,2,1,0:T(8,128)S(1)} %get-tuple-element.78), channel_id=1, replica_groups=mesh['xlo'=2,'z'=16,'core'=2,'xhi'=2,'y'=4] {'z'}, dimensions={0} | all-to-all | bytes 393216 | tf_op jit(solution)/shard_map/all_to_all | solution.py:297
  237.6 7.8 %all-to-all-start.11 = ((f32[16,2,8,128]{3,2,1,0:T(8,128)}), f32[16,2,8,128]{3,2,1,0:T(8,128)S(1)}, u32[]{:S(2)}, u32[]{:S(2)}) async-start(f32[16,2,8,128]{3,2,1,0:T(8,128)} %get-tuple-element.80), calls=%async_computation.11 | async-start | bytes 262144 | tf_op jit(solution)/shard_map/all_to_all | solution.py:297
  245.4 5.6 %collective-permute-start.10 = (f32[2,288,256]{2,1,0:T(8,128)}, f32[2,288,256]{2,1,0:T(8,128)S(1)}, u32[]{:S(2)}, u32[]{:S(2)}) collective-permute-start(f32[2,288,256]{2,1,0:T(8,128)} %copy-done.26), channel_id=1, source_target_pairs={{0,8},{8,16},{16,24},{24,32},{32,40},{40,48},{48,56},{56,64},{64,7... | collective-permute-start | bytes 1769480 | tf_op jit(solution)/shard_map/ppermute | solution.py:289
  251.0 1.9 collective-permute-start.11
  252.9 4.5 %all-to-all-done.11.piece0 = f32[16,2,8,128]{3,2,1,0:T(8,128)S(1)} async-done(((f32[16,2,8,128]{3,2,1,0:T(8,128)}), f32[16,2,8,128]{3,2,1,0:T(8,128)S(1)}, u32[]{:S(2)}, u32[]{:S(2)}) %all-to-all-start.11) | async-done | bytes 131104 | tf_op jit(solution)/shard_map/all_to_all | solution.py:297
  257.4 2.8 collective-permute-start.12
  260.3 6.4 %collective-permute-start.13 = (f32[16,2,8,128]{3,2,1,0:T(8,128)S(1)}, f32[16,2,8,128]{3,2,1,0:T(8,128)S(1)}, u32[]{:S(2)}, u32[]{:S(2)}) collective-permute-start(f32[16,2,8,128]{3,2,1,0:T(8,128)S(1)} %all-to-all-done.11.piece0), channel_id=1, source_target_pairs={{0,8},{8,0},{1,9},{9,1},{2,10},{10,2},{3,11},{11,3},{4,12},{12,4},... | collective-permute-start | bytes 393224 | tf_op jit(solution)/shard_map/ppermute | solution.py:293
  266.6 3.9 collective-permute-start.14
  271.3 1.5 copy-done.7
  272.8 3.0 next_kernel.3
  275.8 14.5 %all_to_all.96.powers = f32[8,32,256]{2,1,0:T(8,128)S(1)} all-to-all(f32[8,32,256]{2,1,0:T(8,128)S(1)} %bitcast.25), channel_id=1, replica_groups=mesh['xlo'=2,'z'=16,'core'=2,'xhi'=2,'y'=4] {'xhi','y'}, dimensions={0} | all-to-all | bytes 524288 | tf_op jit(solution)/shard_map/all_to_all | solution.py:297
  290.9 10.9 %all_to_all.97 = f32[8,32,256]{2,1,0:T(8,128)S(1)} all-to-all(f32[8,32,256]{2,1,0:T(8,128)S(1)} %ratio_kernel.5), channel_id=1, replica_groups=mesh['xlo'=2,'z'=16,'core'=2,'xhi'=2,'y'=4] {'xhi','y'}, dimensions={0} | all-to-all | bytes 524288 | tf_op jit(solution)/shard_map/all_to_all | solution.py:297
  301.8 2.7 backward_kernel.5
  304.6 3.5 all-to-all-start.14
  308.1 4.4 %collective-permute-start.15 = (f32[2,16,3,8,128]{4,3,2,1,0:T(8,128)S(1)}, f32[2,16,3,8,128]{4,3,2,1,0:T(8,128)S(1)}, u32[]{:S(2)}, u32[]{:S(2)}) collective-permute-start(f32[2,16,3,8,128]{4,3,2,1,0:T(8,128)S(1)} %get-tuple-element.88), channel_id=1, source_target_pairs={{0,8},{8,0},{1,9},{9,1},{2,10},{10,2},{3,11},{11,3},{4,12},{12,4},... | collective-permute-start | bytes 1179656 | tf_op jit(solution)/shard_map/ppermute | solution.py:293
  312.6 5.4 %all-to-all-done.14.grads = f32[8,3,32,256]{3,2,1,0:T(8,128)S(1)} async-done(((f32[8,3,32,256]{3,2,1,0:T(8,128)}), f32[8,3,32,256]{3,2,1,0:T(8,128)S(1)}, u32[]{:S(2)}, u32[]{:S(2)}) %all-to-all-start.14) | async-done | bytes 786464 | tf_op jit(solution)/shard_map/all_to_all | solution.py:297
  318.8 6.7 %all-to-all-start.15 = ((f32[8,2,32,256]{3,2,1,0:T(8,128)}), f32[8,2,32,256]{3,2,1,0:T(8,128)S(1)}, u32[]{:S(2)}, u32[]{:S(2)}) async-start(f32[8,2,32,256]{3,2,1,0:T(8,128)} %step_kernel.5), calls=%async_computation.15 | async-start | bytes 1048576 | tf_op jit(solution)/shard_map/all_to_all | solution.py:297
  326.1 2.2 collective-permute-start.16
  328.3 7.0 %collective-permute-done.16.theirs = f32[16,3,8,128]{3,2,1,0:T(8,128)S(1)} collective-permute-done((f32[16,3,8,128]{3,2,1,0:T(8,128)S(1)}, f32[16,3,8,128]{3,2,1,0:T(8,128)S(1)}, u32[]{:S(2)}, u32[]{:S(2)}) %collective-permute-start.16) | collective-permute-done | bytes 196640 | tf_op jit(solution)/shard_map/ppermute | solution.py:293
  335.2 1.5 copy-done.5
  336.7 2.0 place_kernel.5
  338.7 16.6 %all_to_all.98.sums = f32[16,3,8,128]{3,2,1,0:T(8,128)S(1)} all-to-all(f32[16,3,8,128]{3,2,1,0:T(8,128)S(1)} %get-tuple-element.93), channel_id=1, replica_groups=mesh['xlo'=2,'z'=16,'core'=2,'xhi'=2,'y'=4] {'z'}, dimensions={0} | all-to-all | bytes 393216 | tf_op jit(solution)/shard_map/all_to_all | solution.py:297
  356.0 5.9 %all-to-all-start.17 = ((f32[16,2,8,128]{3,2,1,0:T(8,128)}), f32[16,2,8,128]{3,2,1,0:T(8,128)S(1)}, u32[]{:S(2)}, u32[]{:S(2)}) async-start(f32[16,2,8,128]{3,2,1,0:T(8,128)} %get-tuple-element.95), calls=%async_computation.17 | async-start | bytes 262144 | tf_op jit(solution)/shard_map/all_to_all | solution.py:297
  362.0 7.5 %collective-permute-start.17 = (f32[2,288,256]{2,1,0:T(8,128)}, f32[2,288,256]{2,1,0:T(8,128)S(1)}, u32[]{:S(2)}, u32[]{:S(2)}) collective-permute-start(f32[2,288,256]{2,1,0:T(8,128)} %copy-done.27), channel_id=1, source_target_pairs={{0,8},{8,16},{16,24},{24,32},{32,40},{40,48},{48,56},{56,64},{64,7... | collective-permute-start | bytes 1769480 | tf_op jit(solution)/shard_map/ppermute | solution.py:289
  369.5 4.5 %all-to-all-done.17.piece0 = f32[16,2,8,128]{3,2,1,0:T(8,128)S(1)} async-done(((f32[16,2,8,128]{3,2,1,0:T(8,128)}), f32[16,2,8,128]{3,2,1,0:T(8,128)S(1)}, u32[]{:S(2)}, u32[]{:S(2)}) %all-to-all-start.17) | async-done | bytes 131104 | tf_op jit(solution)/shard_map/all_to_all | solution.py:297
  374.0 4.7 %collective-permute-start.18 = (f32[16,2,8,128]{3,2,1,0:T(8,128)S(1)}, f32[16,2,8,128]{3,2,1,0:T(8,128)S(1)}, u32[]{:S(2)}, u32[]{:S(2)}) collective-permute-start(f32[16,2,8,128]{3,2,1,0:T(8,128)S(1)} %all-to-all-done.17.piece0), channel_id=1, source_target_pairs={{0,256},{256,0},{1,257},{257,1},{2,258},{258,2},{3,259},{259,3},{4... | collective-permute-start | bytes 393224 | tf_op jit(solution)/shard_map/ppermute | solution.py:293
  378.6 6.3 %collective-permute-start.19 = (f32[16,2,8,128]{3,2,1,0:T(8,128)S(1)}, f32[16,2,8,128]{3,2,1,0:T(8,128)S(1)}, u32[]{:S(2)}, u32[]{:S(2)}) collective-permute-start(f32[16,2,8,128]{3,2,1,0:T(8,128)S(1)} %all-to-all-done.17.piece0), channel_id=1, source_target_pairs={{0,8},{8,0},{1,9},{9,1},{2,10},{10,2},{3,11},{11,3},{4,12},{12,4},... | collective-permute-start | bytes 393224 | tf_op jit(solution)/shard_map/ppermute | solution.py:293
  384.9 3.2 collective-permute-start.20
  389.1 1.9 last_kernel.1
  (101 shorter events, 30.7 us)
Async XLA Ops:
  0.6 34.1 %copy-start.2 = (bf16[1,3,256,256]{3,2,1,0:T(8,128)(2,1)S(1)}, bf16[1,3,256,256]{3,2,1,0:T(8,128)(2,1)}, u32[]{:S(2)}) copy-start(bf16[1,3,256,256]{3,2,1,0:T(8,128)(2,1)} %measured.5) | copy-start | bytes 1179652
  1.8 12.5 %collective-permute-start = (f32[2,288,256]{2,1,0:T(8,128)S(1)}, f32[2,288,256]{2,1,0:T(8,128)S(1)}, u32[]{:S(2)}, u32[]{:S(2)}) collective-permute-start(f32[2,288,256]{2,1,0:T(8,128)S(1)} %slice.15), channel_id=1, source_target_pairs={{8,0},{16,8},{24,16},{32,24},{40,32},{48,40},{56,48},{64,56},{72,6... | collective-permute-start | bytes 1769480 | tf_op jit(solution)/shard_map/ppermute | solution.py:289
  14.3 1.0 copy-start
  15.3 1.3 copy-start.3
  16.6 1.0 copy-start.14
  17.6 27.6 %copy-start.1 = (bf16[2,2,256,256]{3,2,1,0:T(8,128)(2,1)S(1)}, bf16[2,2,256,256]{3,2,1,0:T(8,128)(2,1)}, u32[]{:S(2)}) copy-start(bf16[2,2,256,256]{3,2,1,0:T(8,128)(2,1)} %constant.33.clone.tables) | copy-start | bytes 1572868
  47.1 0.9 copy-start.10
  48.0 0.8 copy-start.15
  48.8 0.8 copy-start.28
  49.5 15.2 %all-to-all-start.2 = ((f32[8,3,32,256]{3,2,1,0:T(8,128)}), f32[8,3,32,256]{3,2,1,0:T(8,128)S(1)}, u32[]{:S(2)}, u32[]{:S(2)}) async-start(f32[8,3,32,256]{3,2,1,0:T(8,128)} %copy-done.10), calls=%async_computation.2 | async-start | bytes 1572864 | tf_op jit(solution)/shard_map/all_to_all | solution.py:297
  53.1 16.1 %collective-permute-start.1 = (f32[2,16,3,8,128]{4,3,2,1,0:T(8,128)}, f32[2,16,3,8,128]{4,3,2,1,0:T(8,128)}, u32[]{:S(2)}, u32[]{:S(2)}) collective-permute-start(f32[2,16,3,8,128]{4,3,2,1,0:T(8,128)} %copy-done.28), channel_id=1, source_target_pairs={{0,8},{8,0},{1,9},{9,1},{2,10},{10,2},{3,11},{11,3},{4,12},{12,4},... | collective-permute-start | bytes 1179656 | tf_op jit(solution)/shard_map/ppermute | solution.py:293
  65.6 15.7 %all-to-all-start.3 = ((f32[8,2,32,256]{3,2,1,0:T(8,128)}), f32[8,2,32,256]{3,2,1,0:T(8,128)S(1)}, u32[]{:S(2)}, u32[]{:S(2)}) async-start(f32[8,2,32,256]{3,2,1,0:T(8,128)} %step_kernel.3), calls=%async_computation.3 | async-start | bytes 1048576 | tf_op jit(solution)/shard_map/all_to_all | solution.py:297
  69.2 1.0 copy-start.16
  71.3 9.4 %collective-permute-start.2 = (f32[16,3,8,128]{3,2,1,0:T(8,128)S(1)}, f32[16,3,8,128]{3,2,1,0:T(8,128)S(1)}, u32[]{:S(2)}, u32[]{:S(2)}) collective-permute-start(f32[16,3,8,128]{3,2,1,0:T(8,128)S(1)} %get-tuple-element.58), channel_id=1, source_target_pairs={{0,256},{256,0},{1,257},{257,1},{2,258},{258,2},{3,259},{259,3},{4... | collective-permute-start | bytes 589832 | tf_op jit(solution)/shard_map/ppermute | solution.py:293
  80.7 0.7 copy-start.21
  81.4 0.9 copy-start.22
  83.5 1.2 copy-start.8
  84.7 0.8 copy-start.25
  85.6 29.4 %copy-start.23 = (f32[2,288,256]{2,1,0:T(8,128)}, f32[2,288,256]{2,1,0:T(8,128)S(1)}, u32[]{:S(2)}) copy-start(f32[2,288,256]{2,1,0:T(8,128)S(1)} %get-tuple-element.61) | copy-start | bytes 1769476
  115.0 20.7 %all-to-all-start.5 = ((f32[16,2,8,128]{3,2,1,0:T(8,128)}), f32[16,2,8,128]{3,2,1,0:T(8,128)S(1)}, u32[]{:S(2)}, u32[]{:S(2)}) async-start(f32[16,2,8,128]{3,2,1,0:T(8,128)} %get-tuple-element.64), calls=%async_computation.5 | async-start | bytes 262144 | tf_op jit(solution)/shard_map/all_to_all | solution.py:297
  123.7 24.3 %collective-permute-start.3 = (f32[2,288,256]{2,1,0:T(8,128)}, f32[2,288,256]{2,1,0:T(8,128)S(1)}, u32[]{:S(2)}, u32[]{:S(2)}) collective-permute-start(f32[2,288,256]{2,1,0:T(8,128)} %copy-done.25), channel_id=1, source_target_pairs={{0,8},{8,16},{16,24},{24,32},{32,40},{40,48},{48,56},{56,64},{64,7... | collective-permute-start | bytes 1769480 | tf_op jit(solution)/shard_map/ppermute | solution.py:289
  128.3 19.7 %collective-permute-start.4 = (f32[2,288,256]{2,1,0:T(8,128)}, f32[2,288,256]{2,1,0:T(8,128)S(1)}, u32[]{:S(2)}, u32[]{:S(2)}) collective-permute-start(f32[2,288,256]{2,1,0:T(8,128)} %copy-done.23), channel_id=1, source_target_pairs={{8,0},{16,8},{24,16},{32,24},{40,32},{48,40},{56,48},{64,56},{72,6... | collective-permute-start | bytes 1769480 | tf_op jit(solution)/shard_map/ppermute | solution.py:289
  135.7 8.2 %collective-permute-start.5 = (f32[16,2,8,128]{3,2,1,0:T(8,128)S(1)}, f32[16,2,8,128]{3,2,1,0:T(8,128)S(1)}, u32[]{:S(2)}, u32[]{:S(2)}) collective-permute-start(f32[16,2,8,128]{3,2,1,0:T(8,128)S(1)} %all-to-all-done.5.piece0), channel_id=1, source_target_pairs={{0,256},{256,0},{1,257},{257,1},{2,258},{258,2},{3,259},{259,3},{4... | collective-permute-start | bytes 393224 | tf_op jit(solution)/shard_map/ppermute | solution.py:293
  137.6 11.3 %collective-permute-start.6 = (f32[16,2,8,128]{3,2,1,0:T(8,128)S(1)}, f32[16,2,8,128]{3,2,1,0:T(8,128)S(1)}, u32[]{:S(2)}, u32[]{:S(2)}) collective-permute-start(f32[16,2,8,128]{3,2,1,0:T(8,128)S(1)} %all-to-all-done.5.piece0), channel_id=1, source_target_pairs={{0,8},{8,0},{1,9},{9,1},{2,10},{10,2},{3,11},{11,3},{4,12},{12,4},... | collective-permute-start | bytes 393224 | tf_op jit(solution)/shard_map/ppermute | solution.py:293
  143.9 5.1 %collective-permute-start.7 = (f32[16,2,8,128]{3,2,1,0:T(8,128)S(1)}, f32[16,2,8,128]{3,2,1,0:T(8,128)S(1)}, u32[]{:S(2)}, u32[]{:S(2)}) collective-permute-start(f32[16,2,8,128]{3,2,1,0:T(8,128)S(1)} %collective-permute-done.5.piece1), channel_id=1, source_target_pairs={{0,8},{8,0},{1,9},{9,1},{2,10},{10,2},{3,11},{11,3},{4,12},{12,4},... | collective-permute-start | bytes 393224 | tf_op jit(solution)/shard_map/ppermute | solution.py:293
  148.1 0.8 copy-start.12
  149.0 1.5 copy-start.9
  150.5 1.1 copy-start.13
  182.0 0.9 copy-start.11
  182.9 0.8 copy-start.17
  183.7 0.8 copy-start.29
  184.4 13.4 %all-to-all-start.8 = ((f32[8,3,32,256]{3,2,1,0:T(8,128)}), f32[8,3,32,256]{3,2,1,0:T(8,128)S(1)}, u32[]{:S(2)}, u32[]{:S(2)}) async-start(f32[8,3,32,256]{3,2,1,0:T(8,128)} %copy-done.11), calls=%async_computation.8 | async-start | bytes 1572864 | tf_op jit(solution)/shard_map/all_to_all | solution.py:297
  188.0 17.4 %collective-permute-start.8 = (f32[2,16,3,8,128]{4,3,2,1,0:T(8,128)}, f32[2,16,3,8,128]{4,3,2,1,0:T(8,128)}, u32[]{:S(2)}, u32[]{:S(2)}) collective-permute-start(f32[2,16,3,8,128]{4,3,2,1,0:T(8,128)} %copy-done.29), channel_id=1, source_target_pairs={{0,8},{8,0},{1,9},{9,1},{2,10},{10,2},{3,11},{11,3},{4,12},{12,4},... | collective-permute-start | bytes 1179656 | tf_op jit(solution)/shard_map/ppermute | solution.py:293
  198.6 17.5 %all-to-all-start.9 = ((f32[8,2,32,256]{3,2,1,0:T(8,128)}), f32[8,2,32,256]{3,2,1,0:T(8,128)S(1)}, u32[]{:S(2)}, u32[]{:S(2)}) async-start(f32[8,2,32,256]{3,2,1,0:T(8,128)} %step_kernel.4), calls=%async_computation.9 | async-start | bytes 1048576 | tf_op jit(solution)/shard_map/all_to_all | solution.py:297
  205.3 1.0 copy-start.18
  207.4 8.1 %collective-permute-start.9 = (f32[16,3,8,128]{3,2,1,0:T(8,128)S(1)}, f32[16,3,8,128]{3,2,1,0:T(8,128)S(1)}, u32[]{:S(2)}, u32[]{:S(2)}) collective-permute-start(f32[16,3,8,128]{3,2,1,0:T(8,128)S(1)} %get-tuple-element.74), channel_id=1, source_target_pairs={{0,256},{256,0},{1,257},{257,1},{2,258},{258,2},{3,259},{259,3},{4... | collective-permute-start | bytes 589832 | tf_op jit(solution)/shard_map/ppermute | solution.py:293
  215.5 0.7 copy-start.19
  216.2 0.9 copy-start.20
  218.3 1.2 copy-start.6
  219.5 0.8 copy-start.26
  220.4 17.3 %copy-start.24 = (f32[2,288,256]{2,1,0:T(8,128)}, f32[2,288,256]{2,1,0:T(8,128)S(1)}, u32[]{:S(2)}) copy-start(f32[2,288,256]{2,1,0:T(8,128)S(1)} %get-tuple-element.77) | copy-start | bytes 1769476
  237.6 19.8 %all-to-all-start.11 = ((f32[16,2,8,128]{3,2,1,0:T(8,128)}), f32[16,2,8,128]{3,2,1,0:T(8,128)S(1)}, u32[]{:S(2)}, u32[]{:S(2)}) async-start(f32[16,2,8,128]{3,2,1,0:T(8,128)} %get-tuple-element.80), calls=%async_computation.11 | async-start | bytes 262144 | tf_op jit(solution)/shard_map/all_to_all | solution.py:297
  245.4 25.1 %collective-permute-start.10 = (f32[2,288,256]{2,1,0:T(8,128)}, f32[2,288,256]{2,1,0:T(8,128)S(1)}, u32[]{:S(2)}, u32[]{:S(2)}) collective-permute-start(f32[2,288,256]{2,1,0:T(8,128)} %copy-done.26), channel_id=1, source_target_pairs={{0,8},{8,16},{16,24},{24,32},{32,40},{40,48},{48,56},{56,64},{64,7... | collective-permute-start | bytes 1769480 | tf_op jit(solution)/shard_map/ppermute | solution.py:289
  251.0 19.5 %collective-permute-start.11 = (f32[2,288,256]{2,1,0:T(8,128)}, f32[2,288,256]{2,1,0:T(8,128)S(1)}, u32[]{:S(2)}, u32[]{:S(2)}) collective-permute-start(f32[2,288,256]{2,1,0:T(8,128)} %copy-done.24), channel_id=1, source_target_pairs={{8,0},{16,8},{24,16},{32,24},{40,32},{48,40},{56,48},{64,56},{72,6... | collective-permute-start | bytes 1769480 | tf_op jit(solution)/shard_map/ppermute | solution.py:289
  257.4 9.2 %collective-permute-start.12 = (f32[16,2,8,128]{3,2,1,0:T(8,128)S(1)}, f32[16,2,8,128]{3,2,1,0:T(8,128)S(1)}, u32[]{:S(2)}, u32[]{:S(2)}) collective-permute-start(f32[16,2,8,128]{3,2,1,0:T(8,128)S(1)} %all-to-all-done.11.piece0), channel_id=1, source_target_pairs={{0,256},{256,0},{1,257},{257,1},{2,258},{258,2},{3,259},{259,3},{4... | collective-permute-start | bytes 393224 | tf_op jit(solution)/shard_map/ppermute | solution.py:293
  260.3 10.3 %collective-permute-start.13 = (f32[16,2,8,128]{3,2,1,0:T(8,128)S(1)}, f32[16,2,8,128]{3,2,1,0:T(8,128)S(1)}, u32[]{:S(2)}, u32[]{:S(2)}) collective-permute-start(f32[16,2,8,128]{3,2,1,0:T(8,128)S(1)} %all-to-all-done.11.piece0), channel_id=1, source_target_pairs={{0,8},{8,0},{1,9},{9,1},{2,10},{10,2},{3,11},{11,3},{4,12},{12,4},... | collective-permute-start | bytes 393224 | tf_op jit(solution)/shard_map/ppermute | solution.py:293
  266.6 4.7 %collective-permute-start.14 = (f32[16,2,8,128]{3,2,1,0:T(8,128)S(1)}, f32[16,2,8,128]{3,2,1,0:T(8,128)S(1)}, u32[]{:S(2)}, u32[]{:S(2)}) collective-permute-start(f32[16,2,8,128]{3,2,1,0:T(8,128)S(1)} %collective-permute-done.12.piece1), channel_id=1, source_target_pairs={{0,8},{8,0},{1,9},{9,1},{2,10},{10,2},{3,11},{11,3},{4,12},{12,4},... | collective-permute-start | bytes 393224 | tf_op jit(solution)/shard_map/ppermute | solution.py:293
  271.3 1.5 copy-start.7
  275.8 28.8 %copy-start.4 = (f32[2,288,768]{2,1,0:T(8,128)}, f32[2,288,768]{2,1,0:T(8,128)S(1)}, u32[]{:S(2)}) copy-start(f32[2,288,768]{2,1,0:T(8,128)S(1)} %get-tuple-element.86.extended) | copy-start | bytes 5308420
  304.6 13.4 %all-to-all-start.14 = ((f32[8,3,32,256]{3,2,1,0:T(8,128)}), f32[8,3,32,256]{3,2,1,0:T(8,128)S(1)}, u32[]{:S(2)}, u32[]{:S(2)}) async-start(f32[8,3,32,256]{3,2,1,0:T(8,128)} %get-tuple-element.85), calls=%async_computation.14 | async-start | bytes 1572864 | tf_op jit(solution)/shard_map/all_to_all | solution.py:297
  308.1 17.4 %collective-permute-start.15 = (f32[2,16,3,8,128]{4,3,2,1,0:T(8,128)S(1)}, f32[2,16,3,8,128]{4,3,2,1,0:T(8,128)S(1)}, u32[]{:S(2)}, u32[]{:S(2)}) collective-permute-start(f32[2,16,3,8,128]{4,3,2,1,0:T(8,128)S(1)} %get-tuple-element.88), channel_id=1, source_target_pairs={{0,8},{8,0},{1,9},{9,1},{2,10},{10,2},{3,11},{11,3},{4,12},{12,4},... | collective-permute-start | bytes 1179656 | tf_op jit(solution)/shard_map/ppermute | solution.py:293
  318.8 16.4 %all-to-all-start.15 = ((f32[8,2,32,256]{3,2,1,0:T(8,128)}), f32[8,2,32,256]{3,2,1,0:T(8,128)S(1)}, u32[]{:S(2)}, u32[]{:S(2)}) async-start(f32[8,2,32,256]{3,2,1,0:T(8,128)} %step_kernel.5), calls=%async_computation.15 | async-start | bytes 1048576 | tf_op jit(solution)/shard_map/all_to_all | solution.py:297
  326.1 9.1 %collective-permute-start.16 = (f32[16,3,8,128]{3,2,1,0:T(8,128)S(1)}, f32[16,3,8,128]{3,2,1,0:T(8,128)S(1)}, u32[]{:S(2)}, u32[]{:S(2)}) collective-permute-start(f32[16,3,8,128]{3,2,1,0:T(8,128)S(1)} %get-tuple-element.90), channel_id=1, source_target_pairs={{0,256},{256,0},{1,257},{257,1},{2,258},{258,2},{3,259},{259,3},{4... | collective-permute-start | bytes 589832 | tf_op jit(solution)/shard_map/ppermute | solution.py:293
  335.2 1.5 copy-start.5
  338.7 17.3 %copy-start.27 = (f32[2,288,256]{2,1,0:T(8,128)}, f32[2,288,256]{2,1,0:T(8,128)S(1)}, u32[]{:S(2)}) copy-start(f32[2,288,256]{2,1,0:T(8,128)S(1)} %get-tuple-element.92) | copy-start | bytes 1769476
  356.0 17.9 %all-to-all-start.17 = ((f32[16,2,8,128]{3,2,1,0:T(8,128)}), f32[16,2,8,128]{3,2,1,0:T(8,128)S(1)}, u32[]{:S(2)}, u32[]{:S(2)}) async-start(f32[16,2,8,128]{3,2,1,0:T(8,128)} %get-tuple-element.95), calls=%async_computation.17 | async-start | bytes 262144 | tf_op jit(solution)/shard_map/all_to_all | solution.py:297
  362.0 26.2 %collective-permute-start.17 = (f32[2,288,256]{2,1,0:T(8,128)}, f32[2,288,256]{2,1,0:T(8,128)S(1)}, u32[]{:S(2)}, u32[]{:S(2)}) collective-permute-start(f32[2,288,256]{2,1,0:T(8,128)} %copy-done.27), channel_id=1, source_target_pairs={{0,8},{8,16},{16,24},{24,32},{32,40},{40,48},{48,56},{56,64},{64,7... | collective-permute-start | bytes 1769480 | tf_op jit(solution)/shard_map/ppermute | solution.py:289
  374.0 11.0 %collective-permute-start.18 = (f32[16,2,8,128]{3,2,1,0:T(8,128)S(1)}, f32[16,2,8,128]{3,2,1,0:T(8,128)S(1)}, u32[]{:S(2)}, u32[]{:S(2)}) collective-permute-start(f32[16,2,8,128]{3,2,1,0:T(8,128)S(1)} %all-to-all-done.17.piece0), channel_id=1, source_target_pairs={{0,256},{256,0},{1,257},{257,1},{2,258},{258,2},{3,259},{259,3},{4... | collective-permute-start | bytes 393224 | tf_op jit(solution)/shard_map/ppermute | solution.py:293
  378.6 9.5 %collective-permute-start.19 = (f32[16,2,8,128]{3,2,1,0:T(8,128)S(1)}, f32[16,2,8,128]{3,2,1,0:T(8,128)S(1)}, u32[]{:S(2)}, u32[]{:S(2)}) collective-permute-start(f32[16,2,8,128]{3,2,1,0:T(8,128)S(1)} %all-to-all-done.17.piece0), channel_id=1, source_target_pairs={{0,8},{8,0},{1,9},{9,1},{2,10},{10,2},{3,11},{11,3},{4,12},{12,4},... | collective-permute-start | bytes 393224 | tf_op jit(solution)/shard_map/ppermute | solution.py:293
  384.9 4.2 %collective-permute-start.20 = (f32[16,2,8,128]{3,2,1,0:T(8,128)S(1)}, f32[16,2,8,128]{3,2,1,0:T(8,128)S(1)}, u32[]{:S(2)}, u32[]{:S(2)}) collective-permute-start(f32[16,2,8,128]{3,2,1,0:T(8,128)S(1)} %collective-permute-done.18.piece1), channel_id=1, source_target_pairs={{0,8},{8,0},{1,9},{9,1},{2,10},{10,2},{3,11},{11,3},{4,12},{12,4},... | collective-permute-start | bytes 393224 | tf_op jit(solution)/shard_map/ppermute | solution.py:293

commit v2 on v1

--- a/solution.py
+++ b/solution.py
@@ -26,6 +26,7 @@
 RINGS = 16
 ROW_SPAN = SIDE + 8
 COL_SPAN = SIDE + 128
+VMEM_LIMIT = 16 * 1024 * 1024
 
 TILE_AXES = ("xlo", "z", "core")
 MODE_AXES = ("xhi", "y")
@@ -88,13 +89,16 @@
     return rows, cols, row - row_block * 8, col - col_block * 128
 
 
-def forward(scal, extended, view, probe, tables, far, power):
+def take_patch(scal, extended, view):
     rows, cols, row_rest, col_rest = window(scal)
     for part in range(2):
         block = extended[part, rows, cols]
         block = pltpu.roll(block, lax.rem(COL_SPAN - col_rest, COL_SPAN), 1)[:, :SIDE]
         block = pltpu.roll(block, lax.rem(ROW_SPAN - row_rest, ROW_SPAN), 0)[:SIDE]
         view[part] = block
+
+
+def forward(view, probe, tables, far, power):
     view_real, view_imag = view[0], view[1]
     probe_real, probe_imag = probe[0], probe[1]
     far_real, far_imag = transform(
@@ -122,7 +126,8 @@
     def _():
         shard[...] = probe_in[0, :, pl.ds(row, 8), 128:]
 
-    forward(scal, extended, view, probe, tables, far, power)
+    take_patch(scal, extended, view)
+    forward(view, probe, tables, far, power)
 
 
 def untile_probe(scal, pieces, store):
@@ -135,31 +140,19 @@
             store(row, ring % 2 * 128, piece[ring])
 
 
-def next_kernel(
-    scal,
-    part_object,
-    from_left,
-    from_right,
-    piece0,
-    piece1,
-    piece2,
-    piece3,
-    tables,
-    extended,
-    view,
-    probe,
-    far,
-    power,
-):
+def view_kernel(scal, part_object, from_left, from_right, extended, view):
     extended[:, :, :SIDE] = part_object[:, :, :SIDE] + from_left[...]
     extended[:, :, SIDE:WIDTH] = part_object[:, :, SIDE:WIDTH]
     extended[:, :, WIDTH:] = part_object[:, :, WIDTH:] + from_right[...]
-
+    take_patch(scal, extended, view)
+
+
+def next_kernel(scal, view, piece0, piece1, piece2, piece3, tables, probe, far, power):
     def store(row, col, value):
         probe[:, pl.ds(row, 8), col : col + 128] = value
 
     untile_probe(scal, (piece0, piece1, piece2, piece3), store)
-    forward(scal, extended, view, probe, tables, far, power)
+    forward(view, probe, tables, far, power)
 
 
 def last_kernel(
@@ -186,19 +179,12 @@
         copies[mode] = ratio
 
 
-def backward_kernel(scal, far, ratio_in, view, probe, tables, grads, keep, send):
+def backward_kernel(scal, far, ratio_in, view, tables, chi, keep, send):
     ratio = ratio_in[...]
     chi_real, chi_imag = transform(far[0] * ratio, far[1] * ratio, tables, -1.0)
-    probe_real, probe_imag = probe[0], probe[1]
+    chi[0] = chi_real
+    chi[1] = chi_imag
     view_real, view_imag = view[0], view[1]
-    grad_real = probe_real * chi_real + probe_imag * chi_imag
-    grad_imag = probe_real * chi_imag - probe_imag * chi_real
-    light = probe_real * probe_real + probe_imag * probe_imag
-    for mode in range(MODES):
-        rows = slice(mode * SLAB, mode * SLAB + SLAB)
-        grads[mode, 0] = grad_real[rows]
-        grads[mode, 1] = grad_imag[rows]
-        grads[mode, 2] = light[rows]
     sums = (
         view_real * chi_real + view_imag * chi_imag,
         view_real * chi_imag - view_imag * chi_real,
@@ -224,28 +210,46 @@
         put(send, 0)
 
 
+def gradient_kernel(after, chi, probe, grads):
+    del after
+    for mode in range(MODES):
+        rows = slice(mode * SLAB, mode * SLAB + SLAB)
+        chi_real, chi_imag = chi[0, rows], chi[1, rows]
+        probe_real, probe_imag = probe[0, rows], probe[1, rows]
+        grads[mode, 0] = probe_real * chi_real + probe_imag * chi_imag
+        grads[mode, 1] = probe_real * chi_imag - probe_imag * chi_real
+        grads[mode, 2] = probe_real * probe_real + probe_imag * probe_imag
+
+
 def halve_kernel(scal, mine, theirs, keep, send):
     xlo = scal[XLO]
     keep[...] = mine[xlo] + theirs[xlo]
     send[...] = mine[1 - xlo] + theirs[1 - xlo]
 
 
-def step_kernel(grads, copies):
+def step_kernel(after, grads, step):
+    del after
     total = grads[0]
     for mode in range(1, MODES):
         total = total + grads[mode]
-    step = OBJECT_RATE * total[:2] / (total[2:] + OBJECT_DAMP)
-    for mode in range(MODES):
-        copies[mode] = step
-
-
-def place_kernel(scal, steps, extended, mine, theirs, part_object, to_left, to_right, sums):
-    sums[...] = mine[...] + theirs[...]
+    step[...] = OBJECT_RATE * total[:2] / (total[2:] + OBJECT_DAMP)
+
+
+def place_kernel(scal, after, mine, theirs, extended, part_object, to_left, to_right):
+    del after
+    first = scal[MODE] < MODES // 2
     rows, cols, row_rest, col_rest = window(scal)
     part_object[...] = jnp.zeros_like(part_object)
     for part in range(2):
+        own = jnp.concatenate([mine[mode, part] for mode in range(MODES // 2)], axis=0)
+        far = jnp.concatenate([theirs[mode, part] for mode in range(MODES // 2)], axis=0)
         block = jnp.concatenate(
-            [steps[mode, part] for mode in range(MODES)] + [jnp.zeros((8, SIDE), F32)], axis=0
+            [
+                jnp.where(first, own, far),
+                jnp.where(first, far, own),
+                jnp.zeros((ROW_SPAN - SIDE, SIDE), F32),
+            ],
+            axis=0,
         )
         block = pltpu.roll(block, row_rest, 0)
         block = jnp.concatenate([block, jnp.zeros((ROW_SPAN, 128), F32)], axis=1)
@@ -269,17 +273,19 @@
         copies[ring] = new
 
 
-def call(kernel, outs, *args, scalars=True):
+def call(kernel, outs, *args, scalars=True, after=False):
     vmem = pl.BlockSpec(memory_space=pltpu.VMEM)
     in_specs = [vmem] * len(args)
     if scalars:
         in_specs[0] = pl.BlockSpec(memory_space=pltpu.SMEM)
+    if after:
+        in_specs[int(scalars)] = pl.BlockSpec(memory_space=pl.ANY)
     return pl.pallas_call(
         kernel,
         out_shape=[jax.ShapeDtypeStruct(shape, F32) for shape in outs],
         in_specs=in_specs,
         out_specs=[vmem] * len(outs),
-        compiler_params=pltpu.CompilerParams(vmem_limit_bytes=32 * 1024 * 1024),
+        compiler_params=pltpu.CompilerParams(vmem_limit_bytes=VMEM_LIMIT),
         name=kernel.__name__,
     )(*args)
 
@@ -338,52 +344,55 @@
                 tables,
             )
         else:
-            extended, view, probe, far, power = call(
-                next_kernel,
-                [extended_shape, pair, pair, pair, plane],
-                scal,
-                part_object,
-                from_left,
-                from_right,
-                *pieces,
-                tables,
+            extended, view = call(
+                view_kernel, [extended_shape, pair], scal, part_object, from_left, from_right
+            )
+            probe, far, power = call(
+                next_kernel, [pair, pair, plane], scal, view, *pieces, tables
             )
         powers = exchange(power.reshape(MODES, SLAB, SIDE), MODE_AXES)
         (copies,) = call(ratio_kernel, [(MODES, SLAB, SIDE)], scal, powers, measured)
         ratio = exchange(copies, MODE_AXES).reshape(SIDE, SIDE)
-        grads, keep, send = call(
+        chi, keep, send = call(
             backward_kernel,
-            [(MODES, 3, SLAB, SIDE)] + [(2, RINGS, 3, 8, 128)] * 2,
+            [pair] + [(2, RINGS, 3, 8, 128)] * 2,
             scal,
             far,
             ratio,
             view,
-            probe,
             tables,
         )
         received = other(send, "core")
-        grads = exchange(grads, MODE_AXES)
         keep, send = call(halve_kernel, [(RINGS, 3, 8, 128)] * 2, scal, keep, received)
         received = other(send, "xlo")
-        (copies,) = call(step_kernel, [(MODES, 2, SLAB, SIDE)], grads, scalars=False)
-        steps = exchange(copies, MODE_AXES)
-        part_object, to_left, to_right, sums = call(
+        (grads,) = call(
+            gradient_kernel, [(MODES, 3, SLAB, SIDE)], keep, chi, probe, scalars=False, after=True
+        )
+        grads = exchange(grads, MODE_AXES)
+        sums = keep + received
+        (object_step,) = call(
+            step_kernel, [(2, SLAB, SIDE)], sums, grads, scalars=False, after=True
+        )
+        sums = exchange(sums, "z")
+        shard, shards = call(
+            probe_kernel, [(2, 8, 128), (RINGS, 2, 8, 128)], sums, shard, scalars=False
+        )
+        near_steps = lax.all_gather(object_step, "y")
+        far_steps = other(near_steps, "xhi")
+        part_object, to_left, to_right = call(
             place_kernel,
-            [extended_shape, edge, edge, (RINGS, 3, 8, 128)],
+            [extended_shape, edge, edge],
             scal,
-            steps,
+            shards,
+            near_steps,
+            far_steps,
             extended,
-            keep,
-            received,
+            after=True,
         )
         from_left = shift_tile(to_right, 1)
         if step < STEPS - 1:
             from_right = shift_tile(to_left, -1)
-        sums = exchange(sums, "z")
-        shard, copies = call(
-            probe_kernel, [(2, 8, 128), (RINGS, 2, 8, 128)], sums, shard, scalars=False
-        )
-        piece = exchange(copies, "z")
+        piece = exchange(shards, "z")
         beyond = other(piece, "xlo")
         pieces = (piece, beyond, other(piece, "core"), other(beyond, "core"))
     return call(

time: 393 us -> 386 us (0.982)
  starting transfers between devices: 141 us -> 188 us
  blocking collectives: 136 us -> 99.1 us
  waiting for transfers between devices: 53.1 us -> 41.7 us
  local copies, waits for them, and re-layouts: 26 us -> 14.9 us
    all_to_all x9 -> x6, blocking collectives: 136 us -> 68.5 us  [exchange(): return lax.all_to_all(value, axes, 0, 0, tiled=True)]
    all_to_all x9, waiting for transfers between devices: 34.9 us -> 0.02 us  [exchange(): return lax.all_to_all(value, axes, 0, 0, tiled=True)]
    all_gather x0 -> x3, blocking collectives: none -> 30.6 us  [per_device(): near_steps = lax.all_gather(object_step, 'y')]
    ppermute x15 -> x18, waiting for transfers between devices: 17.9 us -> 41.4 us  [other(): return lax.ppermute(value, axis, [(0, 1), (1, 0)])]
    ppermute x15 -> x18, starting transfers between devices: 60.9 us -> 82 us  [other(): return lax.ppermute(value, axis, [(0, 1), (1, 0)])]
    all_to_all x9, starting transfers between devices: 50 us -> 70 us  [exchange(): return lax.all_to_all(value, axes, 0, 0, tiled=True)]
    unnamed x60 -> x30, local copies, waits for them, and re-layouts: 23.7 us -> 12.6 us
    ppermute x6, starting transfers between devices: 30.3 us -> 36.4 us  [shift_tile(): lax.ppermute(value, TILE_AXES, [(i, i + steps) for i in range(first, last)])]
  transfers between devices with their start and end apart: 30 -> 33, of which waited for: 13 -> 9; matrix products, arithmetic and copies ran while one was open for 1% -> 1% of each run, Pallas kernels for 1% -> 3%
where the time goes in v2:
time: 386 us; the launch traced here: 384 us
  starting transfers between devices  188 us (49%)
  blocking collectives  99.1 us (26%)
  waiting for transfers between devices  41.7 us (11%)
  Pallas kernels  33.8 us (9%)
  local copies, waits for them, and re-layouts  14.9 us (4%)
    ppermute x18, starting transfers between devices, other(): return lax.ppermute(value, axis, [(0, 1), (1, 0)])  82 us
    all_to_all x9, starting transfers between devices, exchange(): return lax.all_to_all(value, axes, 0, 0, tiled=True)  70 us
    all_to_all x6, blocking collectives, exchange(): return lax.all_to_all(value, axes, 0, 0, tiled=True)  68.5 us
    ppermute x18, waiting for transfers between devices, other(): return lax.ppermute(value, axis, [(0, 1), (1, 0)])  41.4 us
    ppermute x6, starting transfers between devices, shift_tile(): lax.ppermute(value, TILE_AXES, [(i, i + steps) for i in range(first, last)])  36.4 us
    pallas_call x27, Pallas kernels, call(): pl.pallas_call(kernel, out_shape=[jax.ShapeDtypeStruct(shape, F32) for sh...  33.8 us
    all_gather x3, blocking collectives, per_device(): near_steps = lax.all_gather(object_step, 'y')  30.6 us
    unnamed x30, local copies, waits for them, and re-layouts  12.6 us
  transfers between devices with their start and end apart: 33, of which 9 were waited for; matrix products, arithmetic and copies ran while one was open for 1% of the time, Pallas kernels for 3%

profile of v2, /device:TPU:1, one launch (start us, length us, event | category | flops | bytes accessed | tf_op | source)
XLA Modules:
  0.0 383.6 jit_solution(2510502202619844511)
XLA Ops:
  1.8 8.8 %collective-permute-start = (f32[2,288,256]{2,1,0:T(8,128)S(1)}, f32[2,288,256]{2,1,0:T(8,128)S(1)}, u32[]{:S(2)}, u32[]{:S(2)}) collective-permute-start(f32[2,288,256]{2,1,0:T(8,128)S(1)} %slice.15), channel_id=1, source_target_pairs={{8,0},{16,8},{24,16},{32,24},{40,32},{48,40},{56,48},{64,56},{72,6... | collective-permute-start | bytes 1769480 | tf_op jit(solution)/shard_map/ppermute | solution.py:295
  15.3 1.3 copy-done.3
  17.7 3.0 first_kernel.1
  21.9 14.0 %all_to_all.75.powers = f32[8,32,256]{2,1,0:T(8,128)S(1)} all-to-all(f32[8,32,256]{2,1,0:T(8,128)S(1)} %bitcast.33), channel_id=1, replica_groups=mesh['xlo'=2,'z'=16,'core'=2,'xhi'=2,'y'=4] {'xhi','y'}, dimensions={0} | all-to-all | bytes 524288 | tf_op jit(solution)/shard_map/all_to_all | solution.py:303
  36.5 10.0 %all_to_all.76 = f32[8,32,256]{2,1,0:T(8,128)S(1)} all-to-all(f32[8,32,256]{2,1,0:T(8,128)S(1)} %ratio_kernel.3), channel_id=1, replica_groups=mesh['xlo'=2,'z'=16,'core'=2,'xhi'=2,'y'=4] {'xhi','y'}, dimensions={0} | all-to-all | bytes 524288 | tf_op jit(solution)/shard_map/all_to_all | solution.py:303
  46.5 1.8 backward_kernel.3
  48.3 1.9 collective-permute-start.1
  50.2 1.7 collective-permute-done.1.theirs
  53.5 3.5 all-to-all-start.3
  57.1 12.3 %collective-permute-start.2 = (f32[16,3,8,128]{3,2,1,0:T(8,128)S(1)}, f32[16,3,8,128]{3,2,1,0:T(8,128)S(1)}, u32[]{:S(2)}, u32[]{:S(2)}) collective-permute-start(f32[16,3,8,128]{3,2,1,0:T(8,128)S(1)} %get-tuple-element.52), channel_id=1, source_target_pairs={{0,256},{256,0},{1,257},{257,1},{2,258},{258,2},{3,259},{259,3},{4... | collective-permute-start | bytes 589832 | tf_op jit(solution)/shard_map/ppermute | solution.py:299
  69.4 11.6 %collective-permute-done.2 = f32[16,3,8,128]{3,2,1,0:T(8,128)S(1)} collective-permute-done((f32[16,3,8,128]{3,2,1,0:T(8,128)S(1)}, f32[16,3,8,128]{3,2,1,0:T(8,128)S(1)}, u32[]{:S(2)}, u32[]{:S(2)}) %collective-permute-start.2) | collective-permute-done | bytes 196640 | tf_op jit(solution)/shard_map/ppermute | solution.py:299
  81.7 7.2 %all-to-all-start.2 = ((f32[16,3,8,128]{3,2,1,0:T(8,128)}), f32[16,3,8,128]{3,2,1,0:T(8,128)S(1)}, u32[]{:S(2)}, u32[]{:S(2)}) async-start(f32[16,3,8,128]{3,2,1,0:T(8,128)} %add.21.after), calls=%async_computation.2 | async-start | bytes 393216 | tf_op jit(solution)/shard_map/all_to_all | solution.py:303
  88.9 10.2 %all-gather = f32[8,32,256]{2,1,0:T(8,128)S(1)} all-gather(f32[2,32,256]{2,1,0:T(8,128)S(1)} %step_kernel.3), channel_id=2, replica_groups=mesh['xlo'=2,'z'=16,'core'=2,'xhi'=2,'y'=4] {'y'}, dimensions={0}, use_global_device_ids=true | all-gather | bytes 327680 | tf_op jit(solution)/shard_map/all_gather | solution.py:380
  99.1 5.3 %collective-permute-start.3 = (f32[4,2,32,256]{3,2,1,0:T(8,128)S(1)}, f32[4,2,32,256]{3,2,1,0:T(8,128)S(1)}, u32[]{:S(2)}, u32[]{:S(2)}) collective-permute-start(f32[4,2,32,256]{3,2,1,0:T(8,128)S(1)} %bitcast.31), channel_id=1, source_target_pairs={{0,4},{4,0},{1,5},{5,1},{2,6},{6,2},{3,7},{7,3},{8,12},{12,8},{9,1... | collective-permute-start | bytes 786440 | tf_op jit(solution)/shard_map/ppermute | solution.py:299
  105.2 11.5 %all-to-all-start.4 = ((f32[16,2,8,128]{3,2,1,0:T(8,128)}), f32[16,2,8,128]{3,2,1,0:T(8,128)S(1)}, u32[]{:S(2)}, u32[]{:S(2)}) async-start(f32[16,2,8,128]{3,2,1,0:T(8,128)} %get-tuple-element.54.after), calls=%async_computation.4 | async-start | bytes 262144 | tf_op jit(solution)/shard_map/all_to_all | solution.py:303
  116.7 1.5 copy-done.9
  118.2 2.1 place_kernel.3
  120.3 7.9 %collective-permute-start.4 = (f32[2,288,256]{2,1,0:T(8,128)}, f32[2,288,256]{2,1,0:T(8,128)S(1)}, u32[]{:S(2)}, u32[]{:S(2)}) collective-permute-start(f32[2,288,256]{2,1,0:T(8,128)} %get-tuple-element.59), channel_id=1, source_target_pairs={{0,8},{8,16},{16,24},{24,32},{32,40},{40,48},{48,56},{56,64},{64,7... | collective-permute-start | bytes 1769480 | tf_op jit(solution)/shard_map/ppermute | solution.py:295
  128.3 1.9 collective-permute-start.5
  130.2 1.9 collective-permute-start.6
  132.1 6.2 %collective-permute-start.7 = (f32[16,2,8,128]{3,2,1,0:T(8,128)S(1)}, f32[16,2,8,128]{3,2,1,0:T(8,128)S(1)}, u32[]{:S(2)}, u32[]{:S(2)}) collective-permute-start(f32[16,2,8,128]{3,2,1,0:T(8,128)S(1)} %all-to-all-done.4.piece0), channel_id=1, source_target_pairs={{0,8},{8,0},{1,9},{9,1},{2,10},{10,2},{3,11},{11,3},{4,12},{12,4},... | collective-permute-start | bytes 393224 | tf_op jit(solution)/shard_map/ppermute | solution.py:299
  138.4 4.8 %collective-permute-start.8 = (f32[16,2,8,128]{3,2,1,0:T(8,128)S(1)}, f32[16,2,8,128]{3,2,1,0:T(8,128)S(1)}, u32[]{:S(2)}, u32[]{:S(2)}) collective-permute-start(f32[16,2,8,128]{3,2,1,0:T(8,128)S(1)} %collective-permute-done.6.piece1), channel_id=1, source_target_pairs={{0,8},{8,0},{1,9},{9,1},{2,10},{10,2},{3,11},{11,3},{4,12},{12,4},... | collective-permute-start | bytes 393224 | tf_op jit(solution)/shard_map/ppermute | solution.py:299
  143.2 1.6 view_kernel.2
  146.1 2.5 next_kernel.2
  148.6 10.8 %all_to_all.77.powers = f32[8,32,256]{2,1,0:T(8,128)S(1)} all-to-all(f32[8,32,256]{2,1,0:T(8,128)S(1)} %bitcast.34), channel_id=1, replica_groups=mesh['xlo'=2,'z'=16,'core'=2,'xhi'=2,'y'=4] {'xhi','y'}, dimensions={0} | all-to-all | bytes 524288 | tf_op jit(solution)/shard_map/all_to_all | solution.py:303
  160.0 11.5 %all_to_all.78 = f32[8,32,256]{2,1,0:T(8,128)S(1)} all-to-all(f32[8,32,256]{2,1,0:T(8,128)S(1)} %ratio_kernel.4), channel_id=1, replica_groups=mesh['xlo'=2,'z'=16,'core'=2,'xhi'=2,'y'=4] {'xhi','y'}, dimensions={0} | all-to-all | bytes 524288 | tf_op jit(solution)/shard_map/all_to_all | solution.py:303
  171.4 1.8 backward_kernel.4
  173.2 4.0 %collective-permute-start.9 = (f32[2,16,3,8,128]{4,3,2,1,0:T(8,128)S(1)}, f32[2,16,3,8,128]{4,3,2,1,0:T(8,128)S(1)}, u32[]{:S(2)}, u32[]{:S(2)}) collective-permute-start(f32[2,16,3,8,128]{4,3,2,1,0:T(8,128)S(1)} %get-tuple-element.65), channel_id=1, source_target_pairs={{0,8},{8,0},{1,9},{9,1},{2,10},{10,2},{3,11},{11,3},{4,12},{12,4},... | collective-permute-start | bytes 1179656 | tf_op jit(solution)/shard_map/ppermute | solution.py:299
  177.2 1.3 collective-permute-done.9.theirs
  180.1 3.5 all-to-all-start.8
  183.7 2.4 collective-permute-start.10
  186.1 11.6 %collective-permute-done.10 = f32[16,3,8,128]{3,2,1,0:T(8,128)S(1)} collective-permute-done((f32[16,3,8,128]{3,2,1,0:T(8,128)S(1)}, f32[16,3,8,128]{3,2,1,0:T(8,128)S(1)}, u32[]{:S(2)}, u32[]{:S(2)}) %collective-permute-start.10) | collective-permute-done | bytes 196640 | tf_op jit(solution)/shard_map/ppermute | solution.py:299
  198.5 8.9 %all-to-all-start.7 = ((f32[16,3,8,128]{3,2,1,0:T(8,128)}), f32[16,3,8,128]{3,2,1,0:T(8,128)S(1)}, u32[]{:S(2)}, u32[]{:S(2)}) async-start(f32[16,3,8,128]{3,2,1,0:T(8,128)} %add.22.after), calls=%async_computation.7 | async-start | bytes 393216 | tf_op jit(solution)/shard_map/all_to_all | solution.py:303
  207.4 10.2 %all-gather.1 = f32[8,32,256]{2,1,0:T(8,128)S(1)} all-gather(f32[2,32,256]{2,1,0:T(8,128)S(1)} %step_kernel.4), channel_id=3, replica_groups=mesh['xlo'=2,'z'=16,'core'=2,'xhi'=2,'y'=4] {'y'}, dimensions={0}, use_global_device_ids=true | all-gather | bytes 327680 | tf_op jit(solution)/shard_map/all_gather | solution.py:380
  217.6 5.3 %collective-permute-start.11 = (f32[4,2,32,256]{3,2,1,0:T(8,128)S(1)}, f32[4,2,32,256]{3,2,1,0:T(8,128)S(1)}, u32[]{:S(2)}, u32[]{:S(2)}) collective-permute-start(f32[4,2,32,256]{3,2,1,0:T(8,128)S(1)} %bitcast.29), channel_id=1, source_target_pairs={{0,4},{4,0},{1,5},{5,1},{2,6},{6,2},{3,7},{7,3},{8,12},{12,8},{9,1... | collective-permute-start | bytes 786440 | tf_op jit(solution)/shard_map/ppermute | solution.py:299
  223.6 11.5 %all-to-all-start.9 = ((f32[16,2,8,128]{3,2,1,0:T(8,128)}), f32[16,2,8,128]{3,2,1,0:T(8,128)S(1)}, u32[]{:S(2)}, u32[]{:S(2)}) async-start(f32[16,2,8,128]{3,2,1,0:T(8,128)} %get-tuple-element.69.after), calls=%async_computation.9 | async-start | bytes 262144 | tf_op jit(solution)/shard_map/all_to_all | solution.py:303
  235.1 1.5 copy-done.7
  236.6 2.1 place_kernel.4
  238.8 7.9 %collective-permute-start.12 = (f32[2,288,256]{2,1,0:T(8,128)}, f32[2,288,256]{2,1,0:T(8,128)S(1)}, u32[]{:S(2)}, u32[]{:S(2)}) collective-permute-start(f32[2,288,256]{2,1,0:T(8,128)} %get-tuple-element.74), channel_id=1, source_target_pairs={{0,8},{8,16},{16,24},{24,32},{32,40},{40,48},{48,56},{56,64},{64,7... | collective-permute-start | bytes 1769480 | tf_op jit(solution)/shard_map/ppermute | solution.py:295
  246.7 1.9 collective-permute-start.13
  248.7 1.9 collective-permute-start.14
  250.6 6.1 %collective-permute-start.15 = (f32[16,2,8,128]{3,2,1,0:T(8,128)S(1)}, f32[16,2,8,128]{3,2,1,0:T(8,128)S(1)}, u32[]{:S(2)}, u32[]{:S(2)}) collective-permute-start(f32[16,2,8,128]{3,2,1,0:T(8,128)S(1)} %all-to-all-done.9.piece0), channel_id=1, source_target_pairs={{0,8},{8,0},{1,9},{9,1},{2,10},{10,2},{3,11},{11,3},{4,12},{12,4},... | collective-permute-start | bytes 393224 | tf_op jit(solution)/shard_map/ppermute | solution.py:299
  256.7 5.1 %collective-permute-start.16 = (f32[16,2,8,128]{3,2,1,0:T(8,128)S(1)}, f32[16,2,8,128]{3,2,1,0:T(8,128)S(1)}, u32[]{:S(2)}, u32[]{:S(2)}) collective-permute-start(f32[16,2,8,128]{3,2,1,0:T(8,128)S(1)} %collective-permute-done.14.piece1), channel_id=1, source_target_pairs={{0,8},{8,0},{1,9},{9,1},{2,10},{10,2},{3,11},{11,3},{4,12},{12,4},... | collective-permute-start | bytes 393224 | tf_op jit(solution)/shard_map/ppermute | solution.py:299
  261.8 1.6 view_kernel.3
  264.7 2.5 next_kernel.3
  267.2 10.8 %all_to_all.79.powers = f32[8,32,256]{2,1,0:T(8,128)S(1)} all-to-all(f32[8,32,256]{2,1,0:T(8,128)S(1)} %bitcast.35), channel_id=1, replica_groups=mesh['xlo'=2,'z'=16,'core'=2,'xhi'=2,'y'=4] {'xhi','y'}, dimensions={0} | all-to-all | bytes 524288 | tf_op jit(solution)/shard_map/all_to_all | solution.py:303
  278.6 11.5 %all_to_all.80 = f32[8,32,256]{2,1,0:T(8,128)S(1)} all-to-all(f32[8,32,256]{2,1,0:T(8,128)S(1)} %ratio_kernel.5), channel_id=1, replica_groups=mesh['xlo'=2,'z'=16,'core'=2,'xhi'=2,'y'=4] {'xhi','y'}, dimensions={0} | all-to-all | bytes 524288 | tf_op jit(solution)/shard_map/all_to_all | solution.py:303
  290.0 1.8 backward_kernel.5
  291.8 4.0 %collective-permute-start.17 = (f32[2,16,3,8,128]{4,3,2,1,0:T(8,128)S(1)}, f32[2,16,3,8,128]{4,3,2,1,0:T(8,128)S(1)}, u32[]{:S(2)}, u32[]{:S(2)}) collective-permute-start(f32[2,16,3,8,128]{4,3,2,1,0:T(8,128)S(1)} %get-tuple-element.80), channel_id=1, source_target_pairs={{0,8},{8,0},{1,9},{9,1},{2,10},{10,2},{3,11},{11,3},{4,12},{12,4},... | collective-permute-start | bytes 1179656 | tf_op jit(solution)/shard_map/ppermute | solution.py:299
  295.8 1.3 collective-permute-done.17.theirs
  298.7 3.5 all-to-all-start.13
  302.3 2.5 collective-permute-start.18
  304.8 11.5 %collective-permute-done.18 = f32[16,3,8,128]{3,2,1,0:T(8,128)S(1)} collective-permute-done((f32[16,3,8,128]{3,2,1,0:T(8,128)S(1)}, f32[16,3,8,128]{3,2,1,0:T(8,128)S(1)}, u32[]{:S(2)}, u32[]{:S(2)}) %collective-permute-start.18) | collective-permute-done | bytes 196640 | tf_op jit(solution)/shard_map/ppermute | solution.py:299
  317.0 8.8 %all-to-all-start.12 = ((f32[16,3,8,128]{3,2,1,0:T(8,128)}), f32[16,3,8,128]{3,2,1,0:T(8,128)S(1)}, u32[]{:S(2)}, u32[]{:S(2)}) async-start(f32[16,3,8,128]{3,2,1,0:T(8,128)} %add.23.after), calls=%async_computation.12 | async-start | bytes 393216 | tf_op jit(solution)/shard_map/all_to_all | solution.py:303
  325.9 10.2 %all-gather.2 = f32[8,32,256]{2,1,0:T(8,128)S(1)} all-gather(f32[2,32,256]{2,1,0:T(8,128)S(1)} %step_kernel.5), channel_id=4, replica_groups=mesh['xlo'=2,'z'=16,'core'=2,'xhi'=2,'y'=4] {'y'}, dimensions={0}, use_global_device_ids=true | all-gather | bytes 327680 | tf_op jit(solution)/shard_map/all_gather | solution.py:380
  336.1 5.3 %collective-permute-start.19 = (f32[4,2,32,256]{3,2,1,0:T(8,128)S(1)}, f32[4,2,32,256]{3,2,1,0:T(8,128)S(1)}, u32[]{:S(2)}, u32[]{:S(2)}) collective-permute-start(f32[4,2,32,256]{3,2,1,0:T(8,128)S(1)} %bitcast.27), channel_id=1, source_target_pairs={{0,4},{4,0},{1,5},{5,1},{2,6},{6,2},{3,7},{7,3},{8,12},{12,8},{9,1... | collective-permute-start | bytes 786440 | tf_op jit(solution)/shard_map/ppermute | solution.py:299
  342.2 11.5 %all-to-all-start.14 = ((f32[16,2,8,128]{3,2,1,0:T(8,128)}), f32[16,2,8,128]{3,2,1,0:T(8,128)}, u32[]{:S(2)}, u32[]{:S(2)}) async-start(f32[16,2,8,128]{3,2,1,0:T(8,128)} %get-tuple-element.84.after), calls=%async_computation.14 | async-start | bytes 262144 | tf_op jit(solution)/shard_map/all_to_all | solution.py:303
  356.3 2.1 place_kernel.5
  358.4 7.9 %collective-permute-start.20 = (f32[2,288,256]{2,1,0:T(8,128)}, f32[2,288,256]{2,1,0:T(8,128)S(1)}, u32[]{:S(2)}, u32[]{:S(2)}) collective-permute-start(f32[2,288,256]{2,1,0:T(8,128)} %get-tuple-element.89), channel_id=1, source_target_pairs={{0,8},{8,16},{16,24},{24,32},{32,40},{40,48},{48,56},{56,64},{64,7... | collective-permute-start | bytes 1769480 | tf_op jit(solution)/shard_map/ppermute | solution.py:295
  366.4 1.9 collective-permute-start.21
  368.3 7.1 %collective-permute-start.22 = (f32[16,2,8,128]{3,2,1,0:T(8,128)}, f32[16,2,8,128]{3,2,1,0:T(8,128)S(1)}, u32[]{:S(2)}, u32[]{:S(2)}) collective-permute-start(f32[16,2,8,128]{3,2,1,0:T(8,128)} %all-to-all-done.14.piece0), channel_id=1, source_target_pairs={{0,8},{8,0},{1,9},{9,1},{2,10},{10,2},{3,11},{11,3},{4,12},{12,4},... | collective-permute-start | bytes 393224 | tf_op jit(solution)/shard_map/ppermute | solution.py:299
  375.4 1.3 collective-permute-done.21.piece1
  376.7 3.7 collective-permute-start.23
  381.3 2.2 last_kernel.1
  (85 shorter events, 24.3 us)
Async XLA Ops:
  0.6 35.3 %copy-start.2 = (bf16[1,3,256,256]{3,2,1,0:T(8,128)(2,1)S(1)}, bf16[1,3,256,256]{3,2,1,0:T(8,128)(2,1)}, u32[]{:S(2)}) copy-start(bf16[1,3,256,256]{3,2,1,0:T(8,128)(2,1)} %measured.5) | copy-start | bytes 1179652
  1.8 12.5 %collective-permute-start = (f32[2,288,256]{2,1,0:T(8,128)S(1)}, f32[2,288,256]{2,1,0:T(8,128)S(1)}, u32[]{:S(2)}, u32[]{:S(2)}) collective-permute-start(f32[2,288,256]{2,1,0:T(8,128)S(1)} %slice.15), channel_id=1, source_target_pairs={{8,0},{16,8},{24,16},{32,24},{40,32},{48,40},{56,48},{64,56},{72,6... | collective-permute-start | bytes 1769480 | tf_op jit(solution)/shard_map/ppermute | solution.py:295
  14.3 1.0 copy-start
  15.3 1.3 copy-start.3
  16.6 1.0 copy-start.12
  17.6 28.8 %copy-start.1 = (bf16[2,2,256,256]{3,2,1,0:T(8,128)(2,1)S(1)}, bf16[2,2,256,256]{3,2,1,0:T(8,128)(2,1)}, u32[]{:S(2)}) copy-start(bf16[2,2,256,256]{3,2,1,0:T(8,128)(2,1)} %constant.33.clone.tables) | copy-start | bytes 1572868
  20.7 1.2 copy-start.8
  48.3 3.6 collective-permute-start.1
  53.5 28.2 %all-to-all-start.3 = ((f32[8,3,32,256]{3,2,1,0:T(8,128)}), f32[8,3,32,256]{3,2,1,0:T(8,128)S(1)}, u32[]{:S(2)}, u32[]{:S(2)}) async-start(f32[8,3,32,256]{3,2,1,0:T(8,128)} %gradient_kernel.3), calls=%async_computation.3 | async-start | bytes 1572864 | tf_op jit(solution)/shard_map/all_to_all | solution.py:303
  57.1 24.0 %collective-permute-start.2 = (f32[16,3,8,128]{3,2,1,0:T(8,128)S(1)}, f32[16,3,8,128]{3,2,1,0:T(8,128)S(1)}, u32[]{:S(2)}, u32[]{:S(2)}) collective-permute-start(f32[16,3,8,128]{3,2,1,0:T(8,128)S(1)} %get-tuple-element.52), channel_id=1, source_target_pairs={{0,256},{256,0},{1,257},{257,1},{2,258},{258,2},{3,259},{259,3},{4... | collective-permute-start | bytes 589832 | tf_op jit(solution)/shard_map/ppermute | solution.py:299
  81.7 22.7 %all-to-all-start.2 = ((f32[16,3,8,128]{3,2,1,0:T(8,128)}), f32[16,3,8,128]{3,2,1,0:T(8,128)S(1)}, u32[]{:S(2)}, u32[]{:S(2)}) async-start(f32[16,3,8,128]{3,2,1,0:T(8,128)} %add.21.after), calls=%async_computation.2 | async-start | bytes 393216 | tf_op jit(solution)/shard_map/all_to_all | solution.py:303
  99.1 17.5 %collective-permute-start.3 = (f32[4,2,32,256]{3,2,1,0:T(8,128)S(1)}, f32[4,2,32,256]{3,2,1,0:T(8,128)S(1)}, u32[]{:S(2)}, u32[]{:S(2)}) collective-permute-start(f32[4,2,32,256]{3,2,1,0:T(8,128)S(1)} %bitcast.31), channel_id=1, source_target_pairs={{0,4},{4,0},{1,5},{5,1},{2,6},{6,2},{3,7},{7,3},{8,12},{12,8},{9,1... | collective-permute-start | bytes 786440 | tf_op jit(solution)/shard_map/ppermute | solution.py:299
  105.2 25.0 %all-to-all-start.4 = ((f32[16,2,8,128]{3,2,1,0:T(8,128)}), f32[16,2,8,128]{3,2,1,0:T(8,128)S(1)}, u32[]{:S(2)}, u32[]{:S(2)}) async-start(f32[16,2,8,128]{3,2,1,0:T(8,128)} %get-tuple-element.54.after), calls=%async_computation.4 | async-start | bytes 262144 | tf_op jit(solution)/shard_map/all_to_all | solution.py:303
  116.7 1.5 copy-start.9
  120.3 22.9 %collective-permute-start.4 = (f32[2,288,256]{2,1,0:T(8,128)}, f32[2,288,256]{2,1,0:T(8,128)S(1)}, u32[]{:S(2)}, u32[]{:S(2)}) collective-permute-start(f32[2,288,256]{2,1,0:T(8,128)} %get-tuple-element.59), channel_id=1, source_target_pairs={{0,8},{8,16},{16,24},{24,32},{32,40},{40,48},{48,56},{56,64},{64,7... | collective-permute-start | bytes 1769480 | tf_op jit(solution)/shard_map/ppermute | solution.py:295
  128.3 14.9 %collective-permute-start.5 = (f32[2,288,256]{2,1,0:T(8,128)}, f32[2,288,256]{2,1,0:T(8,128)}, u32[]{:S(2)}, u32[]{:S(2)}) collective-permute-start(f32[2,288,256]{2,1,0:T(8,128)} %get-tuple-element.60), channel_id=1, source_target_pairs={{8,0},{16,8},{24,16},{32,24},{40,32},{48,40},{56,48},{64,56},{72,6... | collective-permute-start | bytes 1769480 | tf_op jit(solution)/shard_map/ppermute | solution.py:295
  130.2 8.2 %collective-permute-start.6 = (f32[16,2,8,128]{3,2,1,0:T(8,128)S(1)}, f32[16,2,8,128]{3,2,1,0:T(8,128)S(1)}, u32[]{:S(2)}, u32[]{:S(2)}) collective-permute-start(f32[16,2,8,128]{3,2,1,0:T(8,128)S(1)} %all-to-all-done.4.piece0), channel_id=1, source_target_pairs={{0,256},{256,0},{1,257},{257,1},{2,258},{258,2},{3,259},{259,3},{4... | collective-permute-start | bytes 393224 | tf_op jit(solution)/shard_map/ppermute | solution.py:299
  132.1 14.0 %collective-permute-start.7 = (f32[16,2,8,128]{3,2,1,0:T(8,128)S(1)}, f32[16,2,8,128]{3,2,1,0:T(8,128)S(1)}, u32[]{:S(2)}, u32[]{:S(2)}) collective-permute-start(f32[16,2,8,128]{3,2,1,0:T(8,128)S(1)} %all-to-all-done.4.piece0), channel_id=1, source_target_pairs={{0,8},{8,0},{1,9},{9,1},{2,10},{10,2},{3,11},{11,3},{4,12},{12,4},... | collective-permute-start | bytes 393224 | tf_op jit(solution)/shard_map/ppermute | solution.py:299
  138.4 7.7 %collective-permute-start.8 = (f32[16,2,8,128]{3,2,1,0:T(8,128)S(1)}, f32[16,2,8,128]{3,2,1,0:T(8,128)S(1)}, u32[]{:S(2)}, u32[]{:S(2)}) collective-permute-start(f32[16,2,8,128]{3,2,1,0:T(8,128)S(1)} %collective-permute-done.6.piece1), channel_id=1, source_target_pairs={{0,8},{8,0},{1,9},{9,1},{2,10},{10,2},{3,11},{11,3},{4,12},{12,4},... | collective-permute-start | bytes 393224 | tf_op jit(solution)/shard_map/ppermute | solution.py:299
  144.8 1.2 copy-start.6
  173.2 5.3 %collective-permute-start.9 = (f32[2,16,3,8,128]{4,3,2,1,0:T(8,128)S(1)}, f32[2,16,3,8,128]{4,3,2,1,0:T(8,128)S(1)}, u32[]{:S(2)}, u32[]{:S(2)}) collective-permute-start(f32[2,16,3,8,128]{4,3,2,1,0:T(8,128)S(1)} %get-tuple-element.65), channel_id=1, source_target_pairs={{0,8},{8,0},{1,9},{9,1},{2,10},{10,2},{3,11},{11,3},{4,12},{12,4},... | collective-permute-start | bytes 1179656 | tf_op jit(solution)/shard_map/ppermute | solution.py:299
  180.1 18.3 %all-to-all-start.8 = ((f32[8,3,32,256]{3,2,1,0:T(8,128)}), f32[8,3,32,256]{3,2,1,0:T(8,128)S(1)}, u32[]{:S(2)}, u32[]{:S(2)}) async-start(f32[8,3,32,256]{3,2,1,0:T(8,128)} %gradient_kernel.4), calls=%async_computation.8 | async-start | bytes 1572864 | tf_op jit(solution)/shard_map/all_to_all | solution.py:303
  183.7 14.1 %collective-permute-start.10 = (f32[16,3,8,128]{3,2,1,0:T(8,128)S(1)}, f32[16,3,8,128]{3,2,1,0:T(8,128)S(1)}, u32[]{:S(2)}, u32[]{:S(2)}) collective-permute-start(f32[16,3,8,128]{3,2,1,0:T(8,128)S(1)} %get-tuple-element.67), channel_id=1, source_target_pairs={{0,256},{256,0},{1,257},{257,1},{2,258},{258,2},{3,259},{259,3},{4... | collective-permute-start | bytes 589832 | tf_op jit(solution)/shard_map/ppermute | solution.py:299
  198.5 24.5 %all-to-all-start.7 = ((f32[16,3,8,128]{3,2,1,0:T(8,128)}), f32[16,3,8,128]{3,2,1,0:T(8,128)S(1)}, u32[]{:S(2)}, u32[]{:S(2)}) async-start(f32[16,3,8,128]{3,2,1,0:T(8,128)} %add.22.after), calls=%async_computation.7 | async-start | bytes 393216 | tf_op jit(solution)/shard_map/all_to_all | solution.py:303
  217.6 17.5 %collective-permute-start.11 = (f32[4,2,32,256]{3,2,1,0:T(8,128)S(1)}, f32[4,2,32,256]{3,2,1,0:T(8,128)S(1)}, u32[]{:S(2)}, u32[]{:S(2)}) collective-permute-start(f32[4,2,32,256]{3,2,1,0:T(8,128)S(1)} %bitcast.29), channel_id=1, source_target_pairs={{0,4},{4,0},{1,5},{5,1},{2,6},{6,2},{3,7},{7,3},{8,12},{12,8},{9,1... | collective-permute-start | bytes 786440 | tf_op jit(solution)/shard_map/ppermute | solution.py:299
  223.6 25.0 %all-to-all-start.9 = ((f32[16,2,8,128]{3,2,1,0:T(8,128)}), f32[16,2,8,128]{3,2,1,0:T(8,128)S(1)}, u32[]{:S(2)}, u32[]{:S(2)}) async-start(f32[16,2,8,128]{3,2,1,0:T(8,128)} %get-tuple-element.69.after), calls=%async_computation.9 | async-start | bytes 262144 | tf_op jit(solution)/shard_map/all_to_all | solution.py:303
  235.1 1.5 copy-start.7
  238.8 23.1 %collective-permute-start.12 = (f32[2,288,256]{2,1,0:T(8,128)}, f32[2,288,256]{2,1,0:T(8,128)S(1)}, u32[]{:S(2)}, u32[]{:S(2)}) collective-permute-start(f32[2,288,256]{2,1,0:T(8,128)} %get-tuple-element.74), channel_id=1, source_target_pairs={{0,8},{8,16},{16,24},{24,32},{32,40},{40,48},{48,56},{56,64},{64,7... | collective-permute-start | bytes 1769480 | tf_op jit(solution)/shard_map/ppermute | solution.py:295
  246.7 15.1 %collective-permute-start.13 = (f32[2,288,256]{2,1,0:T(8,128)}, f32[2,288,256]{2,1,0:T(8,128)}, u32[]{:S(2)}, u32[]{:S(2)}) collective-permute-start(f32[2,288,256]{2,1,0:T(8,128)} %get-tuple-element.75), channel_id=1, source_target_pairs={{8,0},{16,8},{24,16},{32,24},{40,32},{48,40},{56,48},{64,56},{72,6... | collective-permute-start | bytes 1769480 | tf_op jit(solution)/shard_map/ppermute | solution.py:295
  248.7 8.1 %collective-permute-start.14 = (f32[16,2,8,128]{3,2,1,0:T(8,128)S(1)}, f32[16,2,8,128]{3,2,1,0:T(8,128)S(1)}, u32[]{:S(2)}, u32[]{:S(2)}) collective-permute-start(f32[16,2,8,128]{3,2,1,0:T(8,128)S(1)} %all-to-all-done.9.piece0), channel_id=1, source_target_pairs={{0,256},{256,0},{1,257},{257,1},{2,258},{258,2},{3,259},{259,3},{4... | collective-permute-start | bytes 393224 | tf_op jit(solution)/shard_map/ppermute | solution.py:299
  250.6 14.1 %collective-permute-start.15 = (f32[16,2,8,128]{3,2,1,0:T(8,128)S(1)}, f32[16,2,8,128]{3,2,1,0:T(8,128)S(1)}, u32[]{:S(2)}, u32[]{:S(2)}) collective-permute-start(f32[16,2,8,128]{3,2,1,0:T(8,128)S(1)} %all-to-all-done.9.piece0), channel_id=1, source_target_pairs={{0,8},{8,0},{1,9},{9,1},{2,10},{10,2},{3,11},{11,3},{4,12},{12,4},... | collective-permute-start | bytes 393224 | tf_op jit(solution)/shard_map/ppermute | solution.py:299
  256.7 8.0 %collective-permute-start.16 = (f32[16,2,8,128]{3,2,1,0:T(8,128)S(1)}, f32[16,2,8,128]{3,2,1,0:T(8,128)S(1)}, u32[]{:S(2)}, u32[]{:S(2)}) collective-permute-start(f32[16,2,8,128]{3,2,1,0:T(8,128)S(1)} %collective-permute-done.14.piece1), channel_id=1, source_target_pairs={{0,8},{8,0},{1,9},{9,1},{2,10},{10,2},{3,11},{11,3},{4,12},{12,4},... | collective-permute-start | bytes 393224 | tf_op jit(solution)/shard_map/ppermute | solution.py:299
  263.5 1.2 copy-start.4
  291.8 5.3 %collective-permute-start.17 = (f32[2,16,3,8,128]{4,3,2,1,0:T(8,128)S(1)}, f32[2,16,3,8,128]{4,3,2,1,0:T(8,128)S(1)}, u32[]{:S(2)}, u32[]{:S(2)}) collective-permute-start(f32[2,16,3,8,128]{4,3,2,1,0:T(8,128)S(1)} %get-tuple-element.80), channel_id=1, source_target_pairs={{0,8},{8,0},{1,9},{9,1},{2,10},{10,2},{3,11},{11,3},{4,12},{12,4},... | collective-permute-start | bytes 1179656 | tf_op jit(solution)/shard_map/ppermute | solution.py:299
  298.7 18.3 %all-to-all-start.13 = ((f32[8,3,32,256]{3,2,1,0:T(8,128)}), f32[8,3,32,256]{3,2,1,0:T(8,128)S(1)}, u32[]{:S(2)}, u32[]{:S(2)}) async-start(f32[8,3,32,256]{3,2,1,0:T(8,128)} %gradient_kernel.5), calls=%async_computation.13 | async-start | bytes 1572864 | tf_op jit(solution)/shard_map/all_to_all | solution.py:303
  302.3 52.1 %copy-start.5 = (f32[2,288,768]{2,1,0:T(8,128)S(1)}, f32[2,288,768]{2,1,0:T(8,128)}, u32[]{:S(2)}) copy-start(f32[2,288,768]{2,1,0:T(8,128)} %copy-done.4) | copy-start | bytes 5308420
  302.3 14.0 %collective-permute-start.18 = (f32[16,3,8,128]{3,2,1,0:T(8,128)S(1)}, f32[16,3,8,128]{3,2,1,0:T(8,128)S(1)}, u32[]{:S(2)}, u32[]{:S(2)}) collective-permute-start(f32[16,3,8,128]{3,2,1,0:T(8,128)S(1)} %get-tuple-element.82), channel_id=1, source_target_pairs={{0,256},{256,0},{1,257},{257,1},{2,258},{258,2},{3,259},{259,3},{4... | collective-permute-start | bytes 589832 | tf_op jit(solution)/shard_map/ppermute | solution.py:299
  317.0 24.4 %all-to-all-start.12 = ((f32[16,3,8,128]{3,2,1,0:T(8,128)}), f32[16,3,8,128]{3,2,1,0:T(8,128)S(1)}, u32[]{:S(2)}, u32[]{:S(2)}) async-start(f32[16,3,8,128]{3,2,1,0:T(8,128)} %add.23.after), calls=%async_computation.12 | async-start | bytes 393216 | tf_op jit(solution)/shard_map/all_to_all | solution.py:303
  336.1 17.6 %copy-start.10 = (f32[8,32,256]{2,1,0:T(8,128)}, f32[8,32,256]{2,1,0:T(8,128)S(1)}, u32[]{:S(2)}) copy-start(f32[8,32,256]{2,1,0:T(8,128)S(1)} %all-gather.2) | copy-start | bytes 786436
  336.1 17.6 %collective-permute-start.19 = (f32[4,2,32,256]{3,2,1,0:T(8,128)S(1)}, f32[4,2,32,256]{3,2,1,0:T(8,128)S(1)}, u32[]{:S(2)}, u32[]{:S(2)}) collective-permute-start(f32[4,2,32,256]{3,2,1,0:T(8,128)S(1)} %bitcast.27), channel_id=1, source_target_pairs={{0,4},{4,0},{1,5},{5,1},{2,6},{6,2},{3,7},{7,3},{8,12},{12,8},{9,1... | collective-permute-start | bytes 786440 | tf_op jit(solution)/shard_map/ppermute | solution.py:299
  342.2 24.2 %all-to-all-start.14 = ((f32[16,2,8,128]{3,2,1,0:T(8,128)}), f32[16,2,8,128]{3,2,1,0:T(8,128)}, u32[]{:S(2)}, u32[]{:S(2)}) async-start(f32[16,2,8,128]{3,2,1,0:T(8,128)} %get-tuple-element.84.after), calls=%async_computation.14 | async-start | bytes 262144 | tf_op jit(solution)/shard_map/all_to_all | solution.py:303
  353.7 0.7 copy-start.13
  354.4 1.0 copy-start.11
  355.4 0.9 copy-start.14
  358.4 21.9 %collective-permute-start.20 = (f32[2,288,256]{2,1,0:T(8,128)}, f32[2,288,256]{2,1,0:T(8,128)S(1)}, u32[]{:S(2)}, u32[]{:S(2)}) collective-permute-start(f32[2,288,256]{2,1,0:T(8,128)} %get-tuple-element.89), channel_id=1, source_target_pairs={{0,8},{8,16},{16,24},{24,32},{32,40},{40,48},{48,56},{56,64},{64,7... | collective-permute-start | bytes 1769480 | tf_op jit(solution)/shard_map/ppermute | solution.py:295
  366.4 10.3 %collective-permute-start.21 = (f32[16,2,8,128]{3,2,1,0:T(8,128)}, f32[16,2,8,128]{3,2,1,0:T(8,128)S(1)}, u32[]{:S(2)}, u32[]{:S(2)}) collective-permute-start(f32[16,2,8,128]{3,2,1,0:T(8,128)} %all-to-all-done.14.piece0), channel_id=1, source_target_pairs={{0,256},{256,0},{1,257},{257,1},{2,258},{258,2},{3,259},{259,3},{4... | collective-permute-start | bytes 393224 | tf_op jit(solution)/shard_map/ppermute | solution.py:299
  368.3 12.1 %collective-permute-start.22 = (f32[16,2,8,128]{3,2,1,0:T(8,128)}, f32[16,2,8,128]{3,2,1,0:T(8,128)S(1)}, u32[]{:S(2)}, u32[]{:S(2)}) collective-permute-start(f32[16,2,8,128]{3,2,1,0:T(8,128)} %all-to-all-done.14.piece0), channel_id=1, source_target_pairs={{0,8},{8,0},{1,9},{9,1},{2,10},{10,2},{3,11},{11,3},{4,12},{12,4},... | collective-permute-start | bytes 393224 | tf_op jit(solution)/shard_map/ppermute | solution.py:299
  376.7 4.6 %collective-permute-start.23 = (f32[16,2,8,128]{3,2,1,0:T(8,128)S(1)}, f32[16,2,8,128]{3,2,1,0:T(8,128)S(1)}, u32[]{:S(2)}, u32[]{:S(2)}) collective-permute-start(f32[16,2,8,128]{3,2,1,0:T(8,128)S(1)} %collective-permute-done.21.piece1), channel_id=1, source_target_pairs={{0,8},{8,0},{1,9},{9,1},{2,10},{10,2},{3,11},{11,3},{4,12},{12,4},... | collective-permute-start | bytes 393224 | tf_op jit(solution)/shard_map/ppermute | solution.py:299

commit v3 on v2

v3 whole, which is shorter than its diff:
```python
import math

import jax
import jax.numpy as jnp
import numpy as np
from jax import lax
from jax.experimental import pallas as pl
from jax.experimental.pallas import tpu as pltpu
from jax.sharding import Mesh
from jax.sharding import PartitionSpec as P

SOFT_FLOOR = 0.5
OBJECT_RATE = 1.0
OBJECT_DAMP = 0.5
PROBE_RATE = 1.0
PROBE_DAMP = 1.0

SIDE = 256
HEIGHT = 288
WIDTH = 512
WIDE = WIDTH + SIDE
MODES = 8
SLAB = SIDE // MODES
BAND = 2 * SLAB
STEPS = 3
TILES = 64
RINGS = 16
LANES = 128
COL_SPAN = SIDE + LANES
OUT_ROWS = 40
VMEM_LIMIT = 16 * 1024 * 1024

TILE_AXES = ("xlo", "z", "core")
MODE_AXES = ("xhi", "y")

ROW, COL, SLOT, LIVE, MODE, CORE, XLO, RING, HAS_NEXT = range(9)

F32 = jnp.float32
BF16 = jnp.bfloat16


def fourier_tables():
    index = np.arange(SIDE)
    angles = (index[:, None] * index[None, :] % SIDE) * (2.0 * math.pi / SIDE)
    both = np.stack([np.cos(angles), np.sin(angles)]) / math.sqrt(SIDE)
    high = both.astype(jnp.bfloat16)
    low = (both - high.astype(np.float64)).astype(jnp.bfloat16)
    return np.stack([high, low], axis=1)


def halves(value):
    high = value.astype(BF16)
    return high, (value - high.astype(F32)).astype(BF16)


def dot(left, right):
    return jnp.dot(left, right, preferred_element_type=F32)


def rows_transform(real, imag, tables, direction):
    high, low = halves(jnp.concatenate([real, imag], axis=0))

    def by(which):
        return (
            dot(high, tables[which, 0]) + dot(low, tables[which, 0]) + dot(high, tables[which, 1])
        )

    by_cos, by_sin = by(0), by(1)
    return (
        by_cos[:SIDE] + direction * by_sin[SIDE:],
        by_cos[SIDE:] - direction * by_sin[:SIDE],
    )


def columns_transform(real, imag, tables, direction):
    high, low = halves(jnp.concatenate([real, imag], axis=1))

    def by(which):
        return (
            dot(tables[which, 0], high) + dot(tables[which, 0], low) + dot(tables[which, 1], high)
        )

    by_cos, by_sin = by(0), by(1)
    return (
        by_cos[:, :SIDE] + direction * by_sin[:, SIDE:],
        by_cos[:, SIDE:] - direction * by_sin[:, :SIDE],
    )


def swap_blocks(parts):
    lanes = lax.broadcasted_iota(jnp.int32, (parts[0].shape[0], LANES), 1)
    grid = [[part[:, :LANES], part[:, LANES:]] for part in parts]
    grid = [[grid[(m & 3) | (h << 2)][m >> 2] for h in range(2)] for m in range(MODES)]
    for bit in (2, 1):
        shift = bit * SLAB
        low = (lanes & shift) == 0
        new = [None] * MODES
        for m in range(MODES):
            if m & bit:
                continue
            a, b = grid[m], grid[m | bit]
            new[m] = [jnp.where(low, a[h], pltpu.roll(b[h], shift, 1)) for h in range(2)]
            new[m | bit] = [
                jnp.where(low, pltpu.roll(a[h], LANES - shift, 1), b[h]) for h in range(2)
            ]
        grid = new
    return [jnp.concatenate(pair, axis=1) for pair in grid]


def stacked(pieces):
    return jnp.concatenate(list(pieces), axis=0)


def column_window(scal):
    col = scal[COL]
    block = jnp.minimum(col // LANES, WIDTH // LANES - 1)
    return pl.ds(pl.multiple_of(block * LANES, LANES), COL_SPAN), col - block * LANES


def take_patch(scal, band, view):
    cols, rest = column_window(scal)
    for part in range(2):
        block = band[part, :, cols]
        block = pltpu.roll(block, lax.rem(COL_SPAN - rest, COL_SPAN), 1)[:, :SIDE]
        view[part] = pltpu.roll(block, lax.rem(BAND - scal[ROW], BAND), 0)[:SLAB]


def forward(view, probe, tables, spectra):
    view_real = stacked([view[0]] * MODES)
    view_imag = stacked([view[1]] * MODES)
    probe_real = stacked(probe[mode, 0] for mode in range(MODES))
    probe_imag = stacked(probe[mode, 1] for mode in range(MODES))
    both = rows_transform(
        probe_real * view_real - probe_imag * view_imag,
        probe_real * view_imag + probe_imag * view_real,
        tables,
        1.0,
    )
    for part in range(2):
        blocks = [both[part][mode * SLAB : (mode + 1) * SLAB] for mode in range(MODES)]
        for place, block in enumerate(swap_blocks(blocks)):
            spectra[place, part] = block


def split_kernel(probe_in, pieces):
    for place in range(MODES):
        pieces[place] = probe_in[0, :, place * SLAB : (place + 1) * SLAB, :]


def first_kernel(scal, own, beside, probe, tables, band, view, shard, spectra):
    band[:, :, :WIDTH] = own[...]
    band[:, :, WIDTH:] = beside[...]
    take_patch(scal, band, view)
    mode = scal[RING] // 2
    rows = pl.ds(pl.multiple_of(scal[CORE] * 16 + scal[XLO] * 8, 8), 8)

    @pl.when(lax.rem(scal[RING], 2) == 0)
    def _():
        shard[...] = probe[mode, :, rows, :LANES]

    @pl.when(lax.rem(scal[RING], 2) == 1)
    def _():
        shard[...] = probe[mode, :, rows, LANES:]

    forward(view, probe, tables, spectra)


def piece_row(scal, which):
    core = scal[CORE] if which < 2 else 1 - scal[CORE]
    xlo = scal[XLO] if which % 2 == 0 else 1 - scal[XLO]
    return core * 16 + xlo * 8


def next_kernel(scal, view, piece0, piece1, piece2, piece3, tables, probe, spectra):
    for which, piece in enumerate((piece0, piece1, piece2, piece3)):
        rows = pl.ds(pl.multiple_of(piece_row(scal, which), 8), 8)
        for mode in range(MODES):
            probe[mode, :, rows, :LANES] = piece[2 * mode]
            probe[mode, :, rows, LANES:] = piece[2 * mode + 1]
    forward(view, probe, tables, spectra)


def counts_kernel(scal, measured, counts):
    block = measured[0, scal[SLOT]].astype(F32)
    block = pltpu.roll(block, lax.rem(SIDE - scal[MODE] * SLAB, SIDE), 1)[:, :LANES]
    lanes = lax.broadcasted_iota(jnp.int32, block.shape, 1)
    block = jnp.where(lanes < SLAB, block, 0.0)
    block = block + pltpu.roll(block, SLAB, 1)
    counts[...] = block + pltpu.roll(block, 2 * SLAB, 1)


def ratio_kernel(scal, spectra, counts, tables, out):
    real = stacked(spectra[place, 0] for place in range(MODES))
    imag = stacked(spectra[place, 1] for place in range(MODES))
    far_real, far_imag = columns_transform(real, imag, tables, 1.0)
    power = far_real * far_real + far_imag * far_imag
    total = power[:, :LANES] + power[:, LANES:]
    total = total + pltpu.roll(total, 2 * SLAB, 1)
    total = total + pltpu.roll(total, SLAB, 1)
    ratio = jnp.sqrt((counts[...] + SOFT_FLOOR) / (total + SOFT_FLOOR)) - 1.0
    ratio = ratio * scal[LIVE].astype(F32)
    ratio = jnp.concatenate([ratio, ratio], axis=1)
    both = columns_transform(far_real * ratio, far_imag * ratio, tables, -1.0)
    for part in range(2):
        for place in range(MODES):
            out[place, part] = both[part][place * SLAB : (place + 1) * SLAB]


def backward_kernel(scal, spectra, view, tables, chi, keep, send):
    real = stacked(swap_blocks([spectra[place, 0] for place in range(MODES)]))
    imag = stacked(swap_blocks([spectra[place, 1] for place in range(MODES)]))
    chi_real, chi_imag = rows_transform(real, imag, tables, -1.0)
    view_real, view_imag = view[0], view[1]
    sums = []
    for mode in range(MODES):
        real = chi_real[mode * SLAB : (mode + 1) * SLAB]
        imag = chi_imag[mode * SLAB : (mode + 1) * SLAB]
        chi[mode, 0] = real
        chi[mode, 1] = imag
        sums.append(view_real * real + view_imag * imag)
        sums.append(view_real * imag - view_imag * real)
    sums.append((view_real * view_real + view_imag * view_imag) * scal[LIVE].astype(F32))

    @pl.when(scal[CORE] == 0)
    def _():
        for index, value in enumerate(sums):
            keep[index] = value[:16]
            send[index] = value[16:]

    @pl.when(scal[CORE] == 1)
    def _():
        for index, value in enumerate(sums):
            keep[index] = value[16:]
            send[index] = value[:16]


def halve_kernel(scal, mine, theirs, keep, send):
    ours = pl.ds(pl.multiple_of(scal[XLO] * 8, 8), 8)
    others = pl.ds(pl.multiple_of((1 - scal[XLO]) * 8, 8), 8)
    keep[...] = mine[:, ours] + theirs[:, ours]
    send[...] = mine[:, others] + theirs[:, others]


def pack_kernel(mine, theirs, packed):
    for half in range(2):
        lanes = slice(half * LANES, (half + 1) * LANES)
        total = mine[:, :, lanes] + theirs[:, :, lanes]
        for mode in range(MODES):
            packed[2 * mode + half, 0] = total[2 * mode]
            packed[2 * mode + half, 1] = total[2 * mode + 1]
            packed[2 * mode + half, 2] = total[2 * MODES]


def step_kernel(chi, probe, step):
    real = imag = light = 0.0
    for mode in range(MODES):
        probe_real, probe_imag = probe[mode, 0], probe[mode, 1]
        real = real + (probe_real * chi[mode, 0] + probe_imag * chi[mode, 1])
        imag = imag + (probe_real * chi[mode, 1] - probe_imag * chi[mode, 0])
        light = light + (probe_real * probe_real + probe_imag * probe_imag)
    step[0] = OBJECT_RATE * real / (light + OBJECT_DAMP)
    step[1] = OBJECT_RATE * imag / (light + OBJECT_DAMP)


def place_kernel(scal, above, step, below, band, part_band, to_left, to_right):
    cols, rest = column_window(scal)
    height = 3 * SLAB
    part_band[...] = jnp.zeros_like(part_band)
    for part in range(2):
        block = stacked([above[part], step[part], below[part]])
        block = pltpu.roll(block, lax.rem(2 * SLAB + scal[ROW], height), 0)[:BAND]
        block = jnp.concatenate([block, jnp.zeros((BAND, LANES), F32)], axis=1)
        part_band[part, :, cols] = pltpu.roll(block, rest, 1)
    to_left[...] = part_band[:, :, :SIDE]
    to_right[...] = part_band[:, :, WIDTH:]
    part_band[:, :, :WIDTH] = part_band[:, :, :WIDTH] + band[:, :, :WIDTH]
    part_band[:, :, WIDTH:] = (
        part_band[:, :, WIDTH:] * scal[HAS_NEXT].astype(F32) + band[:, :, WIDTH:]
    )


def view_kernel(scal, part_band, from_left, from_right, band, view):
    band[:, :, :SIDE] = part_band[:, :, :SIDE] + from_left[...]
    band[:, :, SIDE:WIDTH] = part_band[:, :, SIDE:WIDTH]
    band[:, :, WIDTH:] = part_band[:, :, WIDTH:] + from_right[...]
    take_patch(scal, band, view)


def probe_kernel(sums, shard_in, shard, copies):
    total = sums[0]
    for ring in range(1, RINGS):
        total = total + sums[ring]
    new = shard_in[...] + PROBE_RATE * total[:2] / (total[2:] + PROBE_DAMP)
    shard[...] = new
    for ring in range(RINGS):
        copies[ring] = new


def out_rows_kernel(scal, part_band, from_left, rows_out):
    rows = pl.ds(pl.multiple_of(scal[MODE] // 2 * 8, 8), OUT_ROWS)
    rows_out[:, :, :SIDE] = part_band[:, rows, :SIDE] + from_left[:, rows, :]
    rows_out[:, :, SIDE:] = part_band[:, rows, SIDE:WIDTH]


def object_kernel(scal, near, far, object_out):
    def write(first, last):
        for place in range(MODES):
            source = first if place < MODES // 2 else last
            row = place * 9 // 2 * 8
            object_out[:, row : row + OUT_ROWS, :] = source[place % (MODES // 2)]

    @pl.when(scal[MODE] < MODES // 2)
    def _():
        write(near, far)

    @pl.when(scal[MODE] >= MODES // 2)
    def _():
        write(far, near)


def probe_out_kernel(scal, piece0, piece1, piece2, piece3, probe_out):
    for which, piece in enumerate((piece0, piece1, piece2, piece3)):
        first = piece_row(scal, which)
        for place in range(MODES):
            rows = pl.ds(pl.multiple_of(first + place * SLAB, 8), 8)
            probe_out[0, :, rows, :LANES] = piece[2 * place]
            probe_out[0, :, rows, LANES:] = piece[2 * place + 1]


def call(kernel, outs, *args, scalars=True, after=()):
    vmem = pl.BlockSpec(memory_space=pltpu.VMEM)
    in_specs = [vmem] * len(args) + [pl.BlockSpec(memory_space=pl.ANY)] * len(after)
    if scalars:
        in_specs[0] = pl.BlockSpec(memory_space=pltpu.SMEM)

    def body(*refs):
        kernel(*refs[: len(args)], *refs[len(args) + len(after) :])

    return pl.pallas_call(
        body,
        out_shape=[jax.ShapeDtypeStruct(shape, F32) for shape in outs],
        in_specs=in_specs,
        out_specs=[vmem] * len(outs),
        compiler_params=pltpu.CompilerParams(vmem_limit_bytes=VMEM_LIMIT),
        name=kernel.__name__,
    )(*args, *after)


def shift(value, axes, count, steps):
    first, last = max(0, -steps), min(count, count - steps)
    return lax.ppermute(value, axes, [(i, i + steps) for i in range(first, last)])


def other(value, axis):
    return lax.ppermute(value, axis, [(0, 1), (1, 0)])


def exchange(value, axes):
    return lax.all_to_all(value, axes, 0, 0, tiled=True)


def four_pieces(piece):
    beyond = other(piece, "xlo")
    return piece, beyond, other(piece, "core"), other(beyond, "core")


def per_device(
    object_tiles, probe_modes, measured, row_offset, col_offset, live_counts, visit_order
):
    tables = jnp.asarray(fourier_tables())
    slots = visit_order[0]
    tile = lax.axis_index(TILE_AXES)
    mode = lax.axis_index(MODE_AXES)
    own = lax.dynamic_slice_in_dim(object_tiles, mode * SLAB, BAND, axis=1)
    beside = shift(own[:, :, :SIDE], TILE_AXES, TILES, -1)
    places = [
        mode,
        lax.axis_index("core"),
        lax.axis_index("xlo"),
        lax.axis_index("z"),
        (tile < TILES - 1).astype(jnp.int32),
    ]
    chosen = slots[:, None] == jnp.arange(STEPS, dtype=jnp.int32)[None, :]
    per_step = [
        jnp.sum(jnp.where(chosen, row_offset, 0), axis=1),
        jnp.sum(jnp.where(chosen, col_offset, 0), axis=1),
        slots,
        (slots < live_counts[0]).astype(jnp.int32),
    ]
    scalars = jnp.stack(
        per_step + [jnp.broadcast_to(place, (STEPS,)) for place in places], axis=1
    )
    slabs = (MODES, 2, SLAB, SIDE)
    slab_pair = (2, SLAB, SIDE)
    band_shape = (2, BAND, WIDE)
    edge = (2, BAND, SIDE)
    (pieces,) = call(split_kernel, [slabs], probe_modes, scalars=False)
    probe = exchange(pieces, MODE_AXES)
    (counts,) = call(counts_kernel, [(SIDE, LANES)], scalars[0], measured)
    for step in range(STEPS):
        scal = scalars[step]
        final = step == STEPS - 1
        if step == 0:
            band, view, shard, spectra = call(
                first_kernel,
                [band_shape, slab_pair, (2, 8, LANES), slabs],
                scal,
                own,
                beside,
                probe,
                tables,
                after=(counts,),
            )
        else:
            band, view = call(
                view_kernel, [band_shape, slab_pair], scal, part_band, from_left, from_right
            )
            probe, spectra = call(
                next_kernel, [slabs, slabs], scal, view, *pieces, tables, after=(counts,)
            )
        spectra = exchange(spectra, MODE_AXES)
        (spectra,) = call(ratio_kernel, [slabs], scal, spectra, counts, tables)
        spectra = exchange(spectra, MODE_AXES)
        chi, keep, send = call(
            backward_kernel,
            [slabs] + [(2 * MODES + 1, 16, SIDE)] * 2,
            scal,
            spectra,
            view,
            tables,
        )
        received = other(send, "core")
        keep, send = call(halve_kernel, [(2 * MODES + 1, 8, SIDE)] * 2, scal, keep, received)
        received = other(send, "xlo")
        (object_step,) = call(
            step_kernel, [slab_pair], chi, probe, scalars=False, after=(keep,)
        )
        above = shift(object_step, MODE_AXES, MODES, 1)
        below = shift(object_step, MODE_AXES, MODES, -1)
        (packed,) = call(
            pack_kernel,
            [(RINGS, 3, 8, LANES)],
            keep,
            received,
            scalars=False,
            after=(above, below) if final else (object_step,),
        )
        sums = exchange(packed, "z")
        if not final:
            (counts,) = call(
                counts_kernel, [(SIDE, LANES)], scalars[step + 1], measured, after=(packed,)
            )
        placing = [scal, above, object_step, below, band]
        if final:
            part_band, _, to_right = call(
                place_kernel, [band_shape, edge, edge], *placing, after=(packed,)
            )
            from_left = shift(to_right, TILE_AXES, TILES, 1)
        shard, shards = call(
            probe_kernel,
            [(2, 8, LANES), (RINGS, 2, 8, LANES)],
            sums,
            shard,
            scalars=False,
            after=(from_left,) if final else (above, below, counts),
        )
        piece = exchange(shards, "z")
        if final:
            (rows_out,) = call(
                out_rows_kernel,
                [(2, OUT_ROWS, WIDTH)],
                scal,
                part_band,
                from_left,
                after=(shards,),
            )
            near = lax.all_gather(rows_out, "y")
            piece, near = lax.optimization_barrier((piece, near))
        else:
            part_band, to_left, to_right = call(
                place_kernel, [band_shape, edge, edge], *placing, after=(shards,)
            )
            from_left = shift(to_right, TILE_AXES, TILES, 1)
            from_right = shift(to_left, TILE_AXES, TILES, -1)
            piece, from_left, from_right = lax.optimization_barrier(
                (piece, from_left, from_right)
            )
            pieces = four_pieces(piece)
    far = other(near, "xhi")
    (object_out,) = call(object_kernel, [(2, HEIGHT, WIDTH)], scal, near, far)
    piece = exchange(piece.reshape(MODES, 4, 8, LANES), MODE_AXES)
    pieces = four_pieces(piece.reshape(RINGS, 2, 8, LANES))
    (probe_out,) = call(probe_out_kernel, [(1, 2, SIDE, SIDE)], scal, *pieces)
    return object_out, probe_out


def solution(mesh):
    grid = Mesh(mesh.devices.reshape(2, 16, 2, 2, 4), TILE_AXES + MODE_AXES)
    return jax.shard_map(
        per_device,
        mesh=grid,
        in_specs=(
            P(None, None, TILE_AXES),
            P(MODE_AXES, None, None, None),
            P(TILE_AXES, None, None, None),
            P(TILE_AXES, None),
            P(TILE_AXES, None),
            P(TILE_AXES),
            P(TILE_AXES, None),
        ),
        out_specs=(P(None, None, TILE_AXES), P(MODE_AXES, None, None, None)),
        check_vma=False,
    )
```

time: 386 us -> 376 us (0.974)
  starting transfers between devices: 188 us -> 159 us
  blocking collectives: 99.1 us -> 119 us
  waiting for transfers between devices: 41.7 us -> 56.3 us
  local copies, waits for them, and re-layouts: 14.9 us -> 4.56 us
    all_to_all x6 -> x7, blocking collectives: 68.5 us -> 104 us  [exchange(): return lax.all_to_all(value, axes, 0, 0, tiled=True)]
    ppermute x18 -> x16, waiting for transfers between devices: 41.4 us -> 12.6 us  [other(): return lax.ppermute(value, axis, [(0, 1), (1, 0)])]
    ppermute x6 -> x12, waiting for transfers between devices: 0.33 us -> 23.6 us  [shift(): lax.ppermute(value, axes, [(i, i + steps) for i in range(first, last)])]
    all_to_all x9 -> x7, waiting for transfers between devices: 0.02 us -> 20 us  [exchange(): return lax.all_to_all(value, axes, 0, 0, tiled=True)]
    ppermute x18 -> x16, starting transfers between devices: 82 us -> 63.8 us  [other(): return lax.ppermute(value, axis, [(0, 1), (1, 0)])]
    all_gather x3 -> x1, blocking collectives: 30.6 us -> 15.3 us  [per_device(): near = lax.all_gather(rows_out, 'y')]
    all_to_all x9 -> x7, starting transfers between devices: 70 us -> 58.2 us  [exchange(): return lax.all_to_all(value, axes, 0, 0, tiled=True)]
    unnamed x30 -> x22, local copies, waits for them, and re-layouts: 12.6 us -> 4.03 us
  transfers between devices with their start and end apart: 33 -> 35, of which waited for: 9 -> 19; matrix products, arithmetic and copies ran while one was open for 1% -> 0% of each run, Pallas kernels for 3% -> 3%
where the time goes in v3:
time: 376 us; the launch traced here: 374 us
  starting transfers between devices  159 us (42%)
  blocking collectives  119 us (32%)
  waiting for transfers between devices  56.3 us (15%)
  Pallas kernels  32.8 us (9%)
  local copies, waits for them, and re-layouts  4.56 us (1%)
    all_to_all x7, blocking collectives, exchange(): return lax.all_to_all(value, axes, 0, 0, tiled=True)  104 us
    ppermute x16, starting transfers between devices, other(): return lax.ppermute(value, axis, [(0, 1), (1, 0)])  63.8 us
    all_to_all x7, starting transfers between devices, exchange(): return lax.all_to_all(value, axes, 0, 0, tiled=True)  58.2 us
    ppermute x12, starting transfers between devices, shift(): lax.ppermute(value, axes, [(i, i + steps) for i in range(first, last)])  37.5 us
    pallas_call x33, Pallas kernels, call(): pl.pallas_call(body, out_shape=[jax.ShapeDtypeStruct(shape, F32) for shap...  32.8 us
    ppermute x12, waiting for transfers between devices, shift(): lax.ppermute(value, axes, [(i, i + steps) for i in range(first, last)])  23.6 us
    all_to_all x7, waiting for transfers between devices, exchange(): return lax.all_to_all(value, axes, 0, 0, tiled=True)  20 us
    all_gather x1, blocking collectives, per_device(): near = lax.all_gather(rows_out, 'y')  15.3 us
  transfers between devices with their start and end apart: 35, of which 19 were waited for; matrix products, arithmetic and copies ran while one was open for 0% of the time, Pallas kernels for 3%

profile of v3, /device:TPU:1, one launch (start us, length us, event | category | flops | bytes accessed | tf_op | source)
XLA Modules:
  0.0 374.3 jit_solution(8394607449340532680)
XLA Ops:
  1.9 8.9 %collective-permute-start = (f32[2,64,256]{2,1,0:T(8,128)S(1)}, f32[2,64,256]{2,1,0:T(8,128)S(1)}, u32[]{:S(2)}, u32[]{:S(2)}) collective-permute-start(f32[2,64,256]{2,1,0:T(8,128)S(1)} %constant_dynamic-slice_fusion.1), channel_id=1, source_target_pairs={{8,0},{16,8},{24,16},{32,24},{40,32},{48,40},{56,48},{64,56},{72,6... | collective-permute-start | bytes 393224 | tf_op jit(solution)/shard_map/ppermute | solution.py:351
  12.7 3.6 all-to-all-start
  18.6 8.3 %all-to-all-done.refs_3_.refs_1_ = f32[8,2,32,256]{3,2,1,0:T(8,128)S(1)} async-done(((f32[8,2,32,256]{3,2,1,0:T(8,128)}), f32[8,2,32,256]{3,2,1,0:T(8,128)S(1)}, u32[]{:S(2)}, u32[]{:S(2)}) %all-to-all-start) | async-done | bytes 524320 | tf_op jit(solution)/shard_map/all_to_all | solution.py:359
  26.9 1.6 first_kernel.1
  28.5 13.6 %all_to_all.70.refs_1_ = f32[8,2,32,256]{3,2,1,0:T(8,128)S(1)} all-to-all(f32[8,2,32,256]{3,2,1,0:T(8,128)S(1)} %get-tuple-element.50), channel_id=1, replica_groups=mesh['xlo'=2,'z'=16,'core'=2,'xhi'=2,'y'=4] {'xhi','y'}, dimensions={0} | all-to-all | bytes 1048576 | tf_op jit(solution)/shard_map/all_to_all | solution.py:359
  42.1 2.2 ratio_kernel.3
  44.3 13.2 %all_to_all.71.refs_1_ = f32[8,2,32,256]{3,2,1,0:T(8,128)S(1)} all-to-all(f32[8,2,32,256]{3,2,1,0:T(8,128)S(1)} %ratio_kernel.3), channel_id=1, replica_groups=mesh['xlo'=2,'z'=16,'core'=2,'xhi'=2,'y'=4] {'xhi','y'}, dimensions={0} | all-to-all | bytes 1048576 | tf_op jit(solution)/shard_map/all_to_all | solution.py:359
  57.6 1.4 backward_kernel.3
  59.0 4.8 %collective-permute-start.1 = (f32[17,16,256]{2,1,0:T(8,128)S(1)}, f32[17,16,256]{2,1,0:T(8,128)S(1)}, u32[]{:S(2)}, u32[]{:S(2)}) collective-permute-start(f32[17,16,256]{2,1,0:T(8,128)S(1)} %get-tuple-element.54), channel_id=1, source_target_pairs={{0,8},{8,0},{1,9},{9,1},{2,10},{10,2},{3,11},{11,3},{4,12},{12,4},... | collective-permute-start | bytes 835592 | tf_op jit(solution)/shard_map/ppermute | solution.py:355
  65.6 6.1 %collective-permute-start.4 = (f32[17,8,256]{2,1,0:T(8,128)S(1)}, f32[17,8,256]{2,1,0:T(8,128)S(1)}, u32[]{:S(2)}, u32[]{:S(2)}) collective-permute-start(f32[17,8,256]{2,1,0:T(8,128)S(1)} %get-tuple-element.57), channel_id=1, source_target_pairs={{0,256},{256,0},{1,257},{257,1},{2,258},{258,2},{3,259},{259,3},{4... | collective-permute-start | bytes 417800 | tf_op jit(solution)/shard_map/ppermute | solution.py:355
  71.9 3.5 collective-permute-done.4.refs_1_
  76.1 9.8 %all-to-all-start.3 = ((f32[16,3,8,128]{3,2,1,0:T(8,128)}), f32[16,3,8,128]{3,2,1,0:T(8,128)S(1)}, u32[]{:S(2)}, u32[]{:S(2)}) async-start(f32[16,3,8,128]{3,2,1,0:T(8,128)} %pack_kernel.3.refs_2_), calls=%async_computation.3 | async-start | bytes 393216 | tf_op jit(solution)/shard_map/all_to_all | solution.py:359
  85.9 1.8 collective-permute-start.2
  89.9 3.2 collective-permute-done.3.refs_3_
  93.1 5.2 %all-to-all-done.3.refs_0_ = f32[16,3,8,128]{3,2,1,0:T(8,128)S(1)} async-done(((f32[16,3,8,128]{3,2,1,0:T(8,128)}), f32[16,3,8,128]{3,2,1,0:T(8,128)S(1)}, u32[]{:S(2)}, u32[]{:S(2)}) %all-to-all-start.3) | async-done | bytes 196640 | tf_op jit(solution)/shard_map/all_to_all | solution.py:359
  99.0 8.6 %all-to-all-start.4 = ((f32[16,2,8,128]{3,2,1,0:T(8,128)}), f32[16,2,8,128]{3,2,1,0:T(8,128)S(1)}, u32[]{:S(2)}, u32[]{:S(2)}) async-start(f32[16,2,8,128]{3,2,1,0:T(8,128)} %get-tuple-element.59.refs_5_), calls=%async_computation.4 | async-start | bytes 262144 | tf_op jit(solution)/shard_map/all_to_all | solution.py:359
  109.1 4.8 %collective-permute-start.5 = (f32[2,64,256]{2,1,0:T(8,128)S(1)}, f32[2,64,256]{2,1,0:T(8,128)S(1)}, u32[]{:S(2)}, u32[]{:S(2)}) collective-permute-start(f32[2,64,256]{2,1,0:T(8,128)S(1)} %get-tuple-element.61), channel_id=1, source_target_pairs={{0,8},{8,16},{16,24},{24,32},{32,40},{40,48},{48,56},{56,64},{64,7... | collective-permute-start | bytes 393224 | tf_op jit(solution)/shard_map/ppermute | solution.py:351
  113.9 1.9 collective-permute-start.6
  116.8 3.7 collective-permute-done.6.refs_3_
  120.5 2.2 collective-permute-start.7
  122.8 4.8 %collective-permute-start.8 = (f32[16,2,8,128]{3,2,1,0:T(8,128)S(1)}, f32[16,2,8,128]{3,2,1,0:T(8,128)S(1)}, u32[]{:S(2)}, u32[]{:S(2)}) collective-permute-start(f32[16,2,8,128]{3,2,1,0:T(8,128)S(1)} %all-to-all-done.4.refs_2_), channel_id=1, source_target_pairs={{0,8},{8,0},{1,9},{9,1},{2,10},{10,2},{3,11},{11,3},{4,12},{12,4},... | collective-permute-start | bytes 393224 | tf_op jit(solution)/shard_map/ppermute | solution.py:355
  127.6 4.3 %collective-permute-start.9 = (f32[16,2,8,128]{3,2,1,0:T(8,128)S(1)}, f32[16,2,8,128]{3,2,1,0:T(8,128)S(1)}, u32[]{:S(2)}, u32[]{:S(2)}) collective-permute-start(f32[16,2,8,128]{3,2,1,0:T(8,128)S(1)} %collective-permute-done.7.refs_3_), channel_id=1, source_target_pairs={{0,8},{8,0},{1,9},{9,1},{2,10},{10,2},{3,11},{11,3},{4,12},{12,4},... | collective-permute-start | bytes 393224 | tf_op jit(solution)/shard_map/ppermute | solution.py:355
  133.6 1.4 next_kernel.2
  135.1 16.5 %all_to_all.72.refs_1_ = f32[8,2,32,256]{3,2,1,0:T(8,128)S(1)} all-to-all(f32[8,2,32,256]{3,2,1,0:T(8,128)S(1)} %get-tuple-element.67), channel_id=1, replica_groups=mesh['xlo'=2,'z'=16,'core'=2,'xhi'=2,'y'=4] {'xhi','y'}, dimensions={0} | all-to-all | bytes 1048576 | tf_op jit(solution)/shard_map/all_to_all | solution.py:359
  151.5 2.2 ratio_kernel.4
  153.8 13.9 %all_to_all.73.refs_1_ = f32[8,2,32,256]{3,2,1,0:T(8,128)S(1)} all-to-all(f32[8,2,32,256]{3,2,1,0:T(8,128)S(1)} %ratio_kernel.4), channel_id=1, replica_groups=mesh['xlo'=2,'z'=16,'core'=2,'xhi'=2,'y'=4] {'xhi','y'}, dimensions={0} | all-to-all | bytes 1048576 | tf_op jit(solution)/shard_map/all_to_all | solution.py:359
  167.7 1.4 backward_kernel.4
  169.1 4.4 %collective-permute-start.10 = (f32[17,16,256]{2,1,0:T(8,128)S(1)}, f32[17,16,256]{2,1,0:T(8,128)S(1)}, u32[]{:S(2)}, u32[]{:S(2)}) collective-permute-start(f32[17,16,256]{2,1,0:T(8,128)S(1)} %get-tuple-element.71), channel_id=1, source_target_pairs={{0,8},{8,0},{1,9},{9,1},{2,10},{10,2},{3,11},{11,3},{4,12},{12,4},... | collective-permute-start | bytes 835592 | tf_op jit(solution)/shard_map/ppermute | solution.py:355
  175.2 2.2 collective-permute-start.13
  177.6 4.4 %collective-permute-done.13.refs_1_ = f32[17,8,256]{2,1,0:T(8,128)S(1)} collective-permute-done((f32[17,8,256]{2,1,0:T(8,128)S(1)}, f32[17,8,256]{2,1,0:T(8,128)S(1)}, u32[]{:S(2)}, u32[]{:S(2)}) %collective-permute-start.13) | collective-permute-done | bytes 139296 | tf_op jit(solution)/shard_map/ppermute | solution.py:355
  182.7 9.3 %all-to-all-start.7 = ((f32[16,3,8,128]{3,2,1,0:T(8,128)}), f32[16,3,8,128]{3,2,1,0:T(8,128)S(1)}, u32[]{:S(2)}, u32[]{:S(2)}) async-start(f32[16,3,8,128]{3,2,1,0:T(8,128)} %pack_kernel.4.refs_2_), calls=%async_computation.7 | async-start | bytes 393216 | tf_op jit(solution)/shard_map/all_to_all | solution.py:359
  192.0 1.8 collective-permute-start.11
  196.0 3.2 collective-permute-done.12.refs_3_
  199.2 5.2 %all-to-all-done.7.refs_0_ = f32[16,3,8,128]{3,2,1,0:T(8,128)S(1)} async-done(((f32[16,3,8,128]{3,2,1,0:T(8,128)}), f32[16,3,8,128]{3,2,1,0:T(8,128)S(1)}, u32[]{:S(2)}, u32[]{:S(2)}) %all-to-all-start.7) | async-done | bytes 196640 | tf_op jit(solution)/shard_map/all_to_all | solution.py:359
  205.0 8.6 %all-to-all-start.8 = ((f32[16,2,8,128]{3,2,1,0:T(8,128)}), f32[16,2,8,128]{3,2,1,0:T(8,128)S(1)}, u32[]{:S(2)}, u32[]{:S(2)}) async-start(f32[16,2,8,128]{3,2,1,0:T(8,128)} %get-tuple-element.76.refs_5_), calls=%async_computation.8 | async-start | bytes 262144 | tf_op jit(solution)/shard_map/all_to_all | solution.py:359
  214.4 4.8 %collective-permute-start.14 = (f32[2,64,256]{2,1,0:T(8,128)S(1)}, f32[2,64,256]{2,1,0:T(8,128)S(1)}, u32[]{:S(2)}, u32[]{:S(2)}) collective-permute-start(f32[2,64,256]{2,1,0:T(8,128)S(1)} %get-tuple-element.78), channel_id=1, source_target_pairs={{0,8},{8,16},{16,24},{24,32},{32,40},{40,48},{48,56},{56,64},{64,7... | collective-permute-start | bytes 393224 | tf_op jit(solution)/shard_map/ppermute | solution.py:351
  219.2 1.9 collective-permute-start.15
  221.1 1.7 collective-permute-done.14.refs_2_
  222.8 3.3 collective-permute-done.15.refs_3_
  226.1 2.2 collective-permute-start.16
  228.3 5.3 %collective-permute-start.17 = (f32[16,2,8,128]{3,2,1,0:T(8,128)S(1)}, f32[16,2,8,128]{3,2,1,0:T(8,128)S(1)}, u32[]{:S(2)}, u32[]{:S(2)}) collective-permute-start(f32[16,2,8,128]{3,2,1,0:T(8,128)S(1)} %all-to-all-done.8.refs_2_), channel_id=1, source_target_pairs={{0,8},{8,0},{1,9},{9,1},{2,10},{10,2},{3,11},{11,3},{4,12},{12,4},... | collective-permute-start | bytes 393224 | tf_op jit(solution)/shard_map/ppermute | solution.py:355
  233.6 4.3 %collective-permute-start.18 = (f32[16,2,8,128]{3,2,1,0:T(8,128)S(1)}, f32[16,2,8,128]{3,2,1,0:T(8,128)S(1)}, u32[]{:S(2)}, u32[]{:S(2)}) collective-permute-start(f32[16,2,8,128]{3,2,1,0:T(8,128)S(1)} %collective-permute-done.16.refs_3_), channel_id=1, source_target_pairs={{0,8},{8,0},{1,9},{9,1},{2,10},{10,2},{3,11},{11,3},{4,12},{12,4},... | collective-permute-start | bytes 393224 | tf_op jit(solution)/shard_map/ppermute | solution.py:355
  238.9 1.4 next_kernel.3
  240.3 16.1 %all_to_all.74.refs_1_ = f32[8,2,32,256]{3,2,1,0:T(8,128)S(1)} all-to-all(f32[8,2,32,256]{3,2,1,0:T(8,128)S(1)} %get-tuple-element.84), channel_id=1, replica_groups=mesh['xlo'=2,'z'=16,'core'=2,'xhi'=2,'y'=4] {'xhi','y'}, dimensions={0} | all-to-all | bytes 1048576 | tf_op jit(solution)/shard_map/all_to_all | solution.py:359
  256.4 2.2 ratio_kernel.5
  258.7 13.2 %all_to_all.75.refs_1_ = f32[8,2,32,256]{3,2,1,0:T(8,128)S(1)} all-to-all(f32[8,2,32,256]{3,2,1,0:T(8,128)S(1)} %ratio_kernel.5), channel_id=1, replica_groups=mesh['xlo'=2,'z'=16,'core'=2,'xhi'=2,'y'=4] {'xhi','y'}, dimensions={0} | all-to-all | bytes 1048576 | tf_op jit(solution)/shard_map/all_to_all | solution.py:359
  271.9 1.4 backward_kernel.5
  273.3 4.8 %collective-permute-start.19 = (f32[17,16,256]{2,1,0:T(8,128)S(1)}, f32[17,16,256]{2,1,0:T(8,128)S(1)}, u32[]{:S(2)}, u32[]{:S(2)}) collective-permute-start(f32[17,16,256]{2,1,0:T(8,128)S(1)} %get-tuple-element.86), channel_id=1, source_target_pairs={{0,8},{8,0},{1,9},{9,1},{2,10},{10,2},{3,11},{11,3},{4,12},{12,4},... | collective-permute-start | bytes 835592 | tf_op jit(solution)/shard_map/ppermute | solution.py:355
  279.9 2.2 collective-permute-start.20
  282.2 1.8 collective-permute-start.21
  285.4 3.7 collective-permute-done.22.refs_3_
  289.8 8.5 %all-to-all-start.11 = ((f32[16,3,8,128]{3,2,1,0:T(8,128)}), f32[16,3,8,128]{3,2,1,0:T(8,128)S(1)}, u32[]{:S(2)}, u32[]{:S(2)}) async-start(f32[16,3,8,128]{3,2,1,0:T(8,128)} %pack_kernel.5.refs_5_), calls=%async_computation.11 | async-start | bytes 393216 | tf_op jit(solution)/shard_map/all_to_all | solution.py:359
  298.4 1.4 place_kernel.5
  299.7 5.8 %collective-permute-start.23 = (f32[2,64,256]{2,1,0:T(8,128)S(1)}, f32[2,64,256]{2,1,0:T(8,128)S(1)}, u32[]{:S(2)}, u32[]{:S(2)}) collective-permute-start(f32[2,64,256]{2,1,0:T(8,128)S(1)} %get-tuple-element.93), channel_id=1, source_target_pairs={{0,8},{8,16},{16,24},{24,32},{32,40},{40,48},{48,56},{56,64},{64,7... | collective-permute-start | bytes 393224 | tf_op jit(solution)/shard_map/ppermute | solution.py:351
  305.5 3.8 %collective-permute-done.23.refs_2_ = f32[2,64,256]{2,1,0:T(8,128)S(1)} collective-permute-done((f32[2,64,256]{2,1,0:T(8,128)S(1)}, f32[2,64,256]{2,1,0:T(8,128)S(1)}, u32[]{:S(2)}, u32[]{:S(2)}) %collective-permute-start.23) | collective-permute-done | bytes 131104 | tf_op jit(solution)/shard_map/ppermute | solution.py:351
  311.4 9.6 %all-to-all-start.12 = ((f32[16,2,8,128]{3,2,1,0:T(8,128)}), f32[16,2,8,128]{3,2,1,0:T(8,128)S(1)}, u32[]{:S(2)}, u32[]{:S(2)}) async-start(f32[16,2,8,128]{3,2,1,0:T(8,128)} %get-tuple-element.94.refs_3_), calls=%async_computation.12 | async-start | bytes 262144 | tf_op jit(solution)/shard_map/all_to_all | solution.py:359
  321.6 15.3 %all-gather = f32[8,40,512]{2,1,0:T(8,128)S(1)} all-gather(f32[2,40,512]{2,1,0:T(8,128)S(1)} %out_rows_kernel.1), channel_id=2, replica_groups=mesh['xlo'=2,'z'=16,'core'=2,'xhi'=2,'y'=4] {'y'}, dimensions={0}, use_global_device_ids=true | all-gather | bytes 819200 | tf_op jit(solution)/shard_map/all_gather | solution.py:477
  336.9 2.3 collective-permute-start.24
  339.3 17.3 %all_to_all.76 = f32[8,4,8,128]{3,2,1,0:T(8,128)S(1)} all-to-all(f32[8,4,8,128]{3,2,1,0:T(8,128)S(1)} %bitcast.23), channel_id=1, replica_groups=mesh['xlo'=2,'z'=16,'core'=2,'xhi'=2,'y'=4] {'xhi','y'}, dimensions={0} | all-to-all | bytes 262144 | tf_op jit(solution)/shard_map/all_to_all | solution.py:359
  356.6 1.9 collective-permute-start.25
  358.5 7.2 %collective-permute-start.26 = (f32[16,2,8,128]{3,2,1,0:T(8,128)S(1)}, f32[16,2,8,128]{3,2,1,0:T(8,128)S(1)}, u32[]{:S(2)}, u32[]{:S(2)}) collective-permute-start(f32[16,2,8,128]{3,2,1,0:T(8,128)S(1)} %bitcast.21), channel_id=1, source_target_pairs={{0,8},{8,0},{1,9},{9,1},{2,10},{10,2},{3,11},{11,3},{4,12},{12,4},... | collective-permute-start | bytes 393224 | tf_op jit(solution)/shard_map/ppermute | solution.py:355
  365.7 4.7 %collective-permute-start.27 = (f32[16,2,8,128]{3,2,1,0:T(8,128)S(1)}, f32[16,2,8,128]{3,2,1,0:T(8,128)S(1)}, u32[]{:S(2)}, u32[]{:S(2)}) collective-permute-start(f32[16,2,8,128]{3,2,1,0:T(8,128)S(1)} %collective-permute-done.25.refs_2_), channel_id=1, source_target_pairs={{0,8},{8,0},{1,9},{9,1},{2,10},{10,2},{3,11},{11,3},{4,12},{12,4},... | collective-permute-start | bytes 393224 | tf_op jit(solution)/shard_map/ppermute | solution.py:355
  371.3 1.4 probe_out_kernel.1
  372.7 1.6 object_kernel.1
  (84 shorter events, 28.8 us)
Async XLA Ops:
  0.6 1.3 copy-start
  0.7 15.7 %copy-start.8 = (s32[1,3]{1,0:T(1,128)S(1)}, s32[1,3]{1,0:T(1,128)}, u32[]{:S(2)}) copy-start(s32[1,3]{1,0:T(1,128)} %param.14) | copy-start | bytes 40
  0.7 15.7 %copy-start.9 = (s32[1,3]{1,0:T(1,128)S(1)}, s32[1,3]{1,0:T(1,128)}, u32[]{:S(2)}) copy-start(s32[1,3]{1,0:T(1,128)} %param.12) | copy-start | bytes 40
  0.7 15.7 %copy-start.10 = (s32[1,3]{1,0:T(1,128)S(1)}, s32[1,3]{1,0:T(1,128)}, u32[]{:S(2)}) copy-start(s32[1,3]{1,0:T(1,128)} %param.11) | copy-start | bytes 40
  1.9 15.8 %copy-start.2 = (bf16[1,3,256,256]{3,2,1,0:T(8,128)(2,1)S(1)}, bf16[1,3,256,256]{3,2,1,0:T(8,128)(2,1)}, u32[]{:S(2)}) copy-start(bf16[1,3,256,256]{3,2,1,0:T(8,128)(2,1)} %refs_1_.5) | copy-start | bytes 1179652
  1.9 16.7 %collective-permute-start = (f32[2,64,256]{2,1,0:T(8,128)S(1)}, f32[2,64,256]{2,1,0:T(8,128)S(1)}, u32[]{:S(2)}, u32[]{:S(2)}) collective-permute-start(f32[2,64,256]{2,1,0:T(8,128)S(1)} %constant_dynamic-slice_fusion.1), channel_id=1, source_target_pairs={{8,0},{16,8},{24,16},{32,24},{40,32},{48,40},{56,48},{64,56},{72,6... | collective-permute-start | bytes 393224 | tf_op jit(solution)/shard_map/ppermute | solution.py:351
  10.8 1.0 copy-start.3
  12.7 14.2 %copy-start.1 = (bf16[2,2,256,256]{3,2,1,0:T(8,128)(2,1)S(1)}, bf16[2,2,256,256]{3,2,1,0:T(8,128)(2,1)}, u32[]{:S(2)}) copy-start(bf16[2,2,256,256]{3,2,1,0:T(8,128)(2,1)} %constant.35.clone.refs_4_.refs_3_.refs_6_) | copy-start | bytes 1572868
  12.7 14.1 %all-to-all-start = ((f32[8,2,32,256]{3,2,1,0:T(8,128)}), f32[8,2,32,256]{3,2,1,0:T(8,128)S(1)}, u32[]{:S(2)}, u32[]{:S(2)}) async-start(f32[8,2,32,256]{3,2,1,0:T(8,128)} %split_kernel.1), calls=%async_computation | async-start | bytes 1048576 | tf_op jit(solution)/shard_map/all_to_all | solution.py:359
  28.5 13.6 %copy-start.6 = (f32[2,8,128]{2,1,0:T(8,128)}, f32[2,8,128]{2,1,0:T(8,128)S(1)}, u32[]{:S(2)}) copy-start(f32[2,8,128]{2,1,0:T(8,128)S(1)} %get-tuple-element.58.refs_1_) | copy-start | bytes 24580
  59.0 6.0 %collective-permute-start.1 = (f32[17,16,256]{2,1,0:T(8,128)S(1)}, f32[17,16,256]{2,1,0:T(8,128)S(1)}, u32[]{:S(2)}, u32[]{:S(2)}) collective-permute-start(f32[17,16,256]{2,1,0:T(8,128)S(1)} %get-tuple-element.54), channel_id=1, source_target_pairs={{0,8},{8,0},{1,9},{9,1},{2,10},{10,2},{3,11},{11,3},{4,12},{12,4},... | collective-permute-start | bytes 835592 | tf_op jit(solution)/shard_map/ppermute | solution.py:355
  65.6 9.8 %collective-permute-start.4 = (f32[17,8,256]{2,1,0:T(8,128)S(1)}, f32[17,8,256]{2,1,0:T(8,128)S(1)}, u32[]{:S(2)}, u32[]{:S(2)}) collective-permute-start(f32[17,8,256]{2,1,0:T(8,128)S(1)} %get-tuple-element.57), channel_id=1, source_target_pairs={{0,256},{256,0},{1,257},{257,1},{2,258},{258,2},{3,259},{259,3},{4... | collective-permute-start | bytes 417800 | tf_op jit(solution)/shard_map/ppermute | solution.py:355
  71.7 26.6 %copy-start.7 = (f32[2,8,128]{2,1,0:T(8,128)S(1)}, f32[2,8,128]{2,1,0:T(8,128)}, u32[]{:S(2)}) copy-start(f32[2,8,128]{2,1,0:T(8,128)} %copy-done.6) | copy-start | bytes 24580
  76.1 22.2 %all-to-all-start.3 = ((f32[16,3,8,128]{3,2,1,0:T(8,128)}), f32[16,3,8,128]{3,2,1,0:T(8,128)S(1)}, u32[]{:S(2)}, u32[]{:S(2)}) async-start(f32[16,3,8,128]{3,2,1,0:T(8,128)} %pack_kernel.3.refs_2_), calls=%async_computation.3 | async-start | bytes 393216 | tf_op jit(solution)/shard_map/all_to_all | solution.py:359
  85.9 4.0 %collective-permute-start.2 = (f32[2,32,256]{2,1,0:T(8,128)S(1)}, f32[2,32,256]{2,1,0:T(8,128)S(1)}, u32[]{:S(2)}, u32[]{:S(2)}) collective-permute-start(f32[2,32,256]{2,1,0:T(8,128)S(1)} %step_kernel.3.refs_2_), channel_id=1, source_target_pairs={{0,1},{1,2},{2,3},{3,4},{4,5},{5,6},{6,7},{8,9},{9,10},{10,11},{11... | collective-permute-start | bytes 196616 | tf_op jit(solution)/shard_map/ppermute | solution.py:351
  87.8 5.3 %collective-permute-start.3 = (f32[2,32,256]{2,1,0:T(8,128)S(1)}, f32[2,32,256]{2,1,0:T(8,128)S(1)}, u32[]{:S(2)}, u32[]{:S(2)}) collective-permute-start(f32[2,32,256]{2,1,0:T(8,128)S(1)} %step_kernel.3.refs_2_), channel_id=1, source_target_pairs={{1,0},{2,1},{3,2},{4,3},{5,4},{6,5},{7,6},{9,8},{10,9},{11,10},{12... | collective-permute-start | bytes 196616 | tf_op jit(solution)/shard_map/ppermute | solution.py:351
  99.0 21.6 %all-to-all-start.4 = ((f32[16,2,8,128]{3,2,1,0:T(8,128)}), f32[16,2,8,128]{3,2,1,0:T(8,128)S(1)}, u32[]{:S(2)}, u32[]{:S(2)}) async-start(f32[16,2,8,128]{3,2,1,0:T(8,128)} %get-tuple-element.59.refs_5_), calls=%async_computation.4 | async-start | bytes 262144 | tf_op jit(solution)/shard_map/all_to_all | solution.py:359
  108.4 0.7 copy-start.4
  109.1 7.7 %collective-permute-start.5 = (f32[2,64,256]{2,1,0:T(8,128)S(1)}, f32[2,64,256]{2,1,0:T(8,128)S(1)}, u32[]{:S(2)}, u32[]{:S(2)}) collective-permute-start(f32[2,64,256]{2,1,0:T(8,128)S(1)} %get-tuple-element.61), channel_id=1, source_target_pairs={{0,8},{8,16},{16,24},{24,32},{32,40},{40,48},{48,56},{56,64},{64,7... | collective-permute-start | bytes 393224 | tf_op jit(solution)/shard_map/ppermute | solution.py:351
  113.9 6.7 %collective-permute-start.6 = (f32[2,64,256]{2,1,0:T(8,128)S(1)}, f32[2,64,256]{2,1,0:T(8,128)S(1)}, u32[]{:S(2)}, u32[]{:S(2)}) collective-permute-start(f32[2,64,256]{2,1,0:T(8,128)S(1)} %get-tuple-element.62), channel_id=1, source_target_pairs={{8,0},{16,8},{24,16},{32,24},{40,32},{48,40},{56,48},{64,56},{72,6... | collective-permute-start | bytes 393224 | tf_op jit(solution)/shard_map/ppermute | solution.py:351
  120.5 7.0 %collective-permute-start.7 = (f32[16,2,8,128]{3,2,1,0:T(8,128)S(1)}, f32[16,2,8,128]{3,2,1,0:T(8,128)S(1)}, u32[]{:S(2)}, u32[]{:S(2)}) collective-permute-start(f32[16,2,8,128]{3,2,1,0:T(8,128)S(1)} %all-to-all-done.4.refs_2_), channel_id=1, source_target_pairs={{0,256},{256,0},{1,257},{257,1},{2,258},{258,2},{3,259},{259,3},{4... | collective-permute-start | bytes 393224 | tf_op jit(solution)/shard_map/ppermute | solution.py:355
  122.8 10.8 %collective-permute-start.8 = (f32[16,2,8,128]{3,2,1,0:T(8,128)S(1)}, f32[16,2,8,128]{3,2,1,0:T(8,128)S(1)}, u32[]{:S(2)}, u32[]{:S(2)}) collective-permute-start(f32[16,2,8,128]{3,2,1,0:T(8,128)S(1)} %all-to-all-done.4.refs_2_), channel_id=1, source_target_pairs={{0,8},{8,0},{1,9},{9,1},{2,10},{10,2},{3,11},{11,3},{4,12},{12,4},... | collective-permute-start | bytes 393224 | tf_op jit(solution)/shard_map/ppermute | solution.py:355
  127.6 6.1 %collective-permute-start.9 = (f32[16,2,8,128]{3,2,1,0:T(8,128)S(1)}, f32[16,2,8,128]{3,2,1,0:T(8,128)S(1)}, u32[]{:S(2)}, u32[]{:S(2)}) collective-permute-start(f32[16,2,8,128]{3,2,1,0:T(8,128)S(1)} %collective-permute-done.7.refs_3_), channel_id=1, source_target_pairs={{0,8},{8,0},{1,9},{9,1},{2,10},{10,2},{3,11},{11,3},{4,12},{12,4},... | collective-permute-start | bytes 393224 | tf_op jit(solution)/shard_map/ppermute | solution.py:355
  131.9 1.0 copy-start.5
  169.1 5.5 %collective-permute-start.10 = (f32[17,16,256]{2,1,0:T(8,128)S(1)}, f32[17,16,256]{2,1,0:T(8,128)S(1)}, u32[]{:S(2)}, u32[]{:S(2)}) collective-permute-start(f32[17,16,256]{2,1,0:T(8,128)S(1)} %get-tuple-element.71), channel_id=1, source_target_pairs={{0,8},{8,0},{1,9},{9,1},{2,10},{10,2},{3,11},{11,3},{4,12},{12,4},... | collective-permute-start | bytes 835592 | tf_op jit(solution)/shard_map/ppermute | solution.py:355
  175.2 6.8 %collective-permute-start.13 = (f32[17,8,256]{2,1,0:T(8,128)S(1)}, f32[17,8,256]{2,1,0:T(8,128)S(1)}, u32[]{:S(2)}, u32[]{:S(2)}) collective-permute-start(f32[17,8,256]{2,1,0:T(8,128)S(1)} %get-tuple-element.74), channel_id=1, source_target_pairs={{0,256},{256,0},{1,257},{257,1},{2,258},{258,2},{3,259},{259,3},{4... | collective-permute-start | bytes 417800 | tf_op jit(solution)/shard_map/ppermute | solution.py:355
  182.7 21.7 %all-to-all-start.7 = ((f32[16,3,8,128]{3,2,1,0:T(8,128)}), f32[16,3,8,128]{3,2,1,0:T(8,128)S(1)}, u32[]{:S(2)}, u32[]{:S(2)}) async-start(f32[16,3,8,128]{3,2,1,0:T(8,128)} %pack_kernel.4.refs_2_), calls=%async_computation.7 | async-start | bytes 393216 | tf_op jit(solution)/shard_map/all_to_all | solution.py:359
  192.0 4.0 %collective-permute-start.11 = (f32[2,32,256]{2,1,0:T(8,128)S(1)}, f32[2,32,256]{2,1,0:T(8,128)S(1)}, u32[]{:S(2)}, u32[]{:S(2)}) collective-permute-start(f32[2,32,256]{2,1,0:T(8,128)S(1)} %step_kernel.4.refs_2_), channel_id=1, source_target_pairs={{0,1},{1,2},{2,3},{3,4},{4,5},{5,6},{6,7},{8,9},{9,10},{10,11},{11... | collective-permute-start | bytes 196616 | tf_op jit(solution)/shard_map/ppermute | solution.py:351
  193.8 5.3 %collective-permute-start.12 = (f32[2,32,256]{2,1,0:T(8,128)S(1)}, f32[2,32,256]{2,1,0:T(8,128)S(1)}, u32[]{:S(2)}, u32[]{:S(2)}) collective-permute-start(f32[2,32,256]{2,1,0:T(8,128)S(1)} %step_kernel.4.refs_2_), channel_id=1, source_target_pairs={{1,0},{2,1},{3,2},{4,3},{5,4},{6,5},{7,6},{9,8},{10,9},{11,10},{12... | collective-permute-start | bytes 196616 | tf_op jit(solution)/shard_map/ppermute | solution.py:351
  205.0 21.0 %all-to-all-start.8 = ((f32[16,2,8,128]{3,2,1,0:T(8,128)}), f32[16,2,8,128]{3,2,1,0:T(8,128)S(1)}, u32[]{:S(2)}, u32[]{:S(2)}) async-start(f32[16,2,8,128]{3,2,1,0:T(8,128)} %get-tuple-element.76.refs_5_), calls=%async_computation.8 | async-start | bytes 262144 | tf_op jit(solution)/shard_map/all_to_all | solution.py:359
  214.4 8.4 %collective-permute-start.14 = (f32[2,64,256]{2,1,0:T(8,128)S(1)}, f32[2,64,256]{2,1,0:T(8,128)S(1)}, u32[]{:S(2)}, u32[]{:S(2)}) collective-permute-start(f32[2,64,256]{2,1,0:T(8,128)S(1)} %get-tuple-element.78), channel_id=1, source_target_pairs={{0,8},{8,16},{16,24},{24,32},{32,40},{40,48},{48,56},{56,64},{64,7... | collective-permute-start | bytes 393224 | tf_op jit(solution)/shard_map/ppermute | solution.py:351
  219.2 6.9 %collective-permute-start.15 = (f32[2,64,256]{2,1,0:T(8,128)S(1)}, f32[2,64,256]{2,1,0:T(8,128)S(1)}, u32[]{:S(2)}, u32[]{:S(2)}) collective-permute-start(f32[2,64,256]{2,1,0:T(8,128)S(1)} %get-tuple-element.79), channel_id=1, source_target_pairs={{8,0},{16,8},{24,16},{32,24},{40,32},{48,40},{56,48},{64,56},{72,6... | collective-permute-start | bytes 393224 | tf_op jit(solution)/shard_map/ppermute | solution.py:351
  226.1 7.5 %collective-permute-start.16 = (f32[16,2,8,128]{3,2,1,0:T(8,128)S(1)}, f32[16,2,8,128]{3,2,1,0:T(8,128)S(1)}, u32[]{:S(2)}, u32[]{:S(2)}) collective-permute-start(f32[16,2,8,128]{3,2,1,0:T(8,128)S(1)} %all-to-all-done.8.refs_2_), channel_id=1, source_target_pairs={{0,256},{256,0},{1,257},{257,1},{2,258},{258,2},{3,259},{259,3},{4... | collective-permute-start | bytes 393224 | tf_op jit(solution)/shard_map/ppermute | solution.py:355
  228.3 10.4 %collective-permute-start.17 = (f32[16,2,8,128]{3,2,1,0:T(8,128)S(1)}, f32[16,2,8,128]{3,2,1,0:T(8,128)S(1)}, u32[]{:S(2)}, u32[]{:S(2)}) collective-permute-start(f32[16,2,8,128]{3,2,1,0:T(8,128)S(1)} %all-to-all-done.8.refs_2_), channel_id=1, source_target_pairs={{0,8},{8,0},{1,9},{9,1},{2,10},{10,2},{3,11},{11,3},{4,12},{12,4},... | collective-permute-start | bytes 393224 | tf_op jit(solution)/shard_map/ppermute | solution.py:355
  233.6 5.3 %collective-permute-start.18 = (f32[16,2,8,128]{3,2,1,0:T(8,128)S(1)}, f32[16,2,8,128]{3,2,1,0:T(8,128)S(1)}, u32[]{:S(2)}, u32[]{:S(2)}) collective-permute-start(f32[16,2,8,128]{3,2,1,0:T(8,128)S(1)} %collective-permute-done.16.refs_3_), channel_id=1, source_target_pairs={{0,8},{8,0},{1,9},{9,1},{2,10},{10,2},{3,11},{11,3},{4,12},{12,4},... | collective-permute-start | bytes 393224 | tf_op jit(solution)/shard_map/ppermute | solution.py:355
  273.3 6.0 %collective-permute-start.19 = (f32[17,16,256]{2,1,0:T(8,128)S(1)}, f32[17,16,256]{2,1,0:T(8,128)S(1)}, u32[]{:S(2)}, u32[]{:S(2)}) collective-permute-start(f32[17,16,256]{2,1,0:T(8,128)S(1)} %get-tuple-element.86), channel_id=1, source_target_pairs={{0,8},{8,0},{1,9},{9,1},{2,10},{10,2},{3,11},{11,3},{4,12},{12,4},... | collective-permute-start | bytes 835592 | tf_op jit(solution)/shard_map/ppermute | solution.py:355
  279.9 9.2 %collective-permute-start.20 = (f32[17,8,256]{2,1,0:T(8,128)S(1)}, f32[17,8,256]{2,1,0:T(8,128)S(1)}, u32[]{:S(2)}, u32[]{:S(2)}) collective-permute-start(f32[17,8,256]{2,1,0:T(8,128)S(1)} %get-tuple-element.88), channel_id=1, source_target_pairs={{0,256},{256,0},{1,257},{257,1},{2,258},{258,2},{3,259},{259,3},{4... | collective-permute-start | bytes 417800 | tf_op jit(solution)/shard_map/ppermute | solution.py:355
  282.2 3.2 collective-permute-start.21
  284.1 5.0 %collective-permute-start.22 = (f32[2,32,256]{2,1,0:T(8,128)S(1)}, f32[2,32,256]{2,1,0:T(8,128)S(1)}, u32[]{:S(2)}, u32[]{:S(2)}) collective-permute-start(f32[2,32,256]{2,1,0:T(8,128)S(1)} %step_kernel.5.refs_2_), channel_id=1, source_target_pairs={{1,0},{2,1},{3,2},{4,3},{5,4},{6,5},{7,6},{9,8},{10,9},{11,10},{12... | collective-permute-start | bytes 196616 | tf_op jit(solution)/shard_map/ppermute | solution.py:351
  289.8 20.9 %all-to-all-start.11 = ((f32[16,3,8,128]{3,2,1,0:T(8,128)}), f32[16,3,8,128]{3,2,1,0:T(8,128)S(1)}, u32[]{:S(2)}, u32[]{:S(2)}) async-start(f32[16,3,8,128]{3,2,1,0:T(8,128)} %pack_kernel.5.refs_5_), calls=%async_computation.11 | async-start | bytes 393216 | tf_op jit(solution)/shard_map/all_to_all | solution.py:359
  299.7 9.6 %collective-permute-start.23 = (f32[2,64,256]{2,1,0:T(8,128)S(1)}, f32[2,64,256]{2,1,0:T(8,128)S(1)}, u32[]{:S(2)}, u32[]{:S(2)}) collective-permute-start(f32[2,64,256]{2,1,0:T(8,128)S(1)} %get-tuple-element.93), channel_id=1, source_target_pairs={{0,8},{8,16},{16,24},{24,32},{32,40},{40,48},{48,56},{56,64},{64,7... | collective-permute-start | bytes 393224 | tf_op jit(solution)/shard_map/ppermute | solution.py:351
  311.4 25.5 %all-to-all-start.12 = ((f32[16,2,8,128]{3,2,1,0:T(8,128)}), f32[16,2,8,128]{3,2,1,0:T(8,128)S(1)}, u32[]{:S(2)}, u32[]{:S(2)}) async-start(f32[16,2,8,128]{3,2,1,0:T(8,128)} %get-tuple-element.94.refs_3_), calls=%async_computation.12 | async-start | bytes 262144 | tf_op jit(solution)/shard_map/all_to_all | solution.py:359
  336.9 35.8 %collective-permute-start.24 = (f32[4,2,40,512]{3,2,1,0:T(8,128)S(1)}, f32[4,2,40,512]{3,2,1,0:T(8,128)S(1)}, u32[]{:S(2)}, u32[]{:S(2)}) collective-permute-start(f32[4,2,40,512]{3,2,1,0:T(8,128)S(1)} %bitcast.18), channel_id=1, source_target_pairs={{0,4},{4,0},{1,5},{5,1},{2,6},{6,2},{3,7},{7,3},{8,12},{12,8},{9,1... | collective-permute-start | bytes 1966088 | tf_op jit(solution)/shard_map/ppermute | solution.py:355
  356.6 9.1 %collective-permute-start.25 = (f32[16,2,8,128]{3,2,1,0:T(8,128)S(1)}, f32[16,2,8,128]{3,2,1,0:T(8,128)S(1)}, u32[]{:S(2)}, u32[]{:S(2)}) collective-permute-start(f32[16,2,8,128]{3,2,1,0:T(8,128)S(1)} %bitcast.20), channel_id=1, source_target_pairs={{0,256},{256,0},{1,257},{257,1},{2,258},{258,2},{3,259},{259,3},{4... | collective-permute-start | bytes 393224 | tf_op jit(solution)/shard_map/ppermute | solution.py:355
  358.5 11.9 %collective-permute-start.26 = (f32[16,2,8,128]{3,2,1,0:T(8,128)S(1)}, f32[16,2,8,128]{3,2,1,0:T(8,128)S(1)}, u32[]{:S(2)}, u32[]{:S(2)}) collective-permute-start(f32[16,2,8,128]{3,2,1,0:T(8,128)S(1)} %bitcast.21), channel_id=1, source_target_pairs={{0,8},{8,0},{1,9},{9,1},{2,10},{10,2},{3,11},{11,3},{4,12},{12,4},... | collective-permute-start | bytes 393224 | tf_op jit(solution)/shard_map/ppermute | solution.py:355
  365.7 5.6 %collective-permute-start.27 = (f32[16,2,8,128]{3,2,1,0:T(8,128)S(1)}, f32[16,2,8,128]{3,2,1,0:T(8,128)S(1)}, u32[]{:S(2)}, u32[]{:S(2)}) collective-permute-start(f32[16,2,8,128]{3,2,1,0:T(8,128)S(1)} %collective-permute-done.25.refs_2_), channel_id=1, source_target_pairs={{0,8},{8,0},{1,9},{9,1},{2,10},{10,2},{3,11},{11,3},{4,12},{12,4},... | collective-permute-start | bytes 393224 | tf_op jit(solution)/shard_map/ppermute | solution.py:355

commit v4 on v3

--- a/solution.py
+++ b/solution.py
@@ -142,11 +142,6 @@
             spectra[place, part] = block
 
 
-def split_kernel(probe_in, pieces):
-    for place in range(MODES):
-        pieces[place] = probe_in[0, :, place * SLAB : (place + 1) * SLAB, :]
-
-
 def first_kernel(scal, own, beside, probe, tables, band, view, shard, spectra):
     band[:, :, :WIDTH] = own[...]
     band[:, :, WIDTH:] = beside[...]
@@ -165,18 +160,13 @@
     forward(view, probe, tables, spectra)
 
 
-def piece_row(scal, which):
-    core = scal[CORE] if which < 2 else 1 - scal[CORE]
-    xlo = scal[XLO] if which % 2 == 0 else 1 - scal[XLO]
-    return core * 16 + xlo * 8
-
-
-def next_kernel(scal, view, piece0, piece1, piece2, piece3, tables, probe, spectra):
-    for which, piece in enumerate((piece0, piece1, piece2, piece3)):
-        rows = pl.ds(pl.multiple_of(piece_row(scal, which), 8), 8)
-        for mode in range(MODES):
-            probe[mode, :, rows, :LANES] = piece[2 * mode]
-            probe[mode, :, rows, LANES:] = piece[2 * mode + 1]
+def next_kernel(view, pieces, tables, probe, spectra):
+    for xlo in range(2):
+        for core in range(2):
+            row = core * 16 + xlo * 8
+            for mode in range(MODES):
+                probe[mode, :, row : row + 8, :LANES] = pieces[xlo, core, 2 * mode]
+                probe[mode, :, row : row + 8, LANES:] = pieces[xlo, core, 2 * mode + 1]
     forward(view, probe, tables, spectra)
 
 
@@ -302,29 +292,59 @@
     rows_out[:, :, SIDE:] = part_band[:, rows, SIDE:WIDTH]
 
 
-def object_kernel(scal, near, far, object_out):
-    def write(first, last):
-        for place in range(MODES):
-            source = first if place < MODES // 2 else last
-            row = place * 9 // 2 * 8
-            object_out[:, row : row + OUT_ROWS, :] = source[place % (MODES // 2)]
-
-    @pl.when(scal[MODE] < MODES // 2)
-    def _():
-        write(near, far)
-
-    @pl.when(scal[MODE] >= MODES // 2)
-    def _():
-        write(far, near)
-
-
-def probe_out_kernel(scal, piece0, piece1, piece2, piece3, probe_out):
-    for which, piece in enumerate((piece0, piece1, piece2, piece3)):
-        first = piece_row(scal, which)
-        for place in range(MODES):
-            rows = pl.ds(pl.multiple_of(first + place * SLAB, 8), 8)
-            probe_out[0, :, rows, :LANES] = piece[2 * place]
-            probe_out[0, :, rows, LANES:] = piece[2 * place + 1]
+def pair_kernel(mine, theirs, pair):
+    pair[0] = mine[...]
+    pair[1] = theirs[...]
+
+
+def object_kernel(scal, own, plus, minus, across, object_out):
+    xhi, y = scal[MODE] // 4, lax.rem(scal[MODE], 4)
+    for source, steps in ((own, 0), (plus, 3), (minus, 1), (across, 2)):
+        for beyond in range(2):
+            half = xhi if beyond == 0 else 1 - xhi
+            place = half * 4 + lax.rem(y + steps, 4)
+            rows = pl.ds(pl.multiple_of(place * 9 // 2 * 8, 8), OUT_ROWS)
+            object_out[:, rows, :] = source[beyond]
+
+
+def probe_out_kernel(pieces, probe_out):
+    for xlo in range(2):
+        for core in range(2):
+            for place in range(MODES):
+                row = place * SLAB + core * 16 + xlo * 8
+                probe_out[0, :, row : row + 8, :LANES] = pieces[xlo, core, 2 * place]
+                probe_out[0, :, row : row + 8, LANES:] = pieces[xlo, core, 2 * place + 1]
+
+
+def own_kernel(place, whole, own, left, sems):
+    rows = pl.ds(pl.multiple_of(place[0] * SLAB, SLAB), BAND)
+    first = pltpu.make_async_copy(whole.at[:, rows, :], own, sems.at[0])
+    second = pltpu.make_async_copy(whole.at[:, rows, pl.ds(0, SIDE)], left, sems.at[1])
+    first.start()
+    second.start()
+    first.wait()
+    second.wait()
+
+
+def take_own(mode, object_tiles, after):
+    vmem = pl.BlockSpec(memory_space=pltpu.VMEM)
+    anywhere = pl.BlockSpec(memory_space=pl.ANY)
+
+    def body(place, whole, _, own, left, sems):
+        own_kernel(place, whole, own, left, sems)
+
+    return pl.pallas_call(
+        body,
+        out_shape=[
+            jax.ShapeDtypeStruct((2, BAND, WIDTH), F32),
+            jax.ShapeDtypeStruct((2, BAND, SIDE), F32),
+        ],
+        in_specs=[pl.BlockSpec(memory_space=pltpu.SMEM), anywhere, anywhere],
+        out_specs=[vmem, vmem],
+        scratch_shapes=[pltpu.SemaphoreType.DMA((2,))],
+        compiler_params=pltpu.CompilerParams(vmem_limit_bytes=VMEM_LIMIT),
+        name="own_kernel",
+    )(mode.astype(jnp.int32).reshape(1), object_tiles, after)
 
 
 def call(kernel, outs, *args, scalars=True, after=()):
@@ -359,9 +379,12 @@
     return lax.all_to_all(value, axes, 0, 0, tiled=True)
 
 
-def four_pieces(piece):
-    beyond = other(piece, "xlo")
-    return piece, beyond, other(piece, "core"), other(beyond, "core")
+def gather_pieces(piece):
+    return lax.all_gather(piece, ("xlo", "core")).reshape(2, 2, RINGS, 2, 8, LANES)
+
+
+def around(value, steps):
+    return lax.ppermute(value, "y", [(i, (i + steps) % 4) for i in range(4)])
 
 
 def per_device(
@@ -371,8 +394,10 @@
     slots = visit_order[0]
     tile = lax.axis_index(TILE_AXES)
     mode = lax.axis_index(MODE_AXES)
-    own = lax.dynamic_slice_in_dim(object_tiles, mode * SLAB, BAND, axis=1)
-    beside = shift(own[:, :, :SIDE], TILE_AXES, TILES, -1)
+    pieces = probe_modes.reshape(2, MODES, SLAB, SIDE).transpose(1, 0, 2, 3)
+    probe = exchange(pieces, MODE_AXES)
+    own, left = take_own(mode, object_tiles, pieces)
+    beside = shift(left, TILE_AXES, TILES, -1)
     places = [
         mode,
         lax.axis_index("core"),
@@ -394,8 +419,6 @@
     slab_pair = (2, SLAB, SIDE)
     band_shape = (2, BAND, WIDE)
     edge = (2, BAND, SIDE)
-    (pieces,) = call(split_kernel, [slabs], probe_modes, scalars=False)
-    probe = exchange(pieces, MODE_AXES)
     (counts,) = call(counts_kernel, [(SIDE, LANES)], scalars[0], measured)
     for step in range(STEPS):
         scal = scalars[step]
@@ -416,7 +439,13 @@
                 view_kernel, [band_shape, slab_pair], scal, part_band, from_left, from_right
             )
             probe, spectra = call(
-                next_kernel, [slabs, slabs], scal, view, *pieces, tables, after=(counts,)
+                next_kernel,
+                [slabs, slabs],
+                view,
+                pieces,
+                tables,
+                scalars=False,
+                after=(counts,),
             )
         spectra = exchange(spectra, MODE_AXES)
         (spectra,) = call(ratio_kernel, [slabs], scal, spectra, counts, tables)
@@ -456,26 +485,30 @@
                 place_kernel, [band_shape, edge, edge], *placing, after=(packed,)
             )
             from_left = shift(to_right, TILE_AXES, TILES, 1)
+            (rows_out,) = call(
+                out_rows_kernel, [(2, OUT_ROWS, WIDTH)], scal, part_band, from_left
+            )
+            far_rows = other(rows_out, "xhi")
         shard, shards = call(
             probe_kernel,
             [(2, 8, LANES), (RINGS, 2, 8, LANES)],
             sums,
             shard,
             scalars=False,
-            after=(from_left,) if final else (above, below, counts),
+            after=(far_rows,) if final else (above, below, counts),
         )
         piece = exchange(shards, "z")
         if final:
-            (rows_out,) = call(
-                out_rows_kernel,
-                [(2, OUT_ROWS, WIDTH)],
-                scal,
-                part_band,
-                from_left,
+            (pair,) = call(
+                pair_kernel,
+                [(2, 2, OUT_ROWS, WIDTH)],
+                rows_out,
+                far_rows,
+                scalars=False,
                 after=(shards,),
             )
-            near = lax.all_gather(rows_out, "y")
-            piece, near = lax.optimization_barrier((piece, near))
+            plus, minus = around(pair, 1), around(pair, -1)
+            piece, plus, minus = lax.optimization_barrier((piece, plus, minus))
         else:
             part_band, to_left, to_right = call(
                 place_kernel, [band_shape, edge, edge], *placing, after=(shards,)
@@ -485,12 +518,19 @@
             piece, from_left, from_right = lax.optimization_barrier(
                 (piece, from_left, from_right)
             )
-            pieces = four_pieces(piece)
-    far = other(near, "xhi")
-    (object_out,) = call(object_kernel, [(2, HEIGHT, WIDTH)], scal, near, far)
+            pieces = gather_pieces(piece)
+    (object_out,) = call(
+        object_kernel,
+        [(2, HEIGHT, WIDTH)],
+        scal,
+        pair,
+        plus,
+        minus,
+        around(pair, 2),
+    )
     piece = exchange(piece.reshape(MODES, 4, 8, LANES), MODE_AXES)
-    pieces = four_pieces(piece.reshape(RINGS, 2, 8, LANES))
-    (probe_out,) = call(probe_out_kernel, [(1, 2, SIDE, SIDE)], scal, *pieces)
+    pieces = gather_pieces(piece.reshape(RINGS, 2, 8, LANES))
+    (probe_out,) = call(probe_out_kernel, [(1, 2, SIDE, SIDE)], pieces, scalars=False)
     return object_out, probe_out
 
 

time: 376 us -> 369 us (0.981)
  blocking collectives: 119 us -> 128 us
  starting transfers between devices: 159 us -> 151 us
    ppermute x16 -> x7, starting transfers between devices: 63.8 us -> 33.9 us  [other(): return lax.ppermute(value, axis, [(0, 1), (1, 0)])]
    all_gather x1 -> x3, blocking collectives: 15.3 us -> 38.6 us  [gather_pieces(): lax.all_gather(piece, ('xlo', 'core')).reshape(2, 2, RINGS, 2, 8, LANES)]
    all_to_all x7 -> x6, blocking collectives: 104 us -> 89.3 us  [exchange(): return lax.all_to_all(value, axes, 0, 0, tiled=True)]
    all_to_all x7 -> x8, starting transfers between devices: 58.2 us -> 70.3 us  [exchange(): return lax.all_to_all(value, axes, 0, 0, tiled=True)]
    ppermute x0 -> x3, starting transfers between devices: none -> 7.2 us  [around(): return lax.ppermute(value, 'y', [(i, (i + steps) % 4) for i in range(4)])]
    ppermute x12, waiting for transfers between devices: 23.6 us -> 16.5 us  [shift(): lax.ppermute(value, axes, [(i, i + steps) for i in range(first, last)])]
    ppermute x0 -> x3, waiting for transfers between devices: none -> 6.52 us  [around(): return lax.ppermute(value, 'y', [(i, (i + steps) % 4) for i in range(4)])]
    unnamed x22 -> x12, local copies, waits for them, and re-layouts: 4.03 us -> 0.02 us
  transfers between devices with their start and end apart: 35 -> 30, of which waited for: 19 -> 23; matrix products, arithmetic and copies ran while one was open for 0% -> 0% of each run, Pallas kernels for 3% -> 2%
where the time goes in v4:
time: 369 us; the launch traced here: 368 us
  starting transfers between devices  151 us (41%)
  blocking collectives  128 us (35%)
  waiting for transfers between devices  53.7 us (15%)
  Pallas kernels  30.4 us (8%)
    all_to_all x6, blocking collectives, exchange(): return lax.all_to_all(value, axes, 0, 0, tiled=True)  89.3 us
    all_to_all x8, starting transfers between devices, exchange(): return lax.all_to_all(value, axes, 0, 0, tiled=True)  70.3 us
    ppermute x12, starting transfers between devices, shift(): lax.ppermute(value, axes, [(i, i + steps) for i in range(first, last)])  39.7 us
    all_gather x3, blocking collectives, gather_pieces(): lax.all_gather(piece, ('xlo', 'core')).reshape(2, 2, RINGS, 2, 8, LANES)  38.6 us
    ppermute x7, starting transfers between devices, other(): return lax.ppermute(value, axis, [(0, 1), (1, 0)])  33.9 us
    pallas_call x33, Pallas kernels, call(): pl.pallas_call(body, out_shape=[jax.ShapeDtypeStruct(shape, F32) for shap...  30.4 us
    ppermute x12, waiting for transfers between devices, shift(): lax.ppermute(value, axes, [(i, i + steps) for i in range(first, last)])  16.5 us
    all_to_all x8, waiting for transfers between devices, exchange(): return lax.all_to_all(value, axes, 0, 0, tiled=True)  16.3 us
  transfers between devices with their start and end apart: 30, of which 23 were waited for; matrix products, arithmetic and copies ran while one was open for 0% of the time, Pallas kernels for 2%

profile of v4, /device:TPU:1, one launch (start us, length us, event | category | flops | bytes accessed | tf_op | source)
XLA Modules:
  0.0 367.5 jit_solution(3897323845804061118)
XLA Ops:
  0.6 2.0 copy.22
  2.6 7.6 %all-to-all-start = ((f32[8,2,32,256]{3,2,1,0:T(8,128)}), f32[8,2,32,256]{3,2,1,0:T(8,128)S(1)}, u32[]{:S(2)}, u32[]{:S(2)}) async-start(f32[8,2,32,256]{3,2,1,0:T(8,128)} %bitcast.23._), calls=%async_computation | async-start | bytes 1048576 | tf_op jit(solution)/shard_map/all_to_all | solution.py:379
  10.3 4.9 %collective-permute-start = (f32[2,64,256]{2,1,0:T(8,128)S(1)}, f32[2,64,256]{2,1,0:T(8,128)S(1)}, u32[]{:S(2)}, u32[]{:S(2)}) collective-permute-start(f32[2,64,256]{2,1,0:T(8,128)S(1)} %get-tuple-element.54), channel_id=1, source_target_pairs={{8,0},{16,8},{24,16},{32,24},{40,32},{48,40},{56,48},{64,56},{72,6... | collective-permute-start | bytes 393224 | tf_op jit(solution)/shard_map/ppermute | solution.py:371
  19.1 1.6 first_kernel.1
  20.7 15.1 %all_to_all.70.refs_1_ = f32[8,2,32,256]{3,2,1,0:T(8,128)S(1)} all-to-all(f32[8,2,32,256]{3,2,1,0:T(8,128)S(1)} %get-tuple-element.55), channel_id=1, replica_groups=mesh['xlo'=2,'z'=16,'core'=2,'xhi'=2,'y'=4] {'xhi','y'}, dimensions={0} | all-to-all | bytes 1048576 | tf_op jit(solution)/shard_map/all_to_all | solution.py:379
  35.7 2.2 ratio_kernel.3
  38.0 12.3 %all_to_all.71.refs_1_ = f32[8,2,32,256]{3,2,1,0:T(8,128)S(1)} all-to-all(f32[8,2,32,256]{3,2,1,0:T(8,128)S(1)} %ratio_kernel.3), channel_id=1, replica_groups=mesh['xlo'=2,'z'=16,'core'=2,'xhi'=2,'y'=4] {'xhi','y'}, dimensions={0} | all-to-all | bytes 1048576 | tf_op jit(solution)/shard_map/all_to_all | solution.py:379
  50.3 1.4 backward_kernel.3
  51.7 5.3 %collective-permute-start.1 = (f32[17,16,256]{2,1,0:T(8,128)S(1)}, f32[17,16,256]{2,1,0:T(8,128)S(1)}, u32[]{:S(2)}, u32[]{:S(2)}) collective-permute-start(f32[17,16,256]{2,1,0:T(8,128)S(1)} %get-tuple-element.59), channel_id=1, source_target_pairs={{0,8},{8,0},{1,9},{9,1},{2,10},{10,2},{3,11},{11,3},{4,12},{12,4},... | collective-permute-start | bytes 835592 | tf_op jit(solution)/shard_map/ppermute | solution.py:375
  58.7 6.7 %collective-permute-start.4 = (f32[17,8,256]{2,1,0:T(8,128)S(1)}, f32[17,8,256]{2,1,0:T(8,128)S(1)}, u32[]{:S(2)}, u32[]{:S(2)}) collective-permute-start(f32[17,8,256]{2,1,0:T(8,128)S(1)} %get-tuple-element.62), channel_id=1, source_target_pairs={{0,256},{256,0},{1,257},{257,1},{2,258},{258,2},{3,259},{259,3},{4... | collective-permute-start | bytes 417800 | tf_op jit(solution)/shard_map/ppermute | solution.py:375
  65.6 3.5 collective-permute-done.4.refs_1_
  69.9 11.7 %all-to-all-start.3 = ((f32[16,3,8,128]{3,2,1,0:T(8,128)}), f32[16,3,8,128]{3,2,1,0:T(8,128)S(1)}, u32[]{:S(2)}, u32[]{:S(2)}) async-start(f32[16,3,8,128]{3,2,1,0:T(8,128)} %pack_kernel.3.refs_2_), calls=%async_computation.3 | async-start | bytes 393216 | tf_op jit(solution)/shard_map/all_to_all | solution.py:379
  81.6 1.3 collective-permute-start.3
  82.9 4.0 %collective-permute-start.2 = (f32[2,32,256]{2,1,0:T(8,128)S(1)}, f32[2,32,256]{2,1,0:T(8,128)S(1)}, u32[]{:S(2)}, u32[]{:S(2)}) collective-permute-start(f32[2,32,256]{2,1,0:T(8,128)S(1)} %step_kernel.3.refs_2_), channel_id=1, source_target_pairs={{0,1},{1,2},{2,3},{3,4},{4,5},{5,6},{6,7},{8,9},{9,10},{10,11},{11... | collective-permute-start | bytes 196616 | tf_op jit(solution)/shard_map/ppermute | solution.py:371
  88.2 5.7 %all-to-all-done.3.refs_0_ = f32[16,3,8,128]{3,2,1,0:T(8,128)S(1)} async-done(((f32[16,3,8,128]{3,2,1,0:T(8,128)}), f32[16,3,8,128]{3,2,1,0:T(8,128)S(1)}, u32[]{:S(2)}, u32[]{:S(2)}) %all-to-all-start.3) | async-done | bytes 196640 | tf_op jit(solution)/shard_map/all_to_all | solution.py:379
  94.6 8.6 %all-to-all-start.4 = ((f32[16,2,8,128]{3,2,1,0:T(8,128)}), f32[16,2,8,128]{3,2,1,0:T(8,128)S(1)}, u32[]{:S(2)}, u32[]{:S(2)}) async-start(f32[16,2,8,128]{3,2,1,0:T(8,128)} %get-tuple-element.64.refs_5_), calls=%async_computation.4 | async-start | bytes 262144 | tf_op jit(solution)/shard_map/all_to_all | solution.py:379
  104.0 4.8 %collective-permute-start.5 = (f32[2,64,256]{2,1,0:T(8,128)S(1)}, f32[2,64,256]{2,1,0:T(8,128)S(1)}, u32[]{:S(2)}, u32[]{:S(2)}) collective-permute-start(f32[2,64,256]{2,1,0:T(8,128)S(1)} %get-tuple-element.66), channel_id=1, source_target_pairs={{0,8},{8,16},{16,24},{24,32},{32,40},{40,48},{48,56},{56,64},{64,7... | collective-permute-start | bytes 393224 | tf_op jit(solution)/shard_map/ppermute | solution.py:371
  108.8 1.9 collective-permute-start.6
  110.7 1.7 collective-permute-done.5.refs_2_
  112.4 3.3 collective-permute-done.6.refs_3_
  115.7 9.6 %all-gather = f32[64,2,8,128]{3,2,1,0:T(8,128)S(1)} all-gather(f32[16,2,8,128]{3,2,1,0:T(8,128)S(1)} %all-to-all-done.4), channel_id=2, replica_groups=mesh['xlo'=2,'z'=16,'core'=2,'xhi'=2,'y'=4] {'xlo','core'}, dimensions={0}, use_global_device_ids=true | all-gather | bytes 655360 | tf_op jit(solution)/shard_map/all_gather | solution.py:383
  126.9 17.4 %all_to_all.72.refs_1_ = f32[8,2,32,256]{3,2,1,0:T(8,128)S(1)} all-to-all(f32[8,2,32,256]{3,2,1,0:T(8,128)S(1)} %get-tuple-element.72), channel_id=1, replica_groups=mesh['xlo'=2,'z'=16,'core'=2,'xhi'=2,'y'=4] {'xhi','y'}, dimensions={0} | all-to-all | bytes 1048576 | tf_op jit(solution)/shard_map/all_to_all | solution.py:379
  144.3 2.2 ratio_kernel.4
  146.5 14.0 %all_to_all.73.refs_1_ = f32[8,2,32,256]{3,2,1,0:T(8,128)S(1)} all-to-all(f32[8,2,32,256]{3,2,1,0:T(8,128)S(1)} %ratio_kernel.4), channel_id=1, replica_groups=mesh['xlo'=2,'z'=16,'core'=2,'xhi'=2,'y'=4] {'xhi','y'}, dimensions={0} | all-to-all | bytes 1048576 | tf_op jit(solution)/shard_map/all_to_all | solution.py:379
  160.5 1.4 backward_kernel.4
  161.9 4.4 %collective-permute-start.7 = (f32[17,16,256]{2,1,0:T(8,128)S(1)}, f32[17,16,256]{2,1,0:T(8,128)S(1)}, u32[]{:S(2)}, u32[]{:S(2)}) collective-permute-start(f32[17,16,256]{2,1,0:T(8,128)S(1)} %get-tuple-element.76), channel_id=1, source_target_pairs={{0,8},{8,0},{1,9},{9,1},{2,10},{10,2},{3,11},{11,3},{4,12},{12,4},... | collective-permute-start | bytes 835592 | tf_op jit(solution)/shard_map/ppermute | solution.py:375
  168.0 1.9 collective-permute-start.10
  170.1 4.7 %collective-permute-done.10.refs_1_ = f32[17,8,256]{2,1,0:T(8,128)S(1)} collective-permute-done((f32[17,8,256]{2,1,0:T(8,128)S(1)}, f32[17,8,256]{2,1,0:T(8,128)S(1)}, u32[]{:S(2)}, u32[]{:S(2)}) %collective-permute-start.10) | collective-permute-done | bytes 139296 | tf_op jit(solution)/shard_map/ppermute | solution.py:375
  175.5 9.0 %all-to-all-start.7 = ((f32[16,3,8,128]{3,2,1,0:T(8,128)}), f32[16,3,8,128]{3,2,1,0:T(8,128)S(1)}, u32[]{:S(2)}, u32[]{:S(2)}) async-start(f32[16,3,8,128]{3,2,1,0:T(8,128)} %pack_kernel.4.refs_2_), calls=%async_computation.7 | async-start | bytes 393216 | tf_op jit(solution)/shard_map/all_to_all | solution.py:379
  184.4 1.3 collective-permute-start.9
  185.7 4.0 %collective-permute-start.8 = (f32[2,32,256]{2,1,0:T(8,128)S(1)}, f32[2,32,256]{2,1,0:T(8,128)S(1)}, u32[]{:S(2)}, u32[]{:S(2)}) collective-permute-start(f32[2,32,256]{2,1,0:T(8,128)S(1)} %step_kernel.4.refs_2_), channel_id=1, source_target_pairs={{0,1},{1,2},{2,3},{3,4},{4,5},{5,6},{6,7},{8,9},{9,10},{10,11},{11... | collective-permute-start | bytes 196616 | tf_op jit(solution)/shard_map/ppermute | solution.py:371
  191.1 5.7 %all-to-all-done.7.refs_0_ = f32[16,3,8,128]{3,2,1,0:T(8,128)S(1)} async-done(((f32[16,3,8,128]{3,2,1,0:T(8,128)}), f32[16,3,8,128]{3,2,1,0:T(8,128)S(1)}, u32[]{:S(2)}, u32[]{:S(2)}) %all-to-all-start.7) | async-done | bytes 196640 | tf_op jit(solution)/shard_map/all_to_all | solution.py:379
  197.5 8.6 %all-to-all-start.8 = ((f32[16,2,8,128]{3,2,1,0:T(8,128)}), f32[16,2,8,128]{3,2,1,0:T(8,128)S(1)}, u32[]{:S(2)}, u32[]{:S(2)}) async-start(f32[16,2,8,128]{3,2,1,0:T(8,128)} %get-tuple-element.81.refs_5_), calls=%async_computation.8 | async-start | bytes 262144 | tf_op jit(solution)/shard_map/all_to_all | solution.py:379
  206.8 4.8 %collective-permute-start.11 = (f32[2,64,256]{2,1,0:T(8,128)S(1)}, f32[2,64,256]{2,1,0:T(8,128)S(1)}, u32[]{:S(2)}, u32[]{:S(2)}) collective-permute-start(f32[2,64,256]{2,1,0:T(8,128)S(1)} %get-tuple-element.83), channel_id=1, source_target_pairs={{0,8},{8,16},{16,24},{24,32},{32,40},{40,48},{48,56},{56,64},{64,7... | collective-permute-start | bytes 393224 | tf_op jit(solution)/shard_map/ppermute | solution.py:371
  211.6 1.9 collective-permute-start.12
  213.5 1.7 collective-permute-done.11.refs_2_
  215.2 3.3 collective-permute-done.12.refs_3_
  218.5 9.8 %all-gather.1 = f32[64,2,8,128]{3,2,1,0:T(8,128)S(1)} all-gather(f32[16,2,8,128]{3,2,1,0:T(8,128)S(1)} %all-to-all-done.8), channel_id=3, replica_groups=mesh['xlo'=2,'z'=16,'core'=2,'xhi'=2,'y'=4] {'xlo','core'}, dimensions={0}, use_global_device_ids=true | all-gather | bytes 655360 | tf_op jit(solution)/shard_map/all_gather | solution.py:383
  229.9 16.6 %all_to_all.74.refs_1_ = f32[8,2,32,256]{3,2,1,0:T(8,128)S(1)} all-to-all(f32[8,2,32,256]{3,2,1,0:T(8,128)S(1)} %get-tuple-element.89), channel_id=1, replica_groups=mesh['xlo'=2,'z'=16,'core'=2,'xhi'=2,'y'=4] {'xhi','y'}, dimensions={0} | all-to-all | bytes 1048576 | tf_op jit(solution)/shard_map/all_to_all | solution.py:379
  246.5 2.2 ratio_kernel.5
  248.7 14.0 %all_to_all.75.refs_1_ = f32[8,2,32,256]{3,2,1,0:T(8,128)S(1)} all-to-all(f32[8,2,32,256]{3,2,1,0:T(8,128)S(1)} %ratio_kernel.5), channel_id=1, replica_groups=mesh['xlo'=2,'z'=16,'core'=2,'xhi'=2,'y'=4] {'xhi','y'}, dimensions={0} | all-to-all | bytes 1048576 | tf_op jit(solution)/shard_map/all_to_all | solution.py:379
  262.7 1.4 backward_kernel.5
  264.1 4.4 %collective-permute-start.13 = (f32[17,16,256]{2,1,0:T(8,128)S(1)}, f32[17,16,256]{2,1,0:T(8,128)S(1)}, u32[]{:S(2)}, u32[]{:S(2)}) collective-permute-start(f32[17,16,256]{2,1,0:T(8,128)S(1)} %get-tuple-element.93), channel_id=1, source_target_pairs={{0,8},{8,0},{1,9},{9,1},{2,10},{10,2},{3,11},{11,3},{4,12},{12,4},... | collective-permute-start | bytes 835592 | tf_op jit(solution)/shard_map/ppermute | solution.py:375
  270.2 2.1 collective-permute-start.16
  272.5 1.3 collective-permute-start.15
  273.8 4.0 %collective-permute-start.14 = (f32[2,32,256]{2,1,0:T(8,128)S(1)}, f32[2,32,256]{2,1,0:T(8,128)S(1)}, u32[]{:S(2)}, u32[]{:S(2)}) collective-permute-start(f32[2,32,256]{2,1,0:T(8,128)S(1)} %step_kernel.5.refs_2_), channel_id=1, source_target_pairs={{0,1},{1,2},{2,3},{3,4},{4,5},{5,6},{6,7},{8,9},{9,10},{10,11},{11... | collective-permute-start | bytes 196616 | tf_op jit(solution)/shard_map/ppermute | solution.py:371
  277.8 1.3 collective-permute-done.14.refs_2_.refs_1_
  279.8 9.5 %all-to-all-start.11 = ((f32[16,3,8,128]{3,2,1,0:T(8,128)}), f32[16,3,8,128]{3,2,1,0:T(8,128)S(1)}, u32[]{:S(2)}, u32[]{:S(2)}) async-start(f32[16,3,8,128]{3,2,1,0:T(8,128)} %pack_kernel.5.refs_5_), calls=%async_computation.11 | async-start | bytes 393216 | tf_op jit(solution)/shard_map/all_to_all | solution.py:379
  289.2 1.4 place_kernel.5
  290.6 5.5 %collective-permute-start.17 = (f32[2,64,256]{2,1,0:T(8,128)S(1)}, f32[2,64,256]{2,1,0:T(8,128)S(1)}, u32[]{:S(2)}, u32[]{:S(2)}) collective-permute-start(f32[2,64,256]{2,1,0:T(8,128)S(1)} %get-tuple-element.98), channel_id=1, source_target_pairs={{0,8},{8,16},{16,24},{24,32},{32,40},{40,48},{48,56},{56,64},{64,7... | collective-permute-start | bytes 393224 | tf_op jit(solution)/shard_map/ppermute | solution.py:371
  296.1 4.0 %collective-permute-done.17.refs_2_ = f32[2,64,256]{2,1,0:T(8,128)S(1)} collective-permute-done((f32[2,64,256]{2,1,0:T(8,128)S(1)}, f32[2,64,256]{2,1,0:T(8,128)S(1)}, u32[]{:S(2)}, u32[]{:S(2)}) %collective-permute-start.17) | collective-permute-done | bytes 131104 | tf_op jit(solution)/shard_map/ppermute | solution.py:371
  300.7 9.2 %collective-permute-start.18 = (f32[2,40,512]{2,1,0:T(8,128)S(1)}, f32[2,40,512]{2,1,0:T(8,128)S(1)}, u32[]{:S(2)}, u32[]{:S(2)}) collective-permute-start(f32[2,40,512]{2,1,0:T(8,128)S(1)} %out_rows_kernel.1.refs_0_), channel_id=1, source_target_pairs={{0,4},{4,0},{1,5},{5,1},{2,6},{6,2},{3,7},{7,3},{8,12},{12,8},{9,1... | collective-permute-start | bytes 491528 | tf_op jit(solution)/shard_map/ppermute | solution.py:375
  309.9 2.7 collective-permute-done.18.refs_2_.refs_1_
  313.3 11.4 %all-to-all-start.12 = ((f32[16,2,8,128]{3,2,1,0:T(8,128)}), f32[16,2,8,128]{3,2,1,0:T(8,128)}, u32[]{:S(2)}, u32[]{:S(2)}) async-start(f32[16,2,8,128]{3,2,1,0:T(8,128)} %get-tuple-element.100.refs_2_), calls=%async_computation.12 | async-start | bytes 262144 | tf_op jit(solution)/shard_map/all_to_all | solution.py:379
  324.7 1.9 collective-permute-start.20
  326.7 3.4 collective-permute-start.19
  330.0 1.9 collective-permute-start.21
  332.0 1.6 collective-permute-done.20.refs_3_
  333.6 2.9 collective-permute-done.19.refs_2_
  336.7 3.9 %all-to-all-start.13 = ((f32[8,4,8,128]{3,2,1,0:T(8,128)}), f32[8,4,8,128]{3,2,1,0:T(8,128)S(1)}, u32[]{:S(2)}, u32[]{:S(2)}) async-start(f32[8,4,8,128]{3,2,1,0:T(8,128)} %bitcast.15), calls=%async_computation.13 | async-start | bytes 262144 | tf_op jit(solution)/shard_map/all_to_all | solution.py:379
  340.6 2.1 collective-permute-done.21.refs_4_
  342.7 1.7 object_kernel.1
  344.4 3.2 all-to-all-done.13
  347.5 19.2 %all_gather.19 = f32[4,16,2,8,128]{4,3,2,1,0:T(8,128)S(1)} all-gather(f32[1,16,2,8,128]{4,3,2,1,0:T(8,128)S(1)} %bitcast.28), channel_id=1, replica_groups=mesh['xlo'=2,'z'=16,'core'=2,'xhi'=2,'y'=4] {'xlo','core'}, dimensions={0}, use_global_device_ids=true | all-gather | bytes 655360 | tf_op jit(solution)/shard_map/all_gather | solution.py:383
  (65 shorter events, 22.0 us)
Async XLA Ops:
  0.6 9.6 %copy-start.2 = (f32[2,288,512]{2,1,0:T(8,128)S(1)}, f32[2,288,512]{2,1,0:T(8,128)}, u32[]{:S(2)}) copy-start(f32[2,288,512]{2,1,0:T(8,128)} %whole.1) | copy-start | bytes 3538948
  2.6 12.7 %copy-start.3 = (s32[1,3]{1,0:T(1,128)S(1)}, s32[1,3]{1,0:T(1,128)}, u32[]{:S(2)}) copy-start(s32[1,3]{1,0:T(1,128)} %param.14) | copy-start | bytes 40
  2.6 12.7 %copy-start.4 = (s32[1,3]{1,0:T(1,128)S(1)}, s32[1,3]{1,0:T(1,128)}, u32[]{:S(2)}) copy-start(s32[1,3]{1,0:T(1,128)} %param.12) | copy-start | bytes 40
  2.6 12.7 %copy-start.5 = (s32[1,3]{1,0:T(1,128)S(1)}, s32[1,3]{1,0:T(1,128)}, u32[]{:S(2)}) copy-start(s32[1,3]{1,0:T(1,128)} %param.11) | copy-start | bytes 40
  2.6 14.1 %copy-start.1 = (bf16[1,3,256,256]{3,2,1,0:T(8,128)(2,1)S(1)}, bf16[1,3,256,256]{3,2,1,0:T(8,128)(2,1)}, u32[]{:S(2)}) copy-start(bf16[1,3,256,256]{3,2,1,0:T(8,128)(2,1)} %refs_1_.5) | copy-start | bytes 1179652
  2.6 16.5 %all-to-all-start = ((f32[8,2,32,256]{3,2,1,0:T(8,128)}), f32[8,2,32,256]{3,2,1,0:T(8,128)S(1)}, u32[]{:S(2)}, u32[]{:S(2)}) async-start(f32[8,2,32,256]{3,2,1,0:T(8,128)} %bitcast.23._), calls=%async_computation | async-start | bytes 1048576 | tf_op jit(solution)/shard_map/all_to_all | solution.py:379
  10.3 8.8 %copy-start = (bf16[2,2,256,256]{3,2,1,0:T(8,128)(2,1)S(1)}, bf16[2,2,256,256]{3,2,1,0:T(8,128)(2,1)}, u32[]{:S(2)}) copy-start(bf16[2,2,256,256]{3,2,1,0:T(8,128)(2,1)} %constant.33.clone.refs_4_.refs_3_.refs_2_) | copy-start | bytes 1572868
  10.3 7.5 %collective-permute-start = (f32[2,64,256]{2,1,0:T(8,128)S(1)}, f32[2,64,256]{2,1,0:T(8,128)S(1)}, u32[]{:S(2)}, u32[]{:S(2)}) collective-permute-start(f32[2,64,256]{2,1,0:T(8,128)S(1)} %get-tuple-element.54), channel_id=1, source_target_pairs={{8,0},{16,8},{24,16},{32,24},{40,32},{48,40},{56,48},{64,56},{72,6... | collective-permute-start | bytes 393224 | tf_op jit(solution)/shard_map/ppermute | solution.py:371
  51.7 6.5 %collective-permute-start.1 = (f32[17,16,256]{2,1,0:T(8,128)S(1)}, f32[17,16,256]{2,1,0:T(8,128)S(1)}, u32[]{:S(2)}, u32[]{:S(2)}) collective-permute-start(f32[17,16,256]{2,1,0:T(8,128)S(1)} %get-tuple-element.59), channel_id=1, source_target_pairs={{0,8},{8,0},{1,9},{9,1},{2,10},{10,2},{3,11},{11,3},{4,12},{12,4},... | collective-permute-start | bytes 835592 | tf_op jit(solution)/shard_map/ppermute | solution.py:375
  58.7 10.5 %collective-permute-start.4 = (f32[17,8,256]{2,1,0:T(8,128)S(1)}, f32[17,8,256]{2,1,0:T(8,128)S(1)}, u32[]{:S(2)}, u32[]{:S(2)}) collective-permute-start(f32[17,8,256]{2,1,0:T(8,128)S(1)} %get-tuple-element.62), channel_id=1, source_target_pairs={{0,256},{256,0},{1,257},{257,1},{2,258},{258,2},{3,259},{259,3},{4... | collective-permute-start | bytes 417800 | tf_op jit(solution)/shard_map/ppermute | solution.py:375
  69.9 24.1 %all-to-all-start.3 = ((f32[16,3,8,128]{3,2,1,0:T(8,128)}), f32[16,3,8,128]{3,2,1,0:T(8,128)S(1)}, u32[]{:S(2)}, u32[]{:S(2)}) async-start(f32[16,3,8,128]{3,2,1,0:T(8,128)} %pack_kernel.3.refs_2_), calls=%async_computation.3 | async-start | bytes 393216 | tf_op jit(solution)/shard_map/all_to_all | solution.py:379
  81.6 6.1 %collective-permute-start.3 = (f32[2,32,256]{2,1,0:T(8,128)S(1)}, f32[2,32,256]{2,1,0:T(8,128)S(1)}, u32[]{:S(2)}, u32[]{:S(2)}) collective-permute-start(f32[2,32,256]{2,1,0:T(8,128)S(1)} %step_kernel.3.refs_2_), channel_id=1, source_target_pairs={{1,0},{2,1},{3,2},{4,3},{5,4},{6,5},{7,6},{9,8},{10,9},{11,10},{12... | collective-permute-start | bytes 196616 | tf_op jit(solution)/shard_map/ppermute | solution.py:371
  82.9 5.3 %collective-permute-start.2 = (f32[2,32,256]{2,1,0:T(8,128)S(1)}, f32[2,32,256]{2,1,0:T(8,128)S(1)}, u32[]{:S(2)}, u32[]{:S(2)}) collective-permute-start(f32[2,32,256]{2,1,0:T(8,128)S(1)} %step_kernel.3.refs_2_), channel_id=1, source_target_pairs={{0,1},{1,2},{2,3},{3,4},{4,5},{5,6},{6,7},{8,9},{9,10},{10,11},{11... | collective-permute-start | bytes 196616 | tf_op jit(solution)/shard_map/ppermute | solution.py:371
  94.6 21.0 %all-to-all-start.4 = ((f32[16,2,8,128]{3,2,1,0:T(8,128)}), f32[16,2,8,128]{3,2,1,0:T(8,128)S(1)}, u32[]{:S(2)}, u32[]{:S(2)}) async-start(f32[16,2,8,128]{3,2,1,0:T(8,128)} %get-tuple-element.64.refs_5_), calls=%async_computation.4 | async-start | bytes 262144 | tf_op jit(solution)/shard_map/all_to_all | solution.py:379
  104.0 8.4 %collective-permute-start.5 = (f32[2,64,256]{2,1,0:T(8,128)S(1)}, f32[2,64,256]{2,1,0:T(8,128)S(1)}, u32[]{:S(2)}, u32[]{:S(2)}) collective-permute-start(f32[2,64,256]{2,1,0:T(8,128)S(1)} %get-tuple-element.66), channel_id=1, source_target_pairs={{0,8},{8,16},{16,24},{24,32},{32,40},{40,48},{48,56},{56,64},{64,7... | collective-permute-start | bytes 393224 | tf_op jit(solution)/shard_map/ppermute | solution.py:371
  108.8 6.9 %collective-permute-start.6 = (f32[2,64,256]{2,1,0:T(8,128)S(1)}, f32[2,64,256]{2,1,0:T(8,128)S(1)}, u32[]{:S(2)}, u32[]{:S(2)}) collective-permute-start(f32[2,64,256]{2,1,0:T(8,128)S(1)} %get-tuple-element.67), channel_id=1, source_target_pairs={{8,0},{16,8},{24,16},{32,24},{40,32},{48,40},{56,48},{64,56},{72,6... | collective-permute-start | bytes 393224 | tf_op jit(solution)/shard_map/ppermute | solution.py:371
  161.9 5.5 %collective-permute-start.7 = (f32[17,16,256]{2,1,0:T(8,128)S(1)}, f32[17,16,256]{2,1,0:T(8,128)S(1)}, u32[]{:S(2)}, u32[]{:S(2)}) collective-permute-start(f32[17,16,256]{2,1,0:T(8,128)S(1)} %get-tuple-element.76), channel_id=1, source_target_pairs={{0,8},{8,0},{1,9},{9,1},{2,10},{10,2},{3,11},{11,3},{4,12},{12,4},... | collective-permute-start | bytes 835592 | tf_op jit(solution)/shard_map/ppermute | solution.py:375
  168.0 6.8 %collective-permute-start.10 = (f32[17,8,256]{2,1,0:T(8,128)S(1)}, f32[17,8,256]{2,1,0:T(8,128)S(1)}, u32[]{:S(2)}, u32[]{:S(2)}) collective-permute-start(f32[17,8,256]{2,1,0:T(8,128)S(1)} %get-tuple-element.79), channel_id=1, source_target_pairs={{0,256},{256,0},{1,257},{257,1},{2,258},{258,2},{3,259},{259,3},{4... | collective-permute-start | bytes 417800 | tf_op jit(solution)/shard_map/ppermute | solution.py:375
  175.5 21.3 %all-to-all-start.7 = ((f32[16,3,8,128]{3,2,1,0:T(8,128)}), f32[16,3,8,128]{3,2,1,0:T(8,128)S(1)}, u32[]{:S(2)}, u32[]{:S(2)}) async-start(f32[16,3,8,128]{3,2,1,0:T(8,128)} %pack_kernel.4.refs_2_), calls=%async_computation.7 | async-start | bytes 393216 | tf_op jit(solution)/shard_map/all_to_all | solution.py:379
  184.4 6.1 %collective-permute-start.9 = (f32[2,32,256]{2,1,0:T(8,128)S(1)}, f32[2,32,256]{2,1,0:T(8,128)S(1)}, u32[]{:S(2)}, u32[]{:S(2)}) collective-permute-start(f32[2,32,256]{2,1,0:T(8,128)S(1)} %step_kernel.4.refs_2_), channel_id=1, source_target_pairs={{1,0},{2,1},{3,2},{4,3},{5,4},{6,5},{7,6},{9,8},{10,9},{11,10},{12... | collective-permute-start | bytes 196616 | tf_op jit(solution)/shard_map/ppermute | solution.py:371
  185.7 5.3 %collective-permute-start.8 = (f32[2,32,256]{2,1,0:T(8,128)S(1)}, f32[2,32,256]{2,1,0:T(8,128)S(1)}, u32[]{:S(2)}, u32[]{:S(2)}) collective-permute-start(f32[2,32,256]{2,1,0:T(8,128)S(1)} %step_kernel.4.refs_2_), channel_id=1, source_target_pairs={{0,1},{1,2},{2,3},{3,4},{4,5},{5,6},{6,7},{8,9},{9,10},{10,11},{11... | collective-permute-start | bytes 196616 | tf_op jit(solution)/shard_map/ppermute | solution.py:371
  197.5 21.0 %all-to-all-start.8 = ((f32[16,2,8,128]{3,2,1,0:T(8,128)}), f32[16,2,8,128]{3,2,1,0:T(8,128)S(1)}, u32[]{:S(2)}, u32[]{:S(2)}) async-start(f32[16,2,8,128]{3,2,1,0:T(8,128)} %get-tuple-element.81.refs_5_), calls=%async_computation.8 | async-start | bytes 262144 | tf_op jit(solution)/shard_map/all_to_all | solution.py:379
  206.8 8.4 %collective-permute-start.11 = (f32[2,64,256]{2,1,0:T(8,128)S(1)}, f32[2,64,256]{2,1,0:T(8,128)S(1)}, u32[]{:S(2)}, u32[]{:S(2)}) collective-permute-start(f32[2,64,256]{2,1,0:T(8,128)S(1)} %get-tuple-element.83), channel_id=1, source_target_pairs={{0,8},{8,16},{16,24},{24,32},{32,40},{40,48},{48,56},{56,64},{64,7... | collective-permute-start | bytes 393224 | tf_op jit(solution)/shard_map/ppermute | solution.py:371
  211.6 6.9 %collective-permute-start.12 = (f32[2,64,256]{2,1,0:T(8,128)S(1)}, f32[2,64,256]{2,1,0:T(8,128)S(1)}, u32[]{:S(2)}, u32[]{:S(2)}) collective-permute-start(f32[2,64,256]{2,1,0:T(8,128)S(1)} %get-tuple-element.84), channel_id=1, source_target_pairs={{8,0},{16,8},{24,16},{32,24},{40,32},{48,40},{56,48},{64,56},{72,6... | collective-permute-start | bytes 393224 | tf_op jit(solution)/shard_map/ppermute | solution.py:371
  264.1 5.5 %collective-permute-start.13 = (f32[17,16,256]{2,1,0:T(8,128)S(1)}, f32[17,16,256]{2,1,0:T(8,128)S(1)}, u32[]{:S(2)}, u32[]{:S(2)}) collective-permute-start(f32[17,16,256]{2,1,0:T(8,128)S(1)} %get-tuple-element.93), channel_id=1, source_target_pairs={{0,8},{8,0},{1,9},{9,1},{2,10},{10,2},{3,11},{11,3},{4,12},{12,4},... | collective-permute-start | bytes 835592 | tf_op jit(solution)/shard_map/ppermute | solution.py:375
  270.2 8.9 %collective-permute-start.16 = (f32[17,8,256]{2,1,0:T(8,128)S(1)}, f32[17,8,256]{2,1,0:T(8,128)S(1)}, u32[]{:S(2)}, u32[]{:S(2)}) collective-permute-start(f32[17,8,256]{2,1,0:T(8,128)S(1)} %get-tuple-element.96), channel_id=1, source_target_pairs={{0,256},{256,0},{1,257},{257,1},{2,258},{258,2},{3,259},{259,3},{4... | collective-permute-start | bytes 417800 | tf_op jit(solution)/shard_map/ppermute | solution.py:375
  272.5 5.3 %collective-permute-start.15 = (f32[2,32,256]{2,1,0:T(8,128)S(1)}, f32[2,32,256]{2,1,0:T(8,128)S(1)}, u32[]{:S(2)}, u32[]{:S(2)}) collective-permute-start(f32[2,32,256]{2,1,0:T(8,128)S(1)} %step_kernel.5.refs_2_), channel_id=1, source_target_pairs={{1,0},{2,1},{3,2},{4,3},{5,4},{6,5},{7,6},{9,8},{10,9},{11,10},{12... | collective-permute-start | bytes 196616 | tf_op jit(solution)/shard_map/ppermute | solution.py:371
  273.8 5.3 %collective-permute-start.14 = (f32[2,32,256]{2,1,0:T(8,128)S(1)}, f32[2,32,256]{2,1,0:T(8,128)S(1)}, u32[]{:S(2)}, u32[]{:S(2)}) collective-permute-start(f32[2,32,256]{2,1,0:T(8,128)S(1)} %step_kernel.5.refs_2_), channel_id=1, source_target_pairs={{0,1},{1,2},{2,3},{3,4},{4,5},{5,6},{6,7},{8,9},{9,10},{10,11},{11... | collective-permute-start | bytes 196616 | tf_op jit(solution)/shard_map/ppermute | solution.py:371
  279.8 32.8 %all-to-all-start.11 = ((f32[16,3,8,128]{3,2,1,0:T(8,128)}), f32[16,3,8,128]{3,2,1,0:T(8,128)S(1)}, u32[]{:S(2)}, u32[]{:S(2)}) async-start(f32[16,3,8,128]{3,2,1,0:T(8,128)} %pack_kernel.5.refs_5_), calls=%async_computation.11 | async-start | bytes 393216 | tf_op jit(solution)/shard_map/all_to_all | solution.py:379
  290.6 9.5 %collective-permute-start.17 = (f32[2,64,256]{2,1,0:T(8,128)S(1)}, f32[2,64,256]{2,1,0:T(8,128)S(1)}, u32[]{:S(2)}, u32[]{:S(2)}) collective-permute-start(f32[2,64,256]{2,1,0:T(8,128)S(1)} %get-tuple-element.98), channel_id=1, source_target_pairs={{0,8},{8,16},{16,24},{24,32},{32,40},{40,48},{48,56},{56,64},{64,7... | collective-permute-start | bytes 393224 | tf_op jit(solution)/shard_map/ppermute | solution.py:371
  300.7 11.9 %collective-permute-start.18 = (f32[2,40,512]{2,1,0:T(8,128)S(1)}, f32[2,40,512]{2,1,0:T(8,128)S(1)}, u32[]{:S(2)}, u32[]{:S(2)}) collective-permute-start(f32[2,40,512]{2,1,0:T(8,128)S(1)} %out_rows_kernel.1.refs_0_), channel_id=1, source_target_pairs={{0,4},{4,0},{1,5},{5,1},{2,6},{6,2},{3,7},{7,3},{8,12},{12,8},{9,1... | collective-permute-start | bytes 491528 | tf_op jit(solution)/shard_map/ppermute | solution.py:375
  313.3 23.5 %all-to-all-start.12 = ((f32[16,2,8,128]{3,2,1,0:T(8,128)}), f32[16,2,8,128]{3,2,1,0:T(8,128)}, u32[]{:S(2)}, u32[]{:S(2)}) async-start(f32[16,2,8,128]{3,2,1,0:T(8,128)} %get-tuple-element.100.refs_2_), calls=%async_computation.12 | async-start | bytes 262144 | tf_op jit(solution)/shard_map/all_to_all | solution.py:379
  324.7 8.8 %collective-permute-start.20 = (f32[2,2,40,512]{3,2,1,0:T(8,128)S(1)}, f32[2,2,40,512]{3,2,1,0:T(8,128)S(1)}, u32[]{:S(2)}, u32[]{:S(2)}) collective-permute-start(f32[2,2,40,512]{3,2,1,0:T(8,128)S(1)} %pair_kernel.1.refs_1_), channel_id=1, source_target_pairs={{0,3},{1,0},{2,1},{3,2},{4,7},{5,4},{6,5},{7,6},{8,11},{9,8},{10,9... | collective-permute-start | bytes 983048 | tf_op jit(solution)/shard_map/ppermute | solution.py:387
  326.7 9.8 %collective-permute-start.19 = (f32[2,2,40,512]{3,2,1,0:T(8,128)S(1)}, f32[2,2,40,512]{3,2,1,0:T(8,128)S(1)}, u32[]{:S(2)}, u32[]{:S(2)}) collective-permute-start(f32[2,2,40,512]{3,2,1,0:T(8,128)S(1)} %pair_kernel.1.refs_1_), channel_id=1, source_target_pairs={{0,1},{1,2},{2,3},{3,0},{4,5},{5,6},{6,7},{7,4},{8,9},{9,10},{10,1... | collective-permute-start | bytes 983048 | tf_op jit(solution)/shard_map/ppermute | solution.py:387
  330.0 12.6 %collective-permute-start.21 = (f32[2,2,40,512]{3,2,1,0:T(8,128)S(1)}, f32[2,2,40,512]{3,2,1,0:T(8,128)S(1)}, u32[]{:S(2)}, u32[]{:S(2)}) collective-permute-start(f32[2,2,40,512]{3,2,1,0:T(8,128)S(1)} %pair_kernel.1.refs_1_), channel_id=1, source_target_pairs={{0,2},{1,3},{2,0},{3,1},{4,6},{5,7},{6,4},{7,5},{8,10},{9,11},{10,... | collective-permute-start | bytes 983048 | tf_op jit(solution)/shard_map/ppermute | solution.py:387
  336.7 10.8 %all-to-all-start.13 = ((f32[8,4,8,128]{3,2,1,0:T(8,128)}), f32[8,4,8,128]{3,2,1,0:T(8,128)S(1)}, u32[]{:S(2)}, u32[]{:S(2)}) async-start(f32[8,4,8,128]{3,2,1,0:T(8,128)} %bitcast.15), calls=%async_computation.13 | async-start | bytes 262144 | tf_op jit(solution)/shard_map/all_to_all | solution.py:379

commit v5 on v4

--- a/solution.py
+++ b/solution.py
@@ -33,10 +33,14 @@
 TILE_AXES = ("xlo", "z", "core")
 MODE_AXES = ("xhi", "y")
 
-ROW, COL, SLOT, LIVE, MODE, CORE, XLO, RING, HAS_NEXT = range(9)
+ROW, COL, SLOT, LIVE, MODE, CORE, XLO, RING, HAS_NEXT, BAND_ID = range(10)
 
 F32 = jnp.float32
 BF16 = jnp.bfloat16
+
+
+def slab_of(place):
+    return place if place < MODES // 2 else 11 - place
 
 
 def fourier_tables():
@@ -142,6 +146,31 @@
             spectra[place, part] = block
 
 
+def split_kernel(probe_in, pieces, sems):
+    copies = []
+    for place in range(MODES):
+        rows = pl.ds(slab_of(place) * SLAB, SLAB)
+        copies.append(
+            pltpu.make_async_copy(probe_in.at[0, :, rows, :], pieces.at[place], sems.at[place])
+        )
+    for copy in copies:
+        copy.start()
+    for copy in copies:
+        copy.wait()
+
+
+def split_probe(probe_modes):
+    anywhere = pl.BlockSpec(memory_space=pl.ANY)
+    return pl.pallas_call(
+        split_kernel,
+        out_shape=jax.ShapeDtypeStruct((MODES, 2, SLAB, SIDE), F32),
+        in_specs=[anywhere],
+        out_specs=anywhere,
+        scratch_shapes=[pltpu.SemaphoreType.DMA((MODES,))],
+        name="split_kernel",
+    )(probe_modes)
+
+
 def first_kernel(scal, own, beside, probe, tables, band, view, shard, spectra):
     band[:, :, :WIDTH] = own[...]
     band[:, :, WIDTH:] = beside[...]
@@ -170,7 +199,9 @@
     forward(view, probe, tables, spectra)
 
 
-def counts_kernel(scal, measured, counts):
+def counts_kernel(scal, measured, counts, flags):
+    for place, which in enumerate((LIVE, CORE, XLO)):
+        flags[place] = jnp.full((8, SIDE), scal[which].astype(F32))
     block = measured[0, scal[SLOT]].astype(F32)
     block = pltpu.roll(block, lax.rem(SIDE - scal[MODE] * SLAB, SIDE), 1)[:, :LANES]
     lanes = lax.broadcasted_iota(jnp.int32, block.shape, 1)
@@ -179,24 +210,25 @@
     counts[...] = block + pltpu.roll(block, 2 * SLAB, 1)
 
 
-def ratio_kernel(scal, spectra, counts, tables, out):
-    real = stacked(spectra[place, 0] for place in range(MODES))
-    imag = stacked(spectra[place, 1] for place in range(MODES))
+def ratio_kernel(spectra, counts, flags, tables, out):
+    real = stacked(spectra[slab_of(index), 0] for index in range(MODES))
+    imag = stacked(spectra[slab_of(index), 1] for index in range(MODES))
     far_real, far_imag = columns_transform(real, imag, tables, 1.0)
     power = far_real * far_real + far_imag * far_imag
     total = power[:, :LANES] + power[:, LANES:]
     total = total + pltpu.roll(total, 2 * SLAB, 1)
     total = total + pltpu.roll(total, SLAB, 1)
     ratio = jnp.sqrt((counts[...] + SOFT_FLOOR) / (total + SOFT_FLOOR)) - 1.0
-    ratio = ratio * scal[LIVE].astype(F32)
+    ratio = ratio * flags[0, 0:1, :LANES]
     ratio = jnp.concatenate([ratio, ratio], axis=1)
     both = columns_transform(far_real * ratio, far_imag * ratio, tables, -1.0)
     for part in range(2):
         for place in range(MODES):
-            out[place, part] = both[part][place * SLAB : (place + 1) * SLAB]
-
-
-def backward_kernel(scal, spectra, view, tables, chi, keep, send):
+            row = slab_of(place) * SLAB
+            out[place, part] = both[part][row : row + SLAB]
+
+
+def backward_kernel(spectra, view, flags, tables, chi, keep, send):
     real = stacked(swap_blocks([spectra[place, 0] for place in range(MODES)]))
     imag = stacked(swap_blocks([spectra[place, 1] for place in range(MODES)]))
     chi_real, chi_imag = rows_transform(real, imag, tables, -1.0)
@@ -209,26 +241,19 @@
         chi[mode, 1] = imag
         sums.append(view_real * real + view_imag * imag)
         sums.append(view_real * imag - view_imag * real)
-    sums.append((view_real * view_real + view_imag * view_imag) * scal[LIVE].astype(F32))
-
-    @pl.when(scal[CORE] == 0)
-    def _():
-        for index, value in enumerate(sums):
-            keep[index] = value[:16]
-            send[index] = value[16:]
-
-    @pl.when(scal[CORE] == 1)
-    def _():
-        for index, value in enumerate(sums):
-            keep[index] = value[16:]
-            send[index] = value[:16]
-
-
-def halve_kernel(scal, mine, theirs, keep, send):
-    ours = pl.ds(pl.multiple_of(scal[XLO] * 8, 8), 8)
-    others = pl.ds(pl.multiple_of((1 - scal[XLO]) * 8, 8), 8)
-    keep[...] = mine[:, ours] + theirs[:, ours]
-    send[...] = mine[:, others] + theirs[:, others]
+    sums.append((view_real * view_real + view_imag * view_imag) * flags[0, 0:1, :])
+    second = jnp.broadcast_to(flags[1, 0:1, :], (16, SIDE)) > 0.5
+    for index, value in enumerate(sums):
+        keep[index] = jnp.where(second, value[16:], value[:16])
+        send[index] = jnp.where(second, value[:16], value[16:])
+
+
+def halve_kernel(mine, theirs, flags, keep, send):
+    second = jnp.broadcast_to(flags[2, 0:1, :], (8, SIDE)) > 0.5
+    for index in range(2 * MODES + 1):
+        value = mine[index] + theirs[index]
+        keep[index] = jnp.where(second, value[8:], value[:8])
+        send[index] = jnp.where(second, value[:8], value[8:])
 
 
 def pack_kernel(mine, theirs, packed):
@@ -236,9 +261,10 @@
         lanes = slice(half * LANES, (half + 1) * LANES)
         total = mine[:, :, lanes] + theirs[:, :, lanes]
         for mode in range(MODES):
-            packed[2 * mode + half, 0] = total[2 * mode]
-            packed[2 * mode + half, 1] = total[2 * mode + 1]
-            packed[2 * mode + half, 2] = total[2 * MODES]
+            place = (2 * mode + half + RINGS // 2) % RINGS
+            packed[place, 0] = total[2 * mode]
+            packed[place, 1] = total[2 * mode + 1]
+            packed[place, 2] = total[2 * MODES]
 
 
 def step_kernel(chi, probe, step):
@@ -287,7 +313,7 @@
 
 
 def out_rows_kernel(scal, part_band, from_left, rows_out):
-    rows = pl.ds(pl.multiple_of(scal[MODE] // 2 * 8, 8), OUT_ROWS)
+    rows = pl.ds(pl.multiple_of(scal[BAND_ID] // 2 * 8, 8), OUT_ROWS)
     rows_out[:, :, :SIDE] = part_band[:, rows, :SIDE] + from_left[:, rows, :]
     rows_out[:, :, SIDE:] = part_band[:, rows, SIDE:WIDTH]
 
@@ -302,8 +328,9 @@
     for source, steps in ((own, 0), (plus, 3), (minus, 1), (across, 2)):
         for beyond in range(2):
             half = xhi if beyond == 0 else 1 - xhi
-            place = half * 4 + lax.rem(y + steps, 4)
-            rows = pl.ds(pl.multiple_of(place * 9 // 2 * 8, 8), OUT_ROWS)
+            column = lax.rem(y + steps, 4)
+            slab = jnp.where(half == 0, column, 7 - column)
+            rows = pl.ds(pl.multiple_of(slab * 9 // 2 * 8, 8), OUT_ROWS)
             object_out[:, rows, :] = source[beyond]
 
 
@@ -311,7 +338,7 @@
     for xlo in range(2):
         for core in range(2):
             for place in range(MODES):
-                row = place * SLAB + core * 16 + xlo * 8
+                row = slab_of(place) * SLAB + core * 16 + xlo * 8
                 probe_out[0, :, row : row + 8, :LANES] = pieces[xlo, core, 2 * place]
                 probe_out[0, :, row : row + 8, LANES:] = pieces[xlo, core, 2 * place + 1]
 
@@ -375,6 +402,17 @@
     return lax.ppermute(value, axis, [(0, 1), (1, 0)])
 
 
+def beside_slab(value, steps):
+    first, last = max(0, -steps), min(MODES, MODES - steps)
+    pairs = [(slab_of(i), slab_of(i + steps)) for i in range(first, last)]
+    return lax.ppermute(value, MODE_AXES, pairs)
+
+
+def exchange_far_first(value):
+    order = [(i + RINGS // 2) % RINGS for i in range(RINGS)]
+    return lax.all_to_all(value, "z", 0, 0, tiled=True, axis_index_groups=[order])
+
+
 def exchange(value, axes):
     return lax.all_to_all(value, axes, 0, 0, tiled=True)
 
@@ -394,9 +432,10 @@
     slots = visit_order[0]
     tile = lax.axis_index(TILE_AXES)
     mode = lax.axis_index(MODE_AXES)
-    pieces = probe_modes.reshape(2, MODES, SLAB, SIDE).transpose(1, 0, 2, 3)
+    slab = jnp.where(mode < MODES // 2, mode, 11 - mode)
+    pieces = split_probe(probe_modes)
     probe = exchange(pieces, MODE_AXES)
-    own, left = take_own(mode, object_tiles, pieces)
+    own, left = take_own(slab, object_tiles, pieces)
     beside = shift(left, TILE_AXES, TILES, -1)
     places = [
         mode,
@@ -404,6 +443,7 @@
         lax.axis_index("xlo"),
         lax.axis_index("z"),
         (tile < TILES - 1).astype(jnp.int32),
+        slab,
     ]
     chosen = slots[:, None] == jnp.arange(STEPS, dtype=jnp.int32)[None, :]
     per_step = [
@@ -419,7 +459,8 @@
     slab_pair = (2, SLAB, SIDE)
     band_shape = (2, BAND, WIDE)
     edge = (2, BAND, SIDE)
-    (counts,) = call(counts_kernel, [(SIDE, LANES)], scalars[0], measured)
+    counts_shapes = [(SIDE, LANES), (3, 8, SIDE)]
+    counts, flags = call(counts_kernel, counts_shapes, scalars[0], measured)
     for step in range(STEPS):
         scal = scalars[step]
         final = step == STEPS - 1
@@ -435,9 +476,6 @@
                 after=(counts,),
             )
         else:
-            band, view = call(
-                view_kernel, [band_shape, slab_pair], scal, part_band, from_left, from_right
-            )
             probe, spectra = call(
                 next_kernel,
                 [slabs, slabs],
@@ -448,24 +486,29 @@
                 after=(counts,),
             )
         spectra = exchange(spectra, MODE_AXES)
-        (spectra,) = call(ratio_kernel, [slabs], scal, spectra, counts, tables)
+        (spectra,) = call(
+            ratio_kernel, [slabs], spectra, counts, flags, tables, scalars=False
+        )
         spectra = exchange(spectra, MODE_AXES)
         chi, keep, send = call(
             backward_kernel,
             [slabs] + [(2 * MODES + 1, 16, SIDE)] * 2,
-            scal,
             spectra,
             view,
+            flags,
             tables,
+            scalars=False,
         )
         received = other(send, "core")
-        keep, send = call(halve_kernel, [(2 * MODES + 1, 8, SIDE)] * 2, scal, keep, received)
+        keep, send = call(
+            halve_kernel, [(2 * MODES + 1, 8, SIDE)] * 2, keep, received, flags, scalars=False
+        )
         received = other(send, "xlo")
         (object_step,) = call(
             step_kernel, [slab_pair], chi, probe, scalars=False, after=(keep,)
         )
-        above = shift(object_step, MODE_AXES, MODES, 1)
-        below = shift(object_step, MODE_AXES, MODES, -1)
+        above = beside_slab(object_step, 1)
+        below = beside_slab(object_step, -1)
         (packed,) = call(
             pack_kernel,
             [(RINGS, 3, 8, LANES)],
@@ -474,10 +517,10 @@
             scalars=False,
             after=(above, below) if final else (object_step,),
         )
-        sums = exchange(packed, "z")
+        sums = exchange_far_first(packed)
         if not final:
-            (counts,) = call(
-                counts_kernel, [(SIDE, LANES)], scalars[step + 1], measured, after=(packed,)
+            counts, flags = call(
+                counts_kernel, counts_shapes, scalars[step + 1], measured, after=(packed,)
             )
         placing = [scal, above, object_step, below, band]
         if final:
@@ -495,37 +538,42 @@
             sums,
             shard,
             scalars=False,
-            after=(far_rows,) if final else (above, below, counts),
+            after=(rows_out,) if final else (above, below, counts),
         )
         piece = exchange(shards, "z")
         if final:
-            (pair,) = call(
-                pair_kernel,
-                [(2, 2, OUT_ROWS, WIDTH)],
-                rows_out,
-                far_rows,
-                scalars=False,
-                after=(shards,),
-            )
-            plus, minus = around(pair, 1), around(pair, -1)
-            piece, plus, minus = lax.optimization_barrier((piece, plus, minus))
+            piece, far_rows = lax.optimization_barrier((piece, far_rows))
         else:
             part_band, to_left, to_right = call(
                 place_kernel, [band_shape, edge, edge], *placing, after=(shards,)
             )
             from_left = shift(to_right, TILE_AXES, TILES, 1)
             from_right = shift(to_left, TILE_AXES, TILES, -1)
-            piece, from_left, from_right = lax.optimization_barrier(
-                (piece, from_left, from_right)
+            band, view = call(
+                view_kernel,
+                [band_shape, slab_pair],
+                scalars[step + 1],
+                part_band,
+                from_left,
+                from_right,
             )
+            piece, view = lax.optimization_barrier((piece, view))
             pieces = gather_pieces(piece)
+    (pair,) = call(
+        pair_kernel,
+        [(2, 2, OUT_ROWS, WIDTH)],
+        rows_out,
+        far_rows,
+        scalars=False,
+        after=(piece,),
+    )
     (object_out,) = call(
         object_kernel,
         [(2, HEIGHT, WIDTH)],
         scal,
         pair,
-        plus,
-        minus,
+        around(pair, 1),
+        around(pair, -1),
         around(pair, 2),
     )
     piece = exchange(piece.reshape(MODES, 4, 8, LANES), MODE_AXES)

time: 369 us -> 363 us (0.984)
  Pallas kernels: 30.4 us -> 42.5 us
  waiting for transfers between devices: 53.7 us -> 43.6 us
    all_to_all x8 -> x4, starting transfers between devices: 70.3 us -> 27.4 us  [exchange(): return lax.all_to_all(value, axes, 0, 0, tiled=True)]
    all_to_all x0 -> x3, starting transfers between devices: none -> 41 us  [exchange_far_first(): lax.all_to_all(value, 'z', 0, 0, tiled=True, axis_index_groups=[order])]
    pallas_call x0 -> x1, Pallas kernels: none -> 17.1 us  [split_probe(): pl.pallas_call(split_kernel, out_shape=jax.ShapeDtypeStruct((MODES, 2, SL...]
    ppermute x0 -> x6, starting transfers between devices: none -> 15.8 us  [beside_slab(): return lax.ppermute(value, MODE_AXES, pairs)]
    ppermute x12 -> x6, starting transfers between devices: 39.7 us -> 26.3 us  [shift(): lax.ppermute(value, axes, [(i, i + steps) for i in range(first, last)])]
    all_to_all x8 -> x4, waiting for transfers between devices: 16.3 us -> 5.69 us  [exchange(): return lax.all_to_all(value, axes, 0, 0, tiled=True)]
    ppermute x3, waiting for transfers between devices: 6.52 us -> 0.01 us  [around(): return lax.ppermute(value, 'y', [(i, (i + steps) % 4) for i in range(4)])]
    all_gather x3, blocking collectives: 38.6 us -> 32.4 us  [gather_pieces(): lax.all_gather(piece, ('xlo', 'core')).reshape(2, 2, RINGS, 2, 8, LANES)]
  transfers between devices with their start and end apart: 30 -> 29, of which waited for: 23 -> 19; matrix products, arithmetic and copies ran while one was open for 0% -> 0% of each run, Pallas kernels for 2% -> 2%
where the time goes in v5:
time: 363 us; the launch traced here: 362 us
  starting transfers between devices  148 us (41%)
  blocking collectives  125 us (34%)
  waiting for transfers between devices  43.6 us (12%)
  Pallas kernels  42.5 us (12%)
    all_to_all x7, blocking collectives, exchange(): return lax.all_to_all(value, axes, 0, 0, tiled=True)  92.9 us
    all_to_all x3, starting transfers between devices, exchange_far_first(): lax.all_to_all(value, 'z', 0, 0, tiled=True, axis_index_groups=[order])  41 us
    all_gather x3, blocking collectives, gather_pieces(): lax.all_gather(piece, ('xlo', 'core')).reshape(2, 2, RINGS, 2, 8, LANES)  32.4 us
    ppermute x7, starting transfers between devices, other(): return lax.ppermute(value, axis, [(0, 1), (1, 0)])  28.2 us
    all_to_all x4, starting transfers between devices, exchange(): return lax.all_to_all(value, axes, 0, 0, tiled=True)  27.4 us
    ppermute x6, starting transfers between devices, shift(): lax.ppermute(value, axes, [(i, i + steps) for i in range(first, last)])  26.3 us
    pallas_call x33, Pallas kernels, call(): pl.pallas_call(body, out_shape=[jax.ShapeDtypeStruct(shape, F32) for shap...  25.4 us
    pallas_call x1, Pallas kernels, split_probe(): pl.pallas_call(split_kernel, out_shape=jax.ShapeDtypeStruct((MODES, 2, SL...  17.1 us
  transfers between devices with their start and end apart: 29, of which 19 were waited for; matrix products, arithmetic and copies ran while one was open for 0% of the time, Pallas kernels for 2%

profile of v5, /device:TPU:1, one launch (start us, length us, event | category | flops | bytes accessed | tf_op | source)
XLA Modules:
  0.0 361.7 jit_solution(13980158953367116343)
XLA Ops:
  0.6 17.1 %split_kernel.1._ = f32[8,2,32,256]{3,2,1,0:T(8,128)} custom-call(f32[1,2,256,256]{3,2,1,0:T(8,128)} %probe_in.1), custom_call_target="tpu_custom_call" | custom-call | tf_op jit(solution)/shard_map/split_kernel/pallas_call | solution.py:164
  17.8 7.6 %all-to-all-start = ((f32[8,2,32,256]{3,2,1,0:T(8,128)}), f32[8,2,32,256]{3,2,1,0:T(8,128)S(1)}, u32[]{:S(2)}, u32[]{:S(2)}) async-start(f32[8,2,32,256]{3,2,1,0:T(8,128)} %split_kernel.1._), calls=%async_computation | async-start | bytes 1048576 | tf_op jit(solution)/shard_map/all_to_all | solution.py:417
  25.5 4.9 %collective-permute-start = (f32[2,64,256]{2,1,0:T(8,128)S(1)}, f32[2,64,256]{2,1,0:T(8,128)S(1)}, u32[]{:S(2)}, u32[]{:S(2)}) collective-permute-start(f32[2,64,256]{2,1,0:T(8,128)S(1)} %get-tuple-element.57), channel_id=1, source_target_pairs={{8,0},{16,8},{24,16},{32,24},{40,32},{48,40},{56,48},{64,56},{72,6... | collective-permute-start | bytes 393224 | tf_op jit(solution)/shard_map/ppermute | solution.py:398
  33.0 1.2 all-to-all-done.refs_3_.refs_1_
  34.2 1.6 first_kernel.1
  35.8 15.1 %all_to_all.70.refs_0_ = f32[8,2,32,256]{3,2,1,0:T(8,128)S(1)} all-to-all(f32[8,2,32,256]{3,2,1,0:T(8,128)S(1)} %get-tuple-element.59), channel_id=1, replica_groups=mesh['xlo'=2,'z'=16,'core'=2,'xhi'=2,'y'=4] {'xhi','y'}, dimensions={0} | all-to-all | bytes 1048576 | tf_op jit(solution)/shard_map/all_to_all | solution.py:417
  50.9 1.7 ratio_kernel.3
  52.6 12.3 %all_to_all.71.refs_0_ = f32[8,2,32,256]{3,2,1,0:T(8,128)S(1)} all-to-all(f32[8,2,32,256]{3,2,1,0:T(8,128)S(1)} %ratio_kernel.3), channel_id=1, replica_groups=mesh['xlo'=2,'z'=16,'core'=2,'xhi'=2,'y'=4] {'xhi','y'}, dimensions={0} | all-to-all | bytes 1048576 | tf_op jit(solution)/shard_map/all_to_all | solution.py:417
  65.7 5.3 %collective-permute-start.1 = (f32[17,16,256]{2,1,0:T(8,128)S(1)}, f32[17,16,256]{2,1,0:T(8,128)S(1)}, u32[]{:S(2)}, u32[]{:S(2)}) collective-permute-start(f32[17,16,256]{2,1,0:T(8,128)S(1)} %get-tuple-element.63), channel_id=1, source_target_pairs={{0,8},{8,0},{1,9},{9,1},{2,10},{10,2},{3,11},{11,3},{4,12},{12,4},... | collective-permute-start | bytes 835592 | tf_op jit(solution)/shard_map/ppermute | solution.py:402
  71.0 1.2 collective-permute-done.1.refs_1_
  72.2 6.7 %collective-permute-start.2 = (f32[17,8,256]{2,1,0:T(8,128)S(1)}, f32[17,8,256]{2,1,0:T(8,128)S(1)}, u32[]{:S(2)}, u32[]{:S(2)}) collective-permute-start(f32[17,8,256]{2,1,0:T(8,128)S(1)} %get-tuple-element.65), channel_id=1, source_target_pairs={{0,256},{256,0},{1,257},{257,1},{2,258},{258,2},{3,259},{259,3},{4... | collective-permute-start | bytes 417800 | tf_op jit(solution)/shard_map/ppermute | solution.py:402
  79.1 3.6 collective-permute-done.2.refs_1_
  83.4 17.0 %all-to-all-start.3 = ((f32[16,3,8,128]{3,2,1,0:T(8,128)}), f32[16,3,8,128]{3,2,1,0:T(8,128)S(1)}, u32[]{:S(2)}, u32[]{:S(2)}) async-start(f32[16,3,8,128]{3,2,1,0:T(8,128)} %pack_kernel.3.refs_2_), calls=%async_computation.3 | async-start | bytes 393216 | tf_op jit(solution)/shard_map/all_to_all | solution.py:413
  100.4 1.3 collective-permute-start.4
  101.7 4.0 %collective-permute-start.3 = (f32[2,32,256]{2,1,0:T(8,128)S(1)}, f32[2,32,256]{2,1,0:T(8,128)S(1)}, u32[]{:S(2)}, u32[]{:S(2)}) collective-permute-start(f32[2,32,256]{2,1,0:T(8,128)S(1)} %step_kernel.3.refs_2_), channel_id=1, source_target_pairs={{0,1},{1,2},{2,3},{3,7},{7,6},{6,5},{5,4},{8,9},{9,10},{10,11},{11... | collective-permute-start | bytes 196616 | tf_op jit(solution)/shard_map/ppermute | solution.py:408
  107.0 2.4 all-to-all-done.3.refs_0_
  110.1 7.6 %all-to-all-start.4 = ((f32[16,2,8,128]{3,2,1,0:T(8,128)}), f32[16,2,8,128]{3,2,1,0:T(8,128)S(1)}, u32[]{:S(2)}, u32[]{:S(2)}) async-start(f32[16,2,8,128]{3,2,1,0:T(8,128)} %get-tuple-element.69.refs_5_), calls=%async_computation.4 | async-start | bytes 262144 | tf_op jit(solution)/shard_map/all_to_all | solution.py:417
  118.5 6.7 %collective-permute-start.5 = (f32[2,64,256]{2,1,0:T(8,128)S(1)}, f32[2,64,256]{2,1,0:T(8,128)S(1)}, u32[]{:S(2)}, u32[]{:S(2)}) collective-permute-start(f32[2,64,256]{2,1,0:T(8,128)S(1)} %get-tuple-element.72), channel_id=1, source_target_pairs={{0,8},{8,16},{16,24},{24,32},{32,40},{40,48},{48,56},{56,64},{64,7... | collective-permute-start | bytes 393224 | tf_op jit(solution)/shard_map/ppermute | solution.py:398
  125.1 1.9 collective-permute-start.6
  127.1 1.1 collective-permute-done.5.refs_2_
  128.2 3.7 %collective-permute-done.6.refs_3_ = f32[2,64,256]{2,1,0:T(8,128)S(1)} collective-permute-done((f32[2,64,256]{2,1,0:T(8,128)S(1)}, f32[2,64,256]{2,1,0:T(8,128)S(1)}, u32[]{:S(2)}, u32[]{:S(2)}) %collective-permute-start.6) | collective-permute-done | bytes 131104 | tf_op jit(solution)/shard_map/ppermute | solution.py:398
  132.6 7.9 %all-gather = f32[64,2,8,128]{3,2,1,0:T(8,128)S(1)} all-gather(f32[16,2,8,128]{3,2,1,0:T(8,128)S(1)} %all-to-all-done.4), channel_id=2, replica_groups=mesh['xlo'=2,'z'=16,'core'=2,'xhi'=2,'y'=4] {'xlo','core'}, dimensions={0}, use_global_device_ids=true | all-gather | bytes 655360 | tf_op jit(solution)/shard_map/all_gather | solution.py:421
  140.5 0.9 next_kernel.2
  141.4 12.8 %all_to_all.72.refs_0_ = f32[8,2,32,256]{3,2,1,0:T(8,128)S(1)} all-to-all(f32[8,2,32,256]{3,2,1,0:T(8,128)S(1)} %get-tuple-element.77), channel_id=1, replica_groups=mesh['xlo'=2,'z'=16,'core'=2,'xhi'=2,'y'=4] {'xhi','y'}, dimensions={0} | all-to-all | bytes 1048576 | tf_op jit(solution)/shard_map/all_to_all | solution.py:417
  154.2 1.7 ratio_kernel.4
  155.9 13.9 %all_to_all.73.refs_0_ = f32[8,2,32,256]{3,2,1,0:T(8,128)S(1)} all-to-all(f32[8,2,32,256]{3,2,1,0:T(8,128)S(1)} %ratio_kernel.4), channel_id=1, replica_groups=mesh['xlo'=2,'z'=16,'core'=2,'xhi'=2,'y'=4] {'xhi','y'}, dimensions={0} | all-to-all | bytes 1048576 | tf_op jit(solution)/shard_map/all_to_all | solution.py:417
  170.7 4.4 %collective-permute-start.7 = (f32[17,16,256]{2,1,0:T(8,128)S(1)}, f32[17,16,256]{2,1,0:T(8,128)S(1)}, u32[]{:S(2)}, u32[]{:S(2)}) collective-permute-start(f32[17,16,256]{2,1,0:T(8,128)S(1)} %get-tuple-element.80), channel_id=1, source_target_pairs={{0,8},{8,0},{1,9},{9,1},{2,10},{10,2},{3,11},{11,3},{4,12},{12,4},... | collective-permute-start | bytes 835592 | tf_op jit(solution)/shard_map/ppermute | solution.py:402
  175.0 1.2 collective-permute-done.7.refs_1_
  176.2 2.9 collective-permute-start.8
  179.3 3.7 %collective-permute-done.8.refs_1_ = f32[17,8,256]{2,1,0:T(8,128)S(1)} collective-permute-done((f32[17,8,256]{2,1,0:T(8,128)S(1)}, f32[17,8,256]{2,1,0:T(8,128)S(1)}, u32[]{:S(2)}, u32[]{:S(2)}) %collective-permute-start.8) | collective-permute-done | bytes 139296 | tf_op jit(solution)/shard_map/ppermute | solution.py:402
  183.7 11.9 %all-to-all-start.7 = ((f32[16,3,8,128]{3,2,1,0:T(8,128)}), f32[16,3,8,128]{3,2,1,0:T(8,128)S(1)}, u32[]{:S(2)}, u32[]{:S(2)}) async-start(f32[16,3,8,128]{3,2,1,0:T(8,128)} %pack_kernel.4.refs_2_), calls=%async_computation.7 | async-start | bytes 393216 | tf_op jit(solution)/shard_map/all_to_all | solution.py:413
  195.6 1.3 collective-permute-start.10
  196.9 4.0 %collective-permute-start.9 = (f32[2,32,256]{2,1,0:T(8,128)S(1)}, f32[2,32,256]{2,1,0:T(8,128)S(1)}, u32[]{:S(2)}, u32[]{:S(2)}) collective-permute-start(f32[2,32,256]{2,1,0:T(8,128)S(1)} %step_kernel.4.refs_2_), channel_id=1, source_target_pairs={{0,1},{1,2},{2,3},{3,7},{7,6},{6,5},{5,4},{8,9},{9,10},{10,11},{11... | collective-permute-start | bytes 196616 | tf_op jit(solution)/shard_map/ppermute | solution.py:408
  202.2 2.4 all-to-all-done.7.refs_0_
  205.3 7.6 %all-to-all-start.8 = ((f32[16,2,8,128]{3,2,1,0:T(8,128)}), f32[16,2,8,128]{3,2,1,0:T(8,128)S(1)}, u32[]{:S(2)}, u32[]{:S(2)}) async-start(f32[16,2,8,128]{3,2,1,0:T(8,128)} %get-tuple-element.87.refs_5_), calls=%async_computation.8 | async-start | bytes 262144 | tf_op jit(solution)/shard_map/all_to_all | solution.py:417
  213.6 6.7 %collective-permute-start.11 = (f32[2,64,256]{2,1,0:T(8,128)S(1)}, f32[2,64,256]{2,1,0:T(8,128)S(1)}, u32[]{:S(2)}, u32[]{:S(2)}) collective-permute-start(f32[2,64,256]{2,1,0:T(8,128)S(1)} %get-tuple-element.90), channel_id=1, source_target_pairs={{0,8},{8,16},{16,24},{24,32},{32,40},{40,48},{48,56},{56,64},{64,7... | collective-permute-start | bytes 393224 | tf_op jit(solution)/shard_map/ppermute | solution.py:398
  220.3 1.9 collective-permute-start.12
  222.2 1.1 collective-permute-done.11.refs_2_
  223.4 3.7 %collective-permute-done.12.refs_3_ = f32[2,64,256]{2,1,0:T(8,128)S(1)} collective-permute-done((f32[2,64,256]{2,1,0:T(8,128)S(1)}, f32[2,64,256]{2,1,0:T(8,128)S(1)}, u32[]{:S(2)}, u32[]{:S(2)}) %collective-permute-start.12) | collective-permute-done | bytes 131104 | tf_op jit(solution)/shard_map/ppermute | solution.py:398
  227.8 8.7 %all-gather.1 = f32[64,2,8,128]{3,2,1,0:T(8,128)S(1)} all-gather(f32[16,2,8,128]{3,2,1,0:T(8,128)S(1)} %all-to-all-done.8), channel_id=3, replica_groups=mesh['xlo'=2,'z'=16,'core'=2,'xhi'=2,'y'=4] {'xlo','core'}, dimensions={0}, use_global_device_ids=true | all-gather | bytes 655360 | tf_op jit(solution)/shard_map/all_gather | solution.py:421
  236.5 0.9 next_kernel.3
  237.3 13.2 %all_to_all.74.refs_0_ = f32[8,2,32,256]{3,2,1,0:T(8,128)S(1)} all-to-all(f32[8,2,32,256]{3,2,1,0:T(8,128)S(1)} %get-tuple-element.95), channel_id=1, replica_groups=mesh['xlo'=2,'z'=16,'core'=2,'xhi'=2,'y'=4] {'xhi','y'}, dimensions={0} | all-to-all | bytes 1048576 | tf_op jit(solution)/shard_map/all_to_all | solution.py:417
  250.5 1.7 ratio_kernel.5
  252.2 14.0 %all_to_all.75.refs_0_ = f32[8,2,32,256]{3,2,1,0:T(8,128)S(1)} all-to-all(f32[8,2,32,256]{3,2,1,0:T(8,128)S(1)} %ratio_kernel.5), channel_id=1, replica_groups=mesh['xlo'=2,'z'=16,'core'=2,'xhi'=2,'y'=4] {'xhi','y'}, dimensions={0} | all-to-all | bytes 1048576 | tf_op jit(solution)/shard_map/all_to_all | solution.py:417
  267.0 4.4 %collective-permute-start.13 = (f32[17,16,256]{2,1,0:T(8,128)S(1)}, f32[17,16,256]{2,1,0:T(8,128)S(1)}, u32[]{:S(2)}, u32[]{:S(2)}) collective-permute-start(f32[17,16,256]{2,1,0:T(8,128)S(1)} %get-tuple-element.100), channel_id=1, source_target_pairs={{0,8},{8,0},{1,9},{9,1},{2,10},{10,2},{3,11},{11,3},{4,12},{12,4},... | collective-permute-start | bytes 835592 | tf_op jit(solution)/shard_map/ppermute | solution.py:402
  271.4 1.2 collective-permute-done.13.refs_1_
  272.6 2.0 collective-permute-start.16
  274.8 1.3 collective-permute-start.15
  276.1 4.0 %collective-permute-start.14 = (f32[2,32,256]{2,1,0:T(8,128)S(1)}, f32[2,32,256]{2,1,0:T(8,128)S(1)}, u32[]{:S(2)}, u32[]{:S(2)}) collective-permute-start(f32[2,32,256]{2,1,0:T(8,128)S(1)} %step_kernel.5.refs_2_), channel_id=1, source_target_pairs={{0,1},{1,2},{2,3},{3,7},{7,6},{6,5},{5,4},{8,9},{9,10},{10,11},{11... | collective-permute-start | bytes 196616 | tf_op jit(solution)/shard_map/ppermute | solution.py:408
  280.1 1.3 collective-permute-done.14.refs_2_.refs_1_
  282.1 12.1 %all-to-all-start.11 = ((f32[16,3,8,128]{3,2,1,0:T(8,128)}), f32[16,3,8,128]{3,2,1,0:T(8,128)S(1)}, u32[]{:S(2)}, u32[]{:S(2)}) async-start(f32[16,3,8,128]{3,2,1,0:T(8,128)} %pack_kernel.5.refs_5_), calls=%async_computation.11 | async-start | bytes 393216 | tf_op jit(solution)/shard_map/all_to_all | solution.py:413
  294.2 1.4 place_kernel.5
  295.6 4.1 %collective-permute-start.17 = (f32[2,64,256]{2,1,0:T(8,128)S(1)}, f32[2,64,256]{2,1,0:T(8,128)S(1)}, u32[]{:S(2)}, u32[]{:S(2)}) collective-permute-start(f32[2,64,256]{2,1,0:T(8,128)S(1)} %get-tuple-element.105), channel_id=1, source_target_pairs={{0,8},{8,16},{16,24},{24,32},{32,40},{40,48},{48,56},{56,64},{64,7... | collective-permute-start | bytes 393224 | tf_op jit(solution)/shard_map/ppermute | solution.py:398
  299.7 5.0 %collective-permute-done.17.refs_2_ = f32[2,64,256]{2,1,0:T(8,128)S(1)} collective-permute-done((f32[2,64,256]{2,1,0:T(8,128)S(1)}, f32[2,64,256]{2,1,0:T(8,128)S(1)}, u32[]{:S(2)}, u32[]{:S(2)}) %collective-permute-start.17) | collective-permute-done | bytes 131104 | tf_op jit(solution)/shard_map/ppermute | solution.py:398
  306.0 4.6 %all-to-all-start.12 = ((f32[16,2,8,128]{3,2,1,0:T(8,128)}), f32[16,2,8,128]{3,2,1,0:T(8,128)S(1)}, u32[]{:S(2)}, u32[]{:S(2)}) async-start(f32[16,2,8,128]{3,2,1,0:T(8,128)} %get-tuple-element.107), calls=%async_computation.12 | async-start | bytes 262144 | tf_op jit(solution)/shard_map/all_to_all | solution.py:417
  310.6 2.6 collective-permute-start.18
  313.2 5.0 %collective-permute-done.18.refs_1_ = f32[2,40,512]{2,1,0:T(8,128)S(1)} collective-permute-done((f32[2,40,512]{2,1,0:T(8,128)S(1)}, f32[2,40,512]{2,1,0:T(8,128)S(1)}, u32[]{:S(2)}, u32[]{:S(2)}) %collective-permute-start.18) | collective-permute-done | bytes 163872 | tf_op jit(solution)/shard_map/ppermute | solution.py:402
  318.2 4.4 %all-to-all-done.12.refs_2_ = f32[16,2,8,128]{3,2,1,0:T(8,128)S(1)} async-done(((f32[16,2,8,128]{3,2,1,0:T(8,128)}), f32[16,2,8,128]{3,2,1,0:T(8,128)S(1)}, u32[]{:S(2)}, u32[]{:S(2)}) %all-to-all-start.12) | async-done | bytes 131104 | tf_op jit(solution)/shard_map/all_to_all | solution.py:417
  322.6 3.5 collective-permute-start.21
  326.1 3.7 %collective-permute-start.20 = (f32[2,2,40,512]{3,2,1,0:T(8,128)S(1)}, f32[2,2,40,512]{3,2,1,0:T(8,128)S(1)}, u32[]{:S(2)}, u32[]{:S(2)}) collective-permute-start(f32[2,2,40,512]{3,2,1,0:T(8,128)S(1)} %pair_kernel.1.refs_1_), channel_id=1, source_target_pairs={{0,3},{1,0},{2,1},{3,2},{4,7},{5,4},{6,5},{7,6},{8,11},{9,8},{10,9... | collective-permute-start | bytes 983048 | tf_op jit(solution)/shard_map/ppermute | solution.py:425
  329.8 1.9 collective-permute-start.19
  331.7 11.7 %all_to_all.76 = f32[8,4,8,128]{3,2,1,0:T(8,128)S(1)} all-to-all(f32[8,4,8,128]{3,2,1,0:T(8,128)S(1)} %bitcast.24), channel_id=1, replica_groups=mesh['xlo'=2,'z'=16,'core'=2,'xhi'=2,'y'=4] {'xhi','y'}, dimensions={0} | all-to-all | bytes 262144 | tf_op jit(solution)/shard_map/all_to_all | solution.py:417
  343.4 15.8 %all_gather.19 = f32[4,16,2,8,128]{4,3,2,1,0:T(8,128)S(1)} all-gather(f32[1,16,2,8,128]{4,3,2,1,0:T(8,128)S(1)} %bitcast.25), channel_id=1, replica_groups=mesh['xlo'=2,'z'=16,'core'=2,'xhi'=2,'y'=4] {'xlo','core'}, dimensions={0}, use_global_device_ids=true | all-gather | bytes 655360 | tf_op jit(solution)/shard_map/all_gather | solution.py:421
  360.0 1.7 object_kernel.1
  (67 shorter events, 16.0 us)
Async XLA Ops:
  0.6 24.8 %copy-start.3 = (f32[2,288,512]{2,1,0:T(8,128)S(1)}, f32[2,288,512]{2,1,0:T(8,128)}, u32[]{:S(2)}) copy-start(f32[2,288,512]{2,1,0:T(8,128)} %whole.1) | copy-start | bytes 3538948
  17.7 7.7 %copy-start.1 = (f32[8,2,32,256]{3,2,1,0:T(8,128)S(1)}, f32[8,2,32,256]{3,2,1,0:T(8,128)}, u32[]{:S(2)}) copy-start(f32[8,2,32,256]{3,2,1,0:T(8,128)} %split_kernel.1._) | copy-start | bytes 1572868
  17.7 12.7 %copy-start.4 = (s32[1,3]{1,0:T(1,128)S(1)}, s32[1,3]{1,0:T(1,128)}, u32[]{:S(2)}) copy-start(s32[1,3]{1,0:T(1,128)} %param.14) | copy-start | bytes 40
  17.7 12.7 %copy-start.5 = (s32[1,3]{1,0:T(1,128)S(1)}, s32[1,3]{1,0:T(1,128)}, u32[]{:S(2)}) copy-start(s32[1,3]{1,0:T(1,128)} %param.12) | copy-start | bytes 40
  17.7 12.7 %copy-start.6 = (s32[1,3]{1,0:T(1,128)S(1)}, s32[1,3]{1,0:T(1,128)}, u32[]{:S(2)}) copy-start(s32[1,3]{1,0:T(1,128)} %param.11) | copy-start | bytes 40
  17.8 16.5 %all-to-all-start = ((f32[8,2,32,256]{3,2,1,0:T(8,128)}), f32[8,2,32,256]{3,2,1,0:T(8,128)S(1)}, u32[]{:S(2)}, u32[]{:S(2)}) async-start(f32[8,2,32,256]{3,2,1,0:T(8,128)} %split_kernel.1._), calls=%async_computation | async-start | bytes 1048576 | tf_op jit(solution)/shard_map/all_to_all | solution.py:417
  25.4 6.5 %copy-start.2 = (bf16[1,3,256,256]{3,2,1,0:T(8,128)(2,1)S(1)}, bf16[1,3,256,256]{3,2,1,0:T(8,128)(2,1)}, u32[]{:S(2)}) copy-start(bf16[1,3,256,256]{3,2,1,0:T(8,128)(2,1)} %refs_1_.5) | copy-start | bytes 1179652
  25.4 8.8 %copy-start = (bf16[2,2,256,256]{3,2,1,0:T(8,128)(2,1)S(1)}, bf16[2,2,256,256]{3,2,1,0:T(8,128)(2,1)}, u32[]{:S(2)}) copy-start(bf16[2,2,256,256]{3,2,1,0:T(8,128)(2,1)} %constant.35.clone.refs_4_.refs_3_.refs_2_) | copy-start | bytes 1572868
  25.5 7.5 %collective-permute-start = (f32[2,64,256]{2,1,0:T(8,128)S(1)}, f32[2,64,256]{2,1,0:T(8,128)S(1)}, u32[]{:S(2)}, u32[]{:S(2)}) collective-permute-start(f32[2,64,256]{2,1,0:T(8,128)S(1)} %get-tuple-element.57), channel_id=1, source_target_pairs={{8,0},{16,8},{24,16},{32,24},{40,32},{48,40},{56,48},{64,56},{72,6... | collective-permute-start | bytes 393224 | tf_op jit(solution)/shard_map/ppermute | solution.py:398
  65.7 6.5 %collective-permute-start.1 = (f32[17,16,256]{2,1,0:T(8,128)S(1)}, f32[17,16,256]{2,1,0:T(8,128)S(1)}, u32[]{:S(2)}, u32[]{:S(2)}) collective-permute-start(f32[17,16,256]{2,1,0:T(8,128)S(1)} %get-tuple-element.63), channel_id=1, source_target_pairs={{0,8},{8,0},{1,9},{9,1},{2,10},{10,2},{3,11},{11,3},{4,12},{12,4},... | collective-permute-start | bytes 835592 | tf_op jit(solution)/shard_map/ppermute | solution.py:402
  72.2 10.5 %collective-permute-start.2 = (f32[17,8,256]{2,1,0:T(8,128)S(1)}, f32[17,8,256]{2,1,0:T(8,128)S(1)}, u32[]{:S(2)}, u32[]{:S(2)}) collective-permute-start(f32[17,8,256]{2,1,0:T(8,128)S(1)} %get-tuple-element.65), channel_id=1, source_target_pairs={{0,256},{256,0},{1,257},{257,1},{2,258},{258,2},{3,259},{259,3},{4... | collective-permute-start | bytes 417800 | tf_op jit(solution)/shard_map/ppermute | solution.py:402
  83.4 26.0 %all-to-all-start.3 = ((f32[16,3,8,128]{3,2,1,0:T(8,128)}), f32[16,3,8,128]{3,2,1,0:T(8,128)S(1)}, u32[]{:S(2)}, u32[]{:S(2)}) async-start(f32[16,3,8,128]{3,2,1,0:T(8,128)} %pack_kernel.3.refs_2_), calls=%async_computation.3 | async-start | bytes 393216 | tf_op jit(solution)/shard_map/all_to_all | solution.py:413
  100.4 6.1 %collective-permute-start.4 = (f32[2,32,256]{2,1,0:T(8,128)S(1)}, f32[2,32,256]{2,1,0:T(8,128)S(1)}, u32[]{:S(2)}, u32[]{:S(2)}) collective-permute-start(f32[2,32,256]{2,1,0:T(8,128)S(1)} %step_kernel.3.refs_2_), channel_id=1, source_target_pairs={{1,0},{2,1},{3,2},{7,3},{6,7},{5,6},{4,5},{9,8},{10,9},{11,10},{15... | collective-permute-start | bytes 196616 | tf_op jit(solution)/shard_map/ppermute | solution.py:408
  101.7 5.3 %collective-permute-start.3 = (f32[2,32,256]{2,1,0:T(8,128)S(1)}, f32[2,32,256]{2,1,0:T(8,128)S(1)}, u32[]{:S(2)}, u32[]{:S(2)}) collective-permute-start(f32[2,32,256]{2,1,0:T(8,128)S(1)} %step_kernel.3.refs_2_), channel_id=1, source_target_pairs={{0,1},{1,2},{2,3},{3,7},{7,6},{6,5},{5,4},{8,9},{9,10},{10,11},{11... | collective-permute-start | bytes 196616 | tf_op jit(solution)/shard_map/ppermute | solution.py:408
  110.1 22.5 %all-to-all-start.4 = ((f32[16,2,8,128]{3,2,1,0:T(8,128)}), f32[16,2,8,128]{3,2,1,0:T(8,128)S(1)}, u32[]{:S(2)}, u32[]{:S(2)}) async-start(f32[16,2,8,128]{3,2,1,0:T(8,128)} %get-tuple-element.69.refs_5_), calls=%async_computation.4 | async-start | bytes 262144 | tf_op jit(solution)/shard_map/all_to_all | solution.py:417
  118.5 9.7 %collective-permute-start.5 = (f32[2,64,256]{2,1,0:T(8,128)S(1)}, f32[2,64,256]{2,1,0:T(8,128)S(1)}, u32[]{:S(2)}, u32[]{:S(2)}) collective-permute-start(f32[2,64,256]{2,1,0:T(8,128)S(1)} %get-tuple-element.72), channel_id=1, source_target_pairs={{0,8},{8,16},{16,24},{24,32},{32,40},{40,48},{48,56},{56,64},{64,7... | collective-permute-start | bytes 393224 | tf_op jit(solution)/shard_map/ppermute | solution.py:398
  125.1 6.8 %collective-permute-start.6 = (f32[2,64,256]{2,1,0:T(8,128)S(1)}, f32[2,64,256]{2,1,0:T(8,128)S(1)}, u32[]{:S(2)}, u32[]{:S(2)}) collective-permute-start(f32[2,64,256]{2,1,0:T(8,128)S(1)} %get-tuple-element.73), channel_id=1, source_target_pairs={{8,0},{16,8},{24,16},{32,24},{40,32},{48,40},{56,48},{64,56},{72,6... | collective-permute-start | bytes 393224 | tf_op jit(solution)/shard_map/ppermute | solution.py:398
  170.7 5.5 %collective-permute-start.7 = (f32[17,16,256]{2,1,0:T(8,128)S(1)}, f32[17,16,256]{2,1,0:T(8,128)S(1)}, u32[]{:S(2)}, u32[]{:S(2)}) collective-permute-start(f32[17,16,256]{2,1,0:T(8,128)S(1)} %get-tuple-element.80), channel_id=1, source_target_pairs={{0,8},{8,0},{1,9},{9,1},{2,10},{10,2},{3,11},{11,3},{4,12},{12,4},... | collective-permute-start | bytes 835592 | tf_op jit(solution)/shard_map/ppermute | solution.py:402
  176.2 6.8 %collective-permute-start.8 = (f32[17,8,256]{2,1,0:T(8,128)S(1)}, f32[17,8,256]{2,1,0:T(8,128)S(1)}, u32[]{:S(2)}, u32[]{:S(2)}) collective-permute-start(f32[17,8,256]{2,1,0:T(8,128)S(1)} %get-tuple-element.82), channel_id=1, source_target_pairs={{0,256},{256,0},{1,257},{257,1},{2,258},{258,2},{3,259},{259,3},{4... | collective-permute-start | bytes 417800 | tf_op jit(solution)/shard_map/ppermute | solution.py:402
  183.7 20.9 %all-to-all-start.7 = ((f32[16,3,8,128]{3,2,1,0:T(8,128)}), f32[16,3,8,128]{3,2,1,0:T(8,128)S(1)}, u32[]{:S(2)}, u32[]{:S(2)}) async-start(f32[16,3,8,128]{3,2,1,0:T(8,128)} %pack_kernel.4.refs_2_), calls=%async_computation.7 | async-start | bytes 393216 | tf_op jit(solution)/shard_map/all_to_all | solution.py:413
  195.6 6.1 %collective-permute-start.10 = (f32[2,32,256]{2,1,0:T(8,128)S(1)}, f32[2,32,256]{2,1,0:T(8,128)S(1)}, u32[]{:S(2)}, u32[]{:S(2)}) collective-permute-start(f32[2,32,256]{2,1,0:T(8,128)S(1)} %step_kernel.4.refs_2_), channel_id=1, source_target_pairs={{1,0},{2,1},{3,2},{7,3},{6,7},{5,6},{4,5},{9,8},{10,9},{11,10},{15... | collective-permute-start | bytes 196616 | tf_op jit(solution)/shard_map/ppermute | solution.py:408
  196.9 5.3 %collective-permute-start.9 = (f32[2,32,256]{2,1,0:T(8,128)S(1)}, f32[2,32,256]{2,1,0:T(8,128)S(1)}, u32[]{:S(2)}, u32[]{:S(2)}) collective-permute-start(f32[2,32,256]{2,1,0:T(8,128)S(1)} %step_kernel.4.refs_2_), channel_id=1, source_target_pairs={{0,1},{1,2},{2,3},{3,7},{7,6},{6,5},{5,4},{8,9},{9,10},{10,11},{11... | collective-permute-start | bytes 196616 | tf_op jit(solution)/shard_map/ppermute | solution.py:408
  205.3 22.5 %all-to-all-start.8 = ((f32[16,2,8,128]{3,2,1,0:T(8,128)}), f32[16,2,8,128]{3,2,1,0:T(8,128)S(1)}, u32[]{:S(2)}, u32[]{:S(2)}) async-start(f32[16,2,8,128]{3,2,1,0:T(8,128)} %get-tuple-element.87.refs_5_), calls=%async_computation.8 | async-start | bytes 262144 | tf_op jit(solution)/shard_map/all_to_all | solution.py:417
  213.6 9.7 %collective-permute-start.11 = (f32[2,64,256]{2,1,0:T(8,128)S(1)}, f32[2,64,256]{2,1,0:T(8,128)S(1)}, u32[]{:S(2)}, u32[]{:S(2)}) collective-permute-start(f32[2,64,256]{2,1,0:T(8,128)S(1)} %get-tuple-element.90), channel_id=1, source_target_pairs={{0,8},{8,16},{16,24},{24,32},{32,40},{40,48},{48,56},{56,64},{64,7... | collective-permute-start | bytes 393224 | tf_op jit(solution)/shard_map/ppermute | solution.py:398
  220.3 6.8 %collective-permute-start.12 = (f32[2,64,256]{2,1,0:T(8,128)S(1)}, f32[2,64,256]{2,1,0:T(8,128)S(1)}, u32[]{:S(2)}, u32[]{:S(2)}) collective-permute-start(f32[2,64,256]{2,1,0:T(8,128)S(1)} %get-tuple-element.91), channel_id=1, source_target_pairs={{8,0},{16,8},{24,16},{32,24},{40,32},{48,40},{56,48},{64,56},{72,6... | collective-permute-start | bytes 393224 | tf_op jit(solution)/shard_map/ppermute | solution.py:398
  267.0 5.5 %collective-permute-start.13 = (f32[17,16,256]{2,1,0:T(8,128)S(1)}, f32[17,16,256]{2,1,0:T(8,128)S(1)}, u32[]{:S(2)}, u32[]{:S(2)}) collective-permute-start(f32[17,16,256]{2,1,0:T(8,128)S(1)} %get-tuple-element.100), channel_id=1, source_target_pairs={{0,8},{8,0},{1,9},{9,1},{2,10},{10,2},{3,11},{11,3},{4,12},{12,4},... | collective-permute-start | bytes 835592 | tf_op jit(solution)/shard_map/ppermute | solution.py:402
  272.6 8.8 %collective-permute-start.16 = (f32[17,8,256]{2,1,0:T(8,128)S(1)}, f32[17,8,256]{2,1,0:T(8,128)S(1)}, u32[]{:S(2)}, u32[]{:S(2)}) collective-permute-start(f32[17,8,256]{2,1,0:T(8,128)S(1)} %get-tuple-element.103), channel_id=1, source_target_pairs={{0,256},{256,0},{1,257},{257,1},{2,258},{258,2},{3,259},{259,3},{4... | collective-permute-start | bytes 417800 | tf_op jit(solution)/shard_map/ppermute | solution.py:402
  274.8 5.3 %collective-permute-start.15 = (f32[2,32,256]{2,1,0:T(8,128)S(1)}, f32[2,32,256]{2,1,0:T(8,128)S(1)}, u32[]{:S(2)}, u32[]{:S(2)}) collective-permute-start(f32[2,32,256]{2,1,0:T(8,128)S(1)} %step_kernel.5.refs_2_), channel_id=1, source_target_pairs={{1,0},{2,1},{3,2},{7,3},{6,7},{5,6},{4,5},{9,8},{10,9},{11,10},{15... | collective-permute-start | bytes 196616 | tf_op jit(solution)/shard_map/ppermute | solution.py:408
  276.1 5.3 %collective-permute-start.14 = (f32[2,32,256]{2,1,0:T(8,128)S(1)}, f32[2,32,256]{2,1,0:T(8,128)S(1)}, u32[]{:S(2)}, u32[]{:S(2)}) collective-permute-start(f32[2,32,256]{2,1,0:T(8,128)S(1)} %step_kernel.5.refs_2_), channel_id=1, source_target_pairs={{0,1},{1,2},{2,3},{3,7},{7,6},{6,5},{5,4},{8,9},{9,10},{10,11},{11... | collective-permute-start | bytes 196616 | tf_op jit(solution)/shard_map/ppermute | solution.py:408
  282.1 23.2 %all-to-all-start.11 = ((f32[16,3,8,128]{3,2,1,0:T(8,128)}), f32[16,3,8,128]{3,2,1,0:T(8,128)S(1)}, u32[]{:S(2)}, u32[]{:S(2)}) async-start(f32[16,3,8,128]{3,2,1,0:T(8,128)} %pack_kernel.5.refs_5_), calls=%async_computation.11 | async-start | bytes 393216 | tf_op jit(solution)/shard_map/all_to_all | solution.py:413
  295.6 9.2 %collective-permute-start.17 = (f32[2,64,256]{2,1,0:T(8,128)S(1)}, f32[2,64,256]{2,1,0:T(8,128)S(1)}, u32[]{:S(2)}, u32[]{:S(2)}) collective-permute-start(f32[2,64,256]{2,1,0:T(8,128)S(1)} %get-tuple-element.105), channel_id=1, source_target_pairs={{0,8},{8,16},{16,24},{24,32},{32,40},{40,48},{48,56},{56,64},{64,7... | collective-permute-start | bytes 393224 | tf_op jit(solution)/shard_map/ppermute | solution.py:398
  306.0 16.6 %all-to-all-start.12 = ((f32[16,2,8,128]{3,2,1,0:T(8,128)}), f32[16,2,8,128]{3,2,1,0:T(8,128)S(1)}, u32[]{:S(2)}, u32[]{:S(2)}) async-start(f32[16,2,8,128]{3,2,1,0:T(8,128)} %get-tuple-element.107), calls=%async_computation.12 | async-start | bytes 262144 | tf_op jit(solution)/shard_map/all_to_all | solution.py:417
  310.6 7.6 %collective-permute-start.18 = (f32[2,40,512]{2,1,0:T(8,128)S(1)}, f32[2,40,512]{2,1,0:T(8,128)S(1)}, u32[]{:S(2)}, u32[]{:S(2)}) collective-permute-start(f32[2,40,512]{2,1,0:T(8,128)S(1)} %out_rows_kernel.1.refs_2_.refs_0_), channel_id=1, source_target_pairs={{0,4},{4,0},{1,5},{5,1},{2,6},{6,2},{3,7},{7,3},{8,12},{12,8},{9,1... | collective-permute-start | bytes 491528 | tf_op jit(solution)/shard_map/ppermute | solution.py:402
  322.6 37.4 %collective-permute-start.21 = (f32[2,2,40,512]{3,2,1,0:T(8,128)S(1)}, f32[2,2,40,512]{3,2,1,0:T(8,128)S(1)}, u32[]{:S(2)}, u32[]{:S(2)}) collective-permute-start(f32[2,2,40,512]{3,2,1,0:T(8,128)S(1)} %pair_kernel.1.refs_1_), channel_id=1, source_target_pairs={{0,2},{1,3},{2,0},{3,1},{4,6},{5,7},{6,4},{7,5},{8,10},{9,11},{10,... | collective-permute-start | bytes 983048 | tf_op jit(solution)/shard_map/ppermute | solution.py:425
  326.1 33.9 %collective-permute-start.20 = (f32[2,2,40,512]{3,2,1,0:T(8,128)S(1)}, f32[2,2,40,512]{3,2,1,0:T(8,128)S(1)}, u32[]{:S(2)}, u32[]{:S(2)}) collective-permute-start(f32[2,2,40,512]{3,2,1,0:T(8,128)S(1)} %pair_kernel.1.refs_1_), channel_id=1, source_target_pairs={{0,3},{1,0},{2,1},{3,2},{4,7},{5,4},{6,5},{7,6},{8,11},{9,8},{10,9... | collective-permute-start | bytes 983048 | tf_op jit(solution)/shard_map/ppermute | solution.py:425
  329.8 30.2 %collective-permute-start.19 = (f32[2,2,40,512]{3,2,1,0:T(8,128)S(1)}, f32[2,2,40,512]{3,2,1,0:T(8,128)S(1)}, u32[]{:S(2)}, u32[]{:S(2)}) collective-permute-start(f32[2,2,40,512]{3,2,1,0:T(8,128)S(1)} %pair_kernel.1.refs_1_), channel_id=1, source_target_pairs={{0,1},{1,2},{2,3},{3,0},{4,5},{5,6},{6,7},{7,4},{8,9},{9,10},{10,1... | collective-permute-start | bytes 983048 | tf_op jit(solution)/shard_map/ppermute | solution.py:425

commit v6 on v5

--- a/solution.py
+++ b/solution.py
@@ -146,29 +146,10 @@
             spectra[place, part] = block
 
 
-def split_kernel(probe_in, pieces, sems):
-    copies = []
+def split_kernel(probe_in, pieces):
     for place in range(MODES):
-        rows = pl.ds(slab_of(place) * SLAB, SLAB)
-        copies.append(
-            pltpu.make_async_copy(probe_in.at[0, :, rows, :], pieces.at[place], sems.at[place])
-        )
-    for copy in copies:
-        copy.start()
-    for copy in copies:
-        copy.wait()
-
-
-def split_probe(probe_modes):
-    anywhere = pl.BlockSpec(memory_space=pl.ANY)
-    return pl.pallas_call(
-        split_kernel,
-        out_shape=jax.ShapeDtypeStruct((MODES, 2, SLAB, SIDE), F32),
-        in_specs=[anywhere],
-        out_specs=anywhere,
-        scratch_shapes=[pltpu.SemaphoreType.DMA((MODES,))],
-        name="split_kernel",
-    )(probe_modes)
+        row = slab_of(place) * SLAB
+        pieces[place] = probe_in[0, :, row : row + SLAB, :]
 
 
 def first_kernel(scal, own, beside, probe, tables, band, view, shard, spectra):
@@ -189,13 +170,19 @@
     forward(view, probe, tables, spectra)
 
 
+def far_place(ring):
+    return (ring + RINGS // 2) % RINGS
+
+
 def next_kernel(view, pieces, tables, probe, spectra):
     for xlo in range(2):
         for core in range(2):
             row = core * 16 + xlo * 8
             for mode in range(MODES):
-                probe[mode, :, row : row + 8, :LANES] = pieces[xlo, core, 2 * mode]
-                probe[mode, :, row : row + 8, LANES:] = pieces[xlo, core, 2 * mode + 1]
+                for half in range(2):
+                    lanes = slice(half * LANES, (half + 1) * LANES)
+                    piece = pieces[xlo, core, 2 * mode + half]
+                    probe[mode, :, row : row + 8, lanes] = piece
     forward(view, probe, tables, spectra)
 
 
@@ -261,7 +248,7 @@
         lanes = slice(half * LANES, (half + 1) * LANES)
         total = mine[:, :, lanes] + theirs[:, :, lanes]
         for mode in range(MODES):
-            place = (2 * mode + half + RINGS // 2) % RINGS
+            place = far_place(2 * mode + half)
             packed[place, 0] = total[2 * mode]
             packed[place, 1] = total[2 * mode + 1]
             packed[place, 2] = total[2 * MODES]
@@ -318,29 +305,43 @@
     rows_out[:, :, SIDE:] = part_band[:, rows, SIDE:WIDTH]
 
 
-def pair_kernel(mine, theirs, pair):
-    pair[0] = mine[...]
-    pair[1] = theirs[...]
-
-
-def object_kernel(scal, own, plus, minus, across, object_out):
-    xhi, y = scal[MODE] // 4, lax.rem(scal[MODE], 4)
-    for source, steps in ((own, 0), (plus, 3), (minus, 1), (across, 2)):
-        for beyond in range(2):
-            half = xhi if beyond == 0 else 1 - xhi
-            column = lax.rem(y + steps, 4)
-            slab = jnp.where(half == 0, column, 7 - column)
-            rows = pl.ds(pl.multiple_of(slab * 9 // 2 * 8, 8), OUT_ROWS)
-            object_out[:, rows, :] = source[beyond]
+def tail_kernel(piece, rows_out, tail):
+    for place in range(MODES):
+        for half in range(2):
+            for part in range(2):
+                row = (half * 2 + part) * 8
+                tail[place, row : row + 8] = piece[2 * place + half, part]
+        for part in range(2):
+            for block in range(WIDTH // LANES):
+                row = 32 + (part * 4 + block) * OUT_ROWS
+                lanes = slice(block * LANES, (block + 1) * LANES)
+                tail[place, row : row + OUT_ROWS] = rows_out[part, :, lanes]
+
+
+def object_kernel(tail, object_out):
+    for place in range(MODES):
+        first = slab_of(place) * 9 // 2 * 8
+        for part in range(2):
+            for block in range(WIDTH // LANES):
+                row = 32 + (part * 4 + block) * OUT_ROWS
+                lanes = slice(block * LANES, (block + 1) * LANES)
+                object_out[part, first : first + OUT_ROWS, lanes] = tail[
+                    place, row : row + OUT_ROWS
+                ]
 
 
 def probe_out_kernel(pieces, probe_out):
     for xlo in range(2):
         for core in range(2):
             for place in range(MODES):
-                row = slab_of(place) * SLAB + core * 16 + xlo * 8
-                probe_out[0, :, row : row + 8, :LANES] = pieces[xlo, core, 2 * place]
-                probe_out[0, :, row : row + 8, LANES:] = pieces[xlo, core, 2 * place + 1]
+                first = slab_of(place) * SLAB + core * 16 + xlo * 8
+                for half in range(2):
+                    lanes = slice(half * LANES, (half + 1) * LANES)
+                    for part in range(2):
+                        row = (half * 2 + part) * 8
+                        probe_out[0, part, first : first + 8, lanes] = pieces[
+                            xlo, core, place, row : row + 8
+                        ]
 
 
 def own_kernel(place, whole, own, left, sems):
@@ -377,11 +378,12 @@
 def call(kernel, outs, *args, scalars=True, after=()):
     vmem = pl.BlockSpec(memory_space=pltpu.VMEM)
     in_specs = [vmem] * len(args) + [pl.BlockSpec(memory_space=pl.ANY)] * len(after)
-    if scalars:
-        in_specs[0] = pl.BlockSpec(memory_space=pltpu.SMEM)
 
     def body(*refs):
-        kernel(*refs[: len(args)], *refs[len(args) + len(after) :])
+        taken = list(refs[: len(args)])
+        if scalars:
+            taken[0] = [taken[0][0, index] for index in range(BAND_ID + 1)]
+        kernel(*taken, *refs[len(args) + len(after) :])
 
     return pl.pallas_call(
         body,
@@ -408,9 +410,9 @@
     return lax.ppermute(value, MODE_AXES, pairs)
 
 
-def exchange_far_first(value):
-    order = [(i + RINGS // 2) % RINGS for i in range(RINGS)]
-    return lax.all_to_all(value, "z", 0, 0, tiled=True, axis_index_groups=[order])
+def exchange_rings(value):
+    groups = [[far_place(ring) for ring in range(RINGS)]]
+    return lax.all_to_all(value, "z", 0, 0, tiled=True, axis_index_groups=groups)
 
 
 def exchange(value, axes):
@@ -418,11 +420,8 @@
 
 
 def gather_pieces(piece):
-    return lax.all_gather(piece, ("xlo", "core")).reshape(2, 2, RINGS, 2, 8, LANES)
-
-
-def around(value, steps):
-    return lax.ppermute(value, "y", [(i, (i + steps) % 4) for i in range(4)])
+    gathered = lax.all_gather(piece, ("xlo", "core"))
+    return gathered.reshape((2, 2) + piece.shape)
 
 
 def per_device(
@@ -433,7 +432,7 @@
     tile = lax.axis_index(TILE_AXES)
     mode = lax.axis_index(MODE_AXES)
     slab = jnp.where(mode < MODES // 2, mode, 11 - mode)
-    pieces = split_probe(probe_modes)
+    (pieces,) = call(split_kernel, [(MODES, 2, SLAB, SIDE)], probe_modes, scalars=False)
     probe = exchange(pieces, MODE_AXES)
     own, left = take_own(slab, object_tiles, pieces)
     beside = shift(left, TILE_AXES, TILES, -1)
@@ -460,9 +459,9 @@
     band_shape = (2, BAND, WIDE)
     edge = (2, BAND, SIDE)
     counts_shapes = [(SIDE, LANES), (3, 8, SIDE)]
-    counts, flags = call(counts_kernel, counts_shapes, scalars[0], measured)
+    counts, flags = call(counts_kernel, counts_shapes, scalars[:1], measured)
     for step in range(STEPS):
-        scal = scalars[step]
+        scal = scalars[step : step + 1]
         final = step == STEPS - 1
         if step == 0:
             band, view, shard, spectra = call(
@@ -515,69 +514,58 @@
             keep,
             received,
             scalars=False,
-            after=(above, below) if final else (object_step,),
-        )
-        sums = exchange_far_first(packed)
-        if not final:
-            counts, flags = call(
-                counts_kernel, counts_shapes, scalars[step + 1], measured, after=(packed,)
-            )
-        placing = [scal, above, object_step, below, band]
+            after=(above, below),
+        )
+        sums = exchange_rings(packed)
+        part_band, to_left, to_right = call(
+            place_kernel,
+            [band_shape, edge, edge],
+            scal,
+            above,
+            object_step,
+            below,
+            band,
+            after=(packed,),
+        )
+        from_left = shift(to_right, TILE_AXES, TILES, 1)
         if final:
-            part_band, _, to_right = call(
-                place_kernel, [band_shape, edge, edge], *placing, after=(packed,)
-            )
-            from_left = shift(to_right, TILE_AXES, TILES, 1)
             (rows_out,) = call(
                 out_rows_kernel, [(2, OUT_ROWS, WIDTH)], scal, part_band, from_left
             )
-            far_rows = other(rows_out, "xhi")
+            before = (rows_out,)
+        else:
+            from_right = shift(to_left, TILE_AXES, TILES, -1)
+            next_scal = scalars[step + 1 : step + 2]
+            counts, flags = call(
+                counts_kernel, counts_shapes, next_scal, measured, after=(packed,)
+            )
+            band, view = call(
+                view_kernel,
+                [band_shape, slab_pair],
+                next_scal,
+                part_band,
+                from_left,
+                from_right,
+            )
+            before = (view, counts)
         shard, shards = call(
             probe_kernel,
             [(2, 8, LANES), (RINGS, 2, 8, LANES)],
             sums,
             shard,
             scalars=False,
-            after=(rows_out,) if final else (above, below, counts),
+            after=before,
         )
         piece = exchange(shards, "z")
-        if final:
-            piece, far_rows = lax.optimization_barrier((piece, far_rows))
-        else:
-            part_band, to_left, to_right = call(
-                place_kernel, [band_shape, edge, edge], *placing, after=(shards,)
-            )
-            from_left = shift(to_right, TILE_AXES, TILES, 1)
-            from_right = shift(to_left, TILE_AXES, TILES, -1)
-            band, view = call(
-                view_kernel,
-                [band_shape, slab_pair],
-                scalars[step + 1],
-                part_band,
-                from_left,
-                from_right,
-            )
-            piece, view = lax.optimization_barrier((piece, view))
+        if not final:
             pieces = gather_pieces(piece)
-    (pair,) = call(
-        pair_kernel,
-        [(2, 2, OUT_ROWS, WIDTH)],
-        rows_out,
-        far_rows,
-        scalars=False,
-        after=(piece,),
-    )
-    (object_out,) = call(
-        object_kernel,
-        [(2, HEIGHT, WIDTH)],
-        scal,
-        pair,
-        around(pair, 1),
-        around(pair, -1),
-        around(pair, 2),
-    )
-    piece = exchange(piece.reshape(MODES, 4, 8, LANES), MODE_AXES)
-    pieces = gather_pieces(piece.reshape(RINGS, 2, 8, LANES))
+    tail_rows = 32 + 8 * OUT_ROWS
+    (tail,) = call(
+        tail_kernel, [(MODES, tail_rows, LANES)], piece, rows_out, scalars=False
+    )
+    tail = exchange(tail, MODE_AXES)
+    pieces = gather_pieces(tail[:, :32])
+    (object_out,) = call(object_kernel, [(2, HEIGHT, WIDTH)], tail, scalars=False)
     (probe_out,) = call(probe_out_kernel, [(1, 2, SIDE, SIDE)], pieces, scalars=False)
     return object_out, probe_out
 

time: 363 us -> 356 us (0.981)
  blocking collectives: 125 us -> 199 us
  starting transfers between devices: 148 us -> 108 us
  Pallas kernels: 42.5 us -> 19.9 us
  waiting for transfers between devices: 43.6 us -> 23.7 us
    all_to_all x7 -> x10, blocking collectives: 92.9 us -> 162 us  [exchange(): return lax.all_to_all(value, axes, 0, 0, tiled=True)]
    all_to_all x4 -> x1, starting transfers between devices: 27.4 us -> 7.62 us  [exchange(): return lax.all_to_all(value, axes, 0, 0, tiled=True)]
    pallas_call x1 -> x0, Pallas kernels: 17.1 us -> none  [split_probe(): pl.pallas_call(split_kernel, out_shape=jax.ShapeDtypeStruct((MODES, 2, SL...]
    ppermute x7 -> x6, waiting for transfers between devices: 15.8 us -> 3.5 us  [other(): return lax.ppermute(value, axis, [(0, 1), (1, 0)])]
    ppermute x3 -> x0, starting transfers between devices: 9.08 us -> none  [around(): return lax.ppermute(value, 'y', [(i, (i + steps) % 4) for i in range(4)])]
    pallas_call x33 -> x34, Pallas kernels: 25.4 us -> 19.8 us  [call(): pl.pallas_call(body, out_shape=[jax.ShapeDtypeStruct(shape, F32) for shap...]
    all_gather x3, blocking collectives: 32.4 us -> 37.3 us  [gather_pieces(): gathered = lax.all_gather(piece, ('xlo', 'core'))]
    all_to_all x3, waiting for transfers between devices: 4.81 us -> 0.01 us  [exchange_rings(): lax.all_to_all(value, 'z', 0, 0, tiled=True, axis_index_groups=groups)]
  transfers between devices with their start and end apart: 29 -> 22, of which waited for: 19 -> 13; matrix products, arithmetic and copies ran while one was open for 0% -> 0% of each run, Pallas kernels for 2% -> 1%
where the time goes in v6:
time: 356 us; the launch traced here: 355 us
  blocking collectives  199 us (56%)
  starting transfers between devices  108 us (30%)
  waiting for transfers between devices  23.7 us (7%)
  Pallas kernels  19.9 us (6%)
    all_to_all x10, blocking collectives, exchange(): return lax.all_to_all(value, axes, 0, 0, tiled=True)  162 us
    all_to_all x3, starting transfers between devices, exchange_rings(): lax.all_to_all(value, 'z', 0, 0, tiled=True, axis_index_groups=groups)  38.8 us
    all_gather x3, blocking collectives, gather_pieces(): gathered = lax.all_gather(piece, ('xlo', 'core'))  37.3 us
    ppermute x6, starting transfers between devices, other(): return lax.ppermute(value, axis, [(0, 1), (1, 0)])  24.6 us
    ppermute x6, starting transfers between devices, shift(): lax.ppermute(value, axes, [(i, i + steps) for i in range(first, last)])  21.6 us
    pallas_call x34, Pallas kernels, call(): pl.pallas_call(body, out_shape=[jax.ShapeDtypeStruct(shape, F32) for shap...  19.8 us
    ppermute x6, starting transfers between devices, beside_slab(): return lax.ppermute(value, MODE_AXES, pairs)  15.8 us
    ppermute x6, waiting for transfers between devices, shift(): lax.ppermute(value, axes, [(i, i + steps) for i in range(first, last)])  14.9 us
  transfers between devices with their start and end apart: 22, of which 13 were waited for; matrix products, arithmetic and copies ran while one was open for 0% of the time, Pallas kernels for 1%

profile of v6, /device:TPU:1, one launch (start us, length us, event | category | flops | bytes accessed | tf_op | source)
XLA Modules:
  0.0 355.0 jit_solution(6520978799819958909)
XLA Ops:
  0.6 1.1 copy-done.3
  1.8 0.8 split_kernel.1._
  2.6 7.6 %all-to-all-start = ((f32[8,2,32,256]{3,2,1,0:T(8,128)}), f32[8,2,32,256]{3,2,1,0:T(8,128)S(1)}, u32[]{:S(2)}, u32[]{:S(2)}) async-start(f32[8,2,32,256]{3,2,1,0:T(8,128)} %split_kernel.1._), calls=%async_computation | async-start | bytes 1048576 | tf_op jit(solution)/shard_map/all_to_all | solution.py:419
  10.3 4.8 %collective-permute-start = (f32[2,64,256]{2,1,0:T(8,128)S(1)}, f32[2,64,256]{2,1,0:T(8,128)S(1)}, u32[]{:S(2)}, u32[]{:S(2)}) collective-permute-start(f32[2,64,256]{2,1,0:T(8,128)S(1)} %get-tuple-element.51), channel_id=1, source_target_pairs={{8,0},{16,8},{24,16},{32,24},{40,32},{48,40},{56,48},{64,56},{72,6... | collective-permute-start | bytes 393224 | tf_op jit(solution)/shard_map/ppermute | solution.py:400
  16.9 0.8 collective-permute-done.refs_2_
  17.7 1.4 all-to-all-done.refs_3_.refs_1_
  19.1 1.1 first_kernel.1
  20.2 14.8 %all_to_all.70.refs_0_ = f32[8,2,32,256]{3,2,1,0:T(8,128)S(1)} all-to-all(f32[8,2,32,256]{3,2,1,0:T(8,128)S(1)} %get-tuple-element.53), channel_id=1, replica_groups=mesh['xlo'=2,'z'=16,'core'=2,'xhi'=2,'y'=4] {'xhi','y'}, dimensions={0} | all-to-all | bytes 1048576 | tf_op jit(solution)/shard_map/all_to_all | solution.py:419
  35.0 1.7 ratio_kernel.3
  36.7 12.4 %all_to_all.71.refs_0_ = f32[8,2,32,256]{3,2,1,0:T(8,128)S(1)} all-to-all(f32[8,2,32,256]{3,2,1,0:T(8,128)S(1)} %ratio_kernel.3), channel_id=1, replica_groups=mesh['xlo'=2,'z'=16,'core'=2,'xhi'=2,'y'=4] {'xhi','y'}, dimensions={0} | all-to-all | bytes 1048576 | tf_op jit(solution)/shard_map/all_to_all | solution.py:419
  49.1 0.8 backward_kernel.3
  50.0 5.3 %collective-permute-start.1 = (f32[17,16,256]{2,1,0:T(8,128)S(1)}, f32[17,16,256]{2,1,0:T(8,128)S(1)}, u32[]{:S(2)}, u32[]{:S(2)}) collective-permute-start(f32[17,16,256]{2,1,0:T(8,128)S(1)} %get-tuple-element.58), channel_id=1, source_target_pairs={{0,8},{8,0},{1,9},{9,1},{2,10},{10,2},{3,11},{11,3},{4,12},{12,4},... | collective-permute-start | bytes 835592 | tf_op jit(solution)/shard_map/ppermute | solution.py:404
  55.3 1.2 collective-permute-done.1.refs_1_
  56.5 6.7 %collective-permute-start.4 = (f32[17,8,256]{2,1,0:T(8,128)S(1)}, f32[17,8,256]{2,1,0:T(8,128)S(1)}, u32[]{:S(2)}, u32[]{:S(2)}) collective-permute-start(f32[17,8,256]{2,1,0:T(8,128)S(1)} %get-tuple-element.61), channel_id=1, source_target_pairs={{0,256},{256,0},{1,257},{257,1},{2,258},{258,2},{3,259},{259,3},{4... | collective-permute-start | bytes 417800 | tf_op jit(solution)/shard_map/ppermute | solution.py:404
  63.4 1.3 collective-permute-start.3
  64.7 4.0 %collective-permute-start.2 = (f32[2,32,256]{2,1,0:T(8,128)S(1)}, f32[2,32,256]{2,1,0:T(8,128)S(1)}, u32[]{:S(2)}, u32[]{:S(2)}) collective-permute-start(f32[2,32,256]{2,1,0:T(8,128)S(1)} %step_kernel.3.refs_2_), channel_id=1, source_target_pairs={{0,1},{1,2},{2,3},{3,7},{7,6},{6,5},{5,4},{8,9},{9,10},{10,11},{11... | collective-permute-start | bytes 196616 | tf_op jit(solution)/shard_map/ppermute | solution.py:410
  68.7 1.3 collective-permute-done.2.refs_2_.refs_1_
  70.0 0.7 pack_kernel.3.refs_5_.refs_2_
  70.7 15.9 %all-to-all-start.3 = ((f32[16,3,8,128]{3,2,1,0:T(8,128)}), f32[16,3,8,128]{3,2,1,0:T(8,128)S(1)}, u32[]{:S(2)}, u32[]{:S(2)}) async-start(f32[16,3,8,128]{3,2,1,0:T(8,128)} %pack_kernel.3.refs_5_.refs_2_), calls=%async_computation.3 | async-start | bytes 393216 | tf_op jit(solution)/shard_map/all_to_all | solution.py:415
  86.9 4.1 %collective-permute-start.5 = (f32[2,64,256]{2,1,0:T(8,128)S(1)}, f32[2,64,256]{2,1,0:T(8,128)S(1)}, u32[]{:S(2)}, u32[]{:S(2)}) collective-permute-start(f32[2,64,256]{2,1,0:T(8,128)S(1)} %get-tuple-element.63), channel_id=1, source_target_pairs={{0,8},{8,16},{16,24},{24,32},{32,40},{40,48},{48,56},{56,64},{64,7... | collective-permute-start | bytes 393224 | tf_op jit(solution)/shard_map/ppermute | solution.py:400
  91.0 1.9 collective-permute-start.6
  93.3 3.8 %collective-permute-done.5.refs_2_ = f32[2,64,256]{2,1,0:T(8,128)S(1)} collective-permute-done((f32[2,64,256]{2,1,0:T(8,128)S(1)}, f32[2,64,256]{2,1,0:T(8,128)S(1)}, u32[]{:S(2)}, u32[]{:S(2)}) %collective-permute-start.5) | collective-permute-done | bytes 131104 | tf_op jit(solution)/shard_map/ppermute | solution.py:400
  97.1 0.7 collective-permute-done.6.refs_3_
  98.2 18.6 %all_to_all.72 = f32[16,2,8,128]{3,2,1,0:T(8,128)S(1)} all-to-all(f32[16,2,8,128]{3,2,1,0:T(8,128)S(1)} %get-tuple-element.68), channel_id=1, replica_groups=mesh['xlo'=2,'z'=16,'core'=2,'xhi'=2,'y'=4] {'z'}, dimensions={0} | all-to-all | bytes 262144 | tf_op jit(solution)/shard_map/all_to_all | solution.py:419
  116.7 10.8 %all-gather = f32[64,2,8,128]{3,2,1,0:T(8,128)S(1)} all-gather(f32[16,2,8,128]{3,2,1,0:T(8,128)S(1)} %all_to_all.72), channel_id=2, replica_groups=mesh['xlo'=2,'z'=16,'core'=2,'xhi'=2,'y'=4] {'xlo','core'}, dimensions={0}, use_global_device_ids=true | all-gather | bytes 655360 | tf_op jit(solution)/shard_map/all_gather | solution.py:423
  127.5 0.9 next_kernel.2
  128.4 16.9 %all_to_all.73.refs_0_ = f32[8,2,32,256]{3,2,1,0:T(8,128)S(1)} all-to-all(f32[8,2,32,256]{3,2,1,0:T(8,128)S(1)} %get-tuple-element.69), channel_id=1, replica_groups=mesh['xlo'=2,'z'=16,'core'=2,'xhi'=2,'y'=4] {'xhi','y'}, dimensions={0} | all-to-all | bytes 1048576 | tf_op jit(solution)/shard_map/all_to_all | solution.py:419
  145.3 1.7 ratio_kernel.4
  147.0 14.0 %all_to_all.74.refs_0_ = f32[8,2,32,256]{3,2,1,0:T(8,128)S(1)} all-to-all(f32[8,2,32,256]{3,2,1,0:T(8,128)S(1)} %ratio_kernel.4), channel_id=1, replica_groups=mesh['xlo'=2,'z'=16,'core'=2,'xhi'=2,'y'=4] {'xhi','y'}, dimensions={0} | all-to-all | bytes 1048576 | tf_op jit(solution)/shard_map/all_to_all | solution.py:419
  160.9 0.8 backward_kernel.4
  161.8 4.4 %collective-permute-start.7 = (f32[17,16,256]{2,1,0:T(8,128)S(1)}, f32[17,16,256]{2,1,0:T(8,128)S(1)}, u32[]{:S(2)}, u32[]{:S(2)}) collective-permute-start(f32[17,16,256]{2,1,0:T(8,128)S(1)} %get-tuple-element.74), channel_id=1, source_target_pairs={{0,8},{8,0},{1,9},{9,1},{2,10},{10,2},{3,11},{11,3},{4,12},{12,4},... | collective-permute-start | bytes 835592 | tf_op jit(solution)/shard_map/ppermute | solution.py:404
  166.1 1.2 collective-permute-done.7.refs_1_
  167.3 1.9 collective-permute-start.10
  169.4 1.3 collective-permute-start.9
  170.7 4.0 %collective-permute-start.8 = (f32[2,32,256]{2,1,0:T(8,128)S(1)}, f32[2,32,256]{2,1,0:T(8,128)S(1)}, u32[]{:S(2)}, u32[]{:S(2)}) collective-permute-start(f32[2,32,256]{2,1,0:T(8,128)S(1)} %step_kernel.4.refs_2_), channel_id=1, source_target_pairs={{0,1},{1,2},{2,3},{3,7},{7,6},{6,5},{5,4},{8,9},{9,10},{10,11},{11... | collective-permute-start | bytes 196616 | tf_op jit(solution)/shard_map/ppermute | solution.py:410
  174.7 1.3 collective-permute-done.8.refs_2_.refs_1_
  176.0 0.7 pack_kernel.4.refs_5_.refs_2_
  176.7 11.5 %all-to-all-start.7 = ((f32[16,3,8,128]{3,2,1,0:T(8,128)}), f32[16,3,8,128]{3,2,1,0:T(8,128)S(1)}, u32[]{:S(2)}, u32[]{:S(2)}) async-start(f32[16,3,8,128]{3,2,1,0:T(8,128)} %pack_kernel.4.refs_5_.refs_2_), calls=%async_computation.7 | async-start | bytes 393216 | tf_op jit(solution)/shard_map/all_to_all | solution.py:415
  188.5 4.4 %collective-permute-start.11 = (f32[2,64,256]{2,1,0:T(8,128)S(1)}, f32[2,64,256]{2,1,0:T(8,128)S(1)}, u32[]{:S(2)}, u32[]{:S(2)}) collective-permute-start(f32[2,64,256]{2,1,0:T(8,128)S(1)} %get-tuple-element.79), channel_id=1, source_target_pairs={{0,8},{8,16},{16,24},{24,32},{32,40},{40,48},{48,56},{56,64},{64,7... | collective-permute-start | bytes 393224 | tf_op jit(solution)/shard_map/ppermute | solution.py:400
  192.9 1.9 collective-permute-start.12
  195.2 3.5 collective-permute-done.11.refs_2_
  198.8 0.7 collective-permute-done.12.refs_3_
  199.8 18.6 %all_to_all.75 = f32[16,2,8,128]{3,2,1,0:T(8,128)S(1)} all-to-all(f32[16,2,8,128]{3,2,1,0:T(8,128)S(1)} %get-tuple-element.84), channel_id=1, replica_groups=mesh['xlo'=2,'z'=16,'core'=2,'xhi'=2,'y'=4] {'z'}, dimensions={0} | all-to-all | bytes 262144 | tf_op jit(solution)/shard_map/all_to_all | solution.py:419
  218.4 10.8 %all-gather.1 = f32[64,2,8,128]{3,2,1,0:T(8,128)S(1)} all-gather(f32[16,2,8,128]{3,2,1,0:T(8,128)S(1)} %all_to_all.75), channel_id=3, replica_groups=mesh['xlo'=2,'z'=16,'core'=2,'xhi'=2,'y'=4] {'xlo','core'}, dimensions={0}, use_global_device_ids=true | all-gather | bytes 655360 | tf_op jit(solution)/shard_map/all_gather | solution.py:423
  229.1 0.9 next_kernel.3
  230.0 16.9 %all_to_all.76.refs_0_ = f32[8,2,32,256]{3,2,1,0:T(8,128)S(1)} all-to-all(f32[8,2,32,256]{3,2,1,0:T(8,128)S(1)} %get-tuple-element.85), channel_id=1, replica_groups=mesh['xlo'=2,'z'=16,'core'=2,'xhi'=2,'y'=4] {'xhi','y'}, dimensions={0} | all-to-all | bytes 1048576 | tf_op jit(solution)/shard_map/all_to_all | solution.py:419
  246.9 1.7 ratio_kernel.5
  248.6 14.0 %all_to_all.77.refs_0_ = f32[8,2,32,256]{3,2,1,0:T(8,128)S(1)} all-to-all(f32[8,2,32,256]{3,2,1,0:T(8,128)S(1)} %ratio_kernel.5), channel_id=1, replica_groups=mesh['xlo'=2,'z'=16,'core'=2,'xhi'=2,'y'=4] {'xhi','y'}, dimensions={0} | all-to-all | bytes 1048576 | tf_op jit(solution)/shard_map/all_to_all | solution.py:419
  262.5 0.8 backward_kernel.5
  263.4 4.4 %collective-permute-start.13 = (f32[17,16,256]{2,1,0:T(8,128)S(1)}, f32[17,16,256]{2,1,0:T(8,128)S(1)}, u32[]{:S(2)}, u32[]{:S(2)}) collective-permute-start(f32[17,16,256]{2,1,0:T(8,128)S(1)} %get-tuple-element.88), channel_id=1, source_target_pairs={{0,8},{8,0},{1,9},{9,1},{2,10},{10,2},{3,11},{11,3},{4,12},{12,4},... | collective-permute-start | bytes 835592 | tf_op jit(solution)/shard_map/ppermute | solution.py:404
  267.7 1.2 collective-permute-done.13.refs_1_
  268.9 1.9 collective-permute-start.14
  271.0 1.3 collective-permute-start.16
  272.3 4.0 %collective-permute-start.15 = (f32[2,32,256]{2,1,0:T(8,128)S(1)}, f32[2,32,256]{2,1,0:T(8,128)S(1)}, u32[]{:S(2)}, u32[]{:S(2)}) collective-permute-start(f32[2,32,256]{2,1,0:T(8,128)S(1)} %step_kernel.5.refs_2_), channel_id=1, source_target_pairs={{0,1},{1,2},{2,3},{3,7},{7,6},{6,5},{5,4},{8,9},{9,10},{10,11},{11... | collective-permute-start | bytes 196616 | tf_op jit(solution)/shard_map/ppermute | solution.py:410
  276.3 1.3 collective-permute-done.15.refs_2_.refs_1_
  278.3 11.5 %all-to-all-start.11 = ((f32[16,3,8,128]{3,2,1,0:T(8,128)}), f32[16,3,8,128]{3,2,1,0:T(8,128)S(1)}, u32[]{:S(2)}, u32[]{:S(2)}) async-start(f32[16,3,8,128]{3,2,1,0:T(8,128)} %pack_kernel.5.refs_5_), calls=%async_computation.11 | async-start | bytes 393216 | tf_op jit(solution)/shard_map/all_to_all | solution.py:415
  289.8 0.9 place_kernel.5
  290.7 4.3 %collective-permute-start.17 = (f32[2,64,256]{2,1,0:T(8,128)S(1)}, f32[2,64,256]{2,1,0:T(8,128)S(1)}, u32[]{:S(2)}, u32[]{:S(2)}) collective-permute-start(f32[2,64,256]{2,1,0:T(8,128)S(1)} %get-tuple-element.96), channel_id=1, source_target_pairs={{0,8},{8,16},{16,24},{24,32},{32,40},{40,48},{48,56},{56,64},{64,7... | collective-permute-start | bytes 393224 | tf_op jit(solution)/shard_map/ppermute | solution.py:400
  295.1 5.3 %collective-permute-done.17.refs_2_ = f32[2,64,256]{2,1,0:T(8,128)S(1)} collective-permute-done((f32[2,64,256]{2,1,0:T(8,128)S(1)}, f32[2,64,256]{2,1,0:T(8,128)S(1)}, u32[]{:S(2)}, u32[]{:S(2)}) %collective-permute-start.17) | collective-permute-done | bytes 131104 | tf_op jit(solution)/shard_map/ppermute | solution.py:400
  301.1 16.4 %all_to_all.78.refs_0_ = f32[16,2,8,128]{3,2,1,0:T(8,128)S(1)} all-to-all(f32[16,2,8,128]{3,2,1,0:T(8,128)S(1)} %get-tuple-element.97), channel_id=1, replica_groups=mesh['xlo'=2,'z'=16,'core'=2,'xhi'=2,'y'=4] {'z'}, dimensions={0} | all-to-all | bytes 262144 | tf_op jit(solution)/shard_map/all_to_all | solution.py:419
  317.6 19.7 %all_to_all.79.refs_0_ = f32[8,352,128]{2,1,0:T(8,128)S(1)} all-to-all(f32[8,352,128]{2,1,0:T(8,128)S(1)} %tail_kernel.1), channel_id=1, replica_groups=mesh['xlo'=2,'z'=16,'core'=2,'xhi'=2,'y'=4] {'xhi','y'}, dimensions={0} | all-to-all | bytes 2883584 | tf_op jit(solution)/shard_map/all_to_all | solution.py:419
  337.3 15.7 %all-gather.2 = f32[32,32,128]{2,1,0:T(8,128)S(1)} all-gather(f32[8,32,128]{2,1,0:T(8,128)S(1)} %slice.19), channel_id=4, replica_groups=mesh['xlo'=2,'z'=16,'core'=2,'xhi'=2,'y'=4] {'xlo','core'}, dimensions={0}, use_global_device_ids=true | all-gather | bytes 655360 | tf_op jit(solution)/shard_map/all_gather | solution.py:423
  353.0 0.8 probe_out_kernel.1
  353.9 1.1 object_kernel.1
  (56 shorter events, 5.1 us)
Async XLA Ops:
  0.6 9.6 %copy-start.2 = (f32[2,288,512]{2,1,0:T(8,128)S(1)}, f32[2,288,512]{2,1,0:T(8,128)}, u32[]{:S(2)}) copy-start(f32[2,288,512]{2,1,0:T(8,128)} %whole.1) | copy-start | bytes 3538948
  0.6 1.1 copy-start.3
  2.6 12.6 %copy-start.4 = (s32[1,3]{1,0:T(1,128)S(1)}, s32[1,3]{1,0:T(1,128)}, u32[]{:S(2)}) copy-start(s32[1,3]{1,0:T(1,128)} %param.14) | copy-start | bytes 40
  2.6 12.6 %copy-start.5 = (s32[1,3]{1,0:T(1,128)S(1)}, s32[1,3]{1,0:T(1,128)}, u32[]{:S(2)}) copy-start(s32[1,3]{1,0:T(1,128)} %param.12) | copy-start | bytes 40
  2.6 12.6 %copy-start.6 = (s32[1,3]{1,0:T(1,128)S(1)}, s32[1,3]{1,0:T(1,128)}, u32[]{:S(2)}) copy-start(s32[1,3]{1,0:T(1,128)} %param.11) | copy-start | bytes 40
  2.6 13.9 %copy-start.1 = (bf16[1,3,256,256]{3,2,1,0:T(8,128)(2,1)S(1)}, bf16[1,3,256,256]{3,2,1,0:T(8,128)(2,1)}, u32[]{:S(2)}) copy-start(bf16[1,3,256,256]{3,2,1,0:T(8,128)(2,1)} %refs_1_.5) | copy-start | bytes 1179652
  2.6 16.5 %copy-start = (bf16[2,2,256,256]{3,2,1,0:T(8,128)(2,1)S(1)}, bf16[2,2,256,256]{3,2,1,0:T(8,128)(2,1)}, u32[]{:S(2)}) copy-start(bf16[2,2,256,256]{3,2,1,0:T(8,128)(2,1)} %constant.35.clone.refs_4_.refs_3_.refs_2_) | copy-start | bytes 1572868
  2.6 16.5 %all-to-all-start = ((f32[8,2,32,256]{3,2,1,0:T(8,128)}), f32[8,2,32,256]{3,2,1,0:T(8,128)S(1)}, u32[]{:S(2)}, u32[]{:S(2)}) async-start(f32[8,2,32,256]{3,2,1,0:T(8,128)} %split_kernel.1._), calls=%async_computation | async-start | bytes 1048576 | tf_op jit(solution)/shard_map/all_to_all | solution.py:419
  10.3 7.3 %collective-permute-start = (f32[2,64,256]{2,1,0:T(8,128)S(1)}, f32[2,64,256]{2,1,0:T(8,128)S(1)}, u32[]{:S(2)}, u32[]{:S(2)}) collective-permute-start(f32[2,64,256]{2,1,0:T(8,128)S(1)} %get-tuple-element.51), channel_id=1, source_target_pairs={{8,0},{16,8},{24,16},{32,24},{40,32},{48,40},{56,48},{64,56},{72,6... | collective-permute-start | bytes 393224 | tf_op jit(solution)/shard_map/ppermute | solution.py:400
  50.0 6.5 %collective-permute-start.1 = (f32[17,16,256]{2,1,0:T(8,128)S(1)}, f32[17,16,256]{2,1,0:T(8,128)S(1)}, u32[]{:S(2)}, u32[]{:S(2)}) collective-permute-start(f32[17,16,256]{2,1,0:T(8,128)S(1)} %get-tuple-element.58), channel_id=1, source_target_pairs={{0,8},{8,0},{1,9},{9,1},{2,10},{10,2},{3,11},{11,3},{4,12},{12,4},... | collective-permute-start | bytes 835592 | tf_op jit(solution)/shard_map/ppermute | solution.py:404
  56.5 13.5 %collective-permute-start.4 = (f32[17,8,256]{2,1,0:T(8,128)S(1)}, f32[17,8,256]{2,1,0:T(8,128)S(1)}, u32[]{:S(2)}, u32[]{:S(2)}) collective-permute-start(f32[17,8,256]{2,1,0:T(8,128)S(1)} %get-tuple-element.61), channel_id=1, source_target_pairs={{0,256},{256,0},{1,257},{257,1},{2,258},{258,2},{3,259},{259,3},{4... | collective-permute-start | bytes 417800 | tf_op jit(solution)/shard_map/ppermute | solution.py:404
  63.4 5.3 %collective-permute-start.3 = (f32[2,32,256]{2,1,0:T(8,128)S(1)}, f32[2,32,256]{2,1,0:T(8,128)S(1)}, u32[]{:S(2)}, u32[]{:S(2)}) collective-permute-start(f32[2,32,256]{2,1,0:T(8,128)S(1)} %step_kernel.3.refs_2_), channel_id=1, source_target_pairs={{1,0},{2,1},{3,2},{7,3},{6,7},{5,6},{4,5},{9,8},{10,9},{11,10},{15... | collective-permute-start | bytes 196616 | tf_op jit(solution)/shard_map/ppermute | solution.py:410
  64.7 5.3 %collective-permute-start.2 = (f32[2,32,256]{2,1,0:T(8,128)S(1)}, f32[2,32,256]{2,1,0:T(8,128)S(1)}, u32[]{:S(2)}, u32[]{:S(2)}) collective-permute-start(f32[2,32,256]{2,1,0:T(8,128)S(1)} %step_kernel.3.refs_2_), channel_id=1, source_target_pairs={{0,1},{1,2},{2,3},{3,7},{7,6},{6,5},{5,4},{8,9},{9,10},{10,11},{11... | collective-permute-start | bytes 196616 | tf_op jit(solution)/shard_map/ppermute | solution.py:410
  70.7 27.4 %all-to-all-start.3 = ((f32[16,3,8,128]{3,2,1,0:T(8,128)}), f32[16,3,8,128]{3,2,1,0:T(8,128)S(1)}, u32[]{:S(2)}, u32[]{:S(2)}) async-start(f32[16,3,8,128]{3,2,1,0:T(8,128)} %pack_kernel.3.refs_5_.refs_2_), calls=%async_computation.3 | async-start | bytes 393216 | tf_op jit(solution)/shard_map/all_to_all | solution.py:415
  86.9 10.3 %collective-permute-start.5 = (f32[2,64,256]{2,1,0:T(8,128)S(1)}, f32[2,64,256]{2,1,0:T(8,128)S(1)}, u32[]{:S(2)}, u32[]{:S(2)}) collective-permute-start(f32[2,64,256]{2,1,0:T(8,128)S(1)} %get-tuple-element.63), channel_id=1, source_target_pairs={{0,8},{8,16},{16,24},{24,32},{32,40},{40,48},{48,56},{56,64},{64,7... | collective-permute-start | bytes 393224 | tf_op jit(solution)/shard_map/ppermute | solution.py:400
  91.0 6.8 %collective-permute-start.6 = (f32[2,64,256]{2,1,0:T(8,128)S(1)}, f32[2,64,256]{2,1,0:T(8,128)S(1)}, u32[]{:S(2)}, u32[]{:S(2)}) collective-permute-start(f32[2,64,256]{2,1,0:T(8,128)S(1)} %get-tuple-element.64), channel_id=1, source_target_pairs={{8,0},{16,8},{24,16},{32,24},{40,32},{48,40},{56,48},{64,56},{72,6... | collective-permute-start | bytes 393224 | tf_op jit(solution)/shard_map/ppermute | solution.py:400
  161.8 5.5 %collective-permute-start.7 = (f32[17,16,256]{2,1,0:T(8,128)S(1)}, f32[17,16,256]{2,1,0:T(8,128)S(1)}, u32[]{:S(2)}, u32[]{:S(2)}) collective-permute-start(f32[17,16,256]{2,1,0:T(8,128)S(1)} %get-tuple-element.74), channel_id=1, source_target_pairs={{0,8},{8,0},{1,9},{9,1},{2,10},{10,2},{3,11},{11,3},{4,12},{12,4},... | collective-permute-start | bytes 835592 | tf_op jit(solution)/shard_map/ppermute | solution.py:404
  167.3 8.7 %collective-permute-start.10 = (f32[17,8,256]{2,1,0:T(8,128)S(1)}, f32[17,8,256]{2,1,0:T(8,128)S(1)}, u32[]{:S(2)}, u32[]{:S(2)}) collective-permute-start(f32[17,8,256]{2,1,0:T(8,128)S(1)} %get-tuple-element.77), channel_id=1, source_target_pairs={{0,256},{256,0},{1,257},{257,1},{2,258},{258,2},{3,259},{259,3},{4... | collective-permute-start | bytes 417800 | tf_op jit(solution)/shard_map/ppermute | solution.py:404
  169.4 5.3 %collective-permute-start.9 = (f32[2,32,256]{2,1,0:T(8,128)S(1)}, f32[2,32,256]{2,1,0:T(8,128)S(1)}, u32[]{:S(2)}, u32[]{:S(2)}) collective-permute-start(f32[2,32,256]{2,1,0:T(8,128)S(1)} %step_kernel.4.refs_2_), channel_id=1, source_target_pairs={{1,0},{2,1},{3,2},{7,3},{6,7},{5,6},{4,5},{9,8},{10,9},{11,10},{15... | collective-permute-start | bytes 196616 | tf_op jit(solution)/shard_map/ppermute | solution.py:410
  170.7 5.3 %collective-permute-start.8 = (f32[2,32,256]{2,1,0:T(8,128)S(1)}, f32[2,32,256]{2,1,0:T(8,128)S(1)}, u32[]{:S(2)}, u32[]{:S(2)}) collective-permute-start(f32[2,32,256]{2,1,0:T(8,128)S(1)} %step_kernel.4.refs_2_), channel_id=1, source_target_pairs={{0,1},{1,2},{2,3},{3,7},{7,6},{6,5},{5,4},{8,9},{9,10},{10,11},{11... | collective-permute-start | bytes 196616 | tf_op jit(solution)/shard_map/ppermute | solution.py:410
  176.7 23.0 %all-to-all-start.7 = ((f32[16,3,8,128]{3,2,1,0:T(8,128)}), f32[16,3,8,128]{3,2,1,0:T(8,128)S(1)}, u32[]{:S(2)}, u32[]{:S(2)}) async-start(f32[16,3,8,128]{3,2,1,0:T(8,128)} %pack_kernel.4.refs_5_.refs_2_), calls=%async_computation.7 | async-start | bytes 393216 | tf_op jit(solution)/shard_map/all_to_all | solution.py:415
  188.5 10.3 %collective-permute-start.11 = (f32[2,64,256]{2,1,0:T(8,128)S(1)}, f32[2,64,256]{2,1,0:T(8,128)S(1)}, u32[]{:S(2)}, u32[]{:S(2)}) collective-permute-start(f32[2,64,256]{2,1,0:T(8,128)S(1)} %get-tuple-element.79), channel_id=1, source_target_pairs={{0,8},{8,16},{16,24},{24,32},{32,40},{40,48},{48,56},{56,64},{64,7... | collective-permute-start | bytes 393224 | tf_op jit(solution)/shard_map/ppermute | solution.py:400
  192.9 6.6 %collective-permute-start.12 = (f32[2,64,256]{2,1,0:T(8,128)S(1)}, f32[2,64,256]{2,1,0:T(8,128)S(1)}, u32[]{:S(2)}, u32[]{:S(2)}) collective-permute-start(f32[2,64,256]{2,1,0:T(8,128)S(1)} %get-tuple-element.80), channel_id=1, source_target_pairs={{8,0},{16,8},{24,16},{32,24},{40,32},{48,40},{56,48},{64,56},{72,6... | collective-permute-start | bytes 393224 | tf_op jit(solution)/shard_map/ppermute | solution.py:400
  263.4 5.5 %collective-permute-start.13 = (f32[17,16,256]{2,1,0:T(8,128)S(1)}, f32[17,16,256]{2,1,0:T(8,128)S(1)}, u32[]{:S(2)}, u32[]{:S(2)}) collective-permute-start(f32[17,16,256]{2,1,0:T(8,128)S(1)} %get-tuple-element.88), channel_id=1, source_target_pairs={{0,8},{8,0},{1,9},{9,1},{2,10},{10,2},{3,11},{11,3},{4,12},{12,4},... | collective-permute-start | bytes 835592 | tf_op jit(solution)/shard_map/ppermute | solution.py:404
  268.9 8.7 %collective-permute-start.14 = (f32[17,8,256]{2,1,0:T(8,128)S(1)}, f32[17,8,256]{2,1,0:T(8,128)S(1)}, u32[]{:S(2)}, u32[]{:S(2)}) collective-permute-start(f32[17,8,256]{2,1,0:T(8,128)S(1)} %get-tuple-element.90), channel_id=1, source_target_pairs={{0,256},{256,0},{1,257},{257,1},{2,258},{258,2},{3,259},{259,3},{4... | collective-permute-start | bytes 417800 | tf_op jit(solution)/shard_map/ppermute | solution.py:404
  271.0 5.3 %collective-permute-start.16 = (f32[2,32,256]{2,1,0:T(8,128)S(1)}, f32[2,32,256]{2,1,0:T(8,128)S(1)}, u32[]{:S(2)}, u32[]{:S(2)}) collective-permute-start(f32[2,32,256]{2,1,0:T(8,128)S(1)} %step_kernel.5.refs_2_), channel_id=1, source_target_pairs={{1,0},{2,1},{3,2},{7,3},{6,7},{5,6},{4,5},{9,8},{10,9},{11,10},{15... | collective-permute-start | bytes 196616 | tf_op jit(solution)/shard_map/ppermute | solution.py:410
  272.3 5.3 %collective-permute-start.15 = (f32[2,32,256]{2,1,0:T(8,128)S(1)}, f32[2,32,256]{2,1,0:T(8,128)S(1)}, u32[]{:S(2)}, u32[]{:S(2)}) collective-permute-start(f32[2,32,256]{2,1,0:T(8,128)S(1)} %step_kernel.5.refs_2_), channel_id=1, source_target_pairs={{0,1},{1,2},{2,3},{3,7},{7,6},{6,5},{5,4},{8,9},{9,10},{10,11},{11... | collective-permute-start | bytes 196616 | tf_op jit(solution)/shard_map/ppermute | solution.py:410
  278.3 22.1 %all-to-all-start.11 = ((f32[16,3,8,128]{3,2,1,0:T(8,128)}), f32[16,3,8,128]{3,2,1,0:T(8,128)S(1)}, u32[]{:S(2)}, u32[]{:S(2)}) async-start(f32[16,3,8,128]{3,2,1,0:T(8,128)} %pack_kernel.5.refs_5_), calls=%async_computation.11 | async-start | bytes 393216 | tf_op jit(solution)/shard_map/all_to_all | solution.py:415
  290.7 9.6 %collective-permute-start.17 = (f32[2,64,256]{2,1,0:T(8,128)S(1)}, f32[2,64,256]{2,1,0:T(8,128)S(1)}, u32[]{:S(2)}, u32[]{:S(2)}) collective-permute-start(f32[2,64,256]{2,1,0:T(8,128)S(1)} %get-tuple-element.96), channel_id=1, source_target_pairs={{0,8},{8,16},{16,24},{24,32},{32,40},{40,48},{48,56},{56,64},{64,7... | collective-permute-start | bytes 393224 | tf_op jit(solution)/shard_map/ppermute | solution.py:400

commit v7 on v6

--- a/solution.py
+++ b/solution.py
@@ -514,31 +514,40 @@
             keep,
             received,
             scalars=False,
-            after=(above, below),
+            after=(above, below) if final else (object_step,),
         )
         sums = exchange_rings(packed)
-        part_band, to_left, to_right = call(
-            place_kernel,
-            [band_shape, edge, edge],
-            scal,
-            above,
-            object_step,
-            below,
-            band,
-            after=(packed,),
-        )
-        from_left = shift(to_right, TILE_AXES, TILES, 1)
+        placing = [scal, above, object_step, below, band]
         if final:
+            part_band, _, to_right = call(
+                place_kernel, [band_shape, edge, edge], *placing, after=(packed,)
+            )
+            from_left = shift(to_right, TILE_AXES, TILES, 1)
             (rows_out,) = call(
                 out_rows_kernel, [(2, OUT_ROWS, WIDTH)], scal, part_band, from_left
             )
             before = (rows_out,)
         else:
-            from_right = shift(to_left, TILE_AXES, TILES, -1)
             next_scal = scalars[step + 1 : step + 2]
             counts, flags = call(
                 counts_kernel, counts_shapes, next_scal, measured, after=(packed,)
             )
+            before = (above, below, counts)
+        shard, shards = call(
+            probe_kernel,
+            [(2, 8, LANES), (RINGS, 2, 8, LANES)],
+            sums,
+            shard,
+            scalars=False,
+            after=before,
+        )
+        piece = exchange(shards, "z")
+        if not final:
+            part_band, to_left, to_right = call(
+                place_kernel, [band_shape, edge, edge], *placing, after=(shards,)
+            )
+            from_left = shift(to_right, TILE_AXES, TILES, 1)
+            from_right = shift(to_left, TILE_AXES, TILES, -1)
             band, view = call(
                 view_kernel,
                 [band_shape, slab_pair],
@@ -547,17 +556,7 @@
                 from_left,
                 from_right,
             )
-            before = (view, counts)
-        shard, shards = call(
-            probe_kernel,
-            [(2, 8, LANES), (RINGS, 2, 8, LANES)],
-            sums,
-            shard,
-            scalars=False,
-            after=before,
-        )
-        piece = exchange(shards, "z")
-        if not final:
+            piece, view = lax.optimization_barrier((piece, view))
             pieces = gather_pieces(piece)
     tail_rows = 32 + 8 * OUT_ROWS
     (tail,) = call(

time: 356 us -> 344 us (0.966)
  blocking collectives: 199 us -> 151 us
  starting transfers between devices: 108 us -> 131 us
  waiting for transfers between devices: 23.7 us -> 36.2 us
    all_to_all x10 -> x8, blocking collectives: 162 us -> 117 us  [exchange(): return lax.all_to_all(value, axes, 0, 0, tiled=True)]
    all_to_all x1 -> x3, starting transfers between devices: 7.62 us -> 22.9 us  [exchange(): return lax.all_to_all(value, axes, 0, 0, tiled=True)]
    ppermute x6, waiting for transfers between devices: 3.5 us -> 10.8 us  [other(): return lax.ppermute(value, axis, [(0, 1), (1, 0)])]
    ppermute x6, starting transfers between devices: 21.6 us -> 26.5 us  [shift(): lax.ppermute(value, axes, [(i, i + steps) for i in range(first, last)])]
    all_to_all x3, waiting for transfers between devices: 0.01 us -> 4.81 us  [exchange_rings(): lax.all_to_all(value, 'z', 0, 0, tiled=True, axis_index_groups=groups)]
    all_gather x3, blocking collectives: 37.3 us -> 33.3 us  [gather_pieces(): gathered = lax.all_gather(piece, ('xlo', 'core'))]
  transfers between devices with their start and end apart: 22 -> 24, of which waited for: 13 -> 17; matrix products, arithmetic and copies ran while one was open for 0% -> 0% of each run, Pallas kernels for 1% -> 1%
where the time goes in v7:
time: 344 us; the launch traced here: 342 us
  blocking collectives  151 us (44%)
  starting transfers between devices  131 us (38%)
  waiting for transfers between devices  36.2 us (11%)
  Pallas kernels  21.2 us (6%)
    all_to_all x8, blocking collectives, exchange(): return lax.all_to_all(value, axes, 0, 0, tiled=True)  117 us
    all_to_all x3, starting transfers between devices, exchange_rings(): lax.all_to_all(value, 'z', 0, 0, tiled=True, axis_index_groups=groups)  40 us
    all_gather x3, blocking collectives, gather_pieces(): gathered = lax.all_gather(piece, ('xlo', 'core'))  33.3 us
    ppermute x6, starting transfers between devices, shift(): lax.ppermute(value, axes, [(i, i + steps) for i in range(first, last)])  26.5 us
    ppermute x6, starting transfers between devices, other(): return lax.ppermute(value, axis, [(0, 1), (1, 0)])  25.6 us
    all_to_all x3, starting transfers between devices, exchange(): return lax.all_to_all(value, axes, 0, 0, tiled=True)  22.9 us
    pallas_call x34, Pallas kernels, call(): pl.pallas_call(body, out_shape=[jax.ShapeDtypeStruct(shape, F32) for shap...  21.1 us
    ppermute x6, waiting for transfers between devices, shift(): lax.ppermute(value, axes, [(i, i + steps) for i in range(first, last)])  16 us
  transfers between devices with their start and end apart: 24, of which 17 were waited for; matrix products, arithmetic and copies ran while one was open for 0% of the time, Pallas kernels for 1%

profile of v7, /device:TPU:1, one launch (start us, length us, event | category | flops | bytes accessed | tf_op | source)
XLA Modules:
  0.0 342.1 jit_solution(16304076604525471890)
XLA Ops:
  0.6 1.1 copy-done.3
  2.6 7.6 %all-to-all-start = ((f32[8,2,32,256]{3,2,1,0:T(8,128)}), f32[8,2,32,256]{3,2,1,0:T(8,128)S(1)}, u32[]{:S(2)}, u32[]{:S(2)}) async-start(f32[8,2,32,256]{3,2,1,0:T(8,128)} %split_kernel.1._), calls=%async_computation | async-start | bytes 1048576 | tf_op jit(solution)/shard_map/all_to_all | solution.py:419
  10.3 4.8 %collective-permute-start = (f32[2,64,256]{2,1,0:T(8,128)S(1)}, f32[2,64,256]{2,1,0:T(8,128)S(1)}, u32[]{:S(2)}, u32[]{:S(2)}) collective-permute-start(f32[2,64,256]{2,1,0:T(8,128)S(1)} %get-tuple-element.55), channel_id=1, source_target_pairs={{8,0},{16,8},{24,16},{32,24},{40,32},{48,40},{56,48},{64,56},{72,6... | collective-permute-start | bytes 393224 | tf_op jit(solution)/shard_map/ppermute | solution.py:400
  17.7 1.4 all-to-all-done.refs_3_.refs_1_
  19.1 1.1 first_kernel.1
  20.2 14.8 %all_to_all.70.refs_0_ = f32[8,2,32,256]{3,2,1,0:T(8,128)S(1)} all-to-all(f32[8,2,32,256]{3,2,1,0:T(8,128)S(1)} %get-tuple-element.57), channel_id=1, replica_groups=mesh['xlo'=2,'z'=16,'core'=2,'xhi'=2,'y'=4] {'xhi','y'}, dimensions={0} | all-to-all | bytes 1048576 | tf_op jit(solution)/shard_map/all_to_all | solution.py:419
  35.0 1.7 ratio_kernel.3
  36.7 12.4 %all_to_all.71.refs_0_ = f32[8,2,32,256]{3,2,1,0:T(8,128)S(1)} all-to-all(f32[8,2,32,256]{3,2,1,0:T(8,128)S(1)} %ratio_kernel.3), channel_id=1, replica_groups=mesh['xlo'=2,'z'=16,'core'=2,'xhi'=2,'y'=4] {'xhi','y'}, dimensions={0} | all-to-all | bytes 1048576 | tf_op jit(solution)/shard_map/all_to_all | solution.py:419
  49.1 0.8 backward_kernel.3
  50.0 5.3 %collective-permute-start.1 = (f32[17,16,256]{2,1,0:T(8,128)S(1)}, f32[17,16,256]{2,1,0:T(8,128)S(1)}, u32[]{:S(2)}, u32[]{:S(2)}) collective-permute-start(f32[17,16,256]{2,1,0:T(8,128)S(1)} %get-tuple-element.61), channel_id=1, source_target_pairs={{0,8},{8,0},{1,9},{9,1},{2,10},{10,2},{3,11},{11,3},{4,12},{12,4},... | collective-permute-start | bytes 835592 | tf_op jit(solution)/shard_map/ppermute | solution.py:404
  55.3 1.2 collective-permute-done.1.refs_1_
  56.5 6.7 %collective-permute-start.2 = (f32[17,8,256]{2,1,0:T(8,128)S(1)}, f32[17,8,256]{2,1,0:T(8,128)S(1)}, u32[]{:S(2)}, u32[]{:S(2)}) collective-permute-start(f32[17,8,256]{2,1,0:T(8,128)S(1)} %get-tuple-element.63), channel_id=1, source_target_pairs={{0,256},{256,0},{1,257},{257,1},{2,258},{258,2},{3,259},{259,3},{4... | collective-permute-start | bytes 417800 | tf_op jit(solution)/shard_map/ppermute | solution.py:404
  63.4 3.6 %collective-permute-done.2.refs_1_ = f32[17,8,256]{2,1,0:T(8,128)S(1)} collective-permute-done((f32[17,8,256]{2,1,0:T(8,128)S(1)}, f32[17,8,256]{2,1,0:T(8,128)S(1)}, u32[]{:S(2)}, u32[]{:S(2)}) %collective-permute-start.2) | collective-permute-done | bytes 139296 | tf_op jit(solution)/shard_map/ppermute | solution.py:404
  67.6 17.0 %all-to-all-start.3 = ((f32[16,3,8,128]{3,2,1,0:T(8,128)}), f32[16,3,8,128]{3,2,1,0:T(8,128)S(1)}, u32[]{:S(2)}, u32[]{:S(2)}) async-start(f32[16,3,8,128]{3,2,1,0:T(8,128)} %pack_kernel.3.refs_2_), calls=%async_computation.3 | async-start | bytes 393216 | tf_op jit(solution)/shard_map/all_to_all | solution.py:415
  84.6 1.3 collective-permute-start.4
  85.9 4.0 %collective-permute-start.3 = (f32[2,32,256]{2,1,0:T(8,128)S(1)}, f32[2,32,256]{2,1,0:T(8,128)S(1)}, u32[]{:S(2)}, u32[]{:S(2)}) collective-permute-start(f32[2,32,256]{2,1,0:T(8,128)S(1)} %step_kernel.3.refs_2_), channel_id=1, source_target_pairs={{0,1},{1,2},{2,3},{3,7},{7,6},{6,5},{5,4},{8,9},{9,10},{10,11},{11... | collective-permute-start | bytes 196616 | tf_op jit(solution)/shard_map/ppermute | solution.py:410
  90.3 0.9 collective-permute-done.3.refs_2_.refs_1_
  91.2 2.4 all-to-all-done.3.refs_0_
  94.3 7.6 %all-to-all-start.4 = ((f32[16,2,8,128]{3,2,1,0:T(8,128)}), f32[16,2,8,128]{3,2,1,0:T(8,128)S(1)}, u32[]{:S(2)}, u32[]{:S(2)}) async-start(f32[16,2,8,128]{3,2,1,0:T(8,128)} %get-tuple-element.67.refs_5_), calls=%async_computation.4 | async-start | bytes 262144 | tf_op jit(solution)/shard_map/all_to_all | solution.py:419
  102.2 6.7 %collective-permute-start.5 = (f32[2,64,256]{2,1,0:T(8,128)S(1)}, f32[2,64,256]{2,1,0:T(8,128)S(1)}, u32[]{:S(2)}, u32[]{:S(2)}) collective-permute-start(f32[2,64,256]{2,1,0:T(8,128)S(1)} %get-tuple-element.70), channel_id=1, source_target_pairs={{0,8},{8,16},{16,24},{24,32},{32,40},{40,48},{48,56},{56,64},{64,7... | collective-permute-start | bytes 393224 | tf_op jit(solution)/shard_map/ppermute | solution.py:400
  108.9 1.9 collective-permute-start.6
  110.9 1.4 collective-permute-done.5.refs_2_
  112.2 3.6 %collective-permute-done.6.refs_3_ = f32[2,64,256]{2,1,0:T(8,128)S(1)} collective-permute-done((f32[2,64,256]{2,1,0:T(8,128)S(1)}, f32[2,64,256]{2,1,0:T(8,128)S(1)}, u32[]{:S(2)}, u32[]{:S(2)}) %collective-permute-start.6) | collective-permute-done | bytes 131104 | tf_op jit(solution)/shard_map/ppermute | solution.py:400
  116.1 8.7 %all-gather = f32[64,2,8,128]{3,2,1,0:T(8,128)S(1)} all-gather(f32[16,2,8,128]{3,2,1,0:T(8,128)S(1)} %all-to-all-done.4), channel_id=2, replica_groups=mesh['xlo'=2,'z'=16,'core'=2,'xhi'=2,'y'=4] {'xlo','core'}, dimensions={0}, use_global_device_ids=true | all-gather | bytes 655360 | tf_op jit(solution)/shard_map/all_gather | solution.py:423
  124.8 0.9 next_kernel.2
  125.6 12.8 %all_to_all.72.refs_0_ = f32[8,2,32,256]{3,2,1,0:T(8,128)S(1)} all-to-all(f32[8,2,32,256]{3,2,1,0:T(8,128)S(1)} %get-tuple-element.75), channel_id=1, replica_groups=mesh['xlo'=2,'z'=16,'core'=2,'xhi'=2,'y'=4] {'xhi','y'}, dimensions={0} | all-to-all | bytes 1048576 | tf_op jit(solution)/shard_map/all_to_all | solution.py:419
  138.4 1.7 ratio_kernel.4
  140.1 13.9 %all_to_all.73.refs_0_ = f32[8,2,32,256]{3,2,1,0:T(8,128)S(1)} all-to-all(f32[8,2,32,256]{3,2,1,0:T(8,128)S(1)} %ratio_kernel.4), channel_id=1, replica_groups=mesh['xlo'=2,'z'=16,'core'=2,'xhi'=2,'y'=4] {'xhi','y'}, dimensions={0} | all-to-all | bytes 1048576 | tf_op jit(solution)/shard_map/all_to_all | solution.py:419
  154.1 0.8 backward_kernel.4
  154.9 4.4 %collective-permute-start.7 = (f32[17,16,256]{2,1,0:T(8,128)S(1)}, f32[17,16,256]{2,1,0:T(8,128)S(1)}, u32[]{:S(2)}, u32[]{:S(2)}) collective-permute-start(f32[17,16,256]{2,1,0:T(8,128)S(1)} %get-tuple-element.78), channel_id=1, source_target_pairs={{0,8},{8,0},{1,9},{9,1},{2,10},{10,2},{3,11},{11,3},{4,12},{12,4},... | collective-permute-start | bytes 835592 | tf_op jit(solution)/shard_map/ppermute | solution.py:404
  159.3 1.2 collective-permute-done.7.refs_1_
  160.5 2.9 collective-permute-start.8
  163.5 3.7 %collective-permute-done.8.refs_1_ = f32[17,8,256]{2,1,0:T(8,128)S(1)} collective-permute-done((f32[17,8,256]{2,1,0:T(8,128)S(1)}, f32[17,8,256]{2,1,0:T(8,128)S(1)}, u32[]{:S(2)}, u32[]{:S(2)}) %collective-permute-start.8) | collective-permute-done | bytes 139296 | tf_op jit(solution)/shard_map/ppermute | solution.py:404
  168.0 11.5 %all-to-all-start.7 = ((f32[16,3,8,128]{3,2,1,0:T(8,128)}), f32[16,3,8,128]{3,2,1,0:T(8,128)S(1)}, u32[]{:S(2)}, u32[]{:S(2)}) async-start(f32[16,3,8,128]{3,2,1,0:T(8,128)} %pack_kernel.4.refs_2_), calls=%async_computation.7 | async-start | bytes 393216 | tf_op jit(solution)/shard_map/all_to_all | solution.py:415
  179.4 1.3 collective-permute-start.10
  180.7 4.0 %collective-permute-start.9 = (f32[2,32,256]{2,1,0:T(8,128)S(1)}, f32[2,32,256]{2,1,0:T(8,128)S(1)}, u32[]{:S(2)}, u32[]{:S(2)}) collective-permute-start(f32[2,32,256]{2,1,0:T(8,128)S(1)} %step_kernel.4.refs_2_), channel_id=1, source_target_pairs={{0,1},{1,2},{2,3},{3,7},{7,6},{6,5},{5,4},{8,9},{9,10},{10,11},{11... | collective-permute-start | bytes 196616 | tf_op jit(solution)/shard_map/ppermute | solution.py:410
  185.1 0.9 collective-permute-done.9.refs_2_.refs_1_
  186.0 2.4 all-to-all-done.7.refs_0_
  189.1 7.6 %all-to-all-start.8 = ((f32[16,2,8,128]{3,2,1,0:T(8,128)}), f32[16,2,8,128]{3,2,1,0:T(8,128)S(1)}, u32[]{:S(2)}, u32[]{:S(2)}) async-start(f32[16,2,8,128]{3,2,1,0:T(8,128)} %get-tuple-element.85.refs_5_), calls=%async_computation.8 | async-start | bytes 262144 | tf_op jit(solution)/shard_map/all_to_all | solution.py:419
  197.0 6.7 %collective-permute-start.11 = (f32[2,64,256]{2,1,0:T(8,128)S(1)}, f32[2,64,256]{2,1,0:T(8,128)S(1)}, u32[]{:S(2)}, u32[]{:S(2)}) collective-permute-start(f32[2,64,256]{2,1,0:T(8,128)S(1)} %get-tuple-element.88), channel_id=1, source_target_pairs={{0,8},{8,16},{16,24},{24,32},{32,40},{40,48},{48,56},{56,64},{64,7... | collective-permute-start | bytes 393224 | tf_op jit(solution)/shard_map/ppermute | solution.py:400
  203.7 1.9 collective-permute-start.12
  205.6 1.4 collective-permute-done.11.refs_2_
  207.0 3.6 %collective-permute-done.12.refs_3_ = f32[2,64,256]{2,1,0:T(8,128)S(1)} collective-permute-done((f32[2,64,256]{2,1,0:T(8,128)S(1)}, f32[2,64,256]{2,1,0:T(8,128)S(1)}, u32[]{:S(2)}, u32[]{:S(2)}) %collective-permute-start.12) | collective-permute-done | bytes 131104 | tf_op jit(solution)/shard_map/ppermute | solution.py:400
  210.9 9.1 %all-gather.1 = f32[64,2,8,128]{3,2,1,0:T(8,128)S(1)} all-gather(f32[16,2,8,128]{3,2,1,0:T(8,128)S(1)} %all-to-all-done.8), channel_id=3, replica_groups=mesh['xlo'=2,'z'=16,'core'=2,'xhi'=2,'y'=4] {'xlo','core'}, dimensions={0}, use_global_device_ids=true | all-gather | bytes 655360 | tf_op jit(solution)/shard_map/all_gather | solution.py:423
  220.0 0.9 next_kernel.3
  220.8 13.2 %all_to_all.74.refs_0_ = f32[8,2,32,256]{3,2,1,0:T(8,128)S(1)} all-to-all(f32[8,2,32,256]{3,2,1,0:T(8,128)S(1)} %get-tuple-element.93), channel_id=1, replica_groups=mesh['xlo'=2,'z'=16,'core'=2,'xhi'=2,'y'=4] {'xhi','y'}, dimensions={0} | all-to-all | bytes 1048576 | tf_op jit(solution)/shard_map/all_to_all | solution.py:419
  234.0 1.7 ratio_kernel.5
  235.7 14.0 %all_to_all.75.refs_0_ = f32[8,2,32,256]{3,2,1,0:T(8,128)S(1)} all-to-all(f32[8,2,32,256]{3,2,1,0:T(8,128)S(1)} %ratio_kernel.5), channel_id=1, replica_groups=mesh['xlo'=2,'z'=16,'core'=2,'xhi'=2,'y'=4] {'xhi','y'}, dimensions={0} | all-to-all | bytes 1048576 | tf_op jit(solution)/shard_map/all_to_all | solution.py:419
  249.7 0.8 backward_kernel.5
  250.5 4.4 %collective-permute-start.13 = (f32[17,16,256]{2,1,0:T(8,128)S(1)}, f32[17,16,256]{2,1,0:T(8,128)S(1)}, u32[]{:S(2)}, u32[]{:S(2)}) collective-permute-start(f32[17,16,256]{2,1,0:T(8,128)S(1)} %get-tuple-element.96), channel_id=1, source_target_pairs={{0,8},{8,0},{1,9},{9,1},{2,10},{10,2},{3,11},{11,3},{4,12},{12,4},... | collective-permute-start | bytes 835592 | tf_op jit(solution)/shard_map/ppermute | solution.py:404
  254.9 1.2 collective-permute-done.13.refs_1_
  256.1 2.0 collective-permute-start.14
  258.3 1.3 collective-permute-start.16
  259.6 4.0 %collective-permute-start.15 = (f32[2,32,256]{2,1,0:T(8,128)S(1)}, f32[2,32,256]{2,1,0:T(8,128)S(1)}, u32[]{:S(2)}, u32[]{:S(2)}) collective-permute-start(f32[2,32,256]{2,1,0:T(8,128)S(1)} %step_kernel.5.refs_2_), channel_id=1, source_target_pairs={{0,1},{1,2},{2,3},{3,7},{7,6},{6,5},{5,4},{8,9},{9,10},{10,11},{11... | collective-permute-start | bytes 196616 | tf_op jit(solution)/shard_map/ppermute | solution.py:410
  263.6 1.3 collective-permute-done.15.refs_2_.refs_1_
  265.6 11.5 %all-to-all-start.11 = ((f32[16,3,8,128]{3,2,1,0:T(8,128)}), f32[16,3,8,128]{3,2,1,0:T(8,128)S(1)}, u32[]{:S(2)}, u32[]{:S(2)}) async-start(f32[16,3,8,128]{3,2,1,0:T(8,128)} %pack_kernel.5.refs_5_), calls=%async_computation.11 | async-start | bytes 393216 | tf_op jit(solution)/shard_map/all_to_all | solution.py:415
  277.1 0.9 place_kernel.5
  278.0 4.4 %collective-permute-start.17 = (f32[2,64,256]{2,1,0:T(8,128)S(1)}, f32[2,64,256]{2,1,0:T(8,128)S(1)}, u32[]{:S(2)}, u32[]{:S(2)}) collective-permute-start(f32[2,64,256]{2,1,0:T(8,128)S(1)} %get-tuple-element.104), channel_id=1, source_target_pairs={{0,8},{8,16},{16,24},{24,32},{32,40},{40,48},{48,56},{56,64},{64,7... | collective-permute-start | bytes 393224 | tf_op jit(solution)/shard_map/ppermute | solution.py:400
  282.4 5.2 %collective-permute-done.17.refs_2_ = f32[2,64,256]{2,1,0:T(8,128)S(1)} collective-permute-done((f32[2,64,256]{2,1,0:T(8,128)S(1)}, f32[2,64,256]{2,1,0:T(8,128)S(1)}, u32[]{:S(2)}, u32[]{:S(2)}) %collective-permute-start.17) | collective-permute-done | bytes 131104 | tf_op jit(solution)/shard_map/ppermute | solution.py:400
  288.4 16.0 %all_to_all.76.refs_0_ = f32[16,2,8,128]{3,2,1,0:T(8,128)S(1)} all-to-all(f32[16,2,8,128]{3,2,1,0:T(8,128)S(1)} %get-tuple-element.105), channel_id=1, replica_groups=mesh['xlo'=2,'z'=16,'core'=2,'xhi'=2,'y'=4] {'z'}, dimensions={0} | all-to-all | bytes 262144 | tf_op jit(solution)/shard_map/all_to_all | solution.py:419
  304.5 20.1 %all_to_all.77.refs_0_ = f32[8,352,128]{2,1,0:T(8,128)S(1)} all-to-all(f32[8,352,128]{2,1,0:T(8,128)S(1)} %tail_kernel.1), channel_id=1, replica_groups=mesh['xlo'=2,'z'=16,'core'=2,'xhi'=2,'y'=4] {'xhi','y'}, dimensions={0} | all-to-all | bytes 2883584 | tf_op jit(solution)/shard_map/all_to_all | solution.py:419
  324.6 15.5 %all-gather.2 = f32[32,32,128]{2,1,0:T(8,128)S(1)} all-gather(f32[8,32,128]{2,1,0:T(8,128)S(1)} %slice.19), channel_id=4, replica_groups=mesh['xlo'=2,'z'=16,'core'=2,'xhi'=2,'y'=4] {'xlo','core'}, dimensions={0}, use_global_device_ids=true | all-gather | bytes 655360 | tf_op jit(solution)/shard_map/all_gather | solution.py:423
  340.2 0.8 probe_out_kernel.1
  341.0 1.1 object_kernel.1
  (58 shorter events, 9.4 us)
Async XLA Ops:
  0.6 9.6 %copy-start.2 = (f32[2,288,512]{2,1,0:T(8,128)S(1)}, f32[2,288,512]{2,1,0:T(8,128)}, u32[]{:S(2)}) copy-start(f32[2,288,512]{2,1,0:T(8,128)} %whole.1) | copy-start | bytes 3538948
  0.6 1.1 copy-start.3
  2.6 12.6 %copy-start.4 = (s32[1,3]{1,0:T(1,128)S(1)}, s32[1,3]{1,0:T(1,128)}, u32[]{:S(2)}) copy-start(s32[1,3]{1,0:T(1,128)} %param.14) | copy-start | bytes 40
  2.6 12.6 %copy-start.5 = (s32[1,3]{1,0:T(1,128)S(1)}, s32[1,3]{1,0:T(1,128)}, u32[]{:S(2)}) copy-start(s32[1,3]{1,0:T(1,128)} %param.12) | copy-start | bytes 40
  2.6 12.6 %copy-start.6 = (s32[1,3]{1,0:T(1,128)S(1)}, s32[1,3]{1,0:T(1,128)}, u32[]{:S(2)}) copy-start(s32[1,3]{1,0:T(1,128)} %param.11) | copy-start | bytes 40
  2.6 13.9 %copy-start.1 = (bf16[1,3,256,256]{3,2,1,0:T(8,128)(2,1)S(1)}, bf16[1,3,256,256]{3,2,1,0:T(8,128)(2,1)}, u32[]{:S(2)}) copy-start(bf16[1,3,256,256]{3,2,1,0:T(8,128)(2,1)} %refs_1_.5) | copy-start | bytes 1179652
  2.6 16.5 %copy-start = (bf16[2,2,256,256]{3,2,1,0:T(8,128)(2,1)S(1)}, bf16[2,2,256,256]{3,2,1,0:T(8,128)(2,1)}, u32[]{:S(2)}) copy-start(bf16[2,2,256,256]{3,2,1,0:T(8,128)(2,1)} %constant.35.clone.refs_4_.refs_3_.refs_2_) | copy-start | bytes 1572868
  2.6 16.5 %all-to-all-start = ((f32[8,2,32,256]{3,2,1,0:T(8,128)}), f32[8,2,32,256]{3,2,1,0:T(8,128)S(1)}, u32[]{:S(2)}, u32[]{:S(2)}) async-start(f32[8,2,32,256]{3,2,1,0:T(8,128)} %split_kernel.1._), calls=%async_computation | async-start | bytes 1048576 | tf_op jit(solution)/shard_map/all_to_all | solution.py:419
  10.3 7.3 %collective-permute-start = (f32[2,64,256]{2,1,0:T(8,128)S(1)}, f32[2,64,256]{2,1,0:T(8,128)S(1)}, u32[]{:S(2)}, u32[]{:S(2)}) collective-permute-start(f32[2,64,256]{2,1,0:T(8,128)S(1)} %get-tuple-element.55), channel_id=1, source_target_pairs={{8,0},{16,8},{24,16},{32,24},{40,32},{48,40},{56,48},{64,56},{72,6... | collective-permute-start | bytes 393224 | tf_op jit(solution)/shard_map/ppermute | solution.py:400
  50.0 6.5 %collective-permute-start.1 = (f32[17,16,256]{2,1,0:T(8,128)S(1)}, f32[17,16,256]{2,1,0:T(8,128)S(1)}, u32[]{:S(2)}, u32[]{:S(2)}) collective-permute-start(f32[17,16,256]{2,1,0:T(8,128)S(1)} %get-tuple-element.61), channel_id=1, source_target_pairs={{0,8},{8,0},{1,9},{9,1},{2,10},{10,2},{3,11},{11,3},{4,12},{12,4},... | collective-permute-start | bytes 835592 | tf_op jit(solution)/shard_map/ppermute | solution.py:404
  56.5 10.5 %collective-permute-start.2 = (f32[17,8,256]{2,1,0:T(8,128)S(1)}, f32[17,8,256]{2,1,0:T(8,128)S(1)}, u32[]{:S(2)}, u32[]{:S(2)}) collective-permute-start(f32[17,8,256]{2,1,0:T(8,128)S(1)} %get-tuple-element.63), channel_id=1, source_target_pairs={{0,256},{256,0},{1,257},{257,1},{2,258},{258,2},{3,259},{259,3},{4... | collective-permute-start | bytes 417800 | tf_op jit(solution)/shard_map/ppermute | solution.py:404
  67.6 26.0 %all-to-all-start.3 = ((f32[16,3,8,128]{3,2,1,0:T(8,128)}), f32[16,3,8,128]{3,2,1,0:T(8,128)S(1)}, u32[]{:S(2)}, u32[]{:S(2)}) async-start(f32[16,3,8,128]{3,2,1,0:T(8,128)} %pack_kernel.3.refs_2_), calls=%async_computation.3 | async-start | bytes 393216 | tf_op jit(solution)/shard_map/all_to_all | solution.py:415
  84.6 5.7 %collective-permute-start.4 = (f32[2,32,256]{2,1,0:T(8,128)S(1)}, f32[2,32,256]{2,1,0:T(8,128)S(1)}, u32[]{:S(2)}, u32[]{:S(2)}) collective-permute-start(f32[2,32,256]{2,1,0:T(8,128)S(1)} %step_kernel.3.refs_2_), channel_id=1, source_target_pairs={{1,0},{2,1},{3,2},{7,3},{6,7},{5,6},{4,5},{9,8},{10,9},{11,10},{15... | collective-permute-start | bytes 196616 | tf_op jit(solution)/shard_map/ppermute | solution.py:410
  85.9 5.3 %collective-permute-start.3 = (f32[2,32,256]{2,1,0:T(8,128)S(1)}, f32[2,32,256]{2,1,0:T(8,128)S(1)}, u32[]{:S(2)}, u32[]{:S(2)}) collective-permute-start(f32[2,32,256]{2,1,0:T(8,128)S(1)} %step_kernel.3.refs_2_), channel_id=1, source_target_pairs={{0,1},{1,2},{2,3},{3,7},{7,6},{6,5},{5,4},{8,9},{9,10},{10,11},{11... | collective-permute-start | bytes 196616 | tf_op jit(solution)/shard_map/ppermute | solution.py:410
  94.3 21.8 %all-to-all-start.4 = ((f32[16,2,8,128]{3,2,1,0:T(8,128)}), f32[16,2,8,128]{3,2,1,0:T(8,128)S(1)}, u32[]{:S(2)}, u32[]{:S(2)}) async-start(f32[16,2,8,128]{3,2,1,0:T(8,128)} %get-tuple-element.67.refs_5_), calls=%async_computation.4 | async-start | bytes 262144 | tf_op jit(solution)/shard_map/all_to_all | solution.py:419
  102.2 10.0 %collective-permute-start.5 = (f32[2,64,256]{2,1,0:T(8,128)S(1)}, f32[2,64,256]{2,1,0:T(8,128)S(1)}, u32[]{:S(2)}, u32[]{:S(2)}) collective-permute-start(f32[2,64,256]{2,1,0:T(8,128)S(1)} %get-tuple-element.70), channel_id=1, source_target_pairs={{0,8},{8,16},{16,24},{24,32},{32,40},{40,48},{48,56},{56,64},{64,7... | collective-permute-start | bytes 393224 | tf_op jit(solution)/shard_map/ppermute | solution.py:400
  108.9 6.9 %collective-permute-start.6 = (f32[2,64,256]{2,1,0:T(8,128)S(1)}, f32[2,64,256]{2,1,0:T(8,128)S(1)}, u32[]{:S(2)}, u32[]{:S(2)}) collective-permute-start(f32[2,64,256]{2,1,0:T(8,128)S(1)} %get-tuple-element.71), channel_id=1, source_target_pairs={{8,0},{16,8},{24,16},{32,24},{40,32},{48,40},{56,48},{64,56},{72,6... | collective-permute-start | bytes 393224 | tf_op jit(solution)/shard_map/ppermute | solution.py:400
  154.9 5.5 %collective-permute-start.7 = (f32[17,16,256]{2,1,0:T(8,128)S(1)}, f32[17,16,256]{2,1,0:T(8,128)S(1)}, u32[]{:S(2)}, u32[]{:S(2)}) collective-permute-start(f32[17,16,256]{2,1,0:T(8,128)S(1)} %get-tuple-element.78), channel_id=1, source_target_pairs={{0,8},{8,0},{1,9},{9,1},{2,10},{10,2},{3,11},{11,3},{4,12},{12,4},... | collective-permute-start | bytes 835592 | tf_op jit(solution)/shard_map/ppermute | solution.py:404
  160.5 6.8 %collective-permute-start.8 = (f32[17,8,256]{2,1,0:T(8,128)S(1)}, f32[17,8,256]{2,1,0:T(8,128)S(1)}, u32[]{:S(2)}, u32[]{:S(2)}) collective-permute-start(f32[17,8,256]{2,1,0:T(8,128)S(1)} %get-tuple-element.80), channel_id=1, source_target_pairs={{0,256},{256,0},{1,257},{257,1},{2,258},{258,2},{3,259},{259,3},{4... | collective-permute-start | bytes 417800 | tf_op jit(solution)/shard_map/ppermute | solution.py:404
  168.0 20.5 %all-to-all-start.7 = ((f32[16,3,8,128]{3,2,1,0:T(8,128)}), f32[16,3,8,128]{3,2,1,0:T(8,128)S(1)}, u32[]{:S(2)}, u32[]{:S(2)}) async-start(f32[16,3,8,128]{3,2,1,0:T(8,128)} %pack_kernel.4.refs_2_), calls=%async_computation.7 | async-start | bytes 393216 | tf_op jit(solution)/shard_map/all_to_all | solution.py:415
  179.4 5.7 %collective-permute-start.10 = (f32[2,32,256]{2,1,0:T(8,128)S(1)}, f32[2,32,256]{2,1,0:T(8,128)S(1)}, u32[]{:S(2)}, u32[]{:S(2)}) collective-permute-start(f32[2,32,256]{2,1,0:T(8,128)S(1)} %step_kernel.4.refs_2_), channel_id=1, source_target_pairs={{1,0},{2,1},{3,2},{7,3},{6,7},{5,6},{4,5},{9,8},{10,9},{11,10},{15... | collective-permute-start | bytes 196616 | tf_op jit(solution)/shard_map/ppermute | solution.py:410
  180.7 5.3 %collective-permute-start.9 = (f32[2,32,256]{2,1,0:T(8,128)S(1)}, f32[2,32,256]{2,1,0:T(8,128)S(1)}, u32[]{:S(2)}, u32[]{:S(2)}) collective-permute-start(f32[2,32,256]{2,1,0:T(8,128)S(1)} %step_kernel.4.refs_2_), channel_id=1, source_target_pairs={{0,1},{1,2},{2,3},{3,7},{7,6},{6,5},{5,4},{8,9},{9,10},{10,11},{11... | collective-permute-start | bytes 196616 | tf_op jit(solution)/shard_map/ppermute | solution.py:410
  189.1 21.8 %all-to-all-start.8 = ((f32[16,2,8,128]{3,2,1,0:T(8,128)}), f32[16,2,8,128]{3,2,1,0:T(8,128)S(1)}, u32[]{:S(2)}, u32[]{:S(2)}) async-start(f32[16,2,8,128]{3,2,1,0:T(8,128)} %get-tuple-element.85.refs_5_), calls=%async_computation.8 | async-start | bytes 262144 | tf_op jit(solution)/shard_map/all_to_all | solution.py:419
  197.0 10.0 %collective-permute-start.11 = (f32[2,64,256]{2,1,0:T(8,128)S(1)}, f32[2,64,256]{2,1,0:T(8,128)S(1)}, u32[]{:S(2)}, u32[]{:S(2)}) collective-permute-start(f32[2,64,256]{2,1,0:T(8,128)S(1)} %get-tuple-element.88), channel_id=1, source_target_pairs={{0,8},{8,16},{16,24},{24,32},{32,40},{40,48},{48,56},{56,64},{64,7... | collective-permute-start | bytes 393224 | tf_op jit(solution)/shard_map/ppermute | solution.py:400
  203.7 6.9 %collective-permute-start.12 = (f32[2,64,256]{2,1,0:T(8,128)S(1)}, f32[2,64,256]{2,1,0:T(8,128)S(1)}, u32[]{:S(2)}, u32[]{:S(2)}) collective-permute-start(f32[2,64,256]{2,1,0:T(8,128)S(1)} %get-tuple-element.89), channel_id=1, source_target_pairs={{8,0},{16,8},{24,16},{32,24},{40,32},{48,40},{56,48},{64,56},{72,6... | collective-permute-start | bytes 393224 | tf_op jit(solution)/shard_map/ppermute | solution.py:400
  250.5 5.5 %collective-permute-start.13 = (f32[17,16,256]{2,1,0:T(8,128)S(1)}, f32[17,16,256]{2,1,0:T(8,128)S(1)}, u32[]{:S(2)}, u32[]{:S(2)}) collective-permute-start(f32[17,16,256]{2,1,0:T(8,128)S(1)} %get-tuple-element.96), channel_id=1, source_target_pairs={{0,8},{8,0},{1,9},{9,1},{2,10},{10,2},{3,11},{11,3},{4,12},{12,4},... | collective-permute-start | bytes 835592 | tf_op jit(solution)/shard_map/ppermute | solution.py:404
  256.1 8.8 %collective-permute-start.14 = (f32[17,8,256]{2,1,0:T(8,128)S(1)}, f32[17,8,256]{2,1,0:T(8,128)S(1)}, u32[]{:S(2)}, u32[]{:S(2)}) collective-permute-start(f32[17,8,256]{2,1,0:T(8,128)S(1)} %get-tuple-element.98), channel_id=1, source_target_pairs={{0,256},{256,0},{1,257},{257,1},{2,258},{258,2},{3,259},{259,3},{4... | collective-permute-start | bytes 417800 | tf_op jit(solution)/shard_map/ppermute | solution.py:404
  258.3 5.3 %collective-permute-start.16 = (f32[2,32,256]{2,1,0:T(8,128)S(1)}, f32[2,32,256]{2,1,0:T(8,128)S(1)}, u32[]{:S(2)}, u32[]{:S(2)}) collective-permute-start(f32[2,32,256]{2,1,0:T(8,128)S(1)} %step_kernel.5.refs_2_), channel_id=1, source_target_pairs={{1,0},{2,1},{3,2},{7,3},{6,7},{5,6},{4,5},{9,8},{10,9},{11,10},{15... | collective-permute-start | bytes 196616 | tf_op jit(solution)/shard_map/ppermute | solution.py:410
  259.6 5.3 %collective-permute-start.15 = (f32[2,32,256]{2,1,0:T(8,128)S(1)}, f32[2,32,256]{2,1,0:T(8,128)S(1)}, u32[]{:S(2)}, u32[]{:S(2)}) collective-permute-start(f32[2,32,256]{2,1,0:T(8,128)S(1)} %step_kernel.5.refs_2_), channel_id=1, source_target_pairs={{0,1},{1,2},{2,3},{3,7},{7,6},{6,5},{5,4},{8,9},{9,10},{10,11},{11... | collective-permute-start | bytes 196616 | tf_op jit(solution)/shard_map/ppermute | solution.py:410
  265.6 22.1 %all-to-all-start.11 = ((f32[16,3,8,128]{3,2,1,0:T(8,128)}), f32[16,3,8,128]{3,2,1,0:T(8,128)S(1)}, u32[]{:S(2)}, u32[]{:S(2)}) async-start(f32[16,3,8,128]{3,2,1,0:T(8,128)} %pack_kernel.5.refs_5_), calls=%async_computation.11 | async-start | bytes 393216 | tf_op jit(solution)/shard_map/all_to_all | solution.py:415
  278.0 9.6 %collective-permute-start.17 = (f32[2,64,256]{2,1,0:T(8,128)S(1)}, f32[2,64,256]{2,1,0:T(8,128)S(1)}, u32[]{:S(2)}, u32[]{:S(2)}) collective-permute-start(f32[2,64,256]{2,1,0:T(8,128)S(1)} %get-tuple-element.104), channel_id=1, source_target_pairs={{0,8},{8,16},{16,24},{24,32},{32,40},{40,48},{48,56},{56,64},{64,7... | collective-permute-start | bytes 393224 | tf_op jit(solution)/shard_map/ppermute | solution.py:400

commit v8 on v7

--- a/solution.py
+++ b/solution.py
@@ -28,6 +28,7 @@
 LANES = 128
 COL_SPAN = SIDE + LANES
 OUT_ROWS = 40
+PROBE_ROWS = 64
 VMEM_LIMIT = 16 * 1024 * 1024
 
 TILE_AXES = ("xlo", "z", "core")
@@ -181,7 +182,7 @@
             for mode in range(MODES):
                 for half in range(2):
                     lanes = slice(half * LANES, (half + 1) * LANES)
-                    piece = pieces[xlo, core, 2 * mode + half]
+                    piece = pieces[core, xlo, 2 * mode + half]
                     probe[mode, :, row : row + 8, lanes] = piece
     forward(view, probe, tables, spectra)
 
@@ -295,8 +296,8 @@
         total = total + sums[ring]
     new = shard_in[...] + PROBE_RATE * total[:2] / (total[2:] + PROBE_DAMP)
     shard[...] = new
-    for ring in range(RINGS):
-        copies[ring] = new
+    for place in range(2 * RINGS):
+        copies[place] = new
 
 
 def out_rows_kernel(scal, part_band, from_left, rows_out):
@@ -307,13 +308,14 @@
 
 def tail_kernel(piece, rows_out, tail):
     for place in range(MODES):
-        for half in range(2):
-            for part in range(2):
-                row = (half * 2 + part) * 8
-                tail[place, row : row + 8] = piece[2 * place + half, part]
+        for xlo in range(2):
+            for half in range(2):
+                for part in range(2):
+                    row = ((xlo * 2 + half) * 2 + part) * 8
+                    tail[place, row : row + 8] = piece[xlo * RINGS + 2 * place + half, part]
         for part in range(2):
             for block in range(WIDTH // LANES):
-                row = 32 + (part * 4 + block) * OUT_ROWS
+                row = PROBE_ROWS + (part * 4 + block) * OUT_ROWS
                 lanes = slice(block * LANES, (block + 1) * LANES)
                 tail[place, row : row + OUT_ROWS] = rows_out[part, :, lanes]
 
@@ -323,7 +325,7 @@
         first = slab_of(place) * 9 // 2 * 8
         for part in range(2):
             for block in range(WIDTH // LANES):
-                row = 32 + (part * 4 + block) * OUT_ROWS
+                row = PROBE_ROWS + (part * 4 + block) * OUT_ROWS
                 lanes = slice(block * LANES, (block + 1) * LANES)
                 object_out[part, first : first + OUT_ROWS, lanes] = tail[
                     place, row : row + OUT_ROWS
@@ -338,9 +340,9 @@
                 for half in range(2):
                     lanes = slice(half * LANES, (half + 1) * LANES)
                     for part in range(2):
-                        row = (half * 2 + part) * 8
+                        row = ((xlo * 2 + half) * 2 + part) * 8
                         probe_out[0, part, first : first + 8, lanes] = pieces[
-                            xlo, core, place, row : row + 8
+                            core, place, row : row + 8
                         ]
 
 
@@ -417,11 +419,6 @@
 
 def exchange(value, axes):
     return lax.all_to_all(value, axes, 0, 0, tiled=True)
-
-
-def gather_pieces(piece):
-    gathered = lax.all_gather(piece, ("xlo", "core"))
-    return gathered.reshape((2, 2) + piece.shape)
 
 
 def per_device(
@@ -535,13 +532,13 @@
             before = (above, below, counts)
         shard, shards = call(
             probe_kernel,
-            [(2, 8, LANES), (RINGS, 2, 8, LANES)],
+            [(2, 8, LANES), (2 * RINGS, 2, 8, LANES)],
             sums,
             shard,
             scalars=False,
             after=before,
         )
-        piece = exchange(shards, "z")
+        piece = exchange(shards, ("xlo", "z"))
         if not final:
             part_band, to_left, to_right = call(
                 place_kernel, [band_shape, edge, edge], *placing, after=(shards,)
@@ -557,13 +554,13 @@
                 from_right,
             )
             piece, view = lax.optimization_barrier((piece, view))
-            pieces = gather_pieces(piece)
-    tail_rows = 32 + 8 * OUT_ROWS
+            pieces = lax.all_gather(piece, "core").reshape(2, 2, RINGS, 2, 8, LANES)
+    tail_rows = PROBE_ROWS + 8 * OUT_ROWS
     (tail,) = call(
         tail_kernel, [(MODES, tail_rows, LANES)], piece, rows_out, scalars=False
     )
     tail = exchange(tail, MODE_AXES)
-    pieces = gather_pieces(tail[:, :32])
+    pieces = lax.all_gather(tail[:, :PROBE_ROWS], "core")
     (object_out,) = call(object_kernel, [(2, HEIGHT, WIDTH)], tail, scalars=False)
     (probe_out,) = call(probe_out_kernel, [(1, 2, SIDE, SIDE)], pieces, scalars=False)
     return object_out, probe_out

time: 344 us -> 353 us (1.026)
  waiting for transfers between devices: 36.2 us -> 43.6 us
    all_to_all x8, blocking collectives: 117 us -> 125 us  [exchange(): return lax.all_to_all(value, axes, 0, 0, tiled=True)]
    all_gather x3, blocking collectives: 33.3 us -> 27.5 us  [the longest x2 17.5 us: per_device(): pieces = lax.all_gather(piece, 'core').reshape(2, 2, RINGS, 2, 8, LANES)]
    all_to_all x3, waiting for transfers between devices: 1.43 us -> 5.13 us  [exchange(): return lax.all_to_all(value, axes, 0, 0, tiled=True)]
  transfers between devices with their start and end apart: 24 -> 24, of which waited for: 17 -> 19; matrix products, arithmetic and copies ran while one was open for 0% -> 0% of each run, Pallas kernels for 1% -> 1%
where the time goes in v8:
time: 353 us; the launch traced here: 352 us
  blocking collectives  152 us (43%)
  starting transfers between devices  131 us (37%)
  waiting for transfers between devices  43.6 us (12%)
  Pallas kernels  21.3 us (6%)
    all_to_all x8, blocking collectives, exchange(): return lax.all_to_all(value, axes, 0, 0, tiled=True)  125 us
    all_to_all x3, starting transfers between devices, exchange_rings(): lax.all_to_all(value, 'z', 0, 0, tiled=True, axis_index_groups=groups)  40 us
    ppermute x6, starting transfers between devices, shift(): lax.ppermute(value, axes, [(i, i + steps) for i in range(first, last)])  26.1 us
    ppermute x6, starting transfers between devices, other(): return lax.ppermute(value, axis, [(0, 1), (1, 0)])  25.7 us
    all_to_all x3, starting transfers between devices, exchange(): return lax.all_to_all(value, axes, 0, 0, tiled=True)  23.7 us
    pallas_call x34, Pallas kernels, call(): pl.pallas_call(body, out_shape=[jax.ShapeDtypeStruct(shape, F32) for shap...  21.2 us
    ppermute x6, waiting for transfers between devices, shift(): lax.ppermute(value, axes, [(i, i + steps) for i in range(first, last)])  19.2 us
    all_gather x2, blocking collectives, per_device(): pieces = lax.all_gather(piece, 'core').reshape(2, 2, RINGS, 2, 8, LANES)  17.5 us
  transfers between devices with their start and end apart: 24, of which 19 were waited for; matrix products, arithmetic and copies ran while one was open for 0% of the time, Pallas kernels for 1%

profile of v8, /device:TPU:1, one launch (start us, length us, event | category | flops | bytes accessed | tf_op | source)
XLA Modules:
  0.0 351.8 jit_solution(15460572226275508289)
XLA Ops:
  0.6 1.1 copy-done.3
  2.6 7.6 %all-to-all-start = ((f32[8,2,32,256]{3,2,1,0:T(8,128)}), f32[8,2,32,256]{3,2,1,0:T(8,128)S(1)}, u32[]{:S(2)}, u32[]{:S(2)}) async-start(f32[8,2,32,256]{3,2,1,0:T(8,128)} %split_kernel.1._), calls=%async_computation | async-start | bytes 1048576 | tf_op jit(solution)/shard_map/all_to_all | solution.py:421
  10.3 4.8 %collective-permute-start = (f32[2,64,256]{2,1,0:T(8,128)S(1)}, f32[2,64,256]{2,1,0:T(8,128)S(1)}, u32[]{:S(2)}, u32[]{:S(2)}) collective-permute-start(f32[2,64,256]{2,1,0:T(8,128)S(1)} %get-tuple-element.55), channel_id=1, source_target_pairs={{8,0},{16,8},{24,16},{32,24},{40,32},{48,40},{56,48},{64,56},{72,6... | collective-permute-start | bytes 393224 | tf_op jit(solution)/shard_map/ppermute | solution.py:402
  17.7 1.4 all-to-all-done.refs_3_.refs_1_
  19.1 1.1 first_kernel.1
  20.2 14.8 %all_to_all.70.refs_0_ = f32[8,2,32,256]{3,2,1,0:T(8,128)S(1)} all-to-all(f32[8,2,32,256]{3,2,1,0:T(8,128)S(1)} %get-tuple-element.57), channel_id=1, replica_groups=mesh['xlo'=2,'z'=16,'core'=2,'xhi'=2,'y'=4] {'xhi','y'}, dimensions={0} | all-to-all | bytes 1048576 | tf_op jit(solution)/shard_map/all_to_all | solution.py:421
  35.0 1.7 ratio_kernel.3
  36.7 12.4 %all_to_all.71.refs_0_ = f32[8,2,32,256]{3,2,1,0:T(8,128)S(1)} all-to-all(f32[8,2,32,256]{3,2,1,0:T(8,128)S(1)} %ratio_kernel.3), channel_id=1, replica_groups=mesh['xlo'=2,'z'=16,'core'=2,'xhi'=2,'y'=4] {'xhi','y'}, dimensions={0} | all-to-all | bytes 1048576 | tf_op jit(solution)/shard_map/all_to_all | solution.py:421
  49.1 0.8 backward_kernel.3
  50.0 5.3 %collective-permute-start.1 = (f32[17,16,256]{2,1,0:T(8,128)S(1)}, f32[17,16,256]{2,1,0:T(8,128)S(1)}, u32[]{:S(2)}, u32[]{:S(2)}) collective-permute-start(f32[17,16,256]{2,1,0:T(8,128)S(1)} %get-tuple-element.61), channel_id=1, source_target_pairs={{0,8},{8,0},{1,9},{9,1},{2,10},{10,2},{3,11},{11,3},{4,12},{12,4},... | collective-permute-start | bytes 835592 | tf_op jit(solution)/shard_map/ppermute | solution.py:406
  55.3 1.2 collective-permute-done.1.refs_1_
  56.5 6.7 %collective-permute-start.2 = (f32[17,8,256]{2,1,0:T(8,128)S(1)}, f32[17,8,256]{2,1,0:T(8,128)S(1)}, u32[]{:S(2)}, u32[]{:S(2)}) collective-permute-start(f32[17,8,256]{2,1,0:T(8,128)S(1)} %get-tuple-element.63), channel_id=1, source_target_pairs={{0,256},{256,0},{1,257},{257,1},{2,258},{258,2},{3,259},{259,3},{4... | collective-permute-start | bytes 417800 | tf_op jit(solution)/shard_map/ppermute | solution.py:406
  63.4 3.6 %collective-permute-done.2.refs_1_ = f32[17,8,256]{2,1,0:T(8,128)S(1)} collective-permute-done((f32[17,8,256]{2,1,0:T(8,128)S(1)}, f32[17,8,256]{2,1,0:T(8,128)S(1)}, u32[]{:S(2)}, u32[]{:S(2)}) %collective-permute-start.2) | collective-permute-done | bytes 139296 | tf_op jit(solution)/shard_map/ppermute | solution.py:406
  67.6 17.0 %all-to-all-start.3 = ((f32[16,3,8,128]{3,2,1,0:T(8,128)}), f32[16,3,8,128]{3,2,1,0:T(8,128)S(1)}, u32[]{:S(2)}, u32[]{:S(2)}) async-start(f32[16,3,8,128]{3,2,1,0:T(8,128)} %pack_kernel.3.refs_2_), calls=%async_computation.3 | async-start | bytes 393216 | tf_op jit(solution)/shard_map/all_to_all | solution.py:417
  84.6 1.3 collective-permute-start.4
  85.9 4.0 %collective-permute-start.3 = (f32[2,32,256]{2,1,0:T(8,128)S(1)}, f32[2,32,256]{2,1,0:T(8,128)S(1)}, u32[]{:S(2)}, u32[]{:S(2)}) collective-permute-start(f32[2,32,256]{2,1,0:T(8,128)S(1)} %step_kernel.3.refs_2_), channel_id=1, source_target_pairs={{0,1},{1,2},{2,3},{3,7},{7,6},{6,5},{5,4},{8,9},{9,10},{10,11},{11... | collective-permute-start | bytes 196616 | tf_op jit(solution)/shard_map/ppermute | solution.py:412
  90.3 0.9 collective-permute-done.3.refs_2_.refs_1_
  91.2 2.4 all-to-all-done.3.refs_0_
  94.4 8.0 %all-to-all-start.4 = ((f32[32,2,8,128]{3,2,1,0:T(8,128)}), f32[32,2,8,128]{3,2,1,0:T(8,128)S(1)}, u32[]{:S(2)}, u32[]{:S(2)}) async-start(f32[32,2,8,128]{3,2,1,0:T(8,128)} %get-tuple-element.67.refs_5_), calls=%async_computation.4 | async-start | bytes 524288 | tf_op jit(solution)/shard_map/all_to_all | solution.py:421
  102.7 6.5 %collective-permute-start.5 = (f32[2,64,256]{2,1,0:T(8,128)S(1)}, f32[2,64,256]{2,1,0:T(8,128)S(1)}, u32[]{:S(2)}, u32[]{:S(2)}) collective-permute-start(f32[2,64,256]{2,1,0:T(8,128)S(1)} %get-tuple-element.70), channel_id=1, source_target_pairs={{0,8},{8,16},{16,24},{24,32},{32,40},{40,48},{48,56},{56,64},{64,7... | collective-permute-start | bytes 393224 | tf_op jit(solution)/shard_map/ppermute | solution.py:402
  109.2 1.9 collective-permute-start.6
  111.1 4.5 %collective-permute-done.5.refs_2_ = f32[2,64,256]{2,1,0:T(8,128)S(1)} collective-permute-done((f32[2,64,256]{2,1,0:T(8,128)S(1)}, f32[2,64,256]{2,1,0:T(8,128)S(1)}, u32[]{:S(2)}, u32[]{:S(2)}) %collective-permute-start.5) | collective-permute-done | bytes 131104 | tf_op jit(solution)/shard_map/ppermute | solution.py:402
  115.7 2.1 collective-permute-done.6.refs_3_
  118.0 1.8 all-to-all-done.4
  119.9 8.8 %all-gather = f32[64,2,8,128]{3,2,1,0:T(8,128)S(1)} all-gather(f32[32,2,8,128]{3,2,1,0:T(8,128)S(1)} %all-to-all-done.4), channel_id=2, replica_groups=mesh['xlo'=2,'z'=16,'core'=2,'xhi'=2,'y'=4] {'core'}, dimensions={0}, use_global_device_ids=true | all-gather | bytes 786432 | tf_op jit(solution)/shard_map/all_gather | solution.py:557
  128.7 0.9 next_kernel.2
  129.5 12.5 %all_to_all.72.refs_0_ = f32[8,2,32,256]{3,2,1,0:T(8,128)S(1)} all-to-all(f32[8,2,32,256]{3,2,1,0:T(8,128)S(1)} %get-tuple-element.75), channel_id=1, replica_groups=mesh['xlo'=2,'z'=16,'core'=2,'xhi'=2,'y'=4] {'xhi','y'}, dimensions={0} | all-to-all | bytes 1048576 | tf_op jit(solution)/shard_map/all_to_all | solution.py:421
  142.1 1.7 ratio_kernel.4
  143.8 13.8 %all_to_all.73.refs_0_ = f32[8,2,32,256]{3,2,1,0:T(8,128)S(1)} all-to-all(f32[8,2,32,256]{3,2,1,0:T(8,128)S(1)} %ratio_kernel.4), channel_id=1, replica_groups=mesh['xlo'=2,'z'=16,'core'=2,'xhi'=2,'y'=4] {'xhi','y'}, dimensions={0} | all-to-all | bytes 1048576 | tf_op jit(solution)/shard_map/all_to_all | solution.py:421
  158.5 4.5 %collective-permute-start.7 = (f32[17,16,256]{2,1,0:T(8,128)S(1)}, f32[17,16,256]{2,1,0:T(8,128)S(1)}, u32[]{:S(2)}, u32[]{:S(2)}) collective-permute-start(f32[17,16,256]{2,1,0:T(8,128)S(1)} %get-tuple-element.78), channel_id=1, source_target_pairs={{0,8},{8,0},{1,9},{9,1},{2,10},{10,2},{3,11},{11,3},{4,12},{12,4},... | collective-permute-start | bytes 835592 | tf_op jit(solution)/shard_map/ppermute | solution.py:406
  162.9 1.2 collective-permute-done.7.refs_1_
  164.1 2.4 collective-permute-start.8
  166.7 4.2 %collective-permute-done.8.refs_1_ = f32[17,8,256]{2,1,0:T(8,128)S(1)} collective-permute-done((f32[17,8,256]{2,1,0:T(8,128)S(1)}, f32[17,8,256]{2,1,0:T(8,128)S(1)}, u32[]{:S(2)}, u32[]{:S(2)}) %collective-permute-start.8) | collective-permute-done | bytes 139296 | tf_op jit(solution)/shard_map/ppermute | solution.py:406
  171.6 11.5 %all-to-all-start.7 = ((f32[16,3,8,128]{3,2,1,0:T(8,128)}), f32[16,3,8,128]{3,2,1,0:T(8,128)S(1)}, u32[]{:S(2)}, u32[]{:S(2)}) async-start(f32[16,3,8,128]{3,2,1,0:T(8,128)} %pack_kernel.4.refs_2_), calls=%async_computation.7 | async-start | bytes 393216 | tf_op jit(solution)/shard_map/all_to_all | solution.py:417
  183.1 1.3 collective-permute-start.10
  184.4 4.0 %collective-permute-start.9 = (f32[2,32,256]{2,1,0:T(8,128)S(1)}, f32[2,32,256]{2,1,0:T(8,128)S(1)}, u32[]{:S(2)}, u32[]{:S(2)}) collective-permute-start(f32[2,32,256]{2,1,0:T(8,128)S(1)} %step_kernel.4.refs_2_), channel_id=1, source_target_pairs={{0,1},{1,2},{2,3},{3,7},{7,6},{6,5},{5,4},{8,9},{9,10},{10,11},{11... | collective-permute-start | bytes 196616 | tf_op jit(solution)/shard_map/ppermute | solution.py:412
  188.7 0.9 collective-permute-done.9.refs_2_.refs_1_
  189.7 2.4 all-to-all-done.7.refs_0_
  192.8 8.1 %all-to-all-start.8 = ((f32[32,2,8,128]{3,2,1,0:T(8,128)}), f32[32,2,8,128]{3,2,1,0:T(8,128)S(1)}, u32[]{:S(2)}, u32[]{:S(2)}) async-start(f32[32,2,8,128]{3,2,1,0:T(8,128)} %get-tuple-element.85.refs_5_), calls=%async_computation.8 | async-start | bytes 524288 | tf_op jit(solution)/shard_map/all_to_all | solution.py:421
  201.2 6.6 %collective-permute-start.11 = (f32[2,64,256]{2,1,0:T(8,128)S(1)}, f32[2,64,256]{2,1,0:T(8,128)S(1)}, u32[]{:S(2)}, u32[]{:S(2)}) collective-permute-start(f32[2,64,256]{2,1,0:T(8,128)S(1)} %get-tuple-element.88), channel_id=1, source_target_pairs={{0,8},{8,16},{16,24},{24,32},{32,40},{40,48},{48,56},{56,64},{64,7... | collective-permute-start | bytes 393224 | tf_op jit(solution)/shard_map/ppermute | solution.py:402
  207.7 1.9 collective-permute-start.12
  209.7 4.4 %collective-permute-done.11.refs_2_ = f32[2,64,256]{2,1,0:T(8,128)S(1)} collective-permute-done((f32[2,64,256]{2,1,0:T(8,128)S(1)}, f32[2,64,256]{2,1,0:T(8,128)S(1)}, u32[]{:S(2)}, u32[]{:S(2)}) %collective-permute-start.11) | collective-permute-done | bytes 131104 | tf_op jit(solution)/shard_map/ppermute | solution.py:402
  214.1 2.1 collective-permute-done.12.refs_3_
  216.5 1.9 all-to-all-done.8
  218.4 8.8 %all-gather.1 = f32[64,2,8,128]{3,2,1,0:T(8,128)S(1)} all-gather(f32[32,2,8,128]{3,2,1,0:T(8,128)S(1)} %all-to-all-done.8), channel_id=3, replica_groups=mesh['xlo'=2,'z'=16,'core'=2,'xhi'=2,'y'=4] {'core'}, dimensions={0}, use_global_device_ids=true | all-gather | bytes 786432 | tf_op jit(solution)/shard_map/all_gather | solution.py:557
  227.1 0.9 next_kernel.3
  228.0 12.9 %all_to_all.74.refs_0_ = f32[8,2,32,256]{3,2,1,0:T(8,128)S(1)} all-to-all(f32[8,2,32,256]{3,2,1,0:T(8,128)S(1)} %get-tuple-element.93), channel_id=1, replica_groups=mesh['xlo'=2,'z'=16,'core'=2,'xhi'=2,'y'=4] {'xhi','y'}, dimensions={0} | all-to-all | bytes 1048576 | tf_op jit(solution)/shard_map/all_to_all | solution.py:421
  240.9 1.7 ratio_kernel.5
  242.6 13.2 %all_to_all.75.refs_0_ = f32[8,2,32,256]{3,2,1,0:T(8,128)S(1)} all-to-all(f32[8,2,32,256]{3,2,1,0:T(8,128)S(1)} %ratio_kernel.5), channel_id=1, replica_groups=mesh['xlo'=2,'z'=16,'core'=2,'xhi'=2,'y'=4] {'xhi','y'}, dimensions={0} | all-to-all | bytes 1048576 | tf_op jit(solution)/shard_map/all_to_all | solution.py:421
  255.8 0.8 backward_kernel.5
  256.7 4.8 %collective-permute-start.13 = (f32[17,16,256]{2,1,0:T(8,128)S(1)}, f32[17,16,256]{2,1,0:T(8,128)S(1)}, u32[]{:S(2)}, u32[]{:S(2)}) collective-permute-start(f32[17,16,256]{2,1,0:T(8,128)S(1)} %get-tuple-element.96), channel_id=1, source_target_pairs={{0,8},{8,0},{1,9},{9,1},{2,10},{10,2},{3,11},{11,3},{4,12},{12,4},... | collective-permute-start | bytes 835592 | tf_op jit(solution)/shard_map/ppermute | solution.py:406
  261.5 1.2 collective-permute-done.13.refs_1_
  262.7 2.0 collective-permute-start.14
  264.9 1.3 collective-permute-start.16
  266.2 4.0 %collective-permute-start.15 = (f32[2,32,256]{2,1,0:T(8,128)S(1)}, f32[2,32,256]{2,1,0:T(8,128)S(1)}, u32[]{:S(2)}, u32[]{:S(2)}) collective-permute-start(f32[2,32,256]{2,1,0:T(8,128)S(1)} %step_kernel.5.refs_2_), channel_id=1, source_target_pairs={{0,1},{1,2},{2,3},{3,7},{7,6},{6,5},{5,4},{8,9},{9,10},{10,11},{11... | collective-permute-start | bytes 196616 | tf_op jit(solution)/shard_map/ppermute | solution.py:412
  270.2 1.3 collective-permute-done.15.refs_2_.refs_1_
  272.2 11.5 %all-to-all-start.11 = ((f32[16,3,8,128]{3,2,1,0:T(8,128)}), f32[16,3,8,128]{3,2,1,0:T(8,128)S(1)}, u32[]{:S(2)}, u32[]{:S(2)}) async-start(f32[16,3,8,128]{3,2,1,0:T(8,128)} %pack_kernel.5.refs_5_), calls=%async_computation.11 | async-start | bytes 393216 | tf_op jit(solution)/shard_map/all_to_all | solution.py:417
  283.7 0.9 place_kernel.5
  284.6 4.4 %collective-permute-start.17 = (f32[2,64,256]{2,1,0:T(8,128)S(1)}, f32[2,64,256]{2,1,0:T(8,128)S(1)}, u32[]{:S(2)}, u32[]{:S(2)}) collective-permute-start(f32[2,64,256]{2,1,0:T(8,128)S(1)} %get-tuple-element.104), channel_id=1, source_target_pairs={{0,8},{8,16},{16,24},{24,32},{32,40},{40,48},{48,56},{56,64},{64,7... | collective-permute-start | bytes 393224 | tf_op jit(solution)/shard_map/ppermute | solution.py:402
  289.0 5.2 %collective-permute-done.17.refs_2_ = f32[2,64,256]{2,1,0:T(8,128)S(1)} collective-permute-done((f32[2,64,256]{2,1,0:T(8,128)S(1)}, f32[2,64,256]{2,1,0:T(8,128)S(1)}, u32[]{:S(2)}, u32[]{:S(2)}) %collective-permute-start.17) | collective-permute-done | bytes 131104 | tf_op jit(solution)/shard_map/ppermute | solution.py:402
  295.0 22.5 %all_to_all.76.refs_0_ = f32[32,2,8,128]{3,2,1,0:T(8,128)S(1)} all-to-all(f32[32,2,8,128]{3,2,1,0:T(8,128)S(1)} %get-tuple-element.105), channel_id=1, replica_groups=mesh['xlo'=2,'z'=16,'core'=2,'xhi'=2,'y'=4] {'xlo','z'}, dimensions={0} | all-to-all | bytes 524288 | tf_op jit(solution)/shard_map/all_to_all | solution.py:421
  317.6 22.4 %all_to_all.77.refs_0_ = f32[8,384,128]{2,1,0:T(8,128)S(1)} all-to-all(f32[8,384,128]{2,1,0:T(8,128)S(1)} %tail_kernel.1), channel_id=1, replica_groups=mesh['xlo'=2,'z'=16,'core'=2,'xhi'=2,'y'=4] {'xhi','y'}, dimensions={0} | all-to-all | bytes 3145728 | tf_op jit(solution)/shard_map/all_to_all | solution.py:421
  340.0 9.9 %all-gather.2 = f32[16,64,128]{2,1,0:T(8,128)S(1)} all-gather(f32[8,64,128]{2,1,0:T(8,128)S(1)} %slice.19), channel_id=4, replica_groups=mesh['xlo'=2,'z'=16,'core'=2,'xhi'=2,'y'=4] {'core'}, dimensions={0}, use_global_device_ids=true | all-gather | bytes 786432 | tf_op jit(solution)/shard_map/all_gather | solution.py:563
  350.7 1.1 object_kernel.1
  (58 shorter events, 11.2 us)
Async XLA Ops:
  0.6 9.6 %copy-start.2 = (f32[2,288,512]{2,1,0:T(8,128)S(1)}, f32[2,288,512]{2,1,0:T(8,128)}, u32[]{:S(2)}) copy-start(f32[2,288,512]{2,1,0:T(8,128)} %whole.1) | copy-start | bytes 3538948
  0.6 1.1 copy-start.3
  2.6 12.6 %copy-start.4 = (s32[1,3]{1,0:T(1,128)S(1)}, s32[1,3]{1,0:T(1,128)}, u32[]{:S(2)}) copy-start(s32[1,3]{1,0:T(1,128)} %param.14) | copy-start | bytes 40
  2.6 12.6 %copy-start.5 = (s32[1,3]{1,0:T(1,128)S(1)}, s32[1,3]{1,0:T(1,128)}, u32[]{:S(2)}) copy-start(s32[1,3]{1,0:T(1,128)} %param.12) | copy-start | bytes 40
  2.6 12.6 %copy-start.6 = (s32[1,3]{1,0:T(1,128)S(1)}, s32[1,3]{1,0:T(1,128)}, u32[]{:S(2)}) copy-start(s32[1,3]{1,0:T(1,128)} %param.11) | copy-start | bytes 40
  2.6 13.9 %copy-start.1 = (bf16[1,3,256,256]{3,2,1,0:T(8,128)(2,1)S(1)}, bf16[1,3,256,256]{3,2,1,0:T(8,128)(2,1)}, u32[]{:S(2)}) copy-start(bf16[1,3,256,256]{3,2,1,0:T(8,128)(2,1)} %refs_1_.5) | copy-start | bytes 1179652
  2.6 16.5 %copy-start = (bf16[2,2,256,256]{3,2,1,0:T(8,128)(2,1)S(1)}, bf16[2,2,256,256]{3,2,1,0:T(8,128)(2,1)}, u32[]{:S(2)}) copy-start(bf16[2,2,256,256]{3,2,1,0:T(8,128)(2,1)} %constant.35.clone.refs_4_.refs_3_.refs_2_) | copy-start | bytes 1572868
  2.6 16.5 %all-to-all-start = ((f32[8,2,32,256]{3,2,1,0:T(8,128)}), f32[8,2,32,256]{3,2,1,0:T(8,128)S(1)}, u32[]{:S(2)}, u32[]{:S(2)}) async-start(f32[8,2,32,256]{3,2,1,0:T(8,128)} %split_kernel.1._), calls=%async_computation | async-start | bytes 1048576 | tf_op jit(solution)/shard_map/all_to_all | solution.py:421
  10.3 7.3 %collective-permute-start = (f32[2,64,256]{2,1,0:T(8,128)S(1)}, f32[2,64,256]{2,1,0:T(8,128)S(1)}, u32[]{:S(2)}, u32[]{:S(2)}) collective-permute-start(f32[2,64,256]{2,1,0:T(8,128)S(1)} %get-tuple-element.55), channel_id=1, source_target_pairs={{8,0},{16,8},{24,16},{32,24},{40,32},{48,40},{56,48},{64,56},{72,6... | collective-permute-start | bytes 393224 | tf_op jit(solution)/shard_map/ppermute | solution.py:402
  50.0 6.5 %collective-permute-start.1 = (f32[17,16,256]{2,1,0:T(8,128)S(1)}, f32[17,16,256]{2,1,0:T(8,128)S(1)}, u32[]{:S(2)}, u32[]{:S(2)}) collective-permute-start(f32[17,16,256]{2,1,0:T(8,128)S(1)} %get-tuple-element.61), channel_id=1, source_target_pairs={{0,8},{8,0},{1,9},{9,1},{2,10},{10,2},{3,11},{11,3},{4,12},{12,4},... | collective-permute-start | bytes 835592 | tf_op jit(solution)/shard_map/ppermute | solution.py:406
  56.5 10.5 %collective-permute-start.2 = (f32[17,8,256]{2,1,0:T(8,128)S(1)}, f32[17,8,256]{2,1,0:T(8,128)S(1)}, u32[]{:S(2)}, u32[]{:S(2)}) collective-permute-start(f32[17,8,256]{2,1,0:T(8,128)S(1)} %get-tuple-element.63), channel_id=1, source_target_pairs={{0,256},{256,0},{1,257},{257,1},{2,258},{258,2},{3,259},{259,3},{4... | collective-permute-start | bytes 417800 | tf_op jit(solution)/shard_map/ppermute | solution.py:406
  67.6 26.0 %all-to-all-start.3 = ((f32[16,3,8,128]{3,2,1,0:T(8,128)}), f32[16,3,8,128]{3,2,1,0:T(8,128)S(1)}, u32[]{:S(2)}, u32[]{:S(2)}) async-start(f32[16,3,8,128]{3,2,1,0:T(8,128)} %pack_kernel.3.refs_2_), calls=%async_computation.3 | async-start | bytes 393216 | tf_op jit(solution)/shard_map/all_to_all | solution.py:417
  84.6 5.7 %collective-permute-start.4 = (f32[2,32,256]{2,1,0:T(8,128)S(1)}, f32[2,32,256]{2,1,0:T(8,128)S(1)}, u32[]{:S(2)}, u32[]{:S(2)}) collective-permute-start(f32[2,32,256]{2,1,0:T(8,128)S(1)} %step_kernel.3.refs_2_), channel_id=1, source_target_pairs={{1,0},{2,1},{3,2},{7,3},{6,7},{5,6},{4,5},{9,8},{10,9},{11,10},{15... | collective-permute-start | bytes 196616 | tf_op jit(solution)/shard_map/ppermute | solution.py:412
  85.9 5.3 %collective-permute-start.3 = (f32[2,32,256]{2,1,0:T(8,128)S(1)}, f32[2,32,256]{2,1,0:T(8,128)S(1)}, u32[]{:S(2)}, u32[]{:S(2)}) collective-permute-start(f32[2,32,256]{2,1,0:T(8,128)S(1)} %step_kernel.3.refs_2_), channel_id=1, source_target_pairs={{0,1},{1,2},{2,3},{3,7},{7,6},{6,5},{5,4},{8,9},{9,10},{10,11},{11... | collective-permute-start | bytes 196616 | tf_op jit(solution)/shard_map/ppermute | solution.py:412
  94.4 25.5 %all-to-all-start.4 = ((f32[32,2,8,128]{3,2,1,0:T(8,128)}), f32[32,2,8,128]{3,2,1,0:T(8,128)S(1)}, u32[]{:S(2)}, u32[]{:S(2)}) async-start(f32[32,2,8,128]{3,2,1,0:T(8,128)} %get-tuple-element.67.refs_5_), calls=%async_computation.4 | async-start | bytes 524288 | tf_op jit(solution)/shard_map/all_to_all | solution.py:421
  102.7 12.9 %collective-permute-start.5 = (f32[2,64,256]{2,1,0:T(8,128)S(1)}, f32[2,64,256]{2,1,0:T(8,128)S(1)}, u32[]{:S(2)}, u32[]{:S(2)}) collective-permute-start(f32[2,64,256]{2,1,0:T(8,128)S(1)} %get-tuple-element.70), channel_id=1, source_target_pairs={{0,8},{8,16},{16,24},{24,32},{32,40},{40,48},{48,56},{56,64},{64,7... | collective-permute-start | bytes 393224 | tf_op jit(solution)/shard_map/ppermute | solution.py:402
  109.2 8.6 %collective-permute-start.6 = (f32[2,64,256]{2,1,0:T(8,128)S(1)}, f32[2,64,256]{2,1,0:T(8,128)S(1)}, u32[]{:S(2)}, u32[]{:S(2)}) collective-permute-start(f32[2,64,256]{2,1,0:T(8,128)S(1)} %get-tuple-element.71), channel_id=1, source_target_pairs={{8,0},{16,8},{24,16},{32,24},{40,32},{48,40},{56,48},{64,56},{72,6... | collective-permute-start | bytes 393224 | tf_op jit(solution)/shard_map/ppermute | solution.py:402
  158.5 5.6 %collective-permute-start.7 = (f32[17,16,256]{2,1,0:T(8,128)S(1)}, f32[17,16,256]{2,1,0:T(8,128)S(1)}, u32[]{:S(2)}, u32[]{:S(2)}) collective-permute-start(f32[17,16,256]{2,1,0:T(8,128)S(1)} %get-tuple-element.78), channel_id=1, source_target_pairs={{0,8},{8,0},{1,9},{9,1},{2,10},{10,2},{3,11},{11,3},{4,12},{12,4},... | collective-permute-start | bytes 835592 | tf_op jit(solution)/shard_map/ppermute | solution.py:406
  164.1 6.8 %collective-permute-start.8 = (f32[17,8,256]{2,1,0:T(8,128)S(1)}, f32[17,8,256]{2,1,0:T(8,128)S(1)}, u32[]{:S(2)}, u32[]{:S(2)}) collective-permute-start(f32[17,8,256]{2,1,0:T(8,128)S(1)} %get-tuple-element.80), channel_id=1, source_target_pairs={{0,256},{256,0},{1,257},{257,1},{2,258},{258,2},{3,259},{259,3},{4... | collective-permute-start | bytes 417800 | tf_op jit(solution)/shard_map/ppermute | solution.py:406
  171.6 20.5 %all-to-all-start.7 = ((f32[16,3,8,128]{3,2,1,0:T(8,128)}), f32[16,3,8,128]{3,2,1,0:T(8,128)S(1)}, u32[]{:S(2)}, u32[]{:S(2)}) async-start(f32[16,3,8,128]{3,2,1,0:T(8,128)} %pack_kernel.4.refs_2_), calls=%async_computation.7 | async-start | bytes 393216 | tf_op jit(solution)/shard_map/all_to_all | solution.py:417
  183.1 5.7 %collective-permute-start.10 = (f32[2,32,256]{2,1,0:T(8,128)S(1)}, f32[2,32,256]{2,1,0:T(8,128)S(1)}, u32[]{:S(2)}, u32[]{:S(2)}) collective-permute-start(f32[2,32,256]{2,1,0:T(8,128)S(1)} %step_kernel.4.refs_2_), channel_id=1, source_target_pairs={{1,0},{2,1},{3,2},{7,3},{6,7},{5,6},{4,5},{9,8},{10,9},{11,10},{15... | collective-permute-start | bytes 196616 | tf_op jit(solution)/shard_map/ppermute | solution.py:412
  184.4 5.3 %collective-permute-start.9 = (f32[2,32,256]{2,1,0:T(8,128)S(1)}, f32[2,32,256]{2,1,0:T(8,128)S(1)}, u32[]{:S(2)}, u32[]{:S(2)}) collective-permute-start(f32[2,32,256]{2,1,0:T(8,128)S(1)} %step_kernel.4.refs_2_), channel_id=1, source_target_pairs={{0,1},{1,2},{2,3},{3,7},{7,6},{6,5},{5,4},{8,9},{9,10},{10,11},{11... | collective-permute-start | bytes 196616 | tf_op jit(solution)/shard_map/ppermute | solution.py:412
  192.8 25.5 %all-to-all-start.8 = ((f32[32,2,8,128]{3,2,1,0:T(8,128)}), f32[32,2,8,128]{3,2,1,0:T(8,128)S(1)}, u32[]{:S(2)}, u32[]{:S(2)}) async-start(f32[32,2,8,128]{3,2,1,0:T(8,128)} %get-tuple-element.85.refs_5_), calls=%async_computation.8 | async-start | bytes 524288 | tf_op jit(solution)/shard_map/all_to_all | solution.py:421
  201.2 12.9 %collective-permute-start.11 = (f32[2,64,256]{2,1,0:T(8,128)S(1)}, f32[2,64,256]{2,1,0:T(8,128)S(1)}, u32[]{:S(2)}, u32[]{:S(2)}) collective-permute-start(f32[2,64,256]{2,1,0:T(8,128)S(1)} %get-tuple-element.88), channel_id=1, source_target_pairs={{0,8},{8,16},{16,24},{24,32},{32,40},{40,48},{48,56},{56,64},{64,7... | collective-permute-start | bytes 393224 | tf_op jit(solution)/shard_map/ppermute | solution.py:402
  207.7 8.5 %collective-permute-start.12 = (f32[2,64,256]{2,1,0:T(8,128)S(1)}, f32[2,64,256]{2,1,0:T(8,128)S(1)}, u32[]{:S(2)}, u32[]{:S(2)}) collective-permute-start(f32[2,64,256]{2,1,0:T(8,128)S(1)} %get-tuple-element.89), channel_id=1, source_target_pairs={{8,0},{16,8},{24,16},{32,24},{40,32},{48,40},{56,48},{64,56},{72,6... | collective-permute-start | bytes 393224 | tf_op jit(solution)/shard_map/ppermute | solution.py:402
  256.7 6.0 %collective-permute-start.13 = (f32[17,16,256]{2,1,0:T(8,128)S(1)}, f32[17,16,256]{2,1,0:T(8,128)S(1)}, u32[]{:S(2)}, u32[]{:S(2)}) collective-permute-start(f32[17,16,256]{2,1,0:T(8,128)S(1)} %get-tuple-element.96), channel_id=1, source_target_pairs={{0,8},{8,0},{1,9},{9,1},{2,10},{10,2},{3,11},{11,3},{4,12},{12,4},... | collective-permute-start | bytes 835592 | tf_op jit(solution)/shard_map/ppermute | solution.py:406
  262.7 8.8 %collective-permute-start.14 = (f32[17,8,256]{2,1,0:T(8,128)S(1)}, f32[17,8,256]{2,1,0:T(8,128)S(1)}, u32[]{:S(2)}, u32[]{:S(2)}) collective-permute-start(f32[17,8,256]{2,1,0:T(8,128)S(1)} %get-tuple-element.98), channel_id=1, source_target_pairs={{0,256},{256,0},{1,257},{257,1},{2,258},{258,2},{3,259},{259,3},{4... | collective-permute-start | bytes 417800 | tf_op jit(solution)/shard_map/ppermute | solution.py:406
  264.9 5.3 %collective-permute-start.16 = (f32[2,32,256]{2,1,0:T(8,128)S(1)}, f32[2,32,256]{2,1,0:T(8,128)S(1)}, u32[]{:S(2)}, u32[]{:S(2)}) collective-permute-start(f32[2,32,256]{2,1,0:T(8,128)S(1)} %step_kernel.5.refs_2_), channel_id=1, source_target_pairs={{1,0},{2,1},{3,2},{7,3},{6,7},{5,6},{4,5},{9,8},{10,9},{11,10},{15... | collective-permute-start | bytes 196616 | tf_op jit(solution)/shard_map/ppermute | solution.py:412
  266.2 5.3 %collective-permute-start.15 = (f32[2,32,256]{2,1,0:T(8,128)S(1)}, f32[2,32,256]{2,1,0:T(8,128)S(1)}, u32[]{:S(2)}, u32[]{:S(2)}) collective-permute-start(f32[2,32,256]{2,1,0:T(8,128)S(1)} %step_kernel.5.refs_2_), channel_id=1, source_target_pairs={{0,1},{1,2},{2,3},{3,7},{7,6},{6,5},{5,4},{8,9},{9,10},{10,11},{11... | collective-permute-start | bytes 196616 | tf_op jit(solution)/shard_map/ppermute | solution.py:412
  272.2 22.1 %all-to-all-start.11 = ((f32[16,3,8,128]{3,2,1,0:T(8,128)}), f32[16,3,8,128]{3,2,1,0:T(8,128)S(1)}, u32[]{:S(2)}, u32[]{:S(2)}) async-start(f32[16,3,8,128]{3,2,1,0:T(8,128)} %pack_kernel.5.refs_5_), calls=%async_computation.11 | async-start | bytes 393216 | tf_op jit(solution)/shard_map/all_to_all | solution.py:417
  284.6 9.6 %collective-permute-start.17 = (f32[2,64,256]{2,1,0:T(8,128)S(1)}, f32[2,64,256]{2,1,0:T(8,128)S(1)}, u32[]{:S(2)}, u32[]{:S(2)}) collective-permute-start(f32[2,64,256]{2,1,0:T(8,128)S(1)} %get-tuple-element.104), channel_id=1, source_target_pairs={{0,8},{8,16},{16,24},{24,32},{32,40},{40,48},{48,56},{56,64},{64,7... | collective-permute-start | bytes 393224 | tf_op jit(solution)/shard_map/ppermute | solution.py:402

commit v9 on v7

--- a/solution.py
+++ b/solution.py
@@ -28,6 +28,7 @@
 LANES = 128
 COL_SPAN = SIDE + LANES
 OUT_ROWS = 40
+MESSAGE = 2 * MODES + 1
 VMEM_LIMIT = 16 * 1024 * 1024
 
 TILE_AXES = ("xlo", "z", "core")
@@ -156,33 +157,28 @@
     band[:, :, :WIDTH] = own[...]
     band[:, :, WIDTH:] = beside[...]
     take_patch(scal, band, view)
-    mode = scal[RING] // 2
     rows = pl.ds(pl.multiple_of(scal[CORE] * 16 + scal[XLO] * 8, 8), 8)
-
-    @pl.when(lax.rem(scal[RING], 2) == 0)
-    def _():
-        shard[...] = probe[mode, :, rows, :LANES]
-
-    @pl.when(lax.rem(scal[RING], 2) == 1)
-    def _():
-        shard[...] = probe[mode, :, rows, LANES:]
-
+    wanted = lax.broadcasted_iota(jnp.int32, (8, LANES), 0) == scal[RING] // 2
+    second = lax.rem(scal[RING], 2) == 1
+    for mode in range(MODES):
+        for part in range(2):
+            block = jnp.where(second, probe[mode, part, rows, LANES:], probe[mode, part, rows, :LANES])
+            index = 2 * mode + part
+            shard[index : index + 1] = jnp.sum(
+                jnp.where(wanted, block, 0.0), axis=0, keepdims=True
+            )
     forward(view, probe, tables, spectra)
-
-
-def far_place(ring):
-    return (ring + RINGS // 2) % RINGS
 
 
 def next_kernel(view, pieces, tables, probe, spectra):
     for xlo in range(2):
         for core in range(2):
             row = core * 16 + xlo * 8
-            for mode in range(MODES):
+            for index in range(2 * MODES):
                 for half in range(2):
                     lanes = slice(half * LANES, (half + 1) * LANES)
-                    piece = pieces[xlo, core, 2 * mode + half]
-                    probe[mode, :, row : row + 8, lanes] = piece
+                    piece = pieces[xlo, core, pl.ds(RINGS * half + index, 8, stride=2 * RINGS), :]
+                    probe[index // 2, index % 2, row : row + 8, lanes] = piece
     forward(view, probe, tables, spectra)
 
 
@@ -244,14 +240,11 @@
 
 
 def pack_kernel(mine, theirs, packed):
-    for half in range(2):
-        lanes = slice(half * LANES, (half + 1) * LANES)
-        total = mine[:, :, lanes] + theirs[:, :, lanes]
-        for mode in range(MODES):
-            place = far_place(2 * mode + half)
-            packed[place, 0] = total[2 * mode]
-            packed[place, 1] = total[2 * mode + 1]
-            packed[place, 2] = total[2 * MODES]
+    for index in range(MESSAGE):
+        total = pltpu.roll(mine[index] + theirs[index], RINGS // 4, 0)
+        for half in range(2):
+            rows = pl.ds(MESSAGE * half + index, 8, stride=2 * MESSAGE)
+            packed[rows, :] = total[:, half * LANES : (half + 1) * LANES]
 
 
 def step_kernel(chi, probe, step):
@@ -290,10 +283,11 @@
 
 
 def probe_kernel(sums, shard_in, shard, copies):
-    total = sums[0]
+    total = sums[:MESSAGE]
     for ring in range(1, RINGS):
-        total = total + sums[ring]
-    new = shard_in[...] + PROBE_RATE * total[:2] / (total[2:] + PROBE_DAMP)
+        total = total + sums[ring * MESSAGE : (ring + 1) * MESSAGE]
+    rows = 2 * MODES
+    new = shard_in[...] + PROBE_RATE * total[:rows] / (total[rows:] + PROBE_DAMP)
     shard[...] = new
     for ring in range(RINGS):
         copies[ring] = new
@@ -310,7 +304,8 @@
         for half in range(2):
             for part in range(2):
                 row = (half * 2 + part) * 8
-                tail[place, row : row + 8] = piece[2 * place + half, part]
+                rows = pl.ds(RINGS * half + 2 * place + part, 8, stride=2 * RINGS)
+                tail[place, row : row + 8] = piece[rows, :]
         for part in range(2):
             for block in range(WIDTH // LANES):
                 row = 32 + (part * 4 + block) * OUT_ROWS
@@ -411,8 +406,10 @@
 
 
 def exchange_rings(value):
-    groups = [[far_place(ring) for ring in range(RINGS)]]
-    return lax.all_to_all(value, "z", 0, 0, tiled=True, axis_index_groups=groups)
+    groups = [[(ring + RINGS // 2) % RINGS for ring in range(RINGS)]]
+    value = value.reshape(RINGS, 1, MESSAGE * LANES)
+    value = lax.all_to_all(value, "z", 0, 0, tiled=True, axis_index_groups=groups)
+    return value.reshape(RINGS * MESSAGE, LANES)
 
 
 def exchange(value, axes):
@@ -466,7 +463,7 @@
         if step == 0:
             band, view, shard, spectra = call(
                 first_kernel,
-                [band_shape, slab_pair, (2, 8, LANES), slabs],
+                [band_shape, slab_pair, (2 * MODES, LANES), slabs],
                 scal,
                 own,
                 beside,
@@ -510,7 +507,7 @@
         below = beside_slab(object_step, -1)
         (packed,) = call(
             pack_kernel,
-            [(RINGS, 3, 8, LANES)],
+            [(RINGS * MESSAGE, LANES)],
             keep,
             received,
             scalars=False,
@@ -535,7 +532,7 @@
             before = (above, below, counts)
         shard, shards = call(
             probe_kernel,
-            [(2, 8, LANES), (RINGS, 2, 8, LANES)],
+            [(2 * MODES, LANES), (RINGS, 2 * MODES, LANES)],
             sums,
             shard,
             scalars=False,
@@ -557,10 +554,14 @@
                 from_right,
             )
             piece, view = lax.optimization_barrier((piece, view))
-            pieces = gather_pieces(piece)
+            pieces = gather_pieces(piece.reshape(2 * MODES * RINGS, LANES))
     tail_rows = 32 + 8 * OUT_ROWS
     (tail,) = call(
-        tail_kernel, [(MODES, tail_rows, LANES)], piece, rows_out, scalars=False
+        tail_kernel,
+        [(MODES, tail_rows, LANES)],
+        piece.reshape(2 * MODES * RINGS, LANES),
+        rows_out,
+        scalars=False,
     )
     tail = exchange(tail, MODE_AXES)
     pieces = gather_pieces(tail[:, :32])

time: 344 us -> 338 us (0.983)
  waiting for transfers between devices: 36.2 us -> 28.8 us
    all_to_all x3, waiting for transfers between devices: 4.81 us -> 0.01 us  [exchange_rings(): lax.all_to_all(value, 'z', 0, 0, tiled=True, axis_index_groups=groups)]
  transfers between devices with their start and end apart: 24 -> 24, of which waited for: 17 -> 15; matrix products, arithmetic and copies ran while one was open for 0% -> 0% of each run, Pallas kernels for 1% -> 1%
where the time goes in v9:
time: 338 us; the launch traced here: 337 us
  blocking collectives  152 us (45%)
  starting transfers between devices  131 us (39%)
  waiting for transfers between devices  28.8 us (9%)
  Pallas kernels  21.6 us (6%)
    all_to_all x8, blocking collectives, exchange(): return lax.all_to_all(value, axes, 0, 0, tiled=True)  119 us
    all_to_all x3, starting transfers between devices, exchange_rings(): lax.all_to_all(value, 'z', 0, 0, tiled=True, axis_index_groups=groups)  40 us
    all_gather x3, blocking collectives, gather_pieces(): gathered = lax.all_gather(piece, ('xlo', 'core'))  32.3 us
    ppermute x6, starting transfers between devices, shift(): lax.ppermute(value, axes, [(i, i + steps) for i in range(first, last)])  27.6 us
    ppermute x6, starting transfers between devices, other(): return lax.ppermute(value, axis, [(0, 1), (1, 0)])  25.8 us
    all_to_all x3, starting transfers between devices, exchange(): return lax.all_to_all(value, axes, 0, 0, tiled=True)  22 us
    pallas_call x34, Pallas kernels, call(): pl.pallas_call(body, out_shape=[jax.ShapeDtypeStruct(shape, F32) for shap...  21.5 us
    ppermute x6, starting transfers between devices, beside_slab(): return lax.ppermute(value, MODE_AXES, pairs)  15.8 us
  transfers between devices with their start and end apart: 24, of which 15 were waited for; matrix products, arithmetic and copies ran while one was open for 0% of the time, Pallas kernels for 1%

profile of v9, /device:TPU:1, one launch (start us, length us, event | category | flops | bytes accessed | tf_op | source)
XLA Modules:
  0.0 336.9 jit_solution(9970910421946026989)
XLA Ops:
  0.6 1.1 copy-done.3
  1.8 0.8 split_kernel.1._
  2.6 7.6 %all-to-all-start = ((f32[8,2,32,256]{3,2,1,0:T(8,128)}), f32[8,2,32,256]{3,2,1,0:T(8,128)S(1)}, u32[]{:S(2)}, u32[]{:S(2)}) async-start(f32[8,2,32,256]{3,2,1,0:T(8,128)} %split_kernel.1._), calls=%async_computation | async-start | bytes 1048576 | tf_op jit(solution)/shard_map/all_to_all | solution.py:416
  10.3 4.8 %collective-permute-start = (f32[2,64,256]{2,1,0:T(8,128)S(1)}, f32[2,64,256]{2,1,0:T(8,128)S(1)}, u32[]{:S(2)}, u32[]{:S(2)}) collective-permute-start(f32[2,64,256]{2,1,0:T(8,128)S(1)} %get-tuple-element.55), channel_id=1, source_target_pairs={{8,0},{16,8},{24,16},{32,24},{40,32},{48,40},{56,48},{64,56},{72,6... | collective-permute-start | bytes 393224 | tf_op jit(solution)/shard_map/ppermute | solution.py:395
  16.9 0.8 collective-permute-done.refs_2_
  17.7 1.4 all-to-all-done.refs_3_.refs_1_
  19.1 1.1 first_kernel.1
  20.2 14.8 %all_to_all.70.refs_0_ = f32[8,2,32,256]{3,2,1,0:T(8,128)S(1)} all-to-all(f32[8,2,32,256]{3,2,1,0:T(8,128)S(1)} %get-tuple-element.57), channel_id=1, replica_groups=mesh['xlo'=2,'z'=16,'core'=2,'xhi'=2,'y'=4] {'xhi','y'}, dimensions={0} | all-to-all | bytes 1048576 | tf_op jit(solution)/shard_map/all_to_all | solution.py:416
  35.0 1.7 ratio_kernel.3
  36.7 12.4 %all_to_all.71.refs_0_ = f32[8,2,32,256]{3,2,1,0:T(8,128)S(1)} all-to-all(f32[8,2,32,256]{3,2,1,0:T(8,128)S(1)} %ratio_kernel.3), channel_id=1, replica_groups=mesh['xlo'=2,'z'=16,'core'=2,'xhi'=2,'y'=4] {'xhi','y'}, dimensions={0} | all-to-all | bytes 1048576 | tf_op jit(solution)/shard_map/all_to_all | solution.py:416
  49.1 0.8 backward_kernel.3
  50.0 5.3 %collective-permute-start.1 = (f32[17,16,256]{2,1,0:T(8,128)S(1)}, f32[17,16,256]{2,1,0:T(8,128)S(1)}, u32[]{:S(2)}, u32[]{:S(2)}) collective-permute-start(f32[17,16,256]{2,1,0:T(8,128)S(1)} %get-tuple-element.61), channel_id=1, source_target_pairs={{0,8},{8,0},{1,9},{9,1},{2,10},{10,2},{3,11},{11,3},{4,12},{12,4},... | collective-permute-start | bytes 835592 | tf_op jit(solution)/shard_map/ppermute | solution.py:399
  55.2 1.2 collective-permute-done.1.refs_1_
  56.4 6.7 %collective-permute-start.2 = (f32[17,8,256]{2,1,0:T(8,128)S(1)}, f32[17,8,256]{2,1,0:T(8,128)S(1)}, u32[]{:S(2)}, u32[]{:S(2)}) collective-permute-start(f32[17,8,256]{2,1,0:T(8,128)S(1)} %get-tuple-element.63), channel_id=1, source_target_pairs={{0,256},{256,0},{1,257},{257,1},{2,258},{258,2},{3,259},{259,3},{4... | collective-permute-start | bytes 417800 | tf_op jit(solution)/shard_map/ppermute | solution.py:399
  63.4 3.6 %collective-permute-done.2.refs_1_ = f32[17,8,256]{2,1,0:T(8,128)S(1)} collective-permute-done((f32[17,8,256]{2,1,0:T(8,128)S(1)}, f32[17,8,256]{2,1,0:T(8,128)S(1)}, u32[]{:S(2)}, u32[]{:S(2)}) %collective-permute-start.2) | collective-permute-done | bytes 139296 | tf_op jit(solution)/shard_map/ppermute | solution.py:399
  67.6 17.0 %all-to-all-start.3 = ((f32[16,1,2176]{2,1,0:T(1,128)}), f32[16,1,2176]{2,1,0:T(1,128)S(1)}, u32[]{:S(2)}, u32[]{:S(2)}) async-start(f32[16,1,2176]{2,1,0:T(1,128)} %bitcast.8), calls=%async_computation.3 | async-start | bytes 278528 | tf_op jit(solution)/shard_map/all_to_all | solution.py:411
  84.6 1.3 collective-permute-start.4
  85.9 4.0 %collective-permute-start.3 = (f32[2,32,256]{2,1,0:T(8,128)S(1)}, f32[2,32,256]{2,1,0:T(8,128)S(1)}, u32[]{:S(2)}, u32[]{:S(2)}) collective-permute-start(f32[2,32,256]{2,1,0:T(8,128)S(1)} %step_kernel.3.refs_2_), channel_id=1, source_target_pairs={{0,1},{1,2},{2,3},{3,7},{7,6},{6,5},{5,4},{8,9},{9,10},{10,11},{11... | collective-permute-start | bytes 196616 | tf_op jit(solution)/shard_map/ppermute | solution.py:405
  90.3 0.9 collective-permute-done.3.refs_2_.refs_1_
  91.9 7.2 %all-to-all-start.4 = ((f32[16,16,128]{2,1,0:T(8,128)}), f32[16,16,128]{2,1,0:T(8,128)S(1)}, u32[]{:S(2)}, u32[]{:S(2)}) async-start(f32[16,16,128]{2,1,0:T(8,128)} %get-tuple-element.67.refs_5_), calls=%async_computation.4 | async-start | bytes 262144 | tf_op jit(solution)/shard_map/all_to_all | solution.py:416
  99.4 7.3 %collective-permute-start.5 = (f32[2,64,256]{2,1,0:T(8,128)S(1)}, f32[2,64,256]{2,1,0:T(8,128)S(1)}, u32[]{:S(2)}, u32[]{:S(2)}) collective-permute-start(f32[2,64,256]{2,1,0:T(8,128)S(1)} %get-tuple-element.70), channel_id=1, source_target_pairs={{0,8},{8,16},{16,24},{24,32},{32,40},{40,48},{48,56},{56,64},{64,7... | collective-permute-start | bytes 393224 | tf_op jit(solution)/shard_map/ppermute | solution.py:395
  106.6 1.9 collective-permute-start.6
  108.6 1.3 collective-permute-done.5.refs_2_
  109.8 3.6 %collective-permute-done.6.refs_3_ = f32[2,64,256]{2,1,0:T(8,128)S(1)} collective-permute-done((f32[2,64,256]{2,1,0:T(8,128)S(1)}, f32[2,64,256]{2,1,0:T(8,128)S(1)}, u32[]{:S(2)}, u32[]{:S(2)}) %collective-permute-start.6) | collective-permute-done | bytes 131104 | tf_op jit(solution)/shard_map/ppermute | solution.py:395
  113.8 8.8 %all_gather.12 = f32[4,256,128]{2,1,0:T(8,128)S(1)} all-gather(f32[1,256,128]{2,1,0:T(8,128)S(1)} %bitcast.28), channel_id=1, replica_groups=mesh['xlo'=2,'z'=16,'core'=2,'xhi'=2,'y'=4] {'xlo','core'}, dimensions={0}, use_global_device_ids=true | all-gather | bytes 655360 | tf_op jit(solution)/shard_map/all_gather | solution.py:420
  122.6 1.1 next_kernel.2
  123.7 12.9 %all_to_all.72.refs_0_ = f32[8,2,32,256]{3,2,1,0:T(8,128)S(1)} all-to-all(f32[8,2,32,256]{3,2,1,0:T(8,128)S(1)} %get-tuple-element.75), channel_id=1, replica_groups=mesh['xlo'=2,'z'=16,'core'=2,'xhi'=2,'y'=4] {'xhi','y'}, dimensions={0} | all-to-all | bytes 1048576 | tf_op jit(solution)/shard_map/all_to_all | solution.py:416
  136.6 1.7 ratio_kernel.4
  138.3 13.8 %all_to_all.73.refs_0_ = f32[8,2,32,256]{3,2,1,0:T(8,128)S(1)} all-to-all(f32[8,2,32,256]{3,2,1,0:T(8,128)S(1)} %ratio_kernel.4), channel_id=1, replica_groups=mesh['xlo'=2,'z'=16,'core'=2,'xhi'=2,'y'=4] {'xhi','y'}, dimensions={0} | all-to-all | bytes 1048576 | tf_op jit(solution)/shard_map/all_to_all | solution.py:416
  152.1 0.8 backward_kernel.4
  153.0 4.4 %collective-permute-start.7 = (f32[17,16,256]{2,1,0:T(8,128)S(1)}, f32[17,16,256]{2,1,0:T(8,128)S(1)}, u32[]{:S(2)}, u32[]{:S(2)}) collective-permute-start(f32[17,16,256]{2,1,0:T(8,128)S(1)} %get-tuple-element.78), channel_id=1, source_target_pairs={{0,8},{8,0},{1,9},{9,1},{2,10},{10,2},{3,11},{11,3},{4,12},{12,4},... | collective-permute-start | bytes 835592 | tf_op jit(solution)/shard_map/ppermute | solution.py:399
  157.4 1.2 collective-permute-done.7.refs_1_
  158.5 2.8 collective-permute-start.8
  161.6 3.8 %collective-permute-done.8.refs_1_ = f32[17,8,256]{2,1,0:T(8,128)S(1)} collective-permute-done((f32[17,8,256]{2,1,0:T(8,128)S(1)}, f32[17,8,256]{2,1,0:T(8,128)S(1)}, u32[]{:S(2)}, u32[]{:S(2)}) %collective-permute-start.8) | collective-permute-done | bytes 139296 | tf_op jit(solution)/shard_map/ppermute | solution.py:399
  166.0 11.5 %all-to-all-start.7 = ((f32[16,1,2176]{2,1,0:T(1,128)}), f32[16,1,2176]{2,1,0:T(1,128)S(1)}, u32[]{:S(2)}, u32[]{:S(2)}) async-start(f32[16,1,2176]{2,1,0:T(1,128)} %bitcast.12), calls=%async_computation.7 | async-start | bytes 278528 | tf_op jit(solution)/shard_map/all_to_all | solution.py:411
  177.5 1.3 collective-permute-start.10
  178.8 4.0 %collective-permute-start.9 = (f32[2,32,256]{2,1,0:T(8,128)S(1)}, f32[2,32,256]{2,1,0:T(8,128)S(1)}, u32[]{:S(2)}, u32[]{:S(2)}) collective-permute-start(f32[2,32,256]{2,1,0:T(8,128)S(1)} %step_kernel.4.refs_2_), channel_id=1, source_target_pairs={{0,1},{1,2},{2,3},{3,7},{7,6},{6,5},{5,4},{8,9},{9,10},{10,11},{11... | collective-permute-start | bytes 196616 | tf_op jit(solution)/shard_map/ppermute | solution.py:405
  183.1 0.9 collective-permute-done.9.refs_2_.refs_1_
  184.8 7.2 %all-to-all-start.8 = ((f32[16,16,128]{2,1,0:T(8,128)}), f32[16,16,128]{2,1,0:T(8,128)S(1)}, u32[]{:S(2)}, u32[]{:S(2)}) async-start(f32[16,16,128]{2,1,0:T(8,128)} %get-tuple-element.85.refs_5_), calls=%async_computation.8 | async-start | bytes 262144 | tf_op jit(solution)/shard_map/all_to_all | solution.py:416
  192.2 7.3 %collective-permute-start.11 = (f32[2,64,256]{2,1,0:T(8,128)S(1)}, f32[2,64,256]{2,1,0:T(8,128)S(1)}, u32[]{:S(2)}, u32[]{:S(2)}) collective-permute-start(f32[2,64,256]{2,1,0:T(8,128)S(1)} %get-tuple-element.88), channel_id=1, source_target_pairs={{0,8},{8,16},{16,24},{24,32},{32,40},{40,48},{48,56},{56,64},{64,7... | collective-permute-start | bytes 393224 | tf_op jit(solution)/shard_map/ppermute | solution.py:395
  199.5 1.9 collective-permute-start.12
  201.4 1.3 collective-permute-done.11.refs_2_
  202.7 3.6 %collective-permute-done.12.refs_3_ = f32[2,64,256]{2,1,0:T(8,128)S(1)} collective-permute-done((f32[2,64,256]{2,1,0:T(8,128)S(1)}, f32[2,64,256]{2,1,0:T(8,128)S(1)}, u32[]{:S(2)}, u32[]{:S(2)}) %collective-permute-start.12) | collective-permute-done | bytes 131104 | tf_op jit(solution)/shard_map/ppermute | solution.py:395
  206.6 9.2 %all_gather.13 = f32[4,256,128]{2,1,0:T(8,128)S(1)} all-gather(f32[1,256,128]{2,1,0:T(8,128)S(1)} %bitcast.29), channel_id=1, replica_groups=mesh['xlo'=2,'z'=16,'core'=2,'xhi'=2,'y'=4] {'xlo','core'}, dimensions={0}, use_global_device_ids=true | all-gather | bytes 655360 | tf_op jit(solution)/shard_map/all_gather | solution.py:420
  215.8 1.1 next_kernel.3
  216.9 13.0 %all_to_all.74.refs_0_ = f32[8,2,32,256]{3,2,1,0:T(8,128)S(1)} all-to-all(f32[8,2,32,256]{3,2,1,0:T(8,128)S(1)} %get-tuple-element.93), channel_id=1, replica_groups=mesh['xlo'=2,'z'=16,'core'=2,'xhi'=2,'y'=4] {'xhi','y'}, dimensions={0} | all-to-all | bytes 1048576 | tf_op jit(solution)/shard_map/all_to_all | solution.py:416
  230.0 1.7 ratio_kernel.5
  231.7 14.0 %all_to_all.75.refs_0_ = f32[8,2,32,256]{3,2,1,0:T(8,128)S(1)} all-to-all(f32[8,2,32,256]{3,2,1,0:T(8,128)S(1)} %ratio_kernel.5), channel_id=1, replica_groups=mesh['xlo'=2,'z'=16,'core'=2,'xhi'=2,'y'=4] {'xhi','y'}, dimensions={0} | all-to-all | bytes 1048576 | tf_op jit(solution)/shard_map/all_to_all | solution.py:416
  245.6 0.8 backward_kernel.5
  246.5 4.4 %collective-permute-start.13 = (f32[17,16,256]{2,1,0:T(8,128)S(1)}, f32[17,16,256]{2,1,0:T(8,128)S(1)}, u32[]{:S(2)}, u32[]{:S(2)}) collective-permute-start(f32[17,16,256]{2,1,0:T(8,128)S(1)} %get-tuple-element.96), channel_id=1, source_target_pairs={{0,8},{8,0},{1,9},{9,1},{2,10},{10,2},{3,11},{11,3},{4,12},{12,4},... | collective-permute-start | bytes 835592 | tf_op jit(solution)/shard_map/ppermute | solution.py:399
  250.8 1.2 collective-permute-done.13.refs_1_
  252.0 2.2 collective-permute-start.14
  254.4 1.3 collective-permute-start.16
  255.7 4.0 %collective-permute-start.15 = (f32[2,32,256]{2,1,0:T(8,128)S(1)}, f32[2,32,256]{2,1,0:T(8,128)S(1)}, u32[]{:S(2)}, u32[]{:S(2)}) collective-permute-start(f32[2,32,256]{2,1,0:T(8,128)S(1)} %step_kernel.5.refs_2_), channel_id=1, source_target_pairs={{0,1},{1,2},{2,3},{3,7},{7,6},{6,5},{5,4},{8,9},{9,10},{10,11},{11... | collective-permute-start | bytes 196616 | tf_op jit(solution)/shard_map/ppermute | solution.py:405
  259.7 1.3 collective-permute-done.15.refs_2_.refs_1_
  261.7 11.5 %all-to-all-start.11 = ((f32[16,1,2176]{2,1,0:T(1,128)}), f32[16,1,2176]{2,1,0:T(1,128)S(1)}, u32[]{:S(2)}, u32[]{:S(2)}) async-start(f32[16,1,2176]{2,1,0:T(1,128)} %bitcast.16), calls=%async_computation.11 | async-start | bytes 278528 | tf_op jit(solution)/shard_map/all_to_all | solution.py:411
  273.2 0.9 place_kernel.5
  274.1 4.4 %collective-permute-start.17 = (f32[2,64,256]{2,1,0:T(8,128)S(1)}, f32[2,64,256]{2,1,0:T(8,128)S(1)}, u32[]{:S(2)}, u32[]{:S(2)}) collective-permute-start(f32[2,64,256]{2,1,0:T(8,128)S(1)} %get-tuple-element.104), channel_id=1, source_target_pairs={{0,8},{8,16},{16,24},{24,32},{32,40},{40,48},{48,56},{56,64},{64,7... | collective-permute-start | bytes 393224 | tf_op jit(solution)/shard_map/ppermute | solution.py:395
  278.5 2.7 collective-permute-done.17.refs_2_
  282.1 17.2 %all_to_all.76 = f32[16,16,128]{2,1,0:T(8,128)S(1)} all-to-all(f32[16,16,128]{2,1,0:T(8,128)S(1)} %get-tuple-element.105), channel_id=1, replica_groups=mesh['xlo'=2,'z'=16,'core'=2,'xhi'=2,'y'=4] {'z'}, dimensions={0} | all-to-all | bytes 262144 | tf_op jit(solution)/shard_map/all_to_all | solution.py:416
  299.4 21.2 %all_to_all.77.refs_0_ = f32[8,352,128]{2,1,0:T(8,128)S(1)} all-to-all(f32[8,352,128]{2,1,0:T(8,128)S(1)} %tail_kernel.1), channel_id=1, replica_groups=mesh['xlo'=2,'z'=16,'core'=2,'xhi'=2,'y'=4] {'xhi','y'}, dimensions={0} | all-to-all | bytes 2883584 | tf_op jit(solution)/shard_map/all_to_all | solution.py:416
  320.7 14.3 %all-gather = f32[32,32,128]{2,1,0:T(8,128)S(1)} all-gather(f32[8,32,128]{2,1,0:T(8,128)S(1)} %slice.19), channel_id=2, replica_groups=mesh['xlo'=2,'z'=16,'core'=2,'xhi'=2,'y'=4] {'xlo','core'}, dimensions={0}, use_global_device_ids=true | all-gather | bytes 655360 | tf_op jit(solution)/shard_map/all_gather | solution.py:420
  335.0 0.8 probe_out_kernel.1
  335.8 1.1 object_kernel.1
  (58 shorter events, 7.7 us)
Async XLA Ops:
  0.6 9.6 %copy-start.2 = (f32[2,288,512]{2,1,0:T(8,128)S(1)}, f32[2,288,512]{2,1,0:T(8,128)}, u32[]{:S(2)}) copy-start(f32[2,288,512]{2,1,0:T(8,128)} %whole.1) | copy-start | bytes 3538948
  0.6 1.1 copy-start.3
  2.6 12.6 %copy-start.4 = (s32[1,3]{1,0:T(1,128)S(1)}, s32[1,3]{1,0:T(1,128)}, u32[]{:S(2)}) copy-start(s32[1,3]{1,0:T(1,128)} %param.14) | copy-start | bytes 40
  2.6 12.6 %copy-start.5 = (s32[1,3]{1,0:T(1,128)S(1)}, s32[1,3]{1,0:T(1,128)}, u32[]{:S(2)}) copy-start(s32[1,3]{1,0:T(1,128)} %param.12) | copy-start | bytes 40
  2.6 12.6 %copy-start.6 = (s32[1,3]{1,0:T(1,128)S(1)}, s32[1,3]{1,0:T(1,128)}, u32[]{:S(2)}) copy-start(s32[1,3]{1,0:T(1,128)} %param.11) | copy-start | bytes 40
  2.6 13.9 %copy-start.1 = (bf16[1,3,256,256]{3,2,1,0:T(8,128)(2,1)S(1)}, bf16[1,3,256,256]{3,2,1,0:T(8,128)(2,1)}, u32[]{:S(2)}) copy-start(bf16[1,3,256,256]{3,2,1,0:T(8,128)(2,1)} %refs_1_.5) | copy-start | bytes 1179652
  2.6 16.5 %copy-start = (bf16[2,2,256,256]{3,2,1,0:T(8,128)(2,1)S(1)}, bf16[2,2,256,256]{3,2,1,0:T(8,128)(2,1)}, u32[]{:S(2)}) copy-start(bf16[2,2,256,256]{3,2,1,0:T(8,128)(2,1)} %constant.35.clone.refs_4_.refs_3_.refs_2_) | copy-start | bytes 1572868
  2.6 16.5 %all-to-all-start = ((f32[8,2,32,256]{3,2,1,0:T(8,128)}), f32[8,2,32,256]{3,2,1,0:T(8,128)S(1)}, u32[]{:S(2)}, u32[]{:S(2)}) async-start(f32[8,2,32,256]{3,2,1,0:T(8,128)} %split_kernel.1._), calls=%async_computation | async-start | bytes 1048576 | tf_op jit(solution)/shard_map/all_to_all | solution.py:416
  10.3 7.3 %collective-permute-start = (f32[2,64,256]{2,1,0:T(8,128)S(1)}, f32[2,64,256]{2,1,0:T(8,128)S(1)}, u32[]{:S(2)}, u32[]{:S(2)}) collective-permute-start(f32[2,64,256]{2,1,0:T(8,128)S(1)} %get-tuple-element.55), channel_id=1, source_target_pairs={{8,0},{16,8},{24,16},{32,24},{40,32},{48,40},{56,48},{64,56},{72,6... | collective-permute-start | bytes 393224 | tf_op jit(solution)/shard_map/ppermute | solution.py:395
  50.0 6.5 %collective-permute-start.1 = (f32[17,16,256]{2,1,0:T(8,128)S(1)}, f32[17,16,256]{2,1,0:T(8,128)S(1)}, u32[]{:S(2)}, u32[]{:S(2)}) collective-permute-start(f32[17,16,256]{2,1,0:T(8,128)S(1)} %get-tuple-element.61), channel_id=1, source_target_pairs={{0,8},{8,0},{1,9},{9,1},{2,10},{10,2},{3,11},{11,3},{4,12},{12,4},... | collective-permute-start | bytes 835592 | tf_op jit(solution)/shard_map/ppermute | solution.py:399
  56.4 10.5 %collective-permute-start.2 = (f32[17,8,256]{2,1,0:T(8,128)S(1)}, f32[17,8,256]{2,1,0:T(8,128)S(1)}, u32[]{:S(2)}, u32[]{:S(2)}) collective-permute-start(f32[17,8,256]{2,1,0:T(8,128)S(1)} %get-tuple-element.63), channel_id=1, source_target_pairs={{0,256},{256,0},{1,257},{257,1},{2,258},{258,2},{3,259},{259,3},{4... | collective-permute-start | bytes 417800 | tf_op jit(solution)/shard_map/ppermute | solution.py:399
  67.6 23.6 %all-to-all-start.3 = ((f32[16,1,2176]{2,1,0:T(1,128)}), f32[16,1,2176]{2,1,0:T(1,128)S(1)}, u32[]{:S(2)}, u32[]{:S(2)}) async-start(f32[16,1,2176]{2,1,0:T(1,128)} %bitcast.8), calls=%async_computation.3 | async-start | bytes 278528 | tf_op jit(solution)/shard_map/all_to_all | solution.py:411
  84.6 5.7 %collective-permute-start.4 = (f32[2,32,256]{2,1,0:T(8,128)S(1)}, f32[2,32,256]{2,1,0:T(8,128)S(1)}, u32[]{:S(2)}, u32[]{:S(2)}) collective-permute-start(f32[2,32,256]{2,1,0:T(8,128)S(1)} %step_kernel.3.refs_2_), channel_id=1, source_target_pairs={{1,0},{2,1},{3,2},{7,3},{6,7},{5,6},{4,5},{9,8},{10,9},{11,10},{15... | collective-permute-start | bytes 196616 | tf_op jit(solution)/shard_map/ppermute | solution.py:405
  85.9 5.3 %collective-permute-start.3 = (f32[2,32,256]{2,1,0:T(8,128)S(1)}, f32[2,32,256]{2,1,0:T(8,128)S(1)}, u32[]{:S(2)}, u32[]{:S(2)}) collective-permute-start(f32[2,32,256]{2,1,0:T(8,128)S(1)} %step_kernel.3.refs_2_), channel_id=1, source_target_pairs={{0,1},{1,2},{2,3},{3,7},{7,6},{6,5},{5,4},{8,9},{9,10},{10,11},{11... | collective-permute-start | bytes 196616 | tf_op jit(solution)/shard_map/ppermute | solution.py:405
  91.9 21.8 %all-to-all-start.4 = ((f32[16,16,128]{2,1,0:T(8,128)}), f32[16,16,128]{2,1,0:T(8,128)S(1)}, u32[]{:S(2)}, u32[]{:S(2)}) async-start(f32[16,16,128]{2,1,0:T(8,128)} %get-tuple-element.67.refs_5_), calls=%async_computation.4 | async-start | bytes 262144 | tf_op jit(solution)/shard_map/all_to_all | solution.py:416
  99.4 10.5 %collective-permute-start.5 = (f32[2,64,256]{2,1,0:T(8,128)S(1)}, f32[2,64,256]{2,1,0:T(8,128)S(1)}, u32[]{:S(2)}, u32[]{:S(2)}) collective-permute-start(f32[2,64,256]{2,1,0:T(8,128)S(1)} %get-tuple-element.70), channel_id=1, source_target_pairs={{0,8},{8,16},{16,24},{24,32},{32,40},{40,48},{48,56},{56,64},{64,7... | collective-permute-start | bytes 393224 | tf_op jit(solution)/shard_map/ppermute | solution.py:395
  106.6 6.8 %collective-permute-start.6 = (f32[2,64,256]{2,1,0:T(8,128)S(1)}, f32[2,64,256]{2,1,0:T(8,128)S(1)}, u32[]{:S(2)}, u32[]{:S(2)}) collective-permute-start(f32[2,64,256]{2,1,0:T(8,128)S(1)} %get-tuple-element.71), channel_id=1, source_target_pairs={{8,0},{16,8},{24,16},{32,24},{40,32},{48,40},{56,48},{64,56},{72,6... | collective-permute-start | bytes 393224 | tf_op jit(solution)/shard_map/ppermute | solution.py:395
  153.0 5.5 %collective-permute-start.7 = (f32[17,16,256]{2,1,0:T(8,128)S(1)}, f32[17,16,256]{2,1,0:T(8,128)S(1)}, u32[]{:S(2)}, u32[]{:S(2)}) collective-permute-start(f32[17,16,256]{2,1,0:T(8,128)S(1)} %get-tuple-element.78), channel_id=1, source_target_pairs={{0,8},{8,0},{1,9},{9,1},{2,10},{10,2},{3,11},{11,3},{4,12},{12,4},... | collective-permute-start | bytes 835592 | tf_op jit(solution)/shard_map/ppermute | solution.py:399
  158.5 6.8 %collective-permute-start.8 = (f32[17,8,256]{2,1,0:T(8,128)S(1)}, f32[17,8,256]{2,1,0:T(8,128)S(1)}, u32[]{:S(2)}, u32[]{:S(2)}) collective-permute-start(f32[17,8,256]{2,1,0:T(8,128)S(1)} %get-tuple-element.80), channel_id=1, source_target_pairs={{0,256},{256,0},{1,257},{257,1},{2,258},{258,2},{3,259},{259,3},{4... | collective-permute-start | bytes 417800 | tf_op jit(solution)/shard_map/ppermute | solution.py:399
  166.0 18.1 %all-to-all-start.7 = ((f32[16,1,2176]{2,1,0:T(1,128)}), f32[16,1,2176]{2,1,0:T(1,128)S(1)}, u32[]{:S(2)}, u32[]{:S(2)}) async-start(f32[16,1,2176]{2,1,0:T(1,128)} %bitcast.12), calls=%async_computation.7 | async-start | bytes 278528 | tf_op jit(solution)/shard_map/all_to_all | solution.py:411
  177.5 5.7 %collective-permute-start.10 = (f32[2,32,256]{2,1,0:T(8,128)S(1)}, f32[2,32,256]{2,1,0:T(8,128)S(1)}, u32[]{:S(2)}, u32[]{:S(2)}) collective-permute-start(f32[2,32,256]{2,1,0:T(8,128)S(1)} %step_kernel.4.refs_2_), channel_id=1, source_target_pairs={{1,0},{2,1},{3,2},{7,3},{6,7},{5,6},{4,5},{9,8},{10,9},{11,10},{15... | collective-permute-start | bytes 196616 | tf_op jit(solution)/shard_map/ppermute | solution.py:405
  178.8 5.3 %collective-permute-start.9 = (f32[2,32,256]{2,1,0:T(8,128)S(1)}, f32[2,32,256]{2,1,0:T(8,128)S(1)}, u32[]{:S(2)}, u32[]{:S(2)}) collective-permute-start(f32[2,32,256]{2,1,0:T(8,128)S(1)} %step_kernel.4.refs_2_), channel_id=1, source_target_pairs={{0,1},{1,2},{2,3},{3,7},{7,6},{6,5},{5,4},{8,9},{9,10},{10,11},{11... | collective-permute-start | bytes 196616 | tf_op jit(solution)/shard_map/ppermute | solution.py:405
  184.8 21.8 %all-to-all-start.8 = ((f32[16,16,128]{2,1,0:T(8,128)}), f32[16,16,128]{2,1,0:T(8,128)S(1)}, u32[]{:S(2)}, u32[]{:S(2)}) async-start(f32[16,16,128]{2,1,0:T(8,128)} %get-tuple-element.85.refs_5_), calls=%async_computation.8 | async-start | bytes 262144 | tf_op jit(solution)/shard_map/all_to_all | solution.py:416
  192.2 10.5 %collective-permute-start.11 = (f32[2,64,256]{2,1,0:T(8,128)S(1)}, f32[2,64,256]{2,1,0:T(8,128)S(1)}, u32[]{:S(2)}, u32[]{:S(2)}) collective-permute-start(f32[2,64,256]{2,1,0:T(8,128)S(1)} %get-tuple-element.88), channel_id=1, source_target_pairs={{0,8},{8,16},{16,24},{24,32},{32,40},{40,48},{48,56},{56,64},{64,7... | collective-permute-start | bytes 393224 | tf_op jit(solution)/shard_map/ppermute | solution.py:395
  199.5 6.8 %collective-permute-start.12 = (f32[2,64,256]{2,1,0:T(8,128)S(1)}, f32[2,64,256]{2,1,0:T(8,128)S(1)}, u32[]{:S(2)}, u32[]{:S(2)}) collective-permute-start(f32[2,64,256]{2,1,0:T(8,128)S(1)} %get-tuple-element.89), channel_id=1, source_target_pairs={{8,0},{16,8},{24,16},{32,24},{40,32},{48,40},{56,48},{64,56},{72,6... | collective-permute-start | bytes 393224 | tf_op jit(solution)/shard_map/ppermute | solution.py:395
  246.5 5.5 %collective-permute-start.13 = (f32[17,16,256]{2,1,0:T(8,128)S(1)}, f32[17,16,256]{2,1,0:T(8,128)S(1)}, u32[]{:S(2)}, u32[]{:S(2)}) collective-permute-start(f32[17,16,256]{2,1,0:T(8,128)S(1)} %get-tuple-element.96), channel_id=1, source_target_pairs={{0,8},{8,0},{1,9},{9,1},{2,10},{10,2},{3,11},{11,3},{4,12},{12,4},... | collective-permute-start | bytes 835592 | tf_op jit(solution)/shard_map/ppermute | solution.py:399
  252.0 9.0 %collective-permute-start.14 = (f32[17,8,256]{2,1,0:T(8,128)S(1)}, f32[17,8,256]{2,1,0:T(8,128)S(1)}, u32[]{:S(2)}, u32[]{:S(2)}) collective-permute-start(f32[17,8,256]{2,1,0:T(8,128)S(1)} %get-tuple-element.98), channel_id=1, source_target_pairs={{0,256},{256,0},{1,257},{257,1},{2,258},{258,2},{3,259},{259,3},{4... | collective-permute-start | bytes 417800 | tf_op jit(solution)/shard_map/ppermute | solution.py:399
  254.4 5.3 %collective-permute-start.16 = (f32[2,32,256]{2,1,0:T(8,128)S(1)}, f32[2,32,256]{2,1,0:T(8,128)S(1)}, u32[]{:S(2)}, u32[]{:S(2)}) collective-permute-start(f32[2,32,256]{2,1,0:T(8,128)S(1)} %step_kernel.5.refs_2_), channel_id=1, source_target_pairs={{1,0},{2,1},{3,2},{7,3},{6,7},{5,6},{4,5},{9,8},{10,9},{11,10},{15... | collective-permute-start | bytes 196616 | tf_op jit(solution)/shard_map/ppermute | solution.py:405
  255.7 5.3 %collective-permute-start.15 = (f32[2,32,256]{2,1,0:T(8,128)S(1)}, f32[2,32,256]{2,1,0:T(8,128)S(1)}, u32[]{:S(2)}, u32[]{:S(2)}) collective-permute-start(f32[2,32,256]{2,1,0:T(8,128)S(1)} %step_kernel.5.refs_2_), channel_id=1, source_target_pairs={{0,1},{1,2},{2,3},{3,7},{7,6},{6,5},{5,4},{8,9},{9,10},{10,11},{11... | collective-permute-start | bytes 196616 | tf_op jit(solution)/shard_map/ppermute | solution.py:405
  261.7 19.7 %all-to-all-start.11 = ((f32[16,1,2176]{2,1,0:T(1,128)}), f32[16,1,2176]{2,1,0:T(1,128)S(1)}, u32[]{:S(2)}, u32[]{:S(2)}) async-start(f32[16,1,2176]{2,1,0:T(1,128)} %bitcast.16), calls=%async_computation.11 | async-start | bytes 278528 | tf_op jit(solution)/shard_map/all_to_all | solution.py:411
  274.1 7.2 %collective-permute-start.17 = (f32[2,64,256]{2,1,0:T(8,128)S(1)}, f32[2,64,256]{2,1,0:T(8,128)S(1)}, u32[]{:S(2)}, u32[]{:S(2)}) collective-permute-start(f32[2,64,256]{2,1,0:T(8,128)S(1)} %get-tuple-element.104), channel_id=1, source_target_pairs={{0,8},{8,16},{16,24},{24,32},{32,40},{40,48},{48,56},{56,64},{64,7... | collective-permute-start | bytes 393224 | tf_op jit(solution)/shard_map/ppermute | solution.py:395

commit v10 on v9

--- a/solution.py
+++ b/solution.py
@@ -47,9 +47,10 @@
 def fourier_tables():
     index = np.arange(SIDE)
     angles = (index[:, None] * index[None, :] % SIDE) * (2.0 * math.pi / SIDE)
-    both = np.stack([np.cos(angles), np.sin(angles)]) / math.sqrt(SIDE)
-    high = both.astype(jnp.bfloat16)
-    low = (both - high.astype(np.float64)).astype(jnp.bfloat16)
+    cosine, sine = np.cos(angles) / math.sqrt(SIDE), np.sin(angles) / math.sqrt(SIDE)
+    exact = np.stack([cosine, cosine + sine, cosine - sine])
+    high = exact.astype(jnp.bfloat16)
+    low = (exact - high.astype(np.float64)).astype(jnp.bfloat16)
     return np.stack([high, low], axis=1)
 
 
@@ -62,34 +63,30 @@
     return jnp.dot(left, right, preferred_element_type=F32)
 
 
+def transform(real, imag, by, direction):
+    turned = direction * imag
+    shared = by(0, real + turned)
+    return shared - by(2, turned), direction * (shared - by(1, real))
+
+
 def rows_transform(real, imag, tables, direction):
-    high, low = halves(jnp.concatenate([real, imag], axis=0))
-
-    def by(which):
+    def by(which, value):
+        high, low = halves(value)
         return (
             dot(high, tables[which, 0]) + dot(low, tables[which, 0]) + dot(high, tables[which, 1])
         )
 
-    by_cos, by_sin = by(0), by(1)
-    return (
-        by_cos[:SIDE] + direction * by_sin[SIDE:],
-        by_cos[SIDE:] - direction * by_sin[:SIDE],
-    )
+    return transform(real, imag, by, direction)
 
 
 def columns_transform(real, imag, tables, direction):
-    high, low = halves(jnp.concatenate([real, imag], axis=1))
-
-    def by(which):
+    def by(which, value):
+        high, low = halves(value)
         return (
             dot(tables[which, 0], high) + dot(tables[which, 0], low) + dot(tables[which, 1], high)
         )
 
-    by_cos, by_sin = by(0), by(1)
-    return (
-        by_cos[:, :SIDE] + direction * by_sin[:, SIDE:],
-        by_cos[:, SIDE:] - direction * by_sin[:, :SIDE],
-    )
+    return transform(real, imag, by, direction)
 
 
 def swap_blocks(parts):
@@ -505,13 +502,18 @@
         )
         above = beside_slab(object_step, 1)
         below = beside_slab(object_step, -1)
+        if not final:
+            next_scal = scalars[step + 1 : step + 2]
+            counts, flags = call(
+                counts_kernel, counts_shapes, next_scal, measured, after=(keep,)
+            )
         (packed,) = call(
             pack_kernel,
             [(RINGS * MESSAGE, LANES)],
             keep,
             received,
             scalars=False,
-            after=(above, below) if final else (object_step,),
+            after=(above, below) if final else (object_step, counts),
         )
         sums = exchange_rings(packed)
         placing = [scal, above, object_step, below, band]
@@ -525,11 +527,7 @@
             )
             before = (rows_out,)
         else:
-            next_scal = scalars[step + 1 : step + 2]
-            counts, flags = call(
-                counts_kernel, counts_shapes, next_scal, measured, after=(packed,)
-            )
-            before = (above, below, counts)
+            before = (above, below)
         shard, shards = call(
             probe_kernel,
             [(2 * MODES, LANES), (RINGS, 2 * MODES, LANES)],

time: 338 us -> 337 us (level)
  no operation moved by 1% of the time
where the time goes in v10:
time: 337 us; the launch traced here: 335 us
  blocking collectives  152 us (45%)
  starting transfers between devices  131 us (39%)
  waiting for transfers between devices  28.8 us (9%)
  Pallas kernels  20.1 us (6%)
    all_to_all x8, blocking collectives, exchange(): return lax.all_to_all(value, axes, 0, 0, tiled=True)  119 us
    all_to_all x3, starting transfers between devices, exchange_rings(): lax.all_to_all(value, 'z', 0, 0, tiled=True, axis_index_groups=groups)  40 us
    all_gather x3, blocking collectives, gather_pieces(): gathered = lax.all_gather(piece, ('xlo', 'core'))  32.4 us
    ppermute x6, starting transfers between devices, shift(): lax.ppermute(value, axes, [(i, i + steps) for i in range(first, last)])  27.6 us
    ppermute x6, starting transfers between devices, other(): return lax.ppermute(value, axis, [(0, 1), (1, 0)])  25.8 us
    all_to_all x3, starting transfers between devices, exchange(): return lax.all_to_all(value, axes, 0, 0, tiled=True)  22 us
    pallas_call x34, Pallas kernels, call(): pl.pallas_call(body, out_shape=[jax.ShapeDtypeStruct(shape, F32) for shap...  20.1 us
    ppermute x6, starting transfers between devices, beside_slab(): return lax.ppermute(value, MODE_AXES, pairs)  15.8 us
  transfers between devices with their start and end apart: 24, of which 15 were waited for; matrix products, arithmetic and copies ran while one was open for 0% of the time, Pallas kernels for 1%

profile of v10, /device:TPU:1, one launch (start us, length us, event | category | flops | bytes accessed | tf_op | source)
XLA Modules:
  0.0 335.4 jit_solution(18063566833982714680)
XLA Ops:
  0.6 1.1 copy-done.3
  1.8 0.8 split_kernel.1._
  2.6 7.6 %all-to-all-start = ((f32[8,2,32,256]{3,2,1,0:T(8,128)}), f32[8,2,32,256]{3,2,1,0:T(8,128)S(1)}, u32[]{:S(2)}, u32[]{:S(2)}) async-start(f32[8,2,32,256]{3,2,1,0:T(8,128)} %split_kernel.1._), calls=%async_computation | async-start | bytes 1048576 | tf_op jit(solution)/shard_map/all_to_all | solution.py:413
  10.3 4.8 %collective-permute-start = (f32[2,64,256]{2,1,0:T(8,128)S(1)}, f32[2,64,256]{2,1,0:T(8,128)S(1)}, u32[]{:S(2)}, u32[]{:S(2)}) collective-permute-start(f32[2,64,256]{2,1,0:T(8,128)S(1)} %get-tuple-element.55), channel_id=1, source_target_pairs={{8,0},{16,8},{24,16},{32,24},{40,32},{48,40},{56,48},{64,56},{72,6... | collective-permute-start | bytes 393224 | tf_op jit(solution)/shard_map/ppermute | solution.py:392
  16.9 0.8 collective-permute-done.refs_2_
  17.7 1.4 all-to-all-done.refs_3_.refs_1_
  19.1 1.0 first_kernel.1
  20.1 14.8 %all_to_all.70.refs_0_ = f32[8,2,32,256]{3,2,1,0:T(8,128)S(1)} all-to-all(f32[8,2,32,256]{3,2,1,0:T(8,128)S(1)} %get-tuple-element.57), channel_id=1, replica_groups=mesh['xlo'=2,'z'=16,'core'=2,'xhi'=2,'y'=4] {'xhi','y'}, dimensions={0} | all-to-all | bytes 1048576 | tf_op jit(solution)/shard_map/all_to_all | solution.py:413
  34.9 1.4 ratio_kernel.3
  36.3 12.4 %all_to_all.71.refs_0_ = f32[8,2,32,256]{3,2,1,0:T(8,128)S(1)} all-to-all(f32[8,2,32,256]{3,2,1,0:T(8,128)S(1)} %ratio_kernel.3), channel_id=1, replica_groups=mesh['xlo'=2,'z'=16,'core'=2,'xhi'=2,'y'=4] {'xhi','y'}, dimensions={0} | all-to-all | bytes 1048576 | tf_op jit(solution)/shard_map/all_to_all | solution.py:413
  48.7 0.7 backward_kernel.3
  49.5 5.3 %collective-permute-start.1 = (f32[17,16,256]{2,1,0:T(8,128)S(1)}, f32[17,16,256]{2,1,0:T(8,128)S(1)}, u32[]{:S(2)}, u32[]{:S(2)}) collective-permute-start(f32[17,16,256]{2,1,0:T(8,128)S(1)} %get-tuple-element.61), channel_id=1, source_target_pairs={{0,8},{8,0},{1,9},{9,1},{2,10},{10,2},{3,11},{11,3},{4,12},{12,4},... | collective-permute-start | bytes 835592 | tf_op jit(solution)/shard_map/ppermute | solution.py:396
  54.8 1.2 collective-permute-done.1.refs_1_
  55.9 6.7 %collective-permute-start.2 = (f32[17,8,256]{2,1,0:T(8,128)S(1)}, f32[17,8,256]{2,1,0:T(8,128)S(1)}, u32[]{:S(2)}, u32[]{:S(2)}) collective-permute-start(f32[17,8,256]{2,1,0:T(8,128)S(1)} %get-tuple-element.63), channel_id=1, source_target_pairs={{0,256},{256,0},{1,257},{257,1},{2,258},{258,2},{3,259},{259,3},{4... | collective-permute-start | bytes 417800 | tf_op jit(solution)/shard_map/ppermute | solution.py:396
  63.2 3.2 collective-permute-done.2.refs_1_
  67.1 17.0 %all-to-all-start.3 = ((f32[16,1,2176]{2,1,0:T(1,128)}), f32[16,1,2176]{2,1,0:T(1,128)S(1)}, u32[]{:S(2)}, u32[]{:S(2)}) async-start(f32[16,1,2176]{2,1,0:T(1,128)} %bitcast.8), calls=%async_computation.3 | async-start | bytes 278528 | tf_op jit(solution)/shard_map/all_to_all | solution.py:408
  84.1 1.3 collective-permute-start.4
  85.4 4.0 %collective-permute-start.3 = (f32[2,32,256]{2,1,0:T(8,128)S(1)}, f32[2,32,256]{2,1,0:T(8,128)S(1)}, u32[]{:S(2)}, u32[]{:S(2)}) collective-permute-start(f32[2,32,256]{2,1,0:T(8,128)S(1)} %step_kernel.3.refs_2_), channel_id=1, source_target_pairs={{0,1},{1,2},{2,3},{3,7},{7,6},{6,5},{5,4},{8,9},{9,10},{10,11},{11... | collective-permute-start | bytes 196616 | tf_op jit(solution)/shard_map/ppermute | solution.py:402
  89.4 1.3 collective-permute-done.3.refs_2_.refs_1_
  91.4 7.2 %all-to-all-start.4 = ((f32[16,16,128]{2,1,0:T(8,128)}), f32[16,16,128]{2,1,0:T(8,128)S(1)}, u32[]{:S(2)}, u32[]{:S(2)}) async-start(f32[16,16,128]{2,1,0:T(8,128)} %get-tuple-element.67.refs_5_), calls=%async_computation.4 | async-start | bytes 262144 | tf_op jit(solution)/shard_map/all_to_all | solution.py:413
  98.9 7.3 %collective-permute-start.5 = (f32[2,64,256]{2,1,0:T(8,128)S(1)}, f32[2,64,256]{2,1,0:T(8,128)S(1)}, u32[]{:S(2)}, u32[]{:S(2)}) collective-permute-start(f32[2,64,256]{2,1,0:T(8,128)S(1)} %get-tuple-element.70), channel_id=1, source_target_pairs={{0,8},{8,16},{16,24},{24,32},{32,40},{40,48},{48,56},{56,64},{64,7... | collective-permute-start | bytes 393224 | tf_op jit(solution)/shard_map/ppermute | solution.py:392
  106.1 1.9 collective-permute-start.6
  108.1 1.3 collective-permute-done.5.refs_2_
  109.4 3.6 %collective-permute-done.6.refs_3_ = f32[2,64,256]{2,1,0:T(8,128)S(1)} collective-permute-done((f32[2,64,256]{2,1,0:T(8,128)S(1)}, f32[2,64,256]{2,1,0:T(8,128)S(1)}, u32[]{:S(2)}, u32[]{:S(2)}) %collective-permute-start.6) | collective-permute-done | bytes 131104 | tf_op jit(solution)/shard_map/ppermute | solution.py:392
  113.3 8.8 %all_gather.12 = f32[4,256,128]{2,1,0:T(8,128)S(1)} all-gather(f32[1,256,128]{2,1,0:T(8,128)S(1)} %bitcast.28), channel_id=1, replica_groups=mesh['xlo'=2,'z'=16,'core'=2,'xhi'=2,'y'=4] {'xlo','core'}, dimensions={0}, use_global_device_ids=true | all-gather | bytes 655360 | tf_op jit(solution)/shard_map/all_gather | solution.py:417
  122.1 1.0 next_kernel.2
  123.1 12.9 %all_to_all.72.refs_0_ = f32[8,2,32,256]{3,2,1,0:T(8,128)S(1)} all-to-all(f32[8,2,32,256]{3,2,1,0:T(8,128)S(1)} %get-tuple-element.75), channel_id=1, replica_groups=mesh['xlo'=2,'z'=16,'core'=2,'xhi'=2,'y'=4] {'xhi','y'}, dimensions={0} | all-to-all | bytes 1048576 | tf_op jit(solution)/shard_map/all_to_all | solution.py:413
  136.0 1.4 ratio_kernel.4
  137.4 13.8 %all_to_all.73.refs_0_ = f32[8,2,32,256]{3,2,1,0:T(8,128)S(1)} all-to-all(f32[8,2,32,256]{3,2,1,0:T(8,128)S(1)} %ratio_kernel.4), channel_id=1, replica_groups=mesh['xlo'=2,'z'=16,'core'=2,'xhi'=2,'y'=4] {'xhi','y'}, dimensions={0} | all-to-all | bytes 1048576 | tf_op jit(solution)/shard_map/all_to_all | solution.py:413
  151.2 0.7 backward_kernel.4
  152.0 4.4 %collective-permute-start.7 = (f32[17,16,256]{2,1,0:T(8,128)S(1)}, f32[17,16,256]{2,1,0:T(8,128)S(1)}, u32[]{:S(2)}, u32[]{:S(2)}) collective-permute-start(f32[17,16,256]{2,1,0:T(8,128)S(1)} %get-tuple-element.78), channel_id=1, source_target_pairs={{0,8},{8,0},{1,9},{9,1},{2,10},{10,2},{3,11},{11,3},{4,12},{12,4},... | collective-permute-start | bytes 835592 | tf_op jit(solution)/shard_map/ppermute | solution.py:396
  156.4 1.2 collective-permute-done.7.refs_1_
  157.6 2.8 collective-permute-start.8
  161.0 3.4 %collective-permute-done.8.refs_1_ = f32[17,8,256]{2,1,0:T(8,128)S(1)} collective-permute-done((f32[17,8,256]{2,1,0:T(8,128)S(1)}, f32[17,8,256]{2,1,0:T(8,128)S(1)}, u32[]{:S(2)}, u32[]{:S(2)}) %collective-permute-start.8) | collective-permute-done | bytes 139296 | tf_op jit(solution)/shard_map/ppermute | solution.py:396
  165.0 11.5 %all-to-all-start.7 = ((f32[16,1,2176]{2,1,0:T(1,128)}), f32[16,1,2176]{2,1,0:T(1,128)S(1)}, u32[]{:S(2)}, u32[]{:S(2)}) async-start(f32[16,1,2176]{2,1,0:T(1,128)} %bitcast.12), calls=%async_computation.7 | async-start | bytes 278528 | tf_op jit(solution)/shard_map/all_to_all | solution.py:408
  176.5 1.3 collective-permute-start.10
  177.8 4.0 %collective-permute-start.9 = (f32[2,32,256]{2,1,0:T(8,128)S(1)}, f32[2,32,256]{2,1,0:T(8,128)S(1)}, u32[]{:S(2)}, u32[]{:S(2)}) collective-permute-start(f32[2,32,256]{2,1,0:T(8,128)S(1)} %step_kernel.4.refs_2_), channel_id=1, source_target_pairs={{0,1},{1,2},{2,3},{3,7},{7,6},{6,5},{5,4},{8,9},{9,10},{10,11},{11... | collective-permute-start | bytes 196616 | tf_op jit(solution)/shard_map/ppermute | solution.py:402
  181.8 1.3 collective-permute-done.9.refs_2_.refs_1_
  183.8 7.2 %all-to-all-start.8 = ((f32[16,16,128]{2,1,0:T(8,128)}), f32[16,16,128]{2,1,0:T(8,128)S(1)}, u32[]{:S(2)}, u32[]{:S(2)}) async-start(f32[16,16,128]{2,1,0:T(8,128)} %get-tuple-element.85.refs_5_), calls=%async_computation.8 | async-start | bytes 262144 | tf_op jit(solution)/shard_map/all_to_all | solution.py:413
  191.3 7.3 %collective-permute-start.11 = (f32[2,64,256]{2,1,0:T(8,128)S(1)}, f32[2,64,256]{2,1,0:T(8,128)S(1)}, u32[]{:S(2)}, u32[]{:S(2)}) collective-permute-start(f32[2,64,256]{2,1,0:T(8,128)S(1)} %get-tuple-element.88), channel_id=1, source_target_pairs={{0,8},{8,16},{16,24},{24,32},{32,40},{40,48},{48,56},{56,64},{64,7... | collective-permute-start | bytes 393224 | tf_op jit(solution)/shard_map/ppermute | solution.py:392
  198.5 1.9 collective-permute-start.12
  200.4 1.3 collective-permute-done.11.refs_2_
  201.7 3.6 %collective-permute-done.12.refs_3_ = f32[2,64,256]{2,1,0:T(8,128)S(1)} collective-permute-done((f32[2,64,256]{2,1,0:T(8,128)S(1)}, f32[2,64,256]{2,1,0:T(8,128)S(1)}, u32[]{:S(2)}, u32[]{:S(2)}) %collective-permute-start.12) | collective-permute-done | bytes 131104 | tf_op jit(solution)/shard_map/ppermute | solution.py:392
  205.6 9.2 %all_gather.13 = f32[4,256,128]{2,1,0:T(8,128)S(1)} all-gather(f32[1,256,128]{2,1,0:T(8,128)S(1)} %bitcast.29), channel_id=1, replica_groups=mesh['xlo'=2,'z'=16,'core'=2,'xhi'=2,'y'=4] {'xlo','core'}, dimensions={0}, use_global_device_ids=true | all-gather | bytes 655360 | tf_op jit(solution)/shard_map/all_gather | solution.py:417
  214.9 1.0 next_kernel.3
  215.9 13.0 %all_to_all.74.refs_0_ = f32[8,2,32,256]{3,2,1,0:T(8,128)S(1)} all-to-all(f32[8,2,32,256]{3,2,1,0:T(8,128)S(1)} %get-tuple-element.93), channel_id=1, replica_groups=mesh['xlo'=2,'z'=16,'core'=2,'xhi'=2,'y'=4] {'xhi','y'}, dimensions={0} | all-to-all | bytes 1048576 | tf_op jit(solution)/shard_map/all_to_all | solution.py:413
  228.9 1.4 ratio_kernel.5
  230.3 14.0 %all_to_all.75.refs_0_ = f32[8,2,32,256]{3,2,1,0:T(8,128)S(1)} all-to-all(f32[8,2,32,256]{3,2,1,0:T(8,128)S(1)} %ratio_kernel.5), channel_id=1, replica_groups=mesh['xlo'=2,'z'=16,'core'=2,'xhi'=2,'y'=4] {'xhi','y'}, dimensions={0} | all-to-all | bytes 1048576 | tf_op jit(solution)/shard_map/all_to_all | solution.py:413
  244.3 0.7 backward_kernel.5
  245.0 4.4 %collective-permute-start.13 = (f32[17,16,256]{2,1,0:T(8,128)S(1)}, f32[17,16,256]{2,1,0:T(8,128)S(1)}, u32[]{:S(2)}, u32[]{:S(2)}) collective-permute-start(f32[17,16,256]{2,1,0:T(8,128)S(1)} %get-tuple-element.96), channel_id=1, source_target_pairs={{0,8},{8,0},{1,9},{9,1},{2,10},{10,2},{3,11},{11,3},{4,12},{12,4},... | collective-permute-start | bytes 835592 | tf_op jit(solution)/shard_map/ppermute | solution.py:396
  249.4 1.2 collective-permute-done.13.refs_1_
  250.6 2.2 collective-permute-start.14
  253.0 1.3 collective-permute-start.16
  254.3 4.0 %collective-permute-start.15 = (f32[2,32,256]{2,1,0:T(8,128)S(1)}, f32[2,32,256]{2,1,0:T(8,128)S(1)}, u32[]{:S(2)}, u32[]{:S(2)}) collective-permute-start(f32[2,32,256]{2,1,0:T(8,128)S(1)} %step_kernel.5.refs_2_), channel_id=1, source_target_pairs={{0,1},{1,2},{2,3},{3,7},{7,6},{6,5},{5,4},{8,9},{9,10},{10,11},{11... | collective-permute-start | bytes 196616 | tf_op jit(solution)/shard_map/ppermute | solution.py:402
  258.3 1.3 collective-permute-done.15.refs_2_.refs_1_
  260.2 11.5 %all-to-all-start.11 = ((f32[16,1,2176]{2,1,0:T(1,128)}), f32[16,1,2176]{2,1,0:T(1,128)S(1)}, u32[]{:S(2)}, u32[]{:S(2)}) async-start(f32[16,1,2176]{2,1,0:T(1,128)} %bitcast.16), calls=%async_computation.11 | async-start | bytes 278528 | tf_op jit(solution)/shard_map/all_to_all | solution.py:408
  271.7 0.9 place_kernel.5
  272.6 4.4 %collective-permute-start.17 = (f32[2,64,256]{2,1,0:T(8,128)S(1)}, f32[2,64,256]{2,1,0:T(8,128)S(1)}, u32[]{:S(2)}, u32[]{:S(2)}) collective-permute-start(f32[2,64,256]{2,1,0:T(8,128)S(1)} %get-tuple-element.104), channel_id=1, source_target_pairs={{0,8},{8,16},{16,24},{24,32},{32,40},{40,48},{48,56},{56,64},{64,7... | collective-permute-start | bytes 393224 | tf_op jit(solution)/shard_map/ppermute | solution.py:392
  277.1 2.7 collective-permute-done.17.refs_2_
  280.6 17.1 %all_to_all.76 = f32[16,16,128]{2,1,0:T(8,128)S(1)} all-to-all(f32[16,16,128]{2,1,0:T(8,128)S(1)} %get-tuple-element.105), channel_id=1, replica_groups=mesh['xlo'=2,'z'=16,'core'=2,'xhi'=2,'y'=4] {'z'}, dimensions={0} | all-to-all | bytes 262144 | tf_op jit(solution)/shard_map/all_to_all | solution.py:413
  297.9 21.3 %all_to_all.77.refs_0_ = f32[8,352,128]{2,1,0:T(8,128)S(1)} all-to-all(f32[8,352,128]{2,1,0:T(8,128)S(1)} %tail_kernel.1), channel_id=1, replica_groups=mesh['xlo'=2,'z'=16,'core'=2,'xhi'=2,'y'=4] {'xhi','y'}, dimensions={0} | all-to-all | bytes 2883584 | tf_op jit(solution)/shard_map/all_to_all | solution.py:413
  319.2 14.3 %all-gather = f32[32,32,128]{2,1,0:T(8,128)S(1)} all-gather(f32[8,32,128]{2,1,0:T(8,128)S(1)} %slice.19), channel_id=2, replica_groups=mesh['xlo'=2,'z'=16,'core'=2,'xhi'=2,'y'=4] {'xlo','core'}, dimensions={0}, use_global_device_ids=true | all-gather | bytes 655360 | tf_op jit(solution)/shard_map/all_gather | solution.py:417
  333.5 0.8 probe_out_kernel.1
  334.4 1.1 object_kernel.1
  (58 shorter events, 7.7 us)
Async XLA Ops:
  0.6 9.6 %copy-start.2 = (f32[2,288,512]{2,1,0:T(8,128)S(1)}, f32[2,288,512]{2,1,0:T(8,128)}, u32[]{:S(2)}) copy-start(f32[2,288,512]{2,1,0:T(8,128)} %whole.1) | copy-start | bytes 3538948
  0.6 1.1 copy-start.3
  2.6 12.6 %copy-start.4 = (s32[1,3]{1,0:T(1,128)S(1)}, s32[1,3]{1,0:T(1,128)}, u32[]{:S(2)}) copy-start(s32[1,3]{1,0:T(1,128)} %param.14) | copy-start | bytes 40
  2.6 12.6 %copy-start.5 = (s32[1,3]{1,0:T(1,128)S(1)}, s32[1,3]{1,0:T(1,128)}, u32[]{:S(2)}) copy-start(s32[1,3]{1,0:T(1,128)} %param.12) | copy-start | bytes 40
  2.6 12.6 %copy-start.6 = (s32[1,3]{1,0:T(1,128)S(1)}, s32[1,3]{1,0:T(1,128)}, u32[]{:S(2)}) copy-start(s32[1,3]{1,0:T(1,128)} %param.11) | copy-start | bytes 40
  2.6 13.9 %copy-start.1 = (bf16[1,3,256,256]{3,2,1,0:T(8,128)(2,1)S(1)}, bf16[1,3,256,256]{3,2,1,0:T(8,128)(2,1)}, u32[]{:S(2)}) copy-start(bf16[1,3,256,256]{3,2,1,0:T(8,128)(2,1)} %refs_1_.5) | copy-start | bytes 1179652
  2.6 16.5 %copy-start = (bf16[3,2,256,256]{3,2,1,0:T(8,128)(2,1)S(1)}, bf16[3,2,256,256]{3,2,1,0:T(8,128)(2,1)}, u32[]{:S(2)}) copy-start(bf16[3,2,256,256]{3,2,1,0:T(8,128)(2,1)} %constant.35.clone.refs_4_.refs_3_.refs_2_) | copy-start | bytes 2359300
  2.6 16.5 %all-to-all-start = ((f32[8,2,32,256]{3,2,1,0:T(8,128)}), f32[8,2,32,256]{3,2,1,0:T(8,128)S(1)}, u32[]{:S(2)}, u32[]{:S(2)}) async-start(f32[8,2,32,256]{3,2,1,0:T(8,128)} %split_kernel.1._), calls=%async_computation | async-start | bytes 1048576 | tf_op jit(solution)/shard_map/all_to_all | solution.py:413
  10.3 7.3 %collective-permute-start = (f32[2,64,256]{2,1,0:T(8,128)S(1)}, f32[2,64,256]{2,1,0:T(8,128)S(1)}, u32[]{:S(2)}, u32[]{:S(2)}) collective-permute-start(f32[2,64,256]{2,1,0:T(8,128)S(1)} %get-tuple-element.55), channel_id=1, source_target_pairs={{8,0},{16,8},{24,16},{32,24},{40,32},{48,40},{56,48},{64,56},{72,6... | collective-permute-start | bytes 393224 | tf_op jit(solution)/shard_map/ppermute | solution.py:392
  49.5 6.5 %collective-permute-start.1 = (f32[17,16,256]{2,1,0:T(8,128)S(1)}, f32[17,16,256]{2,1,0:T(8,128)S(1)}, u32[]{:S(2)}, u32[]{:S(2)}) collective-permute-start(f32[17,16,256]{2,1,0:T(8,128)S(1)} %get-tuple-element.61), channel_id=1, source_target_pairs={{0,8},{8,0},{1,9},{9,1},{2,10},{10,2},{3,11},{11,3},{4,12},{12,4},... | collective-permute-start | bytes 835592 | tf_op jit(solution)/shard_map/ppermute | solution.py:396
  55.9 10.5 %collective-permute-start.2 = (f32[17,8,256]{2,1,0:T(8,128)S(1)}, f32[17,8,256]{2,1,0:T(8,128)S(1)}, u32[]{:S(2)}, u32[]{:S(2)}) collective-permute-start(f32[17,8,256]{2,1,0:T(8,128)S(1)} %get-tuple-element.63), channel_id=1, source_target_pairs={{0,256},{256,0},{1,257},{257,1},{2,258},{258,2},{3,259},{259,3},{4... | collective-permute-start | bytes 417800 | tf_op jit(solution)/shard_map/ppermute | solution.py:396
  67.1 23.6 %all-to-all-start.3 = ((f32[16,1,2176]{2,1,0:T(1,128)}), f32[16,1,2176]{2,1,0:T(1,128)S(1)}, u32[]{:S(2)}, u32[]{:S(2)}) async-start(f32[16,1,2176]{2,1,0:T(1,128)} %bitcast.8), calls=%async_computation.3 | async-start | bytes 278528 | tf_op jit(solution)/shard_map/all_to_all | solution.py:408
  84.1 5.3 %collective-permute-start.4 = (f32[2,32,256]{2,1,0:T(8,128)S(1)}, f32[2,32,256]{2,1,0:T(8,128)S(1)}, u32[]{:S(2)}, u32[]{:S(2)}) collective-permute-start(f32[2,32,256]{2,1,0:T(8,128)S(1)} %step_kernel.3.refs_2_), channel_id=1, source_target_pairs={{1,0},{2,1},{3,2},{7,3},{6,7},{5,6},{4,5},{9,8},{10,9},{11,10},{15... | collective-permute-start | bytes 196616 | tf_op jit(solution)/shard_map/ppermute | solution.py:402
  85.4 5.3 %collective-permute-start.3 = (f32[2,32,256]{2,1,0:T(8,128)S(1)}, f32[2,32,256]{2,1,0:T(8,128)S(1)}, u32[]{:S(2)}, u32[]{:S(2)}) collective-permute-start(f32[2,32,256]{2,1,0:T(8,128)S(1)} %step_kernel.3.refs_2_), channel_id=1, source_target_pairs={{0,1},{1,2},{2,3},{3,7},{7,6},{6,5},{5,4},{8,9},{9,10},{10,11},{11... | collective-permute-start | bytes 196616 | tf_op jit(solution)/shard_map/ppermute | solution.py:402
  91.4 21.8 %all-to-all-start.4 = ((f32[16,16,128]{2,1,0:T(8,128)}), f32[16,16,128]{2,1,0:T(8,128)S(1)}, u32[]{:S(2)}, u32[]{:S(2)}) async-start(f32[16,16,128]{2,1,0:T(8,128)} %get-tuple-element.67.refs_5_), calls=%async_computation.4 | async-start | bytes 262144 | tf_op jit(solution)/shard_map/all_to_all | solution.py:413
  98.9 10.5 %collective-permute-start.5 = (f32[2,64,256]{2,1,0:T(8,128)S(1)}, f32[2,64,256]{2,1,0:T(8,128)S(1)}, u32[]{:S(2)}, u32[]{:S(2)}) collective-permute-start(f32[2,64,256]{2,1,0:T(8,128)S(1)} %get-tuple-element.70), channel_id=1, source_target_pairs={{0,8},{8,16},{16,24},{24,32},{32,40},{40,48},{48,56},{56,64},{64,7... | collective-permute-start | bytes 393224 | tf_op jit(solution)/shard_map/ppermute | solution.py:392
  106.1 6.8 %collective-permute-start.6 = (f32[2,64,256]{2,1,0:T(8,128)S(1)}, f32[2,64,256]{2,1,0:T(8,128)S(1)}, u32[]{:S(2)}, u32[]{:S(2)}) collective-permute-start(f32[2,64,256]{2,1,0:T(8,128)S(1)} %get-tuple-element.71), channel_id=1, source_target_pairs={{8,0},{16,8},{24,16},{32,24},{40,32},{48,40},{56,48},{64,56},{72,6... | collective-permute-start | bytes 393224 | tf_op jit(solution)/shard_map/ppermute | solution.py:392
  152.0 5.5 %collective-permute-start.7 = (f32[17,16,256]{2,1,0:T(8,128)S(1)}, f32[17,16,256]{2,1,0:T(8,128)S(1)}, u32[]{:S(2)}, u32[]{:S(2)}) collective-permute-start(f32[17,16,256]{2,1,0:T(8,128)S(1)} %get-tuple-element.78), channel_id=1, source_target_pairs={{0,8},{8,0},{1,9},{9,1},{2,10},{10,2},{3,11},{11,3},{4,12},{12,4},... | collective-permute-start | bytes 835592 | tf_op jit(solution)/shard_map/ppermute | solution.py:396
  157.6 6.8 %collective-permute-start.8 = (f32[17,8,256]{2,1,0:T(8,128)S(1)}, f32[17,8,256]{2,1,0:T(8,128)S(1)}, u32[]{:S(2)}, u32[]{:S(2)}) collective-permute-start(f32[17,8,256]{2,1,0:T(8,128)S(1)} %get-tuple-element.80), channel_id=1, source_target_pairs={{0,256},{256,0},{1,257},{257,1},{2,258},{258,2},{3,259},{259,3},{4... | collective-permute-start | bytes 417800 | tf_op jit(solution)/shard_map/ppermute | solution.py:396
  165.0 18.1 %all-to-all-start.7 = ((f32[16,1,2176]{2,1,0:T(1,128)}), f32[16,1,2176]{2,1,0:T(1,128)S(1)}, u32[]{:S(2)}, u32[]{:S(2)}) async-start(f32[16,1,2176]{2,1,0:T(1,128)} %bitcast.12), calls=%async_computation.7 | async-start | bytes 278528 | tf_op jit(solution)/shard_map/all_to_all | solution.py:408
  176.5 5.3 %collective-permute-start.10 = (f32[2,32,256]{2,1,0:T(8,128)S(1)}, f32[2,32,256]{2,1,0:T(8,128)S(1)}, u32[]{:S(2)}, u32[]{:S(2)}) collective-permute-start(f32[2,32,256]{2,1,0:T(8,128)S(1)} %step_kernel.4.refs_2_), channel_id=1, source_target_pairs={{1,0},{2,1},{3,2},{7,3},{6,7},{5,6},{4,5},{9,8},{10,9},{11,10},{15... | collective-permute-start | bytes 196616 | tf_op jit(solution)/shard_map/ppermute | solution.py:402
  177.8 5.3 %collective-permute-start.9 = (f32[2,32,256]{2,1,0:T(8,128)S(1)}, f32[2,32,256]{2,1,0:T(8,128)S(1)}, u32[]{:S(2)}, u32[]{:S(2)}) collective-permute-start(f32[2,32,256]{2,1,0:T(8,128)S(1)} %step_kernel.4.refs_2_), channel_id=1, source_target_pairs={{0,1},{1,2},{2,3},{3,7},{7,6},{6,5},{5,4},{8,9},{9,10},{10,11},{11... | collective-permute-start | bytes 196616 | tf_op jit(solution)/shard_map/ppermute | solution.py:402
  183.8 21.8 %all-to-all-start.8 = ((f32[16,16,128]{2,1,0:T(8,128)}), f32[16,16,128]{2,1,0:T(8,128)S(1)}, u32[]{:S(2)}, u32[]{:S(2)}) async-start(f32[16,16,128]{2,1,0:T(8,128)} %get-tuple-element.85.refs_5_), calls=%async_computation.8 | async-start | bytes 262144 | tf_op jit(solution)/shard_map/all_to_all | solution.py:413
  191.3 10.5 %collective-permute-start.11 = (f32[2,64,256]{2,1,0:T(8,128)S(1)}, f32[2,64,256]{2,1,0:T(8,128)S(1)}, u32[]{:S(2)}, u32[]{:S(2)}) collective-permute-start(f32[2,64,256]{2,1,0:T(8,128)S(1)} %get-tuple-element.88), channel_id=1, source_target_pairs={{0,8},{8,16},{16,24},{24,32},{32,40},{40,48},{48,56},{56,64},{64,7... | collective-permute-start | bytes 393224 | tf_op jit(solution)/shard_map/ppermute | solution.py:392
  198.5 6.8 %collective-permute-start.12 = (f32[2,64,256]{2,1,0:T(8,128)S(1)}, f32[2,64,256]{2,1,0:T(8,128)S(1)}, u32[]{:S(2)}, u32[]{:S(2)}) collective-permute-start(f32[2,64,256]{2,1,0:T(8,128)S(1)} %get-tuple-element.89), channel_id=1, source_target_pairs={{8,0},{16,8},{24,16},{32,24},{40,32},{48,40},{56,48},{64,56},{72,6... | collective-permute-start | bytes 393224 | tf_op jit(solution)/shard_map/ppermute | solution.py:392
  245.0 5.5 %collective-permute-start.13 = (f32[17,16,256]{2,1,0:T(8,128)S(1)}, f32[17,16,256]{2,1,0:T(8,128)S(1)}, u32[]{:S(2)}, u32[]{:S(2)}) collective-permute-start(f32[17,16,256]{2,1,0:T(8,128)S(1)} %get-tuple-element.96), channel_id=1, source_target_pairs={{0,8},{8,0},{1,9},{9,1},{2,10},{10,2},{3,11},{11,3},{4,12},{12,4},... | collective-permute-start | bytes 835592 | tf_op jit(solution)/shard_map/ppermute | solution.py:396
  250.6 9.0 %collective-permute-start.14 = (f32[17,8,256]{2,1,0:T(8,128)S(1)}, f32[17,8,256]{2,1,0:T(8,128)S(1)}, u32[]{:S(2)}, u32[]{:S(2)}) collective-permute-start(f32[17,8,256]{2,1,0:T(8,128)S(1)} %get-tuple-element.98), channel_id=1, source_target_pairs={{0,256},{256,0},{1,257},{257,1},{2,258},{258,2},{3,259},{259,3},{4... | collective-permute-start | bytes 417800 | tf_op jit(solution)/shard_map/ppermute | solution.py:396
  253.0 5.3 %collective-permute-start.16 = (f32[2,32,256]{2,1,0:T(8,128)S(1)}, f32[2,32,256]{2,1,0:T(8,128)S(1)}, u32[]{:S(2)}, u32[]{:S(2)}) collective-permute-start(f32[2,32,256]{2,1,0:T(8,128)S(1)} %step_kernel.5.refs_2_), channel_id=1, source_target_pairs={{1,0},{2,1},{3,2},{7,3},{6,7},{5,6},{4,5},{9,8},{10,9},{11,10},{15... | collective-permute-start | bytes 196616 | tf_op jit(solution)/shard_map/ppermute | solution.py:402
  254.3 5.3 %collective-permute-start.15 = (f32[2,32,256]{2,1,0:T(8,128)S(1)}, f32[2,32,256]{2,1,0:T(8,128)S(1)}, u32[]{:S(2)}, u32[]{:S(2)}) collective-permute-start(f32[2,32,256]{2,1,0:T(8,128)S(1)} %step_kernel.5.refs_2_), channel_id=1, source_target_pairs={{0,1},{1,2},{2,3},{3,7},{7,6},{6,5},{5,4},{8,9},{9,10},{10,11},{11... | collective-permute-start | bytes 196616 | tf_op jit(solution)/shard_map/ppermute | solution.py:402
  260.2 19.7 %all-to-all-start.11 = ((f32[16,1,2176]{2,1,0:T(1,128)}), f32[16,1,2176]{2,1,0:T(1,128)S(1)}, u32[]{:S(2)}, u32[]{:S(2)}) async-start(f32[16,1,2176]{2,1,0:T(1,128)} %bitcast.16), calls=%async_computation.11 | async-start | bytes 278528 | tf_op jit(solution)/shard_map/all_to_all | solution.py:408
  272.6 7.2 %collective-permute-start.17 = (f32[2,64,256]{2,1,0:T(8,128)S(1)}, f32[2,64,256]{2,1,0:T(8,128)S(1)}, u32[]{:S(2)}, u32[]{:S(2)}) collective-permute-start(f32[2,64,256]{2,1,0:T(8,128)S(1)} %get-tuple-element.104), channel_id=1, source_target_pairs={{0,8},{8,16},{16,24},{24,32},{32,40},{40,48},{48,56},{56,64},{64,7... | collective-permute-start | bytes 393224 | tf_op jit(solution)/shard_map/ppermute | solution.py:392

commit v11 on v10

--- a/solution.py
+++ b/solution.py
@@ -296,28 +296,32 @@
     rows_out[:, :, SIDE:] = part_band[:, rows, SIDE:WIDTH]
 
 
-def tail_kernel(piece, rows_out, tail):
+def tail_kernel(piece, tail):
     for place in range(MODES):
         for half in range(2):
             for part in range(2):
                 row = (half * 2 + part) * 8
                 rows = pl.ds(RINGS * half + 2 * place + part, 8, stride=2 * RINGS)
                 tail[place, row : row + 8] = piece[rows, :]
+
+
+def spread_kernel(rows_out, spread):
+    for place in range(MODES):
         for part in range(2):
             for block in range(WIDTH // LANES):
-                row = 32 + (part * 4 + block) * OUT_ROWS
+                row = (part * 4 + block) * OUT_ROWS
                 lanes = slice(block * LANES, (block + 1) * LANES)
-                tail[place, row : row + OUT_ROWS] = rows_out[part, :, lanes]
-
-
-def object_kernel(tail, object_out):
+                spread[place, row : row + OUT_ROWS] = rows_out[part, :, lanes]
+
+
+def object_kernel(spread, object_out):
     for place in range(MODES):
         first = slab_of(place) * 9 // 2 * 8
         for part in range(2):
             for block in range(WIDTH // LANES):
-                row = 32 + (part * 4 + block) * OUT_ROWS
+                row = (part * 4 + block) * OUT_ROWS
                 lanes = slice(block * LANES, (block + 1) * LANES)
-                object_out[part, first : first + OUT_ROWS, lanes] = tail[
+                object_out[part, first : first + OUT_ROWS, lanes] = spread[
                     place, row : row + OUT_ROWS
                 ]
 
@@ -525,7 +529,10 @@
             (rows_out,) = call(
                 out_rows_kernel, [(2, OUT_ROWS, WIDTH)], scal, part_band, from_left
             )
-            before = (rows_out,)
+            (spread,) = call(
+                spread_kernel, [(MODES, 8 * OUT_ROWS, LANES)], rows_out, scalars=False
+            )
+            before = (spread,)
         else:
             before = (above, below)
         shard, shards = call(
@@ -536,8 +543,11 @@
             scalars=False,
             after=before,
         )
-        piece = exchange(shards, "z")
-        if not final:
+        if final:
+            spread = exchange(spread, MODE_AXES)
+            piece = lax.all_gather(shard, "z")
+        else:
+            piece = exchange(shards, "z")
             part_band, to_left, to_right = call(
                 place_kernel, [band_shape, edge, edge], *placing, after=(shards,)
             )
@@ -553,17 +563,15 @@
             )
             piece, view = lax.optimization_barrier((piece, view))
             pieces = gather_pieces(piece.reshape(2 * MODES * RINGS, LANES))
-    tail_rows = 32 + 8 * OUT_ROWS
     (tail,) = call(
         tail_kernel,
-        [(MODES, tail_rows, LANES)],
+        [(MODES, 32, LANES)],
         piece.reshape(2 * MODES * RINGS, LANES),
-        rows_out,
         scalars=False,
+        after=(spread,),
     )
-    tail = exchange(tail, MODE_AXES)
-    pieces = gather_pieces(tail[:, :32])
-    (object_out,) = call(object_kernel, [(2, HEIGHT, WIDTH)], tail, scalars=False)
+    pieces = gather_pieces(exchange(tail, MODE_AXES))
+    (object_out,) = call(object_kernel, [(2, HEIGHT, WIDTH)], spread, scalars=False)
     (probe_out,) = call(probe_out_kernel, [(1, 2, SIDE, SIDE)], pieces, scalars=False)
     return object_out, probe_out
 

time: 337 us -> 344 us (1.021)
  blocking collectives: 152 us -> 139 us
  starting transfers between devices: 131 us -> 144 us
  waiting for transfers between devices: 28.8 us -> 34.5 us
    all_to_all x8 -> x6, blocking collectives: 119 us -> 81.1 us  [exchange(): return lax.all_to_all(value, axes, 0, 0, tiled=True)]
    all_gather x0 -> x1, blocking collectives: none -> 24.9 us  [per_device(): piece = lax.all_gather(shard, 'z')]
    all_to_all x3 -> x5, starting transfers between devices: 22 us -> 34.3 us  [exchange(): return lax.all_to_all(value, axes, 0, 0, tiled=True)]
    all_to_all x3 -> x5, waiting for transfers between devices: 1.43 us -> 7.13 us  [exchange(): return lax.all_to_all(value, axes, 0, 0, tiled=True)]
    pallas_call x34 -> x35, Pallas kernels: 20.1 us -> 21.9 us  [call(): pl.pallas_call(body, out_shape=[jax.ShapeDtypeStruct(shape, F32) for shap...]
  transfers between devices with their start and end apart: 24 -> 26, of which waited for: 15 -> 16; matrix products, arithmetic and copies ran while one was open for 0% -> 0% of each run, Pallas kernels for 1% -> 2%
where the time goes in v11:
time: 344 us; the launch traced here: 343 us
  starting transfers between devices  144 us (42%)
  blocking collectives  139 us (40%)
  waiting for transfers between devices  34.5 us (10%)
  Pallas kernels  22 us (6%)
    all_to_all x6, blocking collectives, exchange(): return lax.all_to_all(value, axes, 0, 0, tiled=True)  81.1 us
    all_to_all x3, starting transfers between devices, exchange_rings(): lax.all_to_all(value, 'z', 0, 0, tiled=True, axis_index_groups=groups)  40 us
    all_to_all x5, starting transfers between devices, exchange(): return lax.all_to_all(value, axes, 0, 0, tiled=True)  34.3 us
    all_gather x3, blocking collectives, gather_pieces(): gathered = lax.all_gather(piece, ('xlo', 'core'))  33.2 us
    ppermute x6, starting transfers between devices, shift(): lax.ppermute(value, axes, [(i, i + steps) for i in range(first, last)])  27.7 us
    ppermute x6, starting transfers between devices, other(): return lax.ppermute(value, axis, [(0, 1), (1, 0)])  25.8 us
    all_gather x1, blocking collectives, per_device(): piece = lax.all_gather(shard, 'z')  24.9 us
    pallas_call x35, Pallas kernels, call(): pl.pallas_call(body, out_shape=[jax.ShapeDtypeStruct(shape, F32) for shap...  21.9 us
  transfers between devices with their start and end apart: 26, of which 16 were waited for; matrix products, arithmetic and copies ran while one was open for 0% of the time, Pallas kernels for 2%

profile of v11, /device:TPU:1, one launch (start us, length us, event | category | flops | bytes accessed | tf_op | source)
XLA Modules:
  0.0 342.8 jit_solution(6076675194296430309)
XLA Ops:
  0.6 1.1 copy-done.3
  1.8 0.8 split_kernel.1._
  2.6 7.6 %all-to-all-start = ((f32[8,2,32,256]{3,2,1,0:T(8,128)}), f32[8,2,32,256]{3,2,1,0:T(8,128)S(1)}, u32[]{:S(2)}, u32[]{:S(2)}) async-start(f32[8,2,32,256]{3,2,1,0:T(8,128)} %split_kernel.1._), calls=%async_computation | async-start | bytes 1048576 | tf_op jit(solution)/shard_map/all_to_all | solution.py:417
  10.3 4.9 %collective-permute-start = (f32[2,64,256]{2,1,0:T(8,128)S(1)}, f32[2,64,256]{2,1,0:T(8,128)S(1)}, u32[]{:S(2)}, u32[]{:S(2)}) collective-permute-start(f32[2,64,256]{2,1,0:T(8,128)S(1)} %get-tuple-element.55), channel_id=1, source_target_pairs={{8,0},{16,8},{24,16},{32,24},{40,32},{48,40},{56,48},{64,56},{72,6... | collective-permute-start | bytes 393224 | tf_op jit(solution)/shard_map/ppermute | solution.py:396
  17.0 0.8 collective-permute-done.refs_2_
  17.8 1.3 all-to-all-done.refs_3_.refs_1_
  19.1 1.0 first_kernel.1
  20.1 15.1 %all_to_all.70.refs_0_ = f32[8,2,32,256]{3,2,1,0:T(8,128)S(1)} all-to-all(f32[8,2,32,256]{3,2,1,0:T(8,128)S(1)} %get-tuple-element.57), channel_id=1, replica_groups=mesh['xlo'=2,'z'=16,'core'=2,'xhi'=2,'y'=4] {'xhi','y'}, dimensions={0} | all-to-all | bytes 1048576 | tf_op jit(solution)/shard_map/all_to_all | solution.py:417
  35.2 1.4 ratio_kernel.3
  36.5 12.3 %all_to_all.71.refs_0_ = f32[8,2,32,256]{3,2,1,0:T(8,128)S(1)} all-to-all(f32[8,2,32,256]{3,2,1,0:T(8,128)S(1)} %ratio_kernel.3), channel_id=1, replica_groups=mesh['xlo'=2,'z'=16,'core'=2,'xhi'=2,'y'=4] {'xhi','y'}, dimensions={0} | all-to-all | bytes 1048576 | tf_op jit(solution)/shard_map/all_to_all | solution.py:417
  49.6 5.3 %collective-permute-start.1 = (f32[17,16,256]{2,1,0:T(8,128)S(1)}, f32[17,16,256]{2,1,0:T(8,128)S(1)}, u32[]{:S(2)}, u32[]{:S(2)}) collective-permute-start(f32[17,16,256]{2,1,0:T(8,128)S(1)} %get-tuple-element.61), channel_id=1, source_target_pairs={{0,8},{8,0},{1,9},{9,1},{2,10},{10,2},{3,11},{11,3},{4,12},{12,4},... | collective-permute-start | bytes 835592 | tf_op jit(solution)/shard_map/ppermute | solution.py:400
  54.9 1.2 collective-permute-done.1.refs_1_
  56.1 6.7 %collective-permute-start.2 = (f32[17,8,256]{2,1,0:T(8,128)S(1)}, f32[17,8,256]{2,1,0:T(8,128)S(1)}, u32[]{:S(2)}, u32[]{:S(2)}) collective-permute-start(f32[17,8,256]{2,1,0:T(8,128)S(1)} %get-tuple-element.63), channel_id=1, source_target_pairs={{0,256},{256,0},{1,257},{257,1},{2,258},{258,2},{3,259},{259,3},{4... | collective-permute-start | bytes 417800 | tf_op jit(solution)/shard_map/ppermute | solution.py:400
  63.4 3.2 collective-permute-done.2.refs_1_
  67.2 17.0 %all-to-all-start.3 = ((f32[16,1,2176]{2,1,0:T(1,128)}), f32[16,1,2176]{2,1,0:T(1,128)S(1)}, u32[]{:S(2)}, u32[]{:S(2)}) async-start(f32[16,1,2176]{2,1,0:T(1,128)} %bitcast.8), calls=%async_computation.3 | async-start | bytes 278528 | tf_op jit(solution)/shard_map/all_to_all | solution.py:412
  84.3 1.3 collective-permute-start.4
  85.5 4.0 %collective-permute-start.3 = (f32[2,32,256]{2,1,0:T(8,128)S(1)}, f32[2,32,256]{2,1,0:T(8,128)S(1)}, u32[]{:S(2)}, u32[]{:S(2)}) collective-permute-start(f32[2,32,256]{2,1,0:T(8,128)S(1)} %step_kernel.3.refs_2_), channel_id=1, source_target_pairs={{0,1},{1,2},{2,3},{3,7},{7,6},{6,5},{5,4},{8,9},{9,10},{10,11},{11... | collective-permute-start | bytes 196616 | tf_op jit(solution)/shard_map/ppermute | solution.py:406
  89.5 1.3 collective-permute-done.3.refs_2_.refs_1_
  91.5 7.2 %all-to-all-start.4 = ((f32[16,16,128]{2,1,0:T(8,128)}), f32[16,16,128]{2,1,0:T(8,128)S(1)}, u32[]{:S(2)}, u32[]{:S(2)}) async-start(f32[16,16,128]{2,1,0:T(8,128)} %get-tuple-element.67.refs_5_), calls=%async_computation.4 | async-start | bytes 262144 | tf_op jit(solution)/shard_map/all_to_all | solution.py:417
  99.0 7.3 %collective-permute-start.5 = (f32[2,64,256]{2,1,0:T(8,128)S(1)}, f32[2,64,256]{2,1,0:T(8,128)S(1)}, u32[]{:S(2)}, u32[]{:S(2)}) collective-permute-start(f32[2,64,256]{2,1,0:T(8,128)S(1)} %get-tuple-element.70), channel_id=1, source_target_pairs={{0,8},{8,16},{16,24},{24,32},{32,40},{40,48},{48,56},{56,64},{64,7... | collective-permute-start | bytes 393224 | tf_op jit(solution)/shard_map/ppermute | solution.py:396
  106.3 1.9 collective-permute-start.6
  108.2 1.3 collective-permute-done.5.refs_2_
  109.5 3.6 %collective-permute-done.6.refs_3_ = f32[2,64,256]{2,1,0:T(8,128)S(1)} collective-permute-done((f32[2,64,256]{2,1,0:T(8,128)S(1)}, f32[2,64,256]{2,1,0:T(8,128)S(1)}, u32[]{:S(2)}, u32[]{:S(2)}) %collective-permute-start.6) | collective-permute-done | bytes 131104 | tf_op jit(solution)/shard_map/ppermute | solution.py:396
  113.4 8.8 %all_gather.18 = f32[4,256,128]{2,1,0:T(8,128)S(1)} all-gather(f32[1,256,128]{2,1,0:T(8,128)S(1)} %bitcast.26), channel_id=1, replica_groups=mesh['xlo'=2,'z'=16,'core'=2,'xhi'=2,'y'=4] {'xlo','core'}, dimensions={0}, use_global_device_ids=true | all-gather | bytes 655360 | tf_op jit(solution)/shard_map/all_gather | solution.py:421
  122.2 1.0 next_kernel.2
  123.2 12.9 %all_to_all.72.refs_0_ = f32[8,2,32,256]{3,2,1,0:T(8,128)S(1)} all-to-all(f32[8,2,32,256]{3,2,1,0:T(8,128)S(1)} %get-tuple-element.75), channel_id=1, replica_groups=mesh['xlo'=2,'z'=16,'core'=2,'xhi'=2,'y'=4] {'xhi','y'}, dimensions={0} | all-to-all | bytes 1048576 | tf_op jit(solution)/shard_map/all_to_all | solution.py:417
  136.2 1.4 ratio_kernel.4
  137.6 13.8 %all_to_all.73.refs_0_ = f32[8,2,32,256]{3,2,1,0:T(8,128)S(1)} all-to-all(f32[8,2,32,256]{3,2,1,0:T(8,128)S(1)} %ratio_kernel.4), channel_id=1, replica_groups=mesh['xlo'=2,'z'=16,'core'=2,'xhi'=2,'y'=4] {'xhi','y'}, dimensions={0} | all-to-all | bytes 1048576 | tf_op jit(solution)/shard_map/all_to_all | solution.py:417
  152.1 4.4 %collective-permute-start.7 = (f32[17,16,256]{2,1,0:T(8,128)S(1)}, f32[17,16,256]{2,1,0:T(8,128)S(1)}, u32[]{:S(2)}, u32[]{:S(2)}) collective-permute-start(f32[17,16,256]{2,1,0:T(8,128)S(1)} %get-tuple-element.78), channel_id=1, source_target_pairs={{0,8},{8,0},{1,9},{9,1},{2,10},{10,2},{3,11},{11,3},{4,12},{12,4},... | collective-permute-start | bytes 835592 | tf_op jit(solution)/shard_map/ppermute | solution.py:400
  156.5 1.2 collective-permute-done.7.refs_1_
  157.7 2.8 collective-permute-start.8
  161.1 3.4 collective-permute-done.8.refs_1_
  165.2 11.5 %all-to-all-start.7 = ((f32[16,1,2176]{2,1,0:T(1,128)}), f32[16,1,2176]{2,1,0:T(1,128)S(1)}, u32[]{:S(2)}, u32[]{:S(2)}) async-start(f32[16,1,2176]{2,1,0:T(1,128)} %bitcast.12), calls=%async_computation.7 | async-start | bytes 278528 | tf_op jit(solution)/shard_map/all_to_all | solution.py:412
  176.6 1.3 collective-permute-start.10
  177.9 4.0 %collective-permute-start.9 = (f32[2,32,256]{2,1,0:T(8,128)S(1)}, f32[2,32,256]{2,1,0:T(8,128)S(1)}, u32[]{:S(2)}, u32[]{:S(2)}) collective-permute-start(f32[2,32,256]{2,1,0:T(8,128)S(1)} %step_kernel.4.refs_2_), channel_id=1, source_target_pairs={{0,1},{1,2},{2,3},{3,7},{7,6},{6,5},{5,4},{8,9},{9,10},{10,11},{11... | collective-permute-start | bytes 196616 | tf_op jit(solution)/shard_map/ppermute | solution.py:406
  181.9 1.3 collective-permute-done.9.refs_2_.refs_1_
  183.9 7.2 %all-to-all-start.8 = ((f32[16,16,128]{2,1,0:T(8,128)}), f32[16,16,128]{2,1,0:T(8,128)S(1)}, u32[]{:S(2)}, u32[]{:S(2)}) async-start(f32[16,16,128]{2,1,0:T(8,128)} %get-tuple-element.85.refs_5_), calls=%async_computation.8 | async-start | bytes 262144 | tf_op jit(solution)/shard_map/all_to_all | solution.py:417
  191.4 7.3 %collective-permute-start.11 = (f32[2,64,256]{2,1,0:T(8,128)S(1)}, f32[2,64,256]{2,1,0:T(8,128)S(1)}, u32[]{:S(2)}, u32[]{:S(2)}) collective-permute-start(f32[2,64,256]{2,1,0:T(8,128)S(1)} %get-tuple-element.88), channel_id=1, source_target_pairs={{0,8},{8,16},{16,24},{24,32},{32,40},{40,48},{48,56},{56,64},{64,7... | collective-permute-start | bytes 393224 | tf_op jit(solution)/shard_map/ppermute | solution.py:396
  198.7 1.9 collective-permute-start.12
  200.6 1.3 collective-permute-done.11.refs_2_
  201.9 3.6 %collective-permute-done.12.refs_3_ = f32[2,64,256]{2,1,0:T(8,128)S(1)} collective-permute-done((f32[2,64,256]{2,1,0:T(8,128)S(1)}, f32[2,64,256]{2,1,0:T(8,128)S(1)}, u32[]{:S(2)}, u32[]{:S(2)}) %collective-permute-start.12) | collective-permute-done | bytes 131104 | tf_op jit(solution)/shard_map/ppermute | solution.py:396
  205.8 9.2 %all_gather.19 = f32[4,256,128]{2,1,0:T(8,128)S(1)} all-gather(f32[1,256,128]{2,1,0:T(8,128)S(1)} %bitcast.27), channel_id=1, replica_groups=mesh['xlo'=2,'z'=16,'core'=2,'xhi'=2,'y'=4] {'xlo','core'}, dimensions={0}, use_global_device_ids=true | all-gather | bytes 655360 | tf_op jit(solution)/shard_map/all_gather | solution.py:421
  215.0 1.0 next_kernel.3
  216.0 13.1 %all_to_all.74.refs_0_ = f32[8,2,32,256]{3,2,1,0:T(8,128)S(1)} all-to-all(f32[8,2,32,256]{3,2,1,0:T(8,128)S(1)} %get-tuple-element.93), channel_id=1, replica_groups=mesh['xlo'=2,'z'=16,'core'=2,'xhi'=2,'y'=4] {'xhi','y'}, dimensions={0} | all-to-all | bytes 1048576 | tf_op jit(solution)/shard_map/all_to_all | solution.py:417
  229.0 1.4 ratio_kernel.5
  230.4 14.0 %all_to_all.75.refs_0_ = f32[8,2,32,256]{3,2,1,0:T(8,128)S(1)} all-to-all(f32[8,2,32,256]{3,2,1,0:T(8,128)S(1)} %ratio_kernel.5), channel_id=1, replica_groups=mesh['xlo'=2,'z'=16,'core'=2,'xhi'=2,'y'=4] {'xhi','y'}, dimensions={0} | all-to-all | bytes 1048576 | tf_op jit(solution)/shard_map/all_to_all | solution.py:417
  245.2 4.4 %collective-permute-start.13 = (f32[17,16,256]{2,1,0:T(8,128)S(1)}, f32[17,16,256]{2,1,0:T(8,128)S(1)}, u32[]{:S(2)}, u32[]{:S(2)}) collective-permute-start(f32[17,16,256]{2,1,0:T(8,128)S(1)} %get-tuple-element.98), channel_id=1, source_target_pairs={{0,8},{8,0},{1,9},{9,1},{2,10},{10,2},{3,11},{11,3},{4,12},{12,4},... | collective-permute-start | bytes 835592 | tf_op jit(solution)/shard_map/ppermute | solution.py:400
  249.5 1.2 collective-permute-done.13.refs_1_
  250.7 2.2 collective-permute-start.16
  253.1 1.3 collective-permute-start.15
  254.4 4.0 %collective-permute-start.14 = (f32[2,32,256]{2,1,0:T(8,128)S(1)}, f32[2,32,256]{2,1,0:T(8,128)S(1)}, u32[]{:S(2)}, u32[]{:S(2)}) collective-permute-start(f32[2,32,256]{2,1,0:T(8,128)S(1)} %step_kernel.5.refs_2_), channel_id=1, source_target_pairs={{0,1},{1,2},{2,3},{3,7},{7,6},{6,5},{5,4},{8,9},{9,10},{10,11},{11... | collective-permute-start | bytes 196616 | tf_op jit(solution)/shard_map/ppermute | solution.py:406
  258.4 1.3 collective-permute-done.14.refs_2_.refs_1_
  260.4 11.5 %all-to-all-start.12 = ((f32[16,1,2176]{2,1,0:T(1,128)}), f32[16,1,2176]{2,1,0:T(1,128)S(1)}, u32[]{:S(2)}, u32[]{:S(2)}) async-start(f32[16,1,2176]{2,1,0:T(1,128)} %bitcast.16), calls=%async_computation.12 | async-start | bytes 278528 | tf_op jit(solution)/shard_map/all_to_all | solution.py:412
  271.9 0.9 place_kernel.5
  272.8 4.4 %collective-permute-start.17 = (f32[2,64,256]{2,1,0:T(8,128)S(1)}, f32[2,64,256]{2,1,0:T(8,128)S(1)}, u32[]{:S(2)}, u32[]{:S(2)}) collective-permute-start(f32[2,64,256]{2,1,0:T(8,128)S(1)} %get-tuple-element.103), channel_id=1, source_target_pairs={{0,8},{8,16},{16,24},{24,32},{32,40},{40,48},{48,56},{56,64},{64,7... | collective-permute-start | bytes 393224 | tf_op jit(solution)/shard_map/ppermute | solution.py:396
  277.2 2.7 collective-permute-done.17.refs_2_
  280.1 1.2 spread_kernel.1.refs_2_
  281.3 6.3 %all-to-all-start.11 = ((f32[8,320,128]{2,1,0:T(8,128)}), f32[8,320,128]{2,1,0:T(8,128)S(1)}, u32[]{:S(2)}, u32[]{:S(2)}) async-start(f32[8,320,128]{2,1,0:T(8,128)} %spread_kernel.1.refs_2_), calls=%async_computation.11 | async-start | bytes 2621440 | tf_op jit(solution)/shard_map/all_to_all | solution.py:417
  288.3 24.9 %all-gather.refs_0_ = f32[256,128]{1,0:T(8,128)S(1)} all-gather(f32[16,128]{1,0:T(8,128)S(1)} %get-tuple-element.105), channel_id=2, replica_groups=mesh['xlo'=2,'z'=16,'core'=2,'xhi'=2,'y'=4] {'z'}, dimensions={0}, use_global_device_ids=true | all-gather | bytes 139264 | tf_op jit(solution)/shard_map/all_gather | solution.py:548
  313.9 6.0 %all-to-all-start.13 = ((f32[8,32,128]{2,1,0:T(8,128)}), f32[8,32,128]{2,1,0:T(8,128)S(1)}, u32[]{:S(2)}, u32[]{:S(2)}) async-start(f32[8,32,128]{2,1,0:T(8,128)} %tail_kernel.1), calls=%async_computation.13 | async-start | bytes 262144 | tf_op jit(solution)/shard_map/all_to_all | solution.py:417
  319.9 1.1 object_kernel.1
  321.0 5.8 %all-to-all-done.13 = f32[8,32,128]{2,1,0:T(8,128)S(1)} async-done(((f32[8,32,128]{2,1,0:T(8,128)}), f32[8,32,128]{2,1,0:T(8,128)S(1)}, u32[]{:S(2)}, u32[]{:S(2)}) %all-to-all-start.13) | async-done | bytes 131104 | tf_op jit(solution)/shard_map/all_to_all | solution.py:417
  326.8 15.2 %all-gather.1 = f32[32,32,128]{2,1,0:T(8,128)S(1)} all-gather(f32[8,32,128]{2,1,0:T(8,128)S(1)} %all-to-all-done.13), channel_id=3, replica_groups=mesh['xlo'=2,'z'=16,'core'=2,'xhi'=2,'y'=4] {'xlo','core'}, dimensions={0}, use_global_device_ids=true | all-gather | bytes 655360 | tf_op jit(solution)/shard_map/all_gather | solution.py:421
  342.0 0.8 probe_out_kernel.1
  (61 shorter events, 10.6 us)
Async XLA Ops:
  0.6 9.6 %copy-start.2 = (f32[2,288,512]{2,1,0:T(8,128)S(1)}, f32[2,288,512]{2,1,0:T(8,128)}, u32[]{:S(2)}) copy-start(f32[2,288,512]{2,1,0:T(8,128)} %whole.1) | copy-start | bytes 3538948
  0.6 1.1 copy-start.3
  2.6 12.7 %copy-start.4 = (s32[1,3]{1,0:T(1,128)S(1)}, s32[1,3]{1,0:T(1,128)}, u32[]{:S(2)}) copy-start(s32[1,3]{1,0:T(1,128)} %param.14) | copy-start | bytes 40
  2.6 12.7 %copy-start.5 = (s32[1,3]{1,0:T(1,128)S(1)}, s32[1,3]{1,0:T(1,128)}, u32[]{:S(2)}) copy-start(s32[1,3]{1,0:T(1,128)} %param.12) | copy-start | bytes 40
  2.6 12.7 %copy-start.6 = (s32[1,3]{1,0:T(1,128)S(1)}, s32[1,3]{1,0:T(1,128)}, u32[]{:S(2)}) copy-start(s32[1,3]{1,0:T(1,128)} %param.11) | copy-start | bytes 40
  2.6 14.0 %copy-start.1 = (bf16[1,3,256,256]{3,2,1,0:T(8,128)(2,1)S(1)}, bf16[1,3,256,256]{3,2,1,0:T(8,128)(2,1)}, u32[]{:S(2)}) copy-start(bf16[1,3,256,256]{3,2,1,0:T(8,128)(2,1)} %refs_1_.5) | copy-start | bytes 1179652
  2.6 16.5 %all-to-all-start = ((f32[8,2,32,256]{3,2,1,0:T(8,128)}), f32[8,2,32,256]{3,2,1,0:T(8,128)S(1)}, u32[]{:S(2)}, u32[]{:S(2)}) async-start(f32[8,2,32,256]{3,2,1,0:T(8,128)} %split_kernel.1._), calls=%async_computation | async-start | bytes 1048576 | tf_op jit(solution)/shard_map/all_to_all | solution.py:417
  10.2 8.8 %copy-start = (bf16[3,2,256,256]{3,2,1,0:T(8,128)(2,1)S(1)}, bf16[3,2,256,256]{3,2,1,0:T(8,128)(2,1)}, u32[]{:S(2)}) copy-start(bf16[3,2,256,256]{3,2,1,0:T(8,128)(2,1)} %constant.35.clone.refs_4_.refs_3_.refs_2_) | copy-start | bytes 2359300
  10.3 7.5 %collective-permute-start = (f32[2,64,256]{2,1,0:T(8,128)S(1)}, f32[2,64,256]{2,1,0:T(8,128)S(1)}, u32[]{:S(2)}, u32[]{:S(2)}) collective-permute-start(f32[2,64,256]{2,1,0:T(8,128)S(1)} %get-tuple-element.55), channel_id=1, source_target_pairs={{8,0},{16,8},{24,16},{32,24},{40,32},{48,40},{56,48},{64,56},{72,6... | collective-permute-start | bytes 393224 | tf_op jit(solution)/shard_map/ppermute | solution.py:396
  49.6 6.5 %collective-permute-start.1 = (f32[17,16,256]{2,1,0:T(8,128)S(1)}, f32[17,16,256]{2,1,0:T(8,128)S(1)}, u32[]{:S(2)}, u32[]{:S(2)}) collective-permute-start(f32[17,16,256]{2,1,0:T(8,128)S(1)} %get-tuple-element.61), channel_id=1, source_target_pairs={{0,8},{8,0},{1,9},{9,1},{2,10},{10,2},{3,11},{11,3},{4,12},{12,4},... | collective-permute-start | bytes 835592 | tf_op jit(solution)/shard_map/ppermute | solution.py:400
  56.1 10.5 %collective-permute-start.2 = (f32[17,8,256]{2,1,0:T(8,128)S(1)}, f32[17,8,256]{2,1,0:T(8,128)S(1)}, u32[]{:S(2)}, u32[]{:S(2)}) collective-permute-start(f32[17,8,256]{2,1,0:T(8,128)S(1)} %get-tuple-element.63), channel_id=1, source_target_pairs={{0,256},{256,0},{1,257},{257,1},{2,258},{258,2},{3,259},{259,3},{4... | collective-permute-start | bytes 417800 | tf_op jit(solution)/shard_map/ppermute | solution.py:400
  67.2 23.6 %all-to-all-start.3 = ((f32[16,1,2176]{2,1,0:T(1,128)}), f32[16,1,2176]{2,1,0:T(1,128)S(1)}, u32[]{:S(2)}, u32[]{:S(2)}) async-start(f32[16,1,2176]{2,1,0:T(1,128)} %bitcast.8), calls=%async_computation.3 | async-start | bytes 278528 | tf_op jit(solution)/shard_map/all_to_all | solution.py:412
  84.3 5.3 %collective-permute-start.4 = (f32[2,32,256]{2,1,0:T(8,128)S(1)}, f32[2,32,256]{2,1,0:T(8,128)S(1)}, u32[]{:S(2)}, u32[]{:S(2)}) collective-permute-start(f32[2,32,256]{2,1,0:T(8,128)S(1)} %step_kernel.3.refs_2_), channel_id=1, source_target_pairs={{1,0},{2,1},{3,2},{7,3},{6,7},{5,6},{4,5},{9,8},{10,9},{11,10},{15... | collective-permute-start | bytes 196616 | tf_op jit(solution)/shard_map/ppermute | solution.py:406
  85.5 5.3 %collective-permute-start.3 = (f32[2,32,256]{2,1,0:T(8,128)S(1)}, f32[2,32,256]{2,1,0:T(8,128)S(1)}, u32[]{:S(2)}, u32[]{:S(2)}) collective-permute-start(f32[2,32,256]{2,1,0:T(8,128)S(1)} %step_kernel.3.refs_2_), channel_id=1, source_target_pairs={{0,1},{1,2},{2,3},{3,7},{7,6},{6,5},{5,4},{8,9},{9,10},{10,11},{11... | collective-permute-start | bytes 196616 | tf_op jit(solution)/shard_map/ppermute | solution.py:406
  91.5 21.8 %all-to-all-start.4 = ((f32[16,16,128]{2,1,0:T(8,128)}), f32[16,16,128]{2,1,0:T(8,128)S(1)}, u32[]{:S(2)}, u32[]{:S(2)}) async-start(f32[16,16,128]{2,1,0:T(8,128)} %get-tuple-element.67.refs_5_), calls=%async_computation.4 | async-start | bytes 262144 | tf_op jit(solution)/shard_map/all_to_all | solution.py:417
  99.0 10.5 %collective-permute-start.5 = (f32[2,64,256]{2,1,0:T(8,128)S(1)}, f32[2,64,256]{2,1,0:T(8,128)S(1)}, u32[]{:S(2)}, u32[]{:S(2)}) collective-permute-start(f32[2,64,256]{2,1,0:T(8,128)S(1)} %get-tuple-element.70), channel_id=1, source_target_pairs={{0,8},{8,16},{16,24},{24,32},{32,40},{40,48},{48,56},{56,64},{64,7... | collective-permute-start | bytes 393224 | tf_op jit(solution)/shard_map/ppermute | solution.py:396
  106.3 6.8 %collective-permute-start.6 = (f32[2,64,256]{2,1,0:T(8,128)S(1)}, f32[2,64,256]{2,1,0:T(8,128)S(1)}, u32[]{:S(2)}, u32[]{:S(2)}) collective-permute-start(f32[2,64,256]{2,1,0:T(8,128)S(1)} %get-tuple-element.71), channel_id=1, source_target_pairs={{8,0},{16,8},{24,16},{32,24},{40,32},{48,40},{56,48},{64,56},{72,6... | collective-permute-start | bytes 393224 | tf_op jit(solution)/shard_map/ppermute | solution.py:396
  152.1 5.5 %collective-permute-start.7 = (f32[17,16,256]{2,1,0:T(8,128)S(1)}, f32[17,16,256]{2,1,0:T(8,128)S(1)}, u32[]{:S(2)}, u32[]{:S(2)}) collective-permute-start(f32[17,16,256]{2,1,0:T(8,128)S(1)} %get-tuple-element.78), channel_id=1, source_target_pairs={{0,8},{8,0},{1,9},{9,1},{2,10},{10,2},{3,11},{11,3},{4,12},{12,4},... | collective-permute-start | bytes 835592 | tf_op jit(solution)/shard_map/ppermute | solution.py:400
  157.7 6.8 %collective-permute-start.8 = (f32[17,8,256]{2,1,0:T(8,128)S(1)}, f32[17,8,256]{2,1,0:T(8,128)S(1)}, u32[]{:S(2)}, u32[]{:S(2)}) collective-permute-start(f32[17,8,256]{2,1,0:T(8,128)S(1)} %get-tuple-element.80), channel_id=1, source_target_pairs={{0,256},{256,0},{1,257},{257,1},{2,258},{258,2},{3,259},{259,3},{4... | collective-permute-start | bytes 417800 | tf_op jit(solution)/shard_map/ppermute | solution.py:400
  165.2 18.1 %all-to-all-start.7 = ((f32[16,1,2176]{2,1,0:T(1,128)}), f32[16,1,2176]{2,1,0:T(1,128)S(1)}, u32[]{:S(2)}, u32[]{:S(2)}) async-start(f32[16,1,2176]{2,1,0:T(1,128)} %bitcast.12), calls=%async_computation.7 | async-start | bytes 278528 | tf_op jit(solution)/shard_map/all_to_all | solution.py:412
  176.6 5.3 %collective-permute-start.10 = (f32[2,32,256]{2,1,0:T(8,128)S(1)}, f32[2,32,256]{2,1,0:T(8,128)S(1)}, u32[]{:S(2)}, u32[]{:S(2)}) collective-permute-start(f32[2,32,256]{2,1,0:T(8,128)S(1)} %step_kernel.4.refs_2_), channel_id=1, source_target_pairs={{1,0},{2,1},{3,2},{7,3},{6,7},{5,6},{4,5},{9,8},{10,9},{11,10},{15... | collective-permute-start | bytes 196616 | tf_op jit(solution)/shard_map/ppermute | solution.py:406
  177.9 5.3 %collective-permute-start.9 = (f32[2,32,256]{2,1,0:T(8,128)S(1)}, f32[2,32,256]{2,1,0:T(8,128)S(1)}, u32[]{:S(2)}, u32[]{:S(2)}) collective-permute-start(f32[2,32,256]{2,1,0:T(8,128)S(1)} %step_kernel.4.refs_2_), channel_id=1, source_target_pairs={{0,1},{1,2},{2,3},{3,7},{7,6},{6,5},{5,4},{8,9},{9,10},{10,11},{11... | collective-permute-start | bytes 196616 | tf_op jit(solution)/shard_map/ppermute | solution.py:406
  183.9 21.8 %all-to-all-start.8 = ((f32[16,16,128]{2,1,0:T(8,128)}), f32[16,16,128]{2,1,0:T(8,128)S(1)}, u32[]{:S(2)}, u32[]{:S(2)}) async-start(f32[16,16,128]{2,1,0:T(8,128)} %get-tuple-element.85.refs_5_), calls=%async_computation.8 | async-start | bytes 262144 | tf_op jit(solution)/shard_map/all_to_all | solution.py:417
  191.4 10.5 %collective-permute-start.11 = (f32[2,64,256]{2,1,0:T(8,128)S(1)}, f32[2,64,256]{2,1,0:T(8,128)S(1)}, u32[]{:S(2)}, u32[]{:S(2)}) collective-permute-start(f32[2,64,256]{2,1,0:T(8,128)S(1)} %get-tuple-element.88), channel_id=1, source_target_pairs={{0,8},{8,16},{16,24},{24,32},{32,40},{40,48},{48,56},{56,64},{64,7... | collective-permute-start | bytes 393224 | tf_op jit(solution)/shard_map/ppermute | solution.py:396
  198.7 6.8 %collective-permute-start.12 = (f32[2,64,256]{2,1,0:T(8,128)S(1)}, f32[2,64,256]{2,1,0:T(8,128)S(1)}, u32[]{:S(2)}, u32[]{:S(2)}) collective-permute-start(f32[2,64,256]{2,1,0:T(8,128)S(1)} %get-tuple-element.89), channel_id=1, source_target_pairs={{8,0},{16,8},{24,16},{32,24},{40,32},{48,40},{56,48},{64,56},{72,6... | collective-permute-start | bytes 393224 | tf_op jit(solution)/shard_map/ppermute | solution.py:396
  245.2 5.5 %collective-permute-start.13 = (f32[17,16,256]{2,1,0:T(8,128)S(1)}, f32[17,16,256]{2,1,0:T(8,128)S(1)}, u32[]{:S(2)}, u32[]{:S(2)}) collective-permute-start(f32[17,16,256]{2,1,0:T(8,128)S(1)} %get-tuple-element.98), channel_id=1, source_target_pairs={{0,8},{8,0},{1,9},{9,1},{2,10},{10,2},{3,11},{11,3},{4,12},{12,4},... | collective-permute-start | bytes 835592 | tf_op jit(solution)/shard_map/ppermute | solution.py:400
  250.7 9.0 %collective-permute-start.16 = (f32[17,8,256]{2,1,0:T(8,128)S(1)}, f32[17,8,256]{2,1,0:T(8,128)S(1)}, u32[]{:S(2)}, u32[]{:S(2)}) collective-permute-start(f32[17,8,256]{2,1,0:T(8,128)S(1)} %get-tuple-element.101), channel_id=1, source_target_pairs={{0,256},{256,0},{1,257},{257,1},{2,258},{258,2},{3,259},{259,3},{4... | collective-permute-start | bytes 417800 | tf_op jit(solution)/shard_map/ppermute | solution.py:400
  253.1 5.3 %collective-permute-start.15 = (f32[2,32,256]{2,1,0:T(8,128)S(1)}, f32[2,32,256]{2,1,0:T(8,128)S(1)}, u32[]{:S(2)}, u32[]{:S(2)}) collective-permute-start(f32[2,32,256]{2,1,0:T(8,128)S(1)} %step_kernel.5.refs_2_), channel_id=1, source_target_pairs={{1,0},{2,1},{3,2},{7,3},{6,7},{5,6},{4,5},{9,8},{10,9},{11,10},{15... | collective-permute-start | bytes 196616 | tf_op jit(solution)/shard_map/ppermute | solution.py:406
  254.4 5.3 %collective-permute-start.14 = (f32[2,32,256]{2,1,0:T(8,128)S(1)}, f32[2,32,256]{2,1,0:T(8,128)S(1)}, u32[]{:S(2)}, u32[]{:S(2)}) collective-permute-start(f32[2,32,256]{2,1,0:T(8,128)S(1)} %step_kernel.5.refs_2_), channel_id=1, source_target_pairs={{0,1},{1,2},{2,3},{3,7},{7,6},{6,5},{5,4},{8,9},{9,10},{10,11},{11... | collective-permute-start | bytes 196616 | tf_op jit(solution)/shard_map/ppermute | solution.py:406
  260.4 20.9 %all-to-all-start.12 = ((f32[16,1,2176]{2,1,0:T(1,128)}), f32[16,1,2176]{2,1,0:T(1,128)S(1)}, u32[]{:S(2)}, u32[]{:S(2)}) async-start(f32[16,1,2176]{2,1,0:T(1,128)} %bitcast.16), calls=%async_computation.12 | async-start | bytes 278528 | tf_op jit(solution)/shard_map/all_to_all | solution.py:412
  272.8 7.2 %collective-permute-start.17 = (f32[2,64,256]{2,1,0:T(8,128)S(1)}, f32[2,64,256]{2,1,0:T(8,128)S(1)}, u32[]{:S(2)}, u32[]{:S(2)}) collective-permute-start(f32[2,64,256]{2,1,0:T(8,128)S(1)} %get-tuple-element.103), channel_id=1, source_target_pairs={{0,8},{8,16},{16,24},{24,32},{32,40},{40,48},{48,56},{56,64},{64,7... | collective-permute-start | bytes 393224 | tf_op jit(solution)/shard_map/ppermute | solution.py:396
  281.3 31.9 %all-to-all-start.11 = ((f32[8,320,128]{2,1,0:T(8,128)}), f32[8,320,128]{2,1,0:T(8,128)S(1)}, u32[]{:S(2)}, u32[]{:S(2)}) async-start(f32[8,320,128]{2,1,0:T(8,128)} %spread_kernel.1.refs_2_), calls=%async_computation.11 | async-start | bytes 2621440 | tf_op jit(solution)/shard_map/all_to_all | solution.py:417
  313.9 12.9 %all-to-all-start.13 = ((f32[8,32,128]{2,1,0:T(8,128)}), f32[8,32,128]{2,1,0:T(8,128)S(1)}, u32[]{:S(2)}, u32[]{:S(2)}) async-start(f32[8,32,128]{2,1,0:T(8,128)} %tail_kernel.1), calls=%async_computation.13 | async-start | bytes 262144 | tf_op jit(solution)/shard_map/all_to_all | solution.py:417

commit v12 on v10

--- a/solution.py
+++ b/solution.py
@@ -27,7 +27,7 @@
 RINGS = 16
 LANES = 128
 COL_SPAN = SIDE + LANES
-OUT_ROWS = 40
+OUT_ROWS = HEIGHT // MODES
 MESSAGE = 2 * MODES + 1
 VMEM_LIMIT = 16 * 1024 * 1024
 
@@ -291,9 +291,14 @@
 
 
 def out_rows_kernel(scal, part_band, from_left, rows_out):
-    rows = pl.ds(pl.multiple_of(scal[BAND_ID] // 2 * 8, 8), OUT_ROWS)
-    rows_out[:, :, :SIDE] = part_band[:, rows, :SIDE] + from_left[:, rows, :]
-    rows_out[:, :, SIDE:] = part_band[:, rows, SIDE:WIDTH]
+    slab = scal[BAND_ID]
+    odd = lax.rem(slab, 2) == 1
+    rows = pl.ds(pl.multiple_of(slab // 2 * 8, 8), OUT_ROWS + 4)
+    for part in range(2):
+        edge = part_band[part, rows, :SIDE] + from_left[part, rows, :]
+        block = jnp.concatenate([edge, part_band[part, rows, SIDE:WIDTH]], axis=1)
+        block = jnp.where(odd, pltpu.roll(block, OUT_ROWS, 0), block)
+        rows_out[part] = block[:OUT_ROWS]
 
 
 def tail_kernel(piece, rows_out, tail):
@@ -312,7 +317,7 @@
 
 def object_kernel(tail, object_out):
     for place in range(MODES):
-        first = slab_of(place) * 9 // 2 * 8
+        first = slab_of(place) * OUT_ROWS
         for part in range(2):
             for block in range(WIDTH // LANES):
                 row = 32 + (part * 4 + block) * OUT_ROWS
@@ -513,35 +518,35 @@
             keep,
             received,
             scalars=False,
-            after=(above, below) if final else (object_step, counts),
+            after=(object_step,) if final else (object_step, counts),
         )
         sums = exchange_rings(packed)
-        placing = [scal, above, object_step, below, band]
-        if final:
-            part_band, _, to_right = call(
-                place_kernel, [band_shape, edge, edge], *placing, after=(packed,)
-            )
-            from_left = shift(to_right, TILE_AXES, TILES, 1)
-            (rows_out,) = call(
-                out_rows_kernel, [(2, OUT_ROWS, WIDTH)], scal, part_band, from_left
-            )
-            before = (rows_out,)
-        else:
-            before = (above, below)
         shard, shards = call(
             probe_kernel,
             [(2 * MODES, LANES), (RINGS, 2 * MODES, LANES)],
             sums,
             shard,
             scalars=False,
-            after=before,
+            after=(above, below),
         )
         piece = exchange(shards, "z")
-        if not final:
-            part_band, to_left, to_right = call(
-                place_kernel, [band_shape, edge, edge], *placing, after=(shards,)
+        part_band, to_left, to_right = call(
+            place_kernel,
+            [band_shape, edge, edge],
+            scal,
+            above,
+            object_step,
+            below,
+            band,
+            after=(shards,),
+        )
+        from_left = shift(to_right, TILE_AXES, TILES, 1)
+        if final:
+            (rows_out,) = call(
+                out_rows_kernel, [(2, OUT_ROWS, WIDTH)], scal, part_band, from_left
             )
-            from_left = shift(to_right, TILE_AXES, TILES, 1)
+            piece, rows_out = lax.optimization_barrier((piece, rows_out))
+        else:
             from_right = shift(to_left, TILE_AXES, TILES, -1)
             band, view = call(
                 view_kernel,

time: 337 us -> 329 us (0.976)
  blocking collectives: 152 us -> 129 us
  starting transfers between devices: 131 us -> 141 us
  waiting for transfers between devices: 28.8 us -> 34 us
    all_to_all x8 -> x7, blocking collectives: 119 us -> 97.8 us  [exchange(): return lax.all_to_all(value, axes, 0, 0, tiled=True)]
    all_to_all x3 -> x4, starting transfers between devices: 22 us -> 29.2 us  [exchange(): return lax.all_to_all(value, axes, 0, 0, tiled=True)]
    ppermute x6, waiting for transfers between devices: 10.1 us -> 14.5 us  [other(): return lax.ppermute(value, axis, [(0, 1), (1, 0)])]
  transfers between devices with their start and end apart: 24 -> 25, of which waited for: 15 -> 17; matrix products, arithmetic and copies ran while one was open for 0% -> 0% of each run, Pallas kernels for 1% -> 1%
where the time goes in v12:
time: 329 us; the launch traced here: 328 us
  starting transfers between devices  141 us (43%)
  blocking collectives  129 us (39%)
  waiting for transfers between devices  34 us (10%)
  Pallas kernels  20.2 us (6%)
    all_to_all x7, blocking collectives, exchange(): return lax.all_to_all(value, axes, 0, 0, tiled=True)  97.8 us
    all_to_all x3, starting transfers between devices, exchange_rings(): lax.all_to_all(value, 'z', 0, 0, tiled=True, axis_index_groups=groups)  40 us
    all_gather x3, blocking collectives, gather_pieces(): gathered = lax.all_gather(piece, ('xlo', 'core'))  31 us
    ppermute x6, starting transfers between devices, shift(): lax.ppermute(value, axes, [(i, i + steps) for i in range(first, last)])  30.5 us
    all_to_all x4, starting transfers between devices, exchange(): return lax.all_to_all(value, axes, 0, 0, tiled=True)  29.2 us
    ppermute x6, starting transfers between devices, other(): return lax.ppermute(value, axis, [(0, 1), (1, 0)])  25.8 us
    pallas_call x34, Pallas kernels, call(): pl.pallas_call(body, out_shape=[jax.ShapeDtypeStruct(shape, F32) for shap...  20.2 us
    ppermute x6, starting transfers between devices, beside_slab(): return lax.ppermute(value, MODE_AXES, pairs)  15.8 us
  transfers between devices with their start and end apart: 25, of which 17 were waited for; matrix products, arithmetic and copies ran while one was open for 0% of the time, Pallas kernels for 1%

profile of v12, /device:TPU:1, one launch (start us, length us, event | category | flops | bytes accessed | tf_op | source)
XLA Modules:
  0.0 327.9 jit_solution(7923256282077749673)
XLA Ops:
  0.6 1.1 copy-done.3
  1.8 0.8 split_kernel.1._
  2.6 7.6 %all-to-all-start = ((f32[8,2,32,256]{3,2,1,0:T(8,128)}), f32[8,2,32,256]{3,2,1,0:T(8,128)S(1)}, u32[]{:S(2)}, u32[]{:S(2)}) async-start(f32[8,2,32,256]{3,2,1,0:T(8,128)} %split_kernel.1._), calls=%async_computation | async-start | bytes 1048576 | tf_op jit(solution)/shard_map/all_to_all | solution.py:418
  10.3 4.9 %collective-permute-start = (f32[2,64,256]{2,1,0:T(8,128)S(1)}, f32[2,64,256]{2,1,0:T(8,128)S(1)}, u32[]{:S(2)}, u32[]{:S(2)}) collective-permute-start(f32[2,64,256]{2,1,0:T(8,128)S(1)} %get-tuple-element.57), channel_id=1, source_target_pairs={{8,0},{16,8},{24,16},{32,24},{40,32},{48,40},{56,48},{64,56},{72,6... | collective-permute-start | bytes 393224 | tf_op jit(solution)/shard_map/ppermute | solution.py:397
  17.0 0.8 collective-permute-done.refs_2_
  17.8 1.3 all-to-all-done.refs_3_.refs_1_
  19.1 1.0 first_kernel.1
  20.1 15.1 %all_to_all.70.refs_0_ = f32[8,2,32,256]{3,2,1,0:T(8,128)S(1)} all-to-all(f32[8,2,32,256]{3,2,1,0:T(8,128)S(1)} %get-tuple-element.59), channel_id=1, replica_groups=mesh['xlo'=2,'z'=16,'core'=2,'xhi'=2,'y'=4] {'xhi','y'}, dimensions={0} | all-to-all | bytes 1048576 | tf_op jit(solution)/shard_map/all_to_all | solution.py:418
  35.2 1.4 ratio_kernel.3
  36.5 12.3 %all_to_all.71.refs_0_ = f32[8,2,32,256]{3,2,1,0:T(8,128)S(1)} all-to-all(f32[8,2,32,256]{3,2,1,0:T(8,128)S(1)} %ratio_kernel.3), channel_id=1, replica_groups=mesh['xlo'=2,'z'=16,'core'=2,'xhi'=2,'y'=4] {'xhi','y'}, dimensions={0} | all-to-all | bytes 1048576 | tf_op jit(solution)/shard_map/all_to_all | solution.py:418
  48.8 0.7 backward_kernel.3
  49.6 5.3 %collective-permute-start.1 = (f32[17,16,256]{2,1,0:T(8,128)S(1)}, f32[17,16,256]{2,1,0:T(8,128)S(1)}, u32[]{:S(2)}, u32[]{:S(2)}) collective-permute-start(f32[17,16,256]{2,1,0:T(8,128)S(1)} %get-tuple-element.63), channel_id=1, source_target_pairs={{0,8},{8,0},{1,9},{9,1},{2,10},{10,2},{3,11},{11,3},{4,12},{12,4},... | collective-permute-start | bytes 835592 | tf_op jit(solution)/shard_map/ppermute | solution.py:401
  54.9 1.2 collective-permute-done.1.refs_1_
  56.1 6.7 %collective-permute-start.2 = (f32[17,8,256]{2,1,0:T(8,128)S(1)}, f32[17,8,256]{2,1,0:T(8,128)S(1)}, u32[]{:S(2)}, u32[]{:S(2)}) collective-permute-start(f32[17,8,256]{2,1,0:T(8,128)S(1)} %get-tuple-element.65), channel_id=1, source_target_pairs={{0,256},{256,0},{1,257},{257,1},{2,258},{258,2},{3,259},{259,3},{4... | collective-permute-start | bytes 417800 | tf_op jit(solution)/shard_map/ppermute | solution.py:401
  63.4 3.2 collective-permute-done.2.refs_1_
  67.2 17.0 %all-to-all-start.3 = ((f32[16,1,2176]{2,1,0:T(1,128)}), f32[16,1,2176]{2,1,0:T(1,128)S(1)}, u32[]{:S(2)}, u32[]{:S(2)}) async-start(f32[16,1,2176]{2,1,0:T(1,128)} %bitcast.8), calls=%async_computation.3 | async-start | bytes 278528 | tf_op jit(solution)/shard_map/all_to_all | solution.py:413
  84.3 1.3 collective-permute-start.4
  85.5 4.0 %collective-permute-start.3 = (f32[2,32,256]{2,1,0:T(8,128)S(1)}, f32[2,32,256]{2,1,0:T(8,128)S(1)}, u32[]{:S(2)}, u32[]{:S(2)}) collective-permute-start(f32[2,32,256]{2,1,0:T(8,128)S(1)} %step_kernel.3.refs_2_), channel_id=1, source_target_pairs={{0,1},{1,2},{2,3},{3,7},{7,6},{6,5},{5,4},{8,9},{9,10},{10,11},{11... | collective-permute-start | bytes 196616 | tf_op jit(solution)/shard_map/ppermute | solution.py:407
  89.5 1.3 collective-permute-done.3.refs_2_.refs_1_
  91.5 7.2 %all-to-all-start.4 = ((f32[16,16,128]{2,1,0:T(8,128)}), f32[16,16,128]{2,1,0:T(8,128)S(1)}, u32[]{:S(2)}, u32[]{:S(2)}) async-start(f32[16,16,128]{2,1,0:T(8,128)} %get-tuple-element.69.refs_5_), calls=%async_computation.4 | async-start | bytes 262144 | tf_op jit(solution)/shard_map/all_to_all | solution.py:418
  99.0 7.3 %collective-permute-start.5 = (f32[2,64,256]{2,1,0:T(8,128)S(1)}, f32[2,64,256]{2,1,0:T(8,128)S(1)}, u32[]{:S(2)}, u32[]{:S(2)}) collective-permute-start(f32[2,64,256]{2,1,0:T(8,128)S(1)} %get-tuple-element.72), channel_id=1, source_target_pairs={{0,8},{8,16},{16,24},{24,32},{32,40},{40,48},{48,56},{56,64},{64,7... | collective-permute-start | bytes 393224 | tf_op jit(solution)/shard_map/ppermute | solution.py:397
  106.3 1.9 collective-permute-start.6
  108.2 1.3 collective-permute-done.5.refs_2_
  109.5 3.6 %collective-permute-done.6.refs_3_ = f32[2,64,256]{2,1,0:T(8,128)S(1)} collective-permute-done((f32[2,64,256]{2,1,0:T(8,128)S(1)}, f32[2,64,256]{2,1,0:T(8,128)S(1)}, u32[]{:S(2)}, u32[]{:S(2)}) %collective-permute-start.6) | collective-permute-done | bytes 131104 | tf_op jit(solution)/shard_map/ppermute | solution.py:397
  113.4 8.8 %all_gather.12 = f32[4,256,128]{2,1,0:T(8,128)S(1)} all-gather(f32[1,256,128]{2,1,0:T(8,128)S(1)} %bitcast.28), channel_id=1, replica_groups=mesh['xlo'=2,'z'=16,'core'=2,'xhi'=2,'y'=4] {'xlo','core'}, dimensions={0}, use_global_device_ids=true | all-gather | bytes 655360 | tf_op jit(solution)/shard_map/all_gather | solution.py:422
  122.2 1.0 next_kernel.2
  123.2 12.9 %all_to_all.72.refs_0_ = f32[8,2,32,256]{3,2,1,0:T(8,128)S(1)} all-to-all(f32[8,2,32,256]{3,2,1,0:T(8,128)S(1)} %get-tuple-element.77), channel_id=1, replica_groups=mesh['xlo'=2,'z'=16,'core'=2,'xhi'=2,'y'=4] {'xhi','y'}, dimensions={0} | all-to-all | bytes 1048576 | tf_op jit(solution)/shard_map/all_to_all | solution.py:418
  136.2 1.4 ratio_kernel.4
  137.6 13.8 %all_to_all.73.refs_0_ = f32[8,2,32,256]{3,2,1,0:T(8,128)S(1)} all-to-all(f32[8,2,32,256]{3,2,1,0:T(8,128)S(1)} %ratio_kernel.4), channel_id=1, replica_groups=mesh['xlo'=2,'z'=16,'core'=2,'xhi'=2,'y'=4] {'xhi','y'}, dimensions={0} | all-to-all | bytes 1048576 | tf_op jit(solution)/shard_map/all_to_all | solution.py:418
  151.4 0.7 backward_kernel.4
  152.1 4.4 %collective-permute-start.7 = (f32[17,16,256]{2,1,0:T(8,128)S(1)}, f32[17,16,256]{2,1,0:T(8,128)S(1)}, u32[]{:S(2)}, u32[]{:S(2)}) collective-permute-start(f32[17,16,256]{2,1,0:T(8,128)S(1)} %get-tuple-element.80), channel_id=1, source_target_pairs={{0,8},{8,0},{1,9},{9,1},{2,10},{10,2},{3,11},{11,3},{4,12},{12,4},... | collective-permute-start | bytes 835592 | tf_op jit(solution)/shard_map/ppermute | solution.py:401
  156.5 1.2 collective-permute-done.7.refs_1_
  157.7 2.8 collective-permute-start.8
  161.1 3.4 %collective-permute-done.8.refs_1_ = f32[17,8,256]{2,1,0:T(8,128)S(1)} collective-permute-done((f32[17,8,256]{2,1,0:T(8,128)S(1)}, f32[17,8,256]{2,1,0:T(8,128)S(1)}, u32[]{:S(2)}, u32[]{:S(2)}) %collective-permute-start.8) | collective-permute-done | bytes 139296 | tf_op jit(solution)/shard_map/ppermute | solution.py:401
  165.2 11.5 %all-to-all-start.7 = ((f32[16,1,2176]{2,1,0:T(1,128)}), f32[16,1,2176]{2,1,0:T(1,128)S(1)}, u32[]{:S(2)}, u32[]{:S(2)}) async-start(f32[16,1,2176]{2,1,0:T(1,128)} %bitcast.12), calls=%async_computation.7 | async-start | bytes 278528 | tf_op jit(solution)/shard_map/all_to_all | solution.py:413
  176.6 1.3 collective-permute-start.10
  177.9 4.0 %collective-permute-start.9 = (f32[2,32,256]{2,1,0:T(8,128)S(1)}, f32[2,32,256]{2,1,0:T(8,128)S(1)}, u32[]{:S(2)}, u32[]{:S(2)}) collective-permute-start(f32[2,32,256]{2,1,0:T(8,128)S(1)} %step_kernel.4.refs_2_), channel_id=1, source_target_pairs={{0,1},{1,2},{2,3},{3,7},{7,6},{6,5},{5,4},{8,9},{9,10},{10,11},{11... | collective-permute-start | bytes 196616 | tf_op jit(solution)/shard_map/ppermute | solution.py:407
  181.9 1.3 collective-permute-done.9.refs_2_.refs_1_
  183.9 7.2 %all-to-all-start.8 = ((f32[16,16,128]{2,1,0:T(8,128)}), f32[16,16,128]{2,1,0:T(8,128)S(1)}, u32[]{:S(2)}, u32[]{:S(2)}) async-start(f32[16,16,128]{2,1,0:T(8,128)} %get-tuple-element.87.refs_5_), calls=%async_computation.8 | async-start | bytes 262144 | tf_op jit(solution)/shard_map/all_to_all | solution.py:418
  191.4 7.3 %collective-permute-start.11 = (f32[2,64,256]{2,1,0:T(8,128)S(1)}, f32[2,64,256]{2,1,0:T(8,128)S(1)}, u32[]{:S(2)}, u32[]{:S(2)}) collective-permute-start(f32[2,64,256]{2,1,0:T(8,128)S(1)} %get-tuple-element.90), channel_id=1, source_target_pairs={{0,8},{8,16},{16,24},{24,32},{32,40},{40,48},{48,56},{56,64},{64,7... | collective-permute-start | bytes 393224 | tf_op jit(solution)/shard_map/ppermute | solution.py:397
  198.7 1.9 collective-permute-start.12
  200.6 1.3 collective-permute-done.11.refs_2_
  201.9 3.6 %collective-permute-done.12.refs_3_ = f32[2,64,256]{2,1,0:T(8,128)S(1)} collective-permute-done((f32[2,64,256]{2,1,0:T(8,128)S(1)}, f32[2,64,256]{2,1,0:T(8,128)S(1)}, u32[]{:S(2)}, u32[]{:S(2)}) %collective-permute-start.12) | collective-permute-done | bytes 131104 | tf_op jit(solution)/shard_map/ppermute | solution.py:397
  205.8 9.2 %all_gather.13 = f32[4,256,128]{2,1,0:T(8,128)S(1)} all-gather(f32[1,256,128]{2,1,0:T(8,128)S(1)} %bitcast.29), channel_id=1, replica_groups=mesh['xlo'=2,'z'=16,'core'=2,'xhi'=2,'y'=4] {'xlo','core'}, dimensions={0}, use_global_device_ids=true | all-gather | bytes 655360 | tf_op jit(solution)/shard_map/all_gather | solution.py:422
  215.0 1.0 next_kernel.3
  216.0 13.0 %all_to_all.74.refs_0_ = f32[8,2,32,256]{3,2,1,0:T(8,128)S(1)} all-to-all(f32[8,2,32,256]{3,2,1,0:T(8,128)S(1)} %get-tuple-element.95), channel_id=1, replica_groups=mesh['xlo'=2,'z'=16,'core'=2,'xhi'=2,'y'=4] {'xhi','y'}, dimensions={0} | all-to-all | bytes 1048576 | tf_op jit(solution)/shard_map/all_to_all | solution.py:418
  229.0 1.4 ratio_kernel.5
  230.4 14.0 %all_to_all.75.refs_0_ = f32[8,2,32,256]{3,2,1,0:T(8,128)S(1)} all-to-all(f32[8,2,32,256]{3,2,1,0:T(8,128)S(1)} %ratio_kernel.5), channel_id=1, replica_groups=mesh['xlo'=2,'z'=16,'core'=2,'xhi'=2,'y'=4] {'xhi','y'}, dimensions={0} | all-to-all | bytes 1048576 | tf_op jit(solution)/shard_map/all_to_all | solution.py:418
  245.1 4.4 %collective-permute-start.13 = (f32[17,16,256]{2,1,0:T(8,128)S(1)}, f32[17,16,256]{2,1,0:T(8,128)S(1)}, u32[]{:S(2)}, u32[]{:S(2)}) collective-permute-start(f32[17,16,256]{2,1,0:T(8,128)S(1)} %get-tuple-element.98), channel_id=1, source_target_pairs={{0,8},{8,0},{1,9},{9,1},{2,10},{10,2},{3,11},{11,3},{4,12},{12,4},... | collective-permute-start | bytes 835592 | tf_op jit(solution)/shard_map/ppermute | solution.py:401
  249.5 1.2 collective-permute-done.13.refs_1_
  250.7 2.2 collective-permute-start.14
  253.1 4.4 %collective-permute-done.14.refs_1_ = f32[17,8,256]{2,1,0:T(8,128)S(1)} collective-permute-done((f32[17,8,256]{2,1,0:T(8,128)S(1)}, f32[17,8,256]{2,1,0:T(8,128)S(1)}, u32[]{:S(2)}, u32[]{:S(2)}) %collective-permute-start.14) | collective-permute-done | bytes 139296 | tf_op jit(solution)/shard_map/ppermute | solution.py:401
  258.2 11.5 %all-to-all-start.11 = ((f32[16,1,2176]{2,1,0:T(1,128)}), f32[16,1,2176]{2,1,0:T(1,128)S(1)}, u32[]{:S(2)}, u32[]{:S(2)}) async-start(f32[16,1,2176]{2,1,0:T(1,128)} %bitcast.16), calls=%async_computation.11 | async-start | bytes 278528 | tf_op jit(solution)/shard_map/all_to_all | solution.py:413
  269.6 1.3 collective-permute-start.16
  270.9 4.0 %collective-permute-start.15 = (f32[2,32,256]{2,1,0:T(8,128)S(1)}, f32[2,32,256]{2,1,0:T(8,128)S(1)}, u32[]{:S(2)}, u32[]{:S(2)}) collective-permute-start(f32[2,32,256]{2,1,0:T(8,128)S(1)} %step_kernel.5.refs_2_), channel_id=1, source_target_pairs={{0,1},{1,2},{2,3},{3,7},{7,6},{6,5},{5,4},{8,9},{9,10},{10,11},{11... | collective-permute-start | bytes 196616 | tf_op jit(solution)/shard_map/ppermute | solution.py:407
  274.9 1.3 collective-permute-done.15.refs_2_.refs_1_
  276.9 7.2 %all-to-all-start.12 = ((f32[16,16,128]{2,1,0:T(8,128)}), f32[16,16,128]{2,1,0:T(8,128)S(1)}, u32[]{:S(2)}, u32[]{:S(2)}) async-start(f32[16,16,128]{2,1,0:T(8,128)} %get-tuple-element.104.refs_5_), calls=%async_computation.12 | async-start | bytes 262144 | tf_op jit(solution)/shard_map/all_to_all | solution.py:418
  284.1 0.9 place_kernel.5
  285.0 7.2 %collective-permute-start.17 = (f32[2,64,256]{2,1,0:T(8,128)S(1)}, f32[2,64,256]{2,1,0:T(8,128)S(1)}, u32[]{:S(2)}, u32[]{:S(2)}) collective-permute-start(f32[2,64,256]{2,1,0:T(8,128)S(1)} %get-tuple-element.107), channel_id=1, source_target_pairs={{0,8},{8,16},{16,24},{24,32},{32,40},{40,48},{48,56},{56,64},{64,7... | collective-permute-start | bytes 393224 | tf_op jit(solution)/shard_map/ppermute | solution.py:397
  292.3 3.0 collective-permute-done.17.refs_2_
  296.2 16.7 %all_to_all.76.refs_0_ = f32[8,320,128]{2,1,0:T(8,128)S(1)} all-to-all(f32[8,320,128]{2,1,0:T(8,128)S(1)} %tail_kernel.1), channel_id=1, replica_groups=mesh['xlo'=2,'z'=16,'core'=2,'xhi'=2,'y'=4] {'xhi','y'}, dimensions={0} | all-to-all | bytes 2621440 | tf_op jit(solution)/shard_map/all_to_all | solution.py:418
  312.9 13.0 %all-gather = f32[32,32,128]{2,1,0:T(8,128)S(1)} all-gather(f32[8,32,128]{2,1,0:T(8,128)S(1)} %slice.19), channel_id=2, replica_groups=mesh['xlo'=2,'z'=16,'core'=2,'xhi'=2,'y'=4] {'xlo','core'}, dimensions={0}, use_global_device_ids=true | all-gather | bytes 655360 | tf_op jit(solution)/shard_map/all_gather | solution.py:422
  325.9 0.8 probe_out_kernel.1
  326.8 1.1 object_kernel.1
  (59 shorter events, 9.2 us)
Async XLA Ops:
  0.6 9.6 %copy-start.2 = (f32[2,288,512]{2,1,0:T(8,128)S(1)}, f32[2,288,512]{2,1,0:T(8,128)}, u32[]{:S(2)}) copy-start(f32[2,288,512]{2,1,0:T(8,128)} %whole.1) | copy-start | bytes 3538948
  0.6 1.1 copy-start.3
  2.6 12.7 %copy-start.4 = (s32[1,3]{1,0:T(1,128)S(1)}, s32[1,3]{1,0:T(1,128)}, u32[]{:S(2)}) copy-start(s32[1,3]{1,0:T(1,128)} %param.14) | copy-start | bytes 40
  2.6 12.7 %copy-start.5 = (s32[1,3]{1,0:T(1,128)S(1)}, s32[1,3]{1,0:T(1,128)}, u32[]{:S(2)}) copy-start(s32[1,3]{1,0:T(1,128)} %param.12) | copy-start | bytes 40
  2.6 12.7 %copy-start.6 = (s32[1,3]{1,0:T(1,128)S(1)}, s32[1,3]{1,0:T(1,128)}, u32[]{:S(2)}) copy-start(s32[1,3]{1,0:T(1,128)} %param.11) | copy-start | bytes 40
  2.6 14.0 %copy-start.1 = (bf16[1,3,256,256]{3,2,1,0:T(8,128)(2,1)S(1)}, bf16[1,3,256,256]{3,2,1,0:T(8,128)(2,1)}, u32[]{:S(2)}) copy-start(bf16[1,3,256,256]{3,2,1,0:T(8,128)(2,1)} %refs_1_.5) | copy-start | bytes 1179652
  2.6 16.5 %all-to-all-start = ((f32[8,2,32,256]{3,2,1,0:T(8,128)}), f32[8,2,32,256]{3,2,1,0:T(8,128)S(1)}, u32[]{:S(2)}, u32[]{:S(2)}) async-start(f32[8,2,32,256]{3,2,1,0:T(8,128)} %split_kernel.1._), calls=%async_computation | async-start | bytes 1048576 | tf_op jit(solution)/shard_map/all_to_all | solution.py:418
  10.2 8.8 %copy-start = (bf16[3,2,256,256]{3,2,1,0:T(8,128)(2,1)S(1)}, bf16[3,2,256,256]{3,2,1,0:T(8,128)(2,1)}, u32[]{:S(2)}) copy-start(bf16[3,2,256,256]{3,2,1,0:T(8,128)(2,1)} %constant.35.clone.refs_4_.refs_3_.refs_2_) | copy-start | bytes 2359300
  10.3 7.5 %collective-permute-start = (f32[2,64,256]{2,1,0:T(8,128)S(1)}, f32[2,64,256]{2,1,0:T(8,128)S(1)}, u32[]{:S(2)}, u32[]{:S(2)}) collective-permute-start(f32[2,64,256]{2,1,0:T(8,128)S(1)} %get-tuple-element.57), channel_id=1, source_target_pairs={{8,0},{16,8},{24,16},{32,24},{40,32},{48,40},{56,48},{64,56},{72,6... | collective-permute-start | bytes 393224 | tf_op jit(solution)/shard_map/ppermute | solution.py:397
  49.6 6.5 %collective-permute-start.1 = (f32[17,16,256]{2,1,0:T(8,128)S(1)}, f32[17,16,256]{2,1,0:T(8,128)S(1)}, u32[]{:S(2)}, u32[]{:S(2)}) collective-permute-start(f32[17,16,256]{2,1,0:T(8,128)S(1)} %get-tuple-element.63), channel_id=1, source_target_pairs={{0,8},{8,0},{1,9},{9,1},{2,10},{10,2},{3,11},{11,3},{4,12},{12,4},... | collective-permute-start | bytes 835592 | tf_op jit(solution)/shard_map/ppermute | solution.py:401
  56.1 10.5 %collective-permute-start.2 = (f32[17,8,256]{2,1,0:T(8,128)S(1)}, f32[17,8,256]{2,1,0:T(8,128)S(1)}, u32[]{:S(2)}, u32[]{:S(2)}) collective-permute-start(f32[17,8,256]{2,1,0:T(8,128)S(1)} %get-tuple-element.65), channel_id=1, source_target_pairs={{0,256},{256,0},{1,257},{257,1},{2,258},{258,2},{3,259},{259,3},{4... | collective-permute-start | bytes 417800 | tf_op jit(solution)/shard_map/ppermute | solution.py:401
  67.2 23.6 %all-to-all-start.3 = ((f32[16,1,2176]{2,1,0:T(1,128)}), f32[16,1,2176]{2,1,0:T(1,128)S(1)}, u32[]{:S(2)}, u32[]{:S(2)}) async-start(f32[16,1,2176]{2,1,0:T(1,128)} %bitcast.8), calls=%async_computation.3 | async-start | bytes 278528 | tf_op jit(solution)/shard_map/all_to_all | solution.py:413
  84.3 5.3 %collective-permute-start.4 = (f32[2,32,256]{2,1,0:T(8,128)S(1)}, f32[2,32,256]{2,1,0:T(8,128)S(1)}, u32[]{:S(2)}, u32[]{:S(2)}) collective-permute-start(f32[2,32,256]{2,1,0:T(8,128)S(1)} %step_kernel.3.refs_2_), channel_id=1, source_target_pairs={{1,0},{2,1},{3,2},{7,3},{6,7},{5,6},{4,5},{9,8},{10,9},{11,10},{15... | collective-permute-start | bytes 196616 | tf_op jit(solution)/shard_map/ppermute | solution.py:407
  85.5 5.3 %collective-permute-start.3 = (f32[2,32,256]{2,1,0:T(8,128)S(1)}, f32[2,32,256]{2,1,0:T(8,128)S(1)}, u32[]{:S(2)}, u32[]{:S(2)}) collective-permute-start(f32[2,32,256]{2,1,0:T(8,128)S(1)} %step_kernel.3.refs_2_), channel_id=1, source_target_pairs={{0,1},{1,2},{2,3},{3,7},{7,6},{6,5},{5,4},{8,9},{9,10},{10,11},{11... | collective-permute-start | bytes 196616 | tf_op jit(solution)/shard_map/ppermute | solution.py:407
  91.5 21.8 %all-to-all-start.4 = ((f32[16,16,128]{2,1,0:T(8,128)}), f32[16,16,128]{2,1,0:T(8,128)S(1)}, u32[]{:S(2)}, u32[]{:S(2)}) async-start(f32[16,16,128]{2,1,0:T(8,128)} %get-tuple-element.69.refs_5_), calls=%async_computation.4 | async-start | bytes 262144 | tf_op jit(solution)/shard_map/all_to_all | solution.py:418
  99.0 10.5 %collective-permute-start.5 = (f32[2,64,256]{2,1,0:T(8,128)S(1)}, f32[2,64,256]{2,1,0:T(8,128)S(1)}, u32[]{:S(2)}, u32[]{:S(2)}) collective-permute-start(f32[2,64,256]{2,1,0:T(8,128)S(1)} %get-tuple-element.72), channel_id=1, source_target_pairs={{0,8},{8,16},{16,24},{24,32},{32,40},{40,48},{48,56},{56,64},{64,7... | collective-permute-start | bytes 393224 | tf_op jit(solution)/shard_map/ppermute | solution.py:397
  106.3 6.8 %collective-permute-start.6 = (f32[2,64,256]{2,1,0:T(8,128)S(1)}, f32[2,64,256]{2,1,0:T(8,128)S(1)}, u32[]{:S(2)}, u32[]{:S(2)}) collective-permute-start(f32[2,64,256]{2,1,0:T(8,128)S(1)} %get-tuple-element.73), channel_id=1, source_target_pairs={{8,0},{16,8},{24,16},{32,24},{40,32},{48,40},{56,48},{64,56},{72,6... | collective-permute-start | bytes 393224 | tf_op jit(solution)/shard_map/ppermute | solution.py:397
  152.1 5.5 %collective-permute-start.7 = (f32[17,16,256]{2,1,0:T(8,128)S(1)}, f32[17,16,256]{2,1,0:T(8,128)S(1)}, u32[]{:S(2)}, u32[]{:S(2)}) collective-permute-start(f32[17,16,256]{2,1,0:T(8,128)S(1)} %get-tuple-element.80), channel_id=1, source_target_pairs={{0,8},{8,0},{1,9},{9,1},{2,10},{10,2},{3,11},{11,3},{4,12},{12,4},... | collective-permute-start | bytes 835592 | tf_op jit(solution)/shard_map/ppermute | solution.py:401
  157.7 6.8 %collective-permute-start.8 = (f32[17,8,256]{2,1,0:T(8,128)S(1)}, f32[17,8,256]{2,1,0:T(8,128)S(1)}, u32[]{:S(2)}, u32[]{:S(2)}) collective-permute-start(f32[17,8,256]{2,1,0:T(8,128)S(1)} %get-tuple-element.82), channel_id=1, source_target_pairs={{0,256},{256,0},{1,257},{257,1},{2,258},{258,2},{3,259},{259,3},{4... | collective-permute-start | bytes 417800 | tf_op jit(solution)/shard_map/ppermute | solution.py:401
  165.2 18.1 %all-to-all-start.7 = ((f32[16,1,2176]{2,1,0:T(1,128)}), f32[16,1,2176]{2,1,0:T(1,128)S(1)}, u32[]{:S(2)}, u32[]{:S(2)}) async-start(f32[16,1,2176]{2,1,0:T(1,128)} %bitcast.12), calls=%async_computation.7 | async-start | bytes 278528 | tf_op jit(solution)/shard_map/all_to_all | solution.py:413
  176.6 5.3 %collective-permute-start.10 = (f32[2,32,256]{2,1,0:T(8,128)S(1)}, f32[2,32,256]{2,1,0:T(8,128)S(1)}, u32[]{:S(2)}, u32[]{:S(2)}) collective-permute-start(f32[2,32,256]{2,1,0:T(8,128)S(1)} %step_kernel.4.refs_2_), channel_id=1, source_target_pairs={{1,0},{2,1},{3,2},{7,3},{6,7},{5,6},{4,5},{9,8},{10,9},{11,10},{15... | collective-permute-start | bytes 196616 | tf_op jit(solution)/shard_map/ppermute | solution.py:407
  177.9 5.3 %collective-permute-start.9 = (f32[2,32,256]{2,1,0:T(8,128)S(1)}, f32[2,32,256]{2,1,0:T(8,128)S(1)}, u32[]{:S(2)}, u32[]{:S(2)}) collective-permute-start(f32[2,32,256]{2,1,0:T(8,128)S(1)} %step_kernel.4.refs_2_), channel_id=1, source_target_pairs={{0,1},{1,2},{2,3},{3,7},{7,6},{6,5},{5,4},{8,9},{9,10},{10,11},{11... | collective-permute-start | bytes 196616 | tf_op jit(solution)/shard_map/ppermute | solution.py:407
  183.9 21.8 %all-to-all-start.8 = ((f32[16,16,128]{2,1,0:T(8,128)}), f32[16,16,128]{2,1,0:T(8,128)S(1)}, u32[]{:S(2)}, u32[]{:S(2)}) async-start(f32[16,16,128]{2,1,0:T(8,128)} %get-tuple-element.87.refs_5_), calls=%async_computation.8 | async-start | bytes 262144 | tf_op jit(solution)/shard_map/all_to_all | solution.py:418
  191.4 10.5 %collective-permute-start.11 = (f32[2,64,256]{2,1,0:T(8,128)S(1)}, f32[2,64,256]{2,1,0:T(8,128)S(1)}, u32[]{:S(2)}, u32[]{:S(2)}) collective-permute-start(f32[2,64,256]{2,1,0:T(8,128)S(1)} %get-tuple-element.90), channel_id=1, source_target_pairs={{0,8},{8,16},{16,24},{24,32},{32,40},{40,48},{48,56},{56,64},{64,7... | collective-permute-start | bytes 393224 | tf_op jit(solution)/shard_map/ppermute | solution.py:397
  198.7 6.8 %collective-permute-start.12 = (f32[2,64,256]{2,1,0:T(8,128)S(1)}, f32[2,64,256]{2,1,0:T(8,128)S(1)}, u32[]{:S(2)}, u32[]{:S(2)}) collective-permute-start(f32[2,64,256]{2,1,0:T(8,128)S(1)} %get-tuple-element.91), channel_id=1, source_target_pairs={{8,0},{16,8},{24,16},{32,24},{40,32},{48,40},{56,48},{64,56},{72,6... | collective-permute-start | bytes 393224 | tf_op jit(solution)/shard_map/ppermute | solution.py:397
  245.1 5.5 %collective-permute-start.13 = (f32[17,16,256]{2,1,0:T(8,128)S(1)}, f32[17,16,256]{2,1,0:T(8,128)S(1)}, u32[]{:S(2)}, u32[]{:S(2)}) collective-permute-start(f32[17,16,256]{2,1,0:T(8,128)S(1)} %get-tuple-element.98), channel_id=1, source_target_pairs={{0,8},{8,0},{1,9},{9,1},{2,10},{10,2},{3,11},{11,3},{4,12},{12,4},... | collective-permute-start | bytes 835592 | tf_op jit(solution)/shard_map/ppermute | solution.py:401
  250.7 6.8 %collective-permute-start.14 = (f32[17,8,256]{2,1,0:T(8,128)S(1)}, f32[17,8,256]{2,1,0:T(8,128)S(1)}, u32[]{:S(2)}, u32[]{:S(2)}) collective-permute-start(f32[17,8,256]{2,1,0:T(8,128)S(1)} %get-tuple-element.100), channel_id=1, source_target_pairs={{0,256},{256,0},{1,257},{257,1},{2,258},{258,2},{3,259},{259,3},{4... | collective-permute-start | bytes 417800 | tf_op jit(solution)/shard_map/ppermute | solution.py:401
  258.2 18.1 %all-to-all-start.11 = ((f32[16,1,2176]{2,1,0:T(1,128)}), f32[16,1,2176]{2,1,0:T(1,128)S(1)}, u32[]{:S(2)}, u32[]{:S(2)}) async-start(f32[16,1,2176]{2,1,0:T(1,128)} %bitcast.16), calls=%async_computation.11 | async-start | bytes 278528 | tf_op jit(solution)/shard_map/all_to_all | solution.py:413
  269.6 5.3 %collective-permute-start.16 = (f32[2,32,256]{2,1,0:T(8,128)S(1)}, f32[2,32,256]{2,1,0:T(8,128)S(1)}, u32[]{:S(2)}, u32[]{:S(2)}) collective-permute-start(f32[2,32,256]{2,1,0:T(8,128)S(1)} %step_kernel.5.refs_2_), channel_id=1, source_target_pairs={{1,0},{2,1},{3,2},{7,3},{6,7},{5,6},{4,5},{9,8},{10,9},{11,10},{15... | collective-permute-start | bytes 196616 | tf_op jit(solution)/shard_map/ppermute | solution.py:407
  270.9 5.3 %collective-permute-start.15 = (f32[2,32,256]{2,1,0:T(8,128)S(1)}, f32[2,32,256]{2,1,0:T(8,128)S(1)}, u32[]{:S(2)}, u32[]{:S(2)}) collective-permute-start(f32[2,32,256]{2,1,0:T(8,128)S(1)} %step_kernel.5.refs_2_), channel_id=1, source_target_pairs={{0,1},{1,2},{2,3},{3,7},{7,6},{6,5},{5,4},{8,9},{9,10},{10,11},{11... | collective-permute-start | bytes 196616 | tf_op jit(solution)/shard_map/ppermute | solution.py:407
  276.9 19.2 %all-to-all-start.12 = ((f32[16,16,128]{2,1,0:T(8,128)}), f32[16,16,128]{2,1,0:T(8,128)S(1)}, u32[]{:S(2)}, u32[]{:S(2)}) async-start(f32[16,16,128]{2,1,0:T(8,128)} %get-tuple-element.104.refs_5_), calls=%async_computation.12 | async-start | bytes 262144 | tf_op jit(solution)/shard_map/all_to_all | solution.py:418
  285.0 10.3 %collective-permute-start.17 = (f32[2,64,256]{2,1,0:T(8,128)S(1)}, f32[2,64,256]{2,1,0:T(8,128)S(1)}, u32[]{:S(2)}, u32[]{:S(2)}) collective-permute-start(f32[2,64,256]{2,1,0:T(8,128)S(1)} %get-tuple-element.107), channel_id=1, source_target_pairs={{0,8},{8,16},{16,24},{24,32},{32,40},{40,48},{48,56},{56,64},{64,7... | collective-permute-start | bytes 393224 | tf_op jit(solution)/shard_map/ppermute | solution.py:397

commit v13 on v12

--- a/solution.py
+++ b/solution.py
@@ -315,7 +315,7 @@
                 tail[place, row : row + OUT_ROWS] = rows_out[part, :, lanes]
 
 
-def object_kernel(tail, object_out):
+def last_kernel(tail, pieces, object_out, probe_out):
     for place in range(MODES):
         first = slab_of(place) * OUT_ROWS
         for part in range(2):
@@ -325,9 +325,6 @@
                 object_out[part, first : first + OUT_ROWS, lanes] = tail[
                     place, row : row + OUT_ROWS
                 ]
-
-
-def probe_out_kernel(pieces, probe_out):
     for xlo in range(2):
         for core in range(2):
             for place in range(MODES):
@@ -518,7 +515,7 @@
             keep,
             received,
             scalars=False,
-            after=(object_step,) if final else (object_step, counts),
+            after=(above,) if final else (above, counts),
         )
         sums = exchange_rings(packed)
         shard, shards = call(
@@ -568,9 +565,13 @@
     )
     tail = exchange(tail, MODE_AXES)
     pieces = gather_pieces(tail[:, :32])
-    (object_out,) = call(object_kernel, [(2, HEIGHT, WIDTH)], tail, scalars=False)
-    (probe_out,) = call(probe_out_kernel, [(1, 2, SIDE, SIDE)], pieces, scalars=False)
-    return object_out, probe_out
+    return call(
+        last_kernel,
+        [(2, HEIGHT, WIDTH), (1, 2, SIDE, SIDE)],
+        tail,
+        pieces,
+        scalars=False,
+    )
 
 
 def solution(mesh):

time: 329 us -> 337 us (1.024)
  blocking collectives: 129 us -> 137 us
  starting transfers between devices: 141 us -> 134 us
  waiting for transfers between devices: 34 us -> 40.8 us
    ppermute x6, waiting for transfers between devices: 3.92 us -> 15.2 us  [beside_slab(): return lax.ppermute(value, MODE_AXES, pairs)]
    ppermute x6, waiting for transfers between devices: 14.5 us -> 6.93 us  [other(): return lax.ppermute(value, axis, [(0, 1), (1, 0)])]
    all_to_all x7, blocking collectives: 97.8 us -> 105 us  [exchange(): return lax.all_to_all(value, axes, 0, 0, tiled=True)]
    ppermute x6, starting transfers between devices: 15.8 us -> 9.36 us  [beside_slab(): return lax.ppermute(value, MODE_AXES, pairs)]
    pallas_call x34 -> x33, Pallas kernels: 20.2 us -> 19.5 us  [call(): pl.pallas_call(body, out_shape=[jax.ShapeDtypeStruct(shape, F32) for shap...]
  transfers between devices with their start and end apart: 25 -> 25, of which waited for: 17 -> 23; matrix products, arithmetic and copies ran while one was open for 0% -> 0% of each run, Pallas kernels for 1% -> 1%
where the time goes in v13:
time: 337 us; the launch traced here: 336 us
  blocking collectives  137 us (41%)
  starting transfers between devices  134 us (40%)
  waiting for transfers between devices  40.8 us (12%)
  Pallas kernels  19.6 us (6%)
    all_to_all x7, blocking collectives, exchange(): return lax.all_to_all(value, axes, 0, 0, tiled=True)  105 us
    all_to_all x3, starting transfers between devices, exchange_rings(): lax.all_to_all(value, 'z', 0, 0, tiled=True, axis_index_groups=groups)  40 us
    all_gather x3, blocking collectives, gather_pieces(): gathered = lax.all_gather(piece, ('xlo', 'core'))  32.1 us
    ppermute x6, starting transfers between devices, shift(): lax.ppermute(value, axes, [(i, i + steps) for i in range(first, last)])  30.5 us
    all_to_all x4, starting transfers between devices, exchange(): return lax.all_to_all(value, axes, 0, 0, tiled=True)  30 us
    ppermute x6, starting transfers between devices, other(): return lax.ppermute(value, axis, [(0, 1), (1, 0)])  24.6 us
    pallas_call x33, Pallas kernels, call(): pl.pallas_call(body, out_shape=[jax.ShapeDtypeStruct(shape, F32) for shap...  19.5 us
    ppermute x6, waiting for transfers between devices, beside_slab(): return lax.ppermute(value, MODE_AXES, pairs)  15.2 us
  transfers between devices with their start and end apart: 25, of which 23 were waited for; matrix products, arithmetic and copies ran while one was open for 0% of the time, Pallas kernels for 1%

profile of v13, /device:TPU:1, one launch (start us, length us, event | category | flops | bytes accessed | tf_op | source)
XLA Modules:
  0.0 335.6 jit_solution(5498378954439434223)
XLA Ops:
  0.6 1.1 copy-done.3
  2.6 7.6 %all-to-all-start = ((f32[8,2,32,256]{3,2,1,0:T(8,128)}), f32[8,2,32,256]{3,2,1,0:T(8,128)S(1)}, u32[]{:S(2)}, u32[]{:S(2)}) async-start(f32[8,2,32,256]{3,2,1,0:T(8,128)} %split_kernel.1._), calls=%async_computation | async-start | bytes 1048576 | tf_op jit(solution)/shard_map/all_to_all | solution.py:415
  10.3 4.9 %collective-permute-start = (f32[2,64,256]{2,1,0:T(8,128)S(1)}, f32[2,64,256]{2,1,0:T(8,128)S(1)}, u32[]{:S(2)}, u32[]{:S(2)}) collective-permute-start(f32[2,64,256]{2,1,0:T(8,128)S(1)} %get-tuple-element.57), channel_id=1, source_target_pairs={{8,0},{16,8},{24,16},{32,24},{40,32},{48,40},{56,48},{64,56},{72,6... | collective-permute-start | bytes 393224 | tf_op jit(solution)/shard_map/ppermute | solution.py:394
  17.8 1.3 all-to-all-done.refs_3_.refs_1_
  19.1 1.0 first_kernel.1
  20.1 15.1 %all_to_all.70.refs_0_ = f32[8,2,32,256]{3,2,1,0:T(8,128)S(1)} all-to-all(f32[8,2,32,256]{3,2,1,0:T(8,128)S(1)} %get-tuple-element.59), channel_id=1, replica_groups=mesh['xlo'=2,'z'=16,'core'=2,'xhi'=2,'y'=4] {'xhi','y'}, dimensions={0} | all-to-all | bytes 1048576 | tf_op jit(solution)/shard_map/all_to_all | solution.py:415
  35.2 1.4 ratio_kernel.3
  36.5 12.3 %all_to_all.71.refs_0_ = f32[8,2,32,256]{3,2,1,0:T(8,128)S(1)} all-to-all(f32[8,2,32,256]{3,2,1,0:T(8,128)S(1)} %ratio_kernel.3), channel_id=1, replica_groups=mesh['xlo'=2,'z'=16,'core'=2,'xhi'=2,'y'=4] {'xhi','y'}, dimensions={0} | all-to-all | bytes 1048576 | tf_op jit(solution)/shard_map/all_to_all | solution.py:415
  49.6 5.3 %collective-permute-start.1 = (f32[17,16,256]{2,1,0:T(8,128)S(1)}, f32[17,16,256]{2,1,0:T(8,128)S(1)}, u32[]{:S(2)}, u32[]{:S(2)}) collective-permute-start(f32[17,16,256]{2,1,0:T(8,128)S(1)} %get-tuple-element.63), channel_id=1, source_target_pairs={{0,8},{8,0},{1,9},{9,1},{2,10},{10,2},{3,11},{11,3},{4,12},{12,4},... | collective-permute-start | bytes 835592 | tf_op jit(solution)/shard_map/ppermute | solution.py:398
  54.9 1.2 collective-permute-done.1.refs_1_
  56.1 6.7 %collective-permute-start.2 = (f32[17,8,256]{2,1,0:T(8,128)S(1)}, f32[17,8,256]{2,1,0:T(8,128)S(1)}, u32[]{:S(2)}, u32[]{:S(2)}) collective-permute-start(f32[17,8,256]{2,1,0:T(8,128)S(1)} %get-tuple-element.65), channel_id=1, source_target_pairs={{0,256},{256,0},{1,257},{257,1},{2,258},{258,2},{3,259},{259,3},{4... | collective-permute-start | bytes 417800 | tf_op jit(solution)/shard_map/ppermute | solution.py:398
  63.0 1.8 collective-permute-start.3
  65.2 0.9 collective-permute-done.3.refs_2_.refs_1_
  67.2 17.0 %all-to-all-start.3 = ((f32[16,1,2176]{2,1,0:T(1,128)}), f32[16,1,2176]{2,1,0:T(1,128)S(1)}, u32[]{:S(2)}, u32[]{:S(2)}) async-start(f32[16,1,2176]{2,1,0:T(1,128)} %bitcast.8), calls=%async_computation.3 | async-start | bytes 278528 | tf_op jit(solution)/shard_map/all_to_all | solution.py:410
  84.3 1.3 collective-permute-start.4
  85.5 4.0 %collective-permute-done.4.refs_3_ = f32[2,32,256]{2,1,0:T(8,128)S(1)} collective-permute-done((f32[2,32,256]{2,1,0:T(8,128)S(1)}, f32[2,32,256]{2,1,0:T(8,128)S(1)}, u32[]{:S(2)}, u32[]{:S(2)}) %collective-permute-start.4) | collective-permute-done | bytes 65568 | tf_op jit(solution)/shard_map/ppermute | solution.py:404
  89.5 1.0 all-to-all-done.3
  91.3 7.5 %all-to-all-start.4 = ((f32[16,16,128]{2,1,0:T(8,128)}), f32[16,16,128]{2,1,0:T(8,128)S(1)}, u32[]{:S(2)}, u32[]{:S(2)}) async-start(f32[16,16,128]{2,1,0:T(8,128)} %get-tuple-element.69.refs_5_), calls=%async_computation.4 | async-start | bytes 262144 | tf_op jit(solution)/shard_map/all_to_all | solution.py:415
  99.0 7.3 %collective-permute-start.5 = (f32[2,64,256]{2,1,0:T(8,128)S(1)}, f32[2,64,256]{2,1,0:T(8,128)S(1)}, u32[]{:S(2)}, u32[]{:S(2)}) collective-permute-start(f32[2,64,256]{2,1,0:T(8,128)S(1)} %get-tuple-element.72), channel_id=1, source_target_pairs={{0,8},{8,16},{16,24},{24,32},{32,40},{40,48},{48,56},{56,64},{64,7... | collective-permute-start | bytes 393224 | tf_op jit(solution)/shard_map/ppermute | solution.py:394
  106.3 1.9 collective-permute-start.6
  108.2 1.3 collective-permute-done.5.refs_2_
  109.5 3.6 %collective-permute-done.6.refs_3_ = f32[2,64,256]{2,1,0:T(8,128)S(1)} collective-permute-done((f32[2,64,256]{2,1,0:T(8,128)S(1)}, f32[2,64,256]{2,1,0:T(8,128)S(1)}, u32[]{:S(2)}, u32[]{:S(2)}) %collective-permute-start.6) | collective-permute-done | bytes 131104 | tf_op jit(solution)/shard_map/ppermute | solution.py:394
  113.4 8.8 %all_gather.12 = f32[4,256,128]{2,1,0:T(8,128)S(1)} all-gather(f32[1,256,128]{2,1,0:T(8,128)S(1)} %bitcast.28), channel_id=1, replica_groups=mesh['xlo'=2,'z'=16,'core'=2,'xhi'=2,'y'=4] {'xlo','core'}, dimensions={0}, use_global_device_ids=true | all-gather | bytes 655360 | tf_op jit(solution)/shard_map/all_gather | solution.py:419
  122.2 1.0 next_kernel.2
  123.2 16.0 %all_to_all.72.refs_0_ = f32[8,2,32,256]{3,2,1,0:T(8,128)S(1)} all-to-all(f32[8,2,32,256]{3,2,1,0:T(8,128)S(1)} %get-tuple-element.77), channel_id=1, replica_groups=mesh['xlo'=2,'z'=16,'core'=2,'xhi'=2,'y'=4] {'xhi','y'}, dimensions={0} | all-to-all | bytes 1048576 | tf_op jit(solution)/shard_map/all_to_all | solution.py:415
  139.2 1.4 ratio_kernel.4
  140.6 14.0 %all_to_all.73.refs_0_ = f32[8,2,32,256]{3,2,1,0:T(8,128)S(1)} all-to-all(f32[8,2,32,256]{3,2,1,0:T(8,128)S(1)} %ratio_kernel.4), channel_id=1, replica_groups=mesh['xlo'=2,'z'=16,'core'=2,'xhi'=2,'y'=4] {'xhi','y'}, dimensions={0} | all-to-all | bytes 1048576 | tf_op jit(solution)/shard_map/all_to_all | solution.py:415
  155.3 4.4 %collective-permute-start.7 = (f32[17,16,256]{2,1,0:T(8,128)S(1)}, f32[17,16,256]{2,1,0:T(8,128)S(1)}, u32[]{:S(2)}, u32[]{:S(2)}) collective-permute-start(f32[17,16,256]{2,1,0:T(8,128)S(1)} %get-tuple-element.80), channel_id=1, source_target_pairs={{0,8},{8,0},{1,9},{9,1},{2,10},{10,2},{3,11},{11,3},{4,12},{12,4},... | collective-permute-start | bytes 835592 | tf_op jit(solution)/shard_map/ppermute | solution.py:398
  159.7 1.2 collective-permute-done.7.refs_1_
  160.9 1.9 collective-permute-start.8
  163.0 1.8 collective-permute-start.9
  165.2 0.9 collective-permute-done.9.refs_2_.refs_1_
  166.1 1.5 collective-permute-done.8.refs_1_
  168.3 11.5 %all-to-all-start.7 = ((f32[16,1,2176]{2,1,0:T(1,128)}), f32[16,1,2176]{2,1,0:T(1,128)S(1)}, u32[]{:S(2)}, u32[]{:S(2)}) async-start(f32[16,1,2176]{2,1,0:T(1,128)} %bitcast.12), calls=%async_computation.7 | async-start | bytes 278528 | tf_op jit(solution)/shard_map/all_to_all | solution.py:410
  179.8 1.3 collective-permute-start.10
  181.1 4.0 %collective-permute-done.10.refs_3_ = f32[2,32,256]{2,1,0:T(8,128)S(1)} collective-permute-done((f32[2,32,256]{2,1,0:T(8,128)S(1)}, f32[2,32,256]{2,1,0:T(8,128)S(1)}, u32[]{:S(2)}, u32[]{:S(2)}) %collective-permute-start.10) | collective-permute-done | bytes 65568 | tf_op jit(solution)/shard_map/ppermute | solution.py:404
  185.1 1.0 all-to-all-done.7
  186.8 7.5 %all-to-all-start.8 = ((f32[16,16,128]{2,1,0:T(8,128)}), f32[16,16,128]{2,1,0:T(8,128)S(1)}, u32[]{:S(2)}, u32[]{:S(2)}) async-start(f32[16,16,128]{2,1,0:T(8,128)} %get-tuple-element.87.refs_5_), calls=%async_computation.8 | async-start | bytes 262144 | tf_op jit(solution)/shard_map/all_to_all | solution.py:415
  194.6 7.3 %collective-permute-start.11 = (f32[2,64,256]{2,1,0:T(8,128)S(1)}, f32[2,64,256]{2,1,0:T(8,128)S(1)}, u32[]{:S(2)}, u32[]{:S(2)}) collective-permute-start(f32[2,64,256]{2,1,0:T(8,128)S(1)} %get-tuple-element.90), channel_id=1, source_target_pairs={{0,8},{8,16},{16,24},{24,32},{32,40},{40,48},{48,56},{56,64},{64,7... | collective-permute-start | bytes 393224 | tf_op jit(solution)/shard_map/ppermute | solution.py:394
  201.8 1.9 collective-permute-start.12
  203.8 1.3 collective-permute-done.11.refs_2_
  205.1 3.6 %collective-permute-done.12.refs_3_ = f32[2,64,256]{2,1,0:T(8,128)S(1)} collective-permute-done((f32[2,64,256]{2,1,0:T(8,128)S(1)}, f32[2,64,256]{2,1,0:T(8,128)S(1)}, u32[]{:S(2)}, u32[]{:S(2)}) %collective-permute-start.12) | collective-permute-done | bytes 131104 | tf_op jit(solution)/shard_map/ppermute | solution.py:394
  209.0 8.8 %all_gather.13 = f32[4,256,128]{2,1,0:T(8,128)S(1)} all-gather(f32[1,256,128]{2,1,0:T(8,128)S(1)} %bitcast.29), channel_id=1, replica_groups=mesh['xlo'=2,'z'=16,'core'=2,'xhi'=2,'y'=4] {'xlo','core'}, dimensions={0}, use_global_device_ids=true | all-gather | bytes 655360 | tf_op jit(solution)/shard_map/all_gather | solution.py:419
  217.8 1.0 next_kernel.3
  218.8 16.0 %all_to_all.74.refs_0_ = f32[8,2,32,256]{3,2,1,0:T(8,128)S(1)} all-to-all(f32[8,2,32,256]{3,2,1,0:T(8,128)S(1)} %get-tuple-element.95), channel_id=1, replica_groups=mesh['xlo'=2,'z'=16,'core'=2,'xhi'=2,'y'=4] {'xhi','y'}, dimensions={0} | all-to-all | bytes 1048576 | tf_op jit(solution)/shard_map/all_to_all | solution.py:415
  234.8 1.4 ratio_kernel.5
  236.1 14.0 %all_to_all.75.refs_0_ = f32[8,2,32,256]{3,2,1,0:T(8,128)S(1)} all-to-all(f32[8,2,32,256]{3,2,1,0:T(8,128)S(1)} %ratio_kernel.5), channel_id=1, replica_groups=mesh['xlo'=2,'z'=16,'core'=2,'xhi'=2,'y'=4] {'xhi','y'}, dimensions={0} | all-to-all | bytes 1048576 | tf_op jit(solution)/shard_map/all_to_all | solution.py:415
  250.9 4.4 %collective-permute-start.13 = (f32[17,16,256]{2,1,0:T(8,128)S(1)}, f32[17,16,256]{2,1,0:T(8,128)S(1)}, u32[]{:S(2)}, u32[]{:S(2)}) collective-permute-start(f32[17,16,256]{2,1,0:T(8,128)S(1)} %get-tuple-element.98), channel_id=1, source_target_pairs={{0,8},{8,0},{1,9},{9,1},{2,10},{10,2},{3,11},{11,3},{4,12},{12,4},... | collective-permute-start | bytes 835592 | tf_op jit(solution)/shard_map/ppermute | solution.py:398
  255.2 1.2 collective-permute-done.13.refs_1_
  256.4 1.9 collective-permute-start.14
  258.5 1.8 collective-permute-start.15
  260.4 1.3 collective-permute-done.15.refs_2_.refs_1_
  261.7 1.5 collective-permute-done.14.refs_1_
  263.9 11.5 %all-to-all-start.11 = ((f32[16,1,2176]{2,1,0:T(1,128)}), f32[16,1,2176]{2,1,0:T(1,128)S(1)}, u32[]{:S(2)}, u32[]{:S(2)}) async-start(f32[16,1,2176]{2,1,0:T(1,128)} %bitcast.16), calls=%async_computation.11 | async-start | bytes 278528 | tf_op jit(solution)/shard_map/all_to_all | solution.py:410
  275.4 1.3 collective-permute-start.16
  276.7 4.0 %collective-permute-done.16.refs_3_ = f32[2,32,256]{2,1,0:T(8,128)S(1)} collective-permute-done((f32[2,32,256]{2,1,0:T(8,128)S(1)}, f32[2,32,256]{2,1,0:T(8,128)S(1)}, u32[]{:S(2)}, u32[]{:S(2)}) %collective-permute-start.16) | collective-permute-done | bytes 65568 | tf_op jit(solution)/shard_map/ppermute | solution.py:404
  280.7 1.0 all-to-all-done.11
  282.4 7.5 %all-to-all-start.12 = ((f32[16,16,128]{2,1,0:T(8,128)}), f32[16,16,128]{2,1,0:T(8,128)S(1)}, u32[]{:S(2)}, u32[]{:S(2)}) async-start(f32[16,16,128]{2,1,0:T(8,128)} %get-tuple-element.104.refs_5_), calls=%async_computation.12 | async-start | bytes 262144 | tf_op jit(solution)/shard_map/all_to_all | solution.py:415
  289.9 0.9 place_kernel.5
  290.8 7.2 %collective-permute-start.17 = (f32[2,64,256]{2,1,0:T(8,128)S(1)}, f32[2,64,256]{2,1,0:T(8,128)S(1)}, u32[]{:S(2)}, u32[]{:S(2)}) collective-permute-start(f32[2,64,256]{2,1,0:T(8,128)S(1)} %get-tuple-element.107), channel_id=1, source_target_pairs={{0,8},{8,16},{16,24},{24,32},{32,40},{40,48},{48,56},{56,64},{64,7... | collective-permute-start | bytes 393224 | tf_op jit(solution)/shard_map/ppermute | solution.py:394
  298.0 3.0 collective-permute-done.17.refs_2_
  302.0 17.8 %all_to_all.76.refs_0_ = f32[8,320,128]{2,1,0:T(8,128)S(1)} all-to-all(f32[8,320,128]{2,1,0:T(8,128)S(1)} %tail_kernel.1), channel_id=1, replica_groups=mesh['xlo'=2,'z'=16,'core'=2,'xhi'=2,'y'=4] {'xhi','y'}, dimensions={0} | all-to-all | bytes 2621440 | tf_op jit(solution)/shard_map/all_to_all | solution.py:415
  319.8 14.5 %all-gather = f32[32,32,128]{2,1,0:T(8,128)S(1)} all-gather(f32[8,32,128]{2,1,0:T(8,128)S(1)} %slice.19), channel_id=2, replica_groups=mesh['xlo'=2,'z'=16,'core'=2,'xhi'=2,'y'=4] {'xlo','core'}, dimensions={0}, use_global_device_ids=true | all-gather | bytes 655360 | tf_op jit(solution)/shard_map/all_gather | solution.py:419
  334.3 1.3 last_kernel.1
  (58 shorter events, 12.7 us)
Async XLA Ops:
  0.6 9.6 %copy-start.2 = (f32[2,288,512]{2,1,0:T(8,128)S(1)}, f32[2,288,512]{2,1,0:T(8,128)}, u32[]{:S(2)}) copy-start(f32[2,288,512]{2,1,0:T(8,128)} %whole.1) | copy-start | bytes 3538948
  0.6 1.1 copy-start.3
  2.6 12.7 %copy-start.4 = (s32[1,3]{1,0:T(1,128)S(1)}, s32[1,3]{1,0:T(1,128)}, u32[]{:S(2)}) copy-start(s32[1,3]{1,0:T(1,128)} %param.14) | copy-start | bytes 40
  2.6 12.7 %copy-start.5 = (s32[1,3]{1,0:T(1,128)S(1)}, s32[1,3]{1,0:T(1,128)}, u32[]{:S(2)}) copy-start(s32[1,3]{1,0:T(1,128)} %param.12) | copy-start | bytes 40
  2.6 12.7 %copy-start.6 = (s32[1,3]{1,0:T(1,128)S(1)}, s32[1,3]{1,0:T(1,128)}, u32[]{:S(2)}) copy-start(s32[1,3]{1,0:T(1,128)} %param.11) | copy-start | bytes 40
  2.6 14.0 %copy-start.1 = (bf16[1,3,256,256]{3,2,1,0:T(8,128)(2,1)S(1)}, bf16[1,3,256,256]{3,2,1,0:T(8,128)(2,1)}, u32[]{:S(2)}) copy-start(bf16[1,3,256,256]{3,2,1,0:T(8,128)(2,1)} %refs_1_.5) | copy-start | bytes 1179652
  2.6 16.5 %all-to-all-start = ((f32[8,2,32,256]{3,2,1,0:T(8,128)}), f32[8,2,32,256]{3,2,1,0:T(8,128)S(1)}, u32[]{:S(2)}, u32[]{:S(2)}) async-start(f32[8,2,32,256]{3,2,1,0:T(8,128)} %split_kernel.1._), calls=%async_computation | async-start | bytes 1048576 | tf_op jit(solution)/shard_map/all_to_all | solution.py:415
  10.2 8.8 %copy-start = (bf16[3,2,256,256]{3,2,1,0:T(8,128)(2,1)S(1)}, bf16[3,2,256,256]{3,2,1,0:T(8,128)(2,1)}, u32[]{:S(2)}) copy-start(bf16[3,2,256,256]{3,2,1,0:T(8,128)(2,1)} %constant.35.clone.refs_4_.refs_3_.refs_2_) | copy-start | bytes 2359300
  10.3 7.5 %collective-permute-start = (f32[2,64,256]{2,1,0:T(8,128)S(1)}, f32[2,64,256]{2,1,0:T(8,128)S(1)}, u32[]{:S(2)}, u32[]{:S(2)}) collective-permute-start(f32[2,64,256]{2,1,0:T(8,128)S(1)} %get-tuple-element.57), channel_id=1, source_target_pairs={{8,0},{16,8},{24,16},{32,24},{40,32},{48,40},{56,48},{64,56},{72,6... | collective-permute-start | bytes 393224 | tf_op jit(solution)/shard_map/ppermute | solution.py:394
  49.6 6.5 %collective-permute-start.1 = (f32[17,16,256]{2,1,0:T(8,128)S(1)}, f32[17,16,256]{2,1,0:T(8,128)S(1)}, u32[]{:S(2)}, u32[]{:S(2)}) collective-permute-start(f32[17,16,256]{2,1,0:T(8,128)S(1)} %get-tuple-element.63), channel_id=1, source_target_pairs={{0,8},{8,0},{1,9},{9,1},{2,10},{10,2},{3,11},{11,3},{4,12},{12,4},... | collective-permute-start | bytes 835592 | tf_op jit(solution)/shard_map/ppermute | solution.py:398
  56.1 10.5 %collective-permute-start.2 = (f32[17,8,256]{2,1,0:T(8,128)S(1)}, f32[17,8,256]{2,1,0:T(8,128)S(1)}, u32[]{:S(2)}, u32[]{:S(2)}) collective-permute-start(f32[17,8,256]{2,1,0:T(8,128)S(1)} %get-tuple-element.65), channel_id=1, source_target_pairs={{0,256},{256,0},{1,257},{257,1},{2,258},{258,2},{3,259},{259,3},{4... | collective-permute-start | bytes 417800 | tf_op jit(solution)/shard_map/ppermute | solution.py:398
  63.0 3.2 collective-permute-start.3
  67.2 23.4 %all-to-all-start.3 = ((f32[16,1,2176]{2,1,0:T(1,128)}), f32[16,1,2176]{2,1,0:T(1,128)S(1)}, u32[]{:S(2)}, u32[]{:S(2)}) async-start(f32[16,1,2176]{2,1,0:T(1,128)} %bitcast.8), calls=%async_computation.3 | async-start | bytes 278528 | tf_op jit(solution)/shard_map/all_to_all | solution.py:410
  84.3 5.3 %collective-permute-start.4 = (f32[2,32,256]{2,1,0:T(8,128)S(1)}, f32[2,32,256]{2,1,0:T(8,128)S(1)}, u32[]{:S(2)}, u32[]{:S(2)}) collective-permute-start(f32[2,32,256]{2,1,0:T(8,128)S(1)} %step_kernel.3.refs_2_), channel_id=1, source_target_pairs={{1,0},{2,1},{3,2},{7,3},{6,7},{5,6},{4,5},{9,8},{10,9},{11,10},{15... | collective-permute-start | bytes 196616 | tf_op jit(solution)/shard_map/ppermute | solution.py:404
  91.3 22.1 %all-to-all-start.4 = ((f32[16,16,128]{2,1,0:T(8,128)}), f32[16,16,128]{2,1,0:T(8,128)S(1)}, u32[]{:S(2)}, u32[]{:S(2)}) async-start(f32[16,16,128]{2,1,0:T(8,128)} %get-tuple-element.69.refs_5_), calls=%async_computation.4 | async-start | bytes 262144 | tf_op jit(solution)/shard_map/all_to_all | solution.py:415
  99.0 10.5 %collective-permute-start.5 = (f32[2,64,256]{2,1,0:T(8,128)S(1)}, f32[2,64,256]{2,1,0:T(8,128)S(1)}, u32[]{:S(2)}, u32[]{:S(2)}) collective-permute-start(f32[2,64,256]{2,1,0:T(8,128)S(1)} %get-tuple-element.72), channel_id=1, source_target_pairs={{0,8},{8,16},{16,24},{24,32},{32,40},{40,48},{48,56},{56,64},{64,7... | collective-permute-start | bytes 393224 | tf_op jit(solution)/shard_map/ppermute | solution.py:394
  106.3 6.8 %collective-permute-start.6 = (f32[2,64,256]{2,1,0:T(8,128)S(1)}, f32[2,64,256]{2,1,0:T(8,128)S(1)}, u32[]{:S(2)}, u32[]{:S(2)}) collective-permute-start(f32[2,64,256]{2,1,0:T(8,128)S(1)} %get-tuple-element.73), channel_id=1, source_target_pairs={{8,0},{16,8},{24,16},{32,24},{40,32},{48,40},{56,48},{64,56},{72,6... | collective-permute-start | bytes 393224 | tf_op jit(solution)/shard_map/ppermute | solution.py:394
  155.3 5.5 %collective-permute-start.7 = (f32[17,16,256]{2,1,0:T(8,128)S(1)}, f32[17,16,256]{2,1,0:T(8,128)S(1)}, u32[]{:S(2)}, u32[]{:S(2)}) collective-permute-start(f32[17,16,256]{2,1,0:T(8,128)S(1)} %get-tuple-element.80), channel_id=1, source_target_pairs={{0,8},{8,0},{1,9},{9,1},{2,10},{10,2},{3,11},{11,3},{4,12},{12,4},... | collective-permute-start | bytes 835592 | tf_op jit(solution)/shard_map/ppermute | solution.py:398
  160.9 6.8 %collective-permute-start.8 = (f32[17,8,256]{2,1,0:T(8,128)S(1)}, f32[17,8,256]{2,1,0:T(8,128)S(1)}, u32[]{:S(2)}, u32[]{:S(2)}) collective-permute-start(f32[17,8,256]{2,1,0:T(8,128)S(1)} %get-tuple-element.82), channel_id=1, source_target_pairs={{0,256},{256,0},{1,257},{257,1},{2,258},{258,2},{3,259},{259,3},{4... | collective-permute-start | bytes 417800 | tf_op jit(solution)/shard_map/ppermute | solution.py:398
  163.0 3.2 collective-permute-start.9
  168.3 17.8 %all-to-all-start.7 = ((f32[16,1,2176]{2,1,0:T(1,128)}), f32[16,1,2176]{2,1,0:T(1,128)S(1)}, u32[]{:S(2)}, u32[]{:S(2)}) async-start(f32[16,1,2176]{2,1,0:T(1,128)} %bitcast.12), calls=%async_computation.7 | async-start | bytes 278528 | tf_op jit(solution)/shard_map/all_to_all | solution.py:410
  179.8 5.3 %collective-permute-start.10 = (f32[2,32,256]{2,1,0:T(8,128)S(1)}, f32[2,32,256]{2,1,0:T(8,128)S(1)}, u32[]{:S(2)}, u32[]{:S(2)}) collective-permute-start(f32[2,32,256]{2,1,0:T(8,128)S(1)} %step_kernel.4.refs_2_), channel_id=1, source_target_pairs={{1,0},{2,1},{3,2},{7,3},{6,7},{5,6},{4,5},{9,8},{10,9},{11,10},{15... | collective-permute-start | bytes 196616 | tf_op jit(solution)/shard_map/ppermute | solution.py:404
  186.8 22.1 %all-to-all-start.8 = ((f32[16,16,128]{2,1,0:T(8,128)}), f32[16,16,128]{2,1,0:T(8,128)S(1)}, u32[]{:S(2)}, u32[]{:S(2)}) async-start(f32[16,16,128]{2,1,0:T(8,128)} %get-tuple-element.87.refs_5_), calls=%async_computation.8 | async-start | bytes 262144 | tf_op jit(solution)/shard_map/all_to_all | solution.py:415
  194.6 10.5 %collective-permute-start.11 = (f32[2,64,256]{2,1,0:T(8,128)S(1)}, f32[2,64,256]{2,1,0:T(8,128)S(1)}, u32[]{:S(2)}, u32[]{:S(2)}) collective-permute-start(f32[2,64,256]{2,1,0:T(8,128)S(1)} %get-tuple-element.90), channel_id=1, source_target_pairs={{0,8},{8,16},{16,24},{24,32},{32,40},{40,48},{48,56},{56,64},{64,7... | collective-permute-start | bytes 393224 | tf_op jit(solution)/shard_map/ppermute | solution.py:394
  201.8 6.8 %collective-permute-start.12 = (f32[2,64,256]{2,1,0:T(8,128)S(1)}, f32[2,64,256]{2,1,0:T(8,128)S(1)}, u32[]{:S(2)}, u32[]{:S(2)}) collective-permute-start(f32[2,64,256]{2,1,0:T(8,128)S(1)} %get-tuple-element.91), channel_id=1, source_target_pairs={{8,0},{16,8},{24,16},{32,24},{40,32},{48,40},{56,48},{64,56},{72,6... | collective-permute-start | bytes 393224 | tf_op jit(solution)/shard_map/ppermute | solution.py:394
  250.9 5.5 %collective-permute-start.13 = (f32[17,16,256]{2,1,0:T(8,128)S(1)}, f32[17,16,256]{2,1,0:T(8,128)S(1)}, u32[]{:S(2)}, u32[]{:S(2)}) collective-permute-start(f32[17,16,256]{2,1,0:T(8,128)S(1)} %get-tuple-element.98), channel_id=1, source_target_pairs={{0,8},{8,0},{1,9},{9,1},{2,10},{10,2},{3,11},{11,3},{4,12},{12,4},... | collective-permute-start | bytes 835592 | tf_op jit(solution)/shard_map/ppermute | solution.py:398
  256.4 6.8 %collective-permute-start.14 = (f32[17,8,256]{2,1,0:T(8,128)S(1)}, f32[17,8,256]{2,1,0:T(8,128)S(1)}, u32[]{:S(2)}, u32[]{:S(2)}) collective-permute-start(f32[17,8,256]{2,1,0:T(8,128)S(1)} %get-tuple-element.100), channel_id=1, source_target_pairs={{0,256},{256,0},{1,257},{257,1},{2,258},{258,2},{3,259},{259,3},{4... | collective-permute-start | bytes 417800 | tf_op jit(solution)/shard_map/ppermute | solution.py:398
  258.5 3.2 collective-permute-start.15
  263.9 17.8 %all-to-all-start.11 = ((f32[16,1,2176]{2,1,0:T(1,128)}), f32[16,1,2176]{2,1,0:T(1,128)S(1)}, u32[]{:S(2)}, u32[]{:S(2)}) async-start(f32[16,1,2176]{2,1,0:T(1,128)} %bitcast.16), calls=%async_computation.11 | async-start | bytes 278528 | tf_op jit(solution)/shard_map/all_to_all | solution.py:410
  275.4 5.3 %collective-permute-start.16 = (f32[2,32,256]{2,1,0:T(8,128)S(1)}, f32[2,32,256]{2,1,0:T(8,128)S(1)}, u32[]{:S(2)}, u32[]{:S(2)}) collective-permute-start(f32[2,32,256]{2,1,0:T(8,128)S(1)} %step_kernel.5.refs_2_), channel_id=1, source_target_pairs={{1,0},{2,1},{3,2},{7,3},{6,7},{5,6},{4,5},{9,8},{10,9},{11,10},{15... | collective-permute-start | bytes 196616 | tf_op jit(solution)/shard_map/ppermute | solution.py:404
  282.4 19.4 %all-to-all-start.12 = ((f32[16,16,128]{2,1,0:T(8,128)}), f32[16,16,128]{2,1,0:T(8,128)S(1)}, u32[]{:S(2)}, u32[]{:S(2)}) async-start(f32[16,16,128]{2,1,0:T(8,128)} %get-tuple-element.104.refs_5_), calls=%async_computation.12 | async-start | bytes 262144 | tf_op jit(solution)/shard_map/all_to_all | solution.py:415
  290.8 10.3 %collective-permute-start.17 = (f32[2,64,256]{2,1,0:T(8,128)S(1)}, f32[2,64,256]{2,1,0:T(8,128)S(1)}, u32[]{:S(2)}, u32[]{:S(2)}) collective-permute-start(f32[2,64,256]{2,1,0:T(8,128)S(1)} %get-tuple-element.107), channel_id=1, source_target_pairs={{0,8},{8,16},{16,24},{24,32},{32,40},{40,48},{48,56},{56,64},{64,7... | collective-permute-start | bytes 393224 | tf_op jit(solution)/shard_map/ppermute | solution.py:394

commit v14 on v13

--- a/solution.py
+++ b/solution.py
@@ -255,7 +255,7 @@
     step[1] = OBJECT_RATE * imag / (light + OBJECT_DAMP)
 
 
-def place_kernel(scal, above, step, below, band, part_band, to_left, to_right):
+def place_kernel(scal, above, step, below, band, part_band, to_right, to_left=None):
     cols, rest = column_window(scal)
     height = 3 * SLAB
     part_band[...] = jnp.zeros_like(part_band)
@@ -264,7 +264,8 @@
         block = pltpu.roll(block, lax.rem(2 * SLAB + scal[ROW], height), 0)[:BAND]
         block = jnp.concatenate([block, jnp.zeros((BAND, LANES), F32)], axis=1)
         part_band[part, :, cols] = pltpu.roll(block, rest, 1)
-    to_left[...] = part_band[:, :, :SIDE]
+    if to_left is not None:
+        to_left[...] = part_band[:, :, :SIDE]
     to_right[...] = part_band[:, :, WIDTH:]
     part_band[:, :, :WIDTH] = part_band[:, :, :WIDTH] + band[:, :, :WIDTH]
     part_band[:, :, WIDTH:] = (
@@ -515,7 +516,7 @@
             keep,
             received,
             scalars=False,
-            after=(above,) if final else (above, counts),
+            after=(object_step,) if final else (object_step, counts),
         )
         sums = exchange_rings(packed)
         shard, shards = call(
@@ -527,9 +528,9 @@
             after=(above, below),
         )
         piece = exchange(shards, "z")
-        part_band, to_left, to_right = call(
+        part_band, to_right, *to_left = call(
             place_kernel,
-            [band_shape, edge, edge],
+            [band_shape, edge] if final else [band_shape, edge, edge],
             scal,
             above,
             object_step,
@@ -544,7 +545,7 @@
             )
             piece, rows_out = lax.optimization_barrier((piece, rows_out))
         else:
-            from_right = shift(to_left, TILE_AXES, TILES, -1)
+            from_right = shift(to_left[0], TILE_AXES, TILES, -1)
             band, view = call(
                 view_kernel,
                 [band_shape, slab_pair],

time: 337 us -> 329 us (0.976)
  blocking collectives: 137 us -> 129 us
  starting transfers between devices: 134 us -> 141 us
  waiting for transfers between devices: 40.8 us -> 34.6 us
    ppermute x6, waiting for transfers between devices: 15.2 us -> 3.92 us  [beside_slab(): return lax.ppermute(value, MODE_AXES, pairs)]
    ppermute x6, waiting for transfers between devices: 6.93 us -> 14.5 us  [other(): return lax.ppermute(value, axis, [(0, 1), (1, 0)])]
    all_to_all x7, blocking collectives: 105 us -> 97.8 us  [exchange(): return lax.all_to_all(value, axes, 0, 0, tiled=True)]
    ppermute x6, starting transfers between devices: 9.36 us -> 15.8 us  [beside_slab(): return lax.ppermute(value, MODE_AXES, pairs)]
  transfers between devices with their start and end apart: 25 -> 25, of which waited for: 23 -> 17; matrix products, arithmetic and copies ran while one was open for 0% -> 0% of each run, Pallas kernels for 1% -> 1%
where the time goes in v14:
time: 329 us; the launch traced here: 327 us
  starting transfers between devices  141 us (43%)
  blocking collectives  129 us (39%)
  waiting for transfers between devices  34.6 us (11%)
  Pallas kernels  18.9 us (6%)
    all_to_all x7, blocking collectives, exchange(): return lax.all_to_all(value, axes, 0, 0, tiled=True)  97.8 us
    all_to_all x3, starting transfers between devices, exchange_rings(): lax.all_to_all(value, 'z', 0, 0, tiled=True, axis_index_groups=groups)  40 us
    all_gather x3, blocking collectives, gather_pieces(): gathered = lax.all_gather(piece, ('xlo', 'core'))  31 us
    ppermute x6, starting transfers between devices, shift(): lax.ppermute(value, axes, [(i, i + steps) for i in range(first, last)])  30.5 us
    all_to_all x4, starting transfers between devices, exchange(): return lax.all_to_all(value, axes, 0, 0, tiled=True)  29.2 us
    ppermute x6, starting transfers between devices, other(): return lax.ppermute(value, axis, [(0, 1), (1, 0)])  25.8 us
    pallas_call x33, Pallas kernels, call(): pl.pallas_call(body, out_shape=[jax.ShapeDtypeStruct(shape, F32) for shap...  18.9 us
    ppermute x6, starting transfers between devices, beside_slab(): return lax.ppermute(value, MODE_AXES, pairs)  15.8 us
  transfers between devices with their start and end apart: 25, of which 17 were waited for; matrix products, arithmetic and copies ran while one was open for 0% of the time, Pallas kernels for 1%

profile of v14, /device:TPU:1, one launch (start us, length us, event | category | flops | bytes accessed | tf_op | source)
XLA Modules:
  0.0 327.2 jit_solution(11406700463606666020)
XLA Ops:
  0.6 1.1 copy-done.3
  1.8 0.8 split_kernel.1._
  2.6 7.6 %all-to-all-start = ((f32[8,2,32,256]{3,2,1,0:T(8,128)}), f32[8,2,32,256]{3,2,1,0:T(8,128)S(1)}, u32[]{:S(2)}, u32[]{:S(2)}) async-start(f32[8,2,32,256]{3,2,1,0:T(8,128)} %split_kernel.1._), calls=%async_computation | async-start | bytes 1048576 | tf_op jit(solution)/shard_map/all_to_all | solution.py:416
  10.3 4.9 %collective-permute-start = (f32[2,64,256]{2,1,0:T(8,128)S(1)}, f32[2,64,256]{2,1,0:T(8,128)S(1)}, u32[]{:S(2)}, u32[]{:S(2)}) collective-permute-start(f32[2,64,256]{2,1,0:T(8,128)S(1)} %get-tuple-element.57), channel_id=1, source_target_pairs={{8,0},{16,8},{24,16},{32,24},{40,32},{48,40},{56,48},{64,56},{72,6... | collective-permute-start | bytes 393224 | tf_op jit(solution)/shard_map/ppermute | solution.py:395
  17.0 0.8 collective-permute-done.refs_2_
  17.8 1.3 all-to-all-done.refs_3_.refs_1_
  19.1 1.0 first_kernel.1
  20.1 15.1 %all_to_all.70.refs_0_ = f32[8,2,32,256]{3,2,1,0:T(8,128)S(1)} all-to-all(f32[8,2,32,256]{3,2,1,0:T(8,128)S(1)} %get-tuple-element.59), channel_id=1, replica_groups=mesh['xlo'=2,'z'=16,'core'=2,'xhi'=2,'y'=4] {'xhi','y'}, dimensions={0} | all-to-all | bytes 1048576 | tf_op jit(solution)/shard_map/all_to_all | solution.py:416
  35.2 1.4 ratio_kernel.3
  36.5 12.3 %all_to_all.71.refs_0_ = f32[8,2,32,256]{3,2,1,0:T(8,128)S(1)} all-to-all(f32[8,2,32,256]{3,2,1,0:T(8,128)S(1)} %ratio_kernel.3), channel_id=1, replica_groups=mesh['xlo'=2,'z'=16,'core'=2,'xhi'=2,'y'=4] {'xhi','y'}, dimensions={0} | all-to-all | bytes 1048576 | tf_op jit(solution)/shard_map/all_to_all | solution.py:416
  48.8 0.7 backward_kernel.3
  49.6 5.3 %collective-permute-start.1 = (f32[17,16,256]{2,1,0:T(8,128)S(1)}, f32[17,16,256]{2,1,0:T(8,128)S(1)}, u32[]{:S(2)}, u32[]{:S(2)}) collective-permute-start(f32[17,16,256]{2,1,0:T(8,128)S(1)} %get-tuple-element.63), channel_id=1, source_target_pairs={{0,8},{8,0},{1,9},{9,1},{2,10},{10,2},{3,11},{11,3},{4,12},{12,4},... | collective-permute-start | bytes 835592 | tf_op jit(solution)/shard_map/ppermute | solution.py:399
  54.9 1.2 collective-permute-done.1.refs_1_
  56.1 6.7 %collective-permute-start.2 = (f32[17,8,256]{2,1,0:T(8,128)S(1)}, f32[17,8,256]{2,1,0:T(8,128)S(1)}, u32[]{:S(2)}, u32[]{:S(2)}) collective-permute-start(f32[17,8,256]{2,1,0:T(8,128)S(1)} %get-tuple-element.65), channel_id=1, source_target_pairs={{0,256},{256,0},{1,257},{257,1},{2,258},{258,2},{3,259},{259,3},{4... | collective-permute-start | bytes 417800 | tf_op jit(solution)/shard_map/ppermute | solution.py:399
  63.4 3.2 collective-permute-done.2.refs_1_
  67.2 17.0 %all-to-all-start.3 = ((f32[16,1,2176]{2,1,0:T(1,128)}), f32[16,1,2176]{2,1,0:T(1,128)S(1)}, u32[]{:S(2)}, u32[]{:S(2)}) async-start(f32[16,1,2176]{2,1,0:T(1,128)} %bitcast.8), calls=%async_computation.3 | async-start | bytes 278528 | tf_op jit(solution)/shard_map/all_to_all | solution.py:411
  84.3 1.3 collective-permute-start.4
  85.5 4.0 %collective-permute-start.3 = (f32[2,32,256]{2,1,0:T(8,128)S(1)}, f32[2,32,256]{2,1,0:T(8,128)S(1)}, u32[]{:S(2)}, u32[]{:S(2)}) collective-permute-start(f32[2,32,256]{2,1,0:T(8,128)S(1)} %step_kernel.3.refs_2_), channel_id=1, source_target_pairs={{0,1},{1,2},{2,3},{3,7},{7,6},{6,5},{5,4},{8,9},{9,10},{10,11},{11... | collective-permute-start | bytes 196616 | tf_op jit(solution)/shard_map/ppermute | solution.py:405
  89.5 1.3 collective-permute-done.3.refs_2_.refs_1_
  91.5 7.2 %all-to-all-start.4 = ((f32[16,16,128]{2,1,0:T(8,128)}), f32[16,16,128]{2,1,0:T(8,128)S(1)}, u32[]{:S(2)}, u32[]{:S(2)}) async-start(f32[16,16,128]{2,1,0:T(8,128)} %get-tuple-element.69.refs_5_), calls=%async_computation.4 | async-start | bytes 262144 | tf_op jit(solution)/shard_map/all_to_all | solution.py:416
  99.0 7.3 %collective-permute-start.5 = (f32[2,64,256]{2,1,0:T(8,128)S(1)}, f32[2,64,256]{2,1,0:T(8,128)S(1)}, u32[]{:S(2)}, u32[]{:S(2)}) collective-permute-start(f32[2,64,256]{2,1,0:T(8,128)S(1)} %get-tuple-element.72), channel_id=1, source_target_pairs={{0,8},{8,16},{16,24},{24,32},{32,40},{40,48},{48,56},{56,64},{64,7... | collective-permute-start | bytes 393224 | tf_op jit(solution)/shard_map/ppermute | solution.py:395
  106.3 1.9 collective-permute-start.6
  108.2 1.3 collective-permute-done.5.refs_2_
  109.5 3.6 %collective-permute-done.6.refs_3_ = f32[2,64,256]{2,1,0:T(8,128)S(1)} collective-permute-done((f32[2,64,256]{2,1,0:T(8,128)S(1)}, f32[2,64,256]{2,1,0:T(8,128)S(1)}, u32[]{:S(2)}, u32[]{:S(2)}) %collective-permute-start.6) | collective-permute-done | bytes 131104 | tf_op jit(solution)/shard_map/ppermute | solution.py:395
  113.4 8.8 %all_gather.12 = f32[4,256,128]{2,1,0:T(8,128)S(1)} all-gather(f32[1,256,128]{2,1,0:T(8,128)S(1)} %bitcast.28), channel_id=1, replica_groups=mesh['xlo'=2,'z'=16,'core'=2,'xhi'=2,'y'=4] {'xlo','core'}, dimensions={0}, use_global_device_ids=true | all-gather | bytes 655360 | tf_op jit(solution)/shard_map/all_gather | solution.py:420
  122.2 1.0 next_kernel.2
  123.2 12.9 %all_to_all.72.refs_0_ = f32[8,2,32,256]{3,2,1,0:T(8,128)S(1)} all-to-all(f32[8,2,32,256]{3,2,1,0:T(8,128)S(1)} %get-tuple-element.77), channel_id=1, replica_groups=mesh['xlo'=2,'z'=16,'core'=2,'xhi'=2,'y'=4] {'xhi','y'}, dimensions={0} | all-to-all | bytes 1048576 | tf_op jit(solution)/shard_map/all_to_all | solution.py:416
  136.2 1.4 ratio_kernel.4
  137.6 13.8 %all_to_all.73.refs_0_ = f32[8,2,32,256]{3,2,1,0:T(8,128)S(1)} all-to-all(f32[8,2,32,256]{3,2,1,0:T(8,128)S(1)} %ratio_kernel.4), channel_id=1, replica_groups=mesh['xlo'=2,'z'=16,'core'=2,'xhi'=2,'y'=4] {'xhi','y'}, dimensions={0} | all-to-all | bytes 1048576 | tf_op jit(solution)/shard_map/all_to_all | solution.py:416
  151.4 0.7 backward_kernel.4
  152.1 4.4 %collective-permute-start.7 = (f32[17,16,256]{2,1,0:T(8,128)S(1)}, f32[17,16,256]{2,1,0:T(8,128)S(1)}, u32[]{:S(2)}, u32[]{:S(2)}) collective-permute-start(f32[17,16,256]{2,1,0:T(8,128)S(1)} %get-tuple-element.80), channel_id=1, source_target_pairs={{0,8},{8,0},{1,9},{9,1},{2,10},{10,2},{3,11},{11,3},{4,12},{12,4},... | collective-permute-start | bytes 835592 | tf_op jit(solution)/shard_map/ppermute | solution.py:399
  156.5 1.2 collective-permute-done.7.refs_1_
  157.7 2.8 collective-permute-start.8
  161.1 3.4 %collective-permute-done.8.refs_1_ = f32[17,8,256]{2,1,0:T(8,128)S(1)} collective-permute-done((f32[17,8,256]{2,1,0:T(8,128)S(1)}, f32[17,8,256]{2,1,0:T(8,128)S(1)}, u32[]{:S(2)}, u32[]{:S(2)}) %collective-permute-start.8) | collective-permute-done | bytes 139296 | tf_op jit(solution)/shard_map/ppermute | solution.py:399
  165.2 11.5 %all-to-all-start.7 = ((f32[16,1,2176]{2,1,0:T(1,128)}), f32[16,1,2176]{2,1,0:T(1,128)S(1)}, u32[]{:S(2)}, u32[]{:S(2)}) async-start(f32[16,1,2176]{2,1,0:T(1,128)} %bitcast.12), calls=%async_computation.7 | async-start | bytes 278528 | tf_op jit(solution)/shard_map/all_to_all | solution.py:411
  176.6 1.3 collective-permute-start.10
  177.9 4.0 %collective-permute-start.9 = (f32[2,32,256]{2,1,0:T(8,128)S(1)}, f32[2,32,256]{2,1,0:T(8,128)S(1)}, u32[]{:S(2)}, u32[]{:S(2)}) collective-permute-start(f32[2,32,256]{2,1,0:T(8,128)S(1)} %step_kernel.4.refs_2_), channel_id=1, source_target_pairs={{0,1},{1,2},{2,3},{3,7},{7,6},{6,5},{5,4},{8,9},{9,10},{10,11},{11... | collective-permute-start | bytes 196616 | tf_op jit(solution)/shard_map/ppermute | solution.py:405
  181.9 1.3 collective-permute-done.9.refs_2_.refs_1_
  183.9 7.2 %all-to-all-start.8 = ((f32[16,16,128]{2,1,0:T(8,128)}), f32[16,16,128]{2,1,0:T(8,128)S(1)}, u32[]{:S(2)}, u32[]{:S(2)}) async-start(f32[16,16,128]{2,1,0:T(8,128)} %get-tuple-element.87.refs_5_), calls=%async_computation.8 | async-start | bytes 262144 | tf_op jit(solution)/shard_map/all_to_all | solution.py:416
  191.4 7.3 %collective-permute-start.11 = (f32[2,64,256]{2,1,0:T(8,128)S(1)}, f32[2,64,256]{2,1,0:T(8,128)S(1)}, u32[]{:S(2)}, u32[]{:S(2)}) collective-permute-start(f32[2,64,256]{2,1,0:T(8,128)S(1)} %get-tuple-element.90), channel_id=1, source_target_pairs={{0,8},{8,16},{16,24},{24,32},{32,40},{40,48},{48,56},{56,64},{64,7... | collective-permute-start | bytes 393224 | tf_op jit(solution)/shard_map/ppermute | solution.py:395
  198.7 1.9 collective-permute-start.12
  200.6 1.3 collective-permute-done.11.refs_2_
  201.9 3.6 %collective-permute-done.12.refs_3_ = f32[2,64,256]{2,1,0:T(8,128)S(1)} collective-permute-done((f32[2,64,256]{2,1,0:T(8,128)S(1)}, f32[2,64,256]{2,1,0:T(8,128)S(1)}, u32[]{:S(2)}, u32[]{:S(2)}) %collective-permute-start.12) | collective-permute-done | bytes 131104 | tf_op jit(solution)/shard_map/ppermute | solution.py:395
  205.8 9.2 %all_gather.13 = f32[4,256,128]{2,1,0:T(8,128)S(1)} all-gather(f32[1,256,128]{2,1,0:T(8,128)S(1)} %bitcast.29), channel_id=1, replica_groups=mesh['xlo'=2,'z'=16,'core'=2,'xhi'=2,'y'=4] {'xlo','core'}, dimensions={0}, use_global_device_ids=true | all-gather | bytes 655360 | tf_op jit(solution)/shard_map/all_gather | solution.py:420
  215.0 1.0 next_kernel.3
  216.0 13.0 %all_to_all.74.refs_0_ = f32[8,2,32,256]{3,2,1,0:T(8,128)S(1)} all-to-all(f32[8,2,32,256]{3,2,1,0:T(8,128)S(1)} %get-tuple-element.95), channel_id=1, replica_groups=mesh['xlo'=2,'z'=16,'core'=2,'xhi'=2,'y'=4] {'xhi','y'}, dimensions={0} | all-to-all | bytes 1048576 | tf_op jit(solution)/shard_map/all_to_all | solution.py:416
  229.0 1.4 ratio_kernel.5
  230.4 14.0 %all_to_all.75.refs_0_ = f32[8,2,32,256]{3,2,1,0:T(8,128)S(1)} all-to-all(f32[8,2,32,256]{3,2,1,0:T(8,128)S(1)} %ratio_kernel.5), channel_id=1, replica_groups=mesh['xlo'=2,'z'=16,'core'=2,'xhi'=2,'y'=4] {'xhi','y'}, dimensions={0} | all-to-all | bytes 1048576 | tf_op jit(solution)/shard_map/all_to_all | solution.py:416
  244.4 0.7 backward_kernel.5
  245.1 4.4 %collective-permute-start.13 = (f32[17,16,256]{2,1,0:T(8,128)S(1)}, f32[17,16,256]{2,1,0:T(8,128)S(1)}, u32[]{:S(2)}, u32[]{:S(2)}) collective-permute-start(f32[17,16,256]{2,1,0:T(8,128)S(1)} %get-tuple-element.98), channel_id=1, source_target_pairs={{0,8},{8,0},{1,9},{9,1},{2,10},{10,2},{3,11},{11,3},{4,12},{12,4},... | collective-permute-start | bytes 835592 | tf_op jit(solution)/shard_map/ppermute | solution.py:399
  249.5 1.2 collective-permute-done.13.refs_1_
  250.7 2.2 collective-permute-start.14
  253.1 4.4 %collective-permute-done.14.refs_1_ = f32[17,8,256]{2,1,0:T(8,128)S(1)} collective-permute-done((f32[17,8,256]{2,1,0:T(8,128)S(1)}, f32[17,8,256]{2,1,0:T(8,128)S(1)}, u32[]{:S(2)}, u32[]{:S(2)}) %collective-permute-start.14) | collective-permute-done | bytes 139296 | tf_op jit(solution)/shard_map/ppermute | solution.py:399
  258.2 11.5 %all-to-all-start.11 = ((f32[16,1,2176]{2,1,0:T(1,128)}), f32[16,1,2176]{2,1,0:T(1,128)S(1)}, u32[]{:S(2)}, u32[]{:S(2)}) async-start(f32[16,1,2176]{2,1,0:T(1,128)} %bitcast.16), calls=%async_computation.11 | async-start | bytes 278528 | tf_op jit(solution)/shard_map/all_to_all | solution.py:411
  269.6 1.3 collective-permute-start.16
  270.9 4.0 %collective-permute-start.15 = (f32[2,32,256]{2,1,0:T(8,128)S(1)}, f32[2,32,256]{2,1,0:T(8,128)S(1)}, u32[]{:S(2)}, u32[]{:S(2)}) collective-permute-start(f32[2,32,256]{2,1,0:T(8,128)S(1)} %step_kernel.5.refs_2_), channel_id=1, source_target_pairs={{0,1},{1,2},{2,3},{3,7},{7,6},{6,5},{5,4},{8,9},{9,10},{10,11},{11... | collective-permute-start | bytes 196616 | tf_op jit(solution)/shard_map/ppermute | solution.py:405
  274.9 1.3 collective-permute-done.15.refs_2_.refs_1_
  276.9 7.2 %all-to-all-start.12 = ((f32[16,16,128]{2,1,0:T(8,128)}), f32[16,16,128]{2,1,0:T(8,128)S(1)}, u32[]{:S(2)}, u32[]{:S(2)}) async-start(f32[16,16,128]{2,1,0:T(8,128)} %get-tuple-element.104.refs_5_), calls=%async_computation.12 | async-start | bytes 262144 | tf_op jit(solution)/shard_map/all_to_all | solution.py:416
  284.4 7.3 %collective-permute-start.17 = (f32[2,64,256]{2,1,0:T(8,128)S(1)}, f32[2,64,256]{2,1,0:T(8,128)S(1)}, u32[]{:S(2)}, u32[]{:S(2)}) collective-permute-start(f32[2,64,256]{2,1,0:T(8,128)S(1)} %get-tuple-element.107), channel_id=1, source_target_pairs={{0,8},{8,16},{16,24},{24,32},{32,40},{40,48},{48,56},{56,64},{64,7... | collective-permute-start | bytes 393224 | tf_op jit(solution)/shard_map/ppermute | solution.py:395
  291.7 3.2 collective-permute-done.17.refs_2_
  295.0 1.1 all-to-all-done.12
  296.2 16.7 %all_to_all.76.refs_0_ = f32[8,320,128]{2,1,0:T(8,128)S(1)} all-to-all(f32[8,320,128]{2,1,0:T(8,128)S(1)} %tail_kernel.1), channel_id=1, replica_groups=mesh['xlo'=2,'z'=16,'core'=2,'xhi'=2,'y'=4] {'xhi','y'}, dimensions={0} | all-to-all | bytes 2621440 | tf_op jit(solution)/shard_map/all_to_all | solution.py:416
  312.9 13.0 %all-gather = f32[32,32,128]{2,1,0:T(8,128)S(1)} all-gather(f32[8,32,128]{2,1,0:T(8,128)S(1)} %slice.19), channel_id=2, replica_groups=mesh['xlo'=2,'z'=16,'core'=2,'xhi'=2,'y'=4] {'xlo','core'}, dimensions={0}, use_global_device_ids=true | all-gather | bytes 655360 | tf_op jit(solution)/shard_map/all_gather | solution.py:420
  325.9 1.3 last_kernel.1
  (58 shorter events, 8.1 us)
Async XLA Ops:
  0.6 9.6 %copy-start.2 = (f32[2,288,512]{2,1,0:T(8,128)S(1)}, f32[2,288,512]{2,1,0:T(8,128)}, u32[]{:S(2)}) copy-start(f32[2,288,512]{2,1,0:T(8,128)} %whole.1) | copy-start | bytes 3538948
  0.6 1.1 copy-start.3
  2.6 12.7 %copy-start.4 = (s32[1,3]{1,0:T(1,128)S(1)}, s32[1,3]{1,0:T(1,128)}, u32[]{:S(2)}) copy-start(s32[1,3]{1,0:T(1,128)} %param.14) | copy-start | bytes 40
  2.6 12.7 %copy-start.5 = (s32[1,3]{1,0:T(1,128)S(1)}, s32[1,3]{1,0:T(1,128)}, u32[]{:S(2)}) copy-start(s32[1,3]{1,0:T(1,128)} %param.12) | copy-start | bytes 40
  2.6 12.7 %copy-start.6 = (s32[1,3]{1,0:T(1,128)S(1)}, s32[1,3]{1,0:T(1,128)}, u32[]{:S(2)}) copy-start(s32[1,3]{1,0:T(1,128)} %param.11) | copy-start | bytes 40
  2.6 14.0 %copy-start.1 = (bf16[1,3,256,256]{3,2,1,0:T(8,128)(2,1)S(1)}, bf16[1,3,256,256]{3,2,1,0:T(8,128)(2,1)}, u32[]{:S(2)}) copy-start(bf16[1,3,256,256]{3,2,1,0:T(8,128)(2,1)} %refs_1_.5) | copy-start | bytes 1179652
  2.6 16.5 %all-to-all-start = ((f32[8,2,32,256]{3,2,1,0:T(8,128)}), f32[8,2,32,256]{3,2,1,0:T(8,128)S(1)}, u32[]{:S(2)}, u32[]{:S(2)}) async-start(f32[8,2,32,256]{3,2,1,0:T(8,128)} %split_kernel.1._), calls=%async_computation | async-start | bytes 1048576 | tf_op jit(solution)/shard_map/all_to_all | solution.py:416
  10.2 8.8 %copy-start = (bf16[3,2,256,256]{3,2,1,0:T(8,128)(2,1)S(1)}, bf16[3,2,256,256]{3,2,1,0:T(8,128)(2,1)}, u32[]{:S(2)}) copy-start(bf16[3,2,256,256]{3,2,1,0:T(8,128)(2,1)} %constant.35.clone.refs_4_.refs_3_.refs_2_) | copy-start | bytes 2359300
  10.3 7.5 %collective-permute-start = (f32[2,64,256]{2,1,0:T(8,128)S(1)}, f32[2,64,256]{2,1,0:T(8,128)S(1)}, u32[]{:S(2)}, u32[]{:S(2)}) collective-permute-start(f32[2,64,256]{2,1,0:T(8,128)S(1)} %get-tuple-element.57), channel_id=1, source_target_pairs={{8,0},{16,8},{24,16},{32,24},{40,32},{48,40},{56,48},{64,56},{72,6... | collective-permute-start | bytes 393224 | tf_op jit(solution)/shard_map/ppermute | solution.py:395
  49.6 6.5 %collective-permute-start.1 = (f32[17,16,256]{2,1,0:T(8,128)S(1)}, f32[17,16,256]{2,1,0:T(8,128)S(1)}, u32[]{:S(2)}, u32[]{:S(2)}) collective-permute-start(f32[17,16,256]{2,1,0:T(8,128)S(1)} %get-tuple-element.63), channel_id=1, source_target_pairs={{0,8},{8,0},{1,9},{9,1},{2,10},{10,2},{3,11},{11,3},{4,12},{12,4},... | collective-permute-start | bytes 835592 | tf_op jit(solution)/shard_map/ppermute | solution.py:399
  56.1 10.5 %collective-permute-start.2 = (f32[17,8,256]{2,1,0:T(8,128)S(1)}, f32[17,8,256]{2,1,0:T(8,128)S(1)}, u32[]{:S(2)}, u32[]{:S(2)}) collective-permute-start(f32[17,8,256]{2,1,0:T(8,128)S(1)} %get-tuple-element.65), channel_id=1, source_target_pairs={{0,256},{256,0},{1,257},{257,1},{2,258},{258,2},{3,259},{259,3},{4... | collective-permute-start | bytes 417800 | tf_op jit(solution)/shard_map/ppermute | solution.py:399
  67.2 23.6 %all-to-all-start.3 = ((f32[16,1,2176]{2,1,0:T(1,128)}), f32[16,1,2176]{2,1,0:T(1,128)S(1)}, u32[]{:S(2)}, u32[]{:S(2)}) async-start(f32[16,1,2176]{2,1,0:T(1,128)} %bitcast.8), calls=%async_computation.3 | async-start | bytes 278528 | tf_op jit(solution)/shard_map/all_to_all | solution.py:411
  84.3 5.3 %collective-permute-start.4 = (f32[2,32,256]{2,1,0:T(8,128)S(1)}, f32[2,32,256]{2,1,0:T(8,128)S(1)}, u32[]{:S(2)}, u32[]{:S(2)}) collective-permute-start(f32[2,32,256]{2,1,0:T(8,128)S(1)} %step_kernel.3.refs_2_), channel_id=1, source_target_pairs={{1,0},{2,1},{3,2},{7,3},{6,7},{5,6},{4,5},{9,8},{10,9},{11,10},{15... | collective-permute-start | bytes 196616 | tf_op jit(solution)/shard_map/ppermute | solution.py:405
  85.5 5.3 %collective-permute-start.3 = (f32[2,32,256]{2,1,0:T(8,128)S(1)}, f32[2,32,256]{2,1,0:T(8,128)S(1)}, u32[]{:S(2)}, u32[]{:S(2)}) collective-permute-start(f32[2,32,256]{2,1,0:T(8,128)S(1)} %step_kernel.3.refs_2_), channel_id=1, source_target_pairs={{0,1},{1,2},{2,3},{3,7},{7,6},{6,5},{5,4},{8,9},{9,10},{10,11},{11... | collective-permute-start | bytes 196616 | tf_op jit(solution)/shard_map/ppermute | solution.py:405
  91.5 21.8 %all-to-all-start.4 = ((f32[16,16,128]{2,1,0:T(8,128)}), f32[16,16,128]{2,1,0:T(8,128)S(1)}, u32[]{:S(2)}, u32[]{:S(2)}) async-start(f32[16,16,128]{2,1,0:T(8,128)} %get-tuple-element.69.refs_5_), calls=%async_computation.4 | async-start | bytes 262144 | tf_op jit(solution)/shard_map/all_to_all | solution.py:416
  99.0 10.5 %collective-permute-start.5 = (f32[2,64,256]{2,1,0:T(8,128)S(1)}, f32[2,64,256]{2,1,0:T(8,128)S(1)}, u32[]{:S(2)}, u32[]{:S(2)}) collective-permute-start(f32[2,64,256]{2,1,0:T(8,128)S(1)} %get-tuple-element.72), channel_id=1, source_target_pairs={{0,8},{8,16},{16,24},{24,32},{32,40},{40,48},{48,56},{56,64},{64,7... | collective-permute-start | bytes 393224 | tf_op jit(solution)/shard_map/ppermute | solution.py:395
  106.3 6.8 %collective-permute-start.6 = (f32[2,64,256]{2,1,0:T(8,128)S(1)}, f32[2,64,256]{2,1,0:T(8,128)S(1)}, u32[]{:S(2)}, u32[]{:S(2)}) collective-permute-start(f32[2,64,256]{2,1,0:T(8,128)S(1)} %get-tuple-element.73), channel_id=1, source_target_pairs={{8,0},{16,8},{24,16},{32,24},{40,32},{48,40},{56,48},{64,56},{72,6... | collective-permute-start | bytes 393224 | tf_op jit(solution)/shard_map/ppermute | solution.py:395
  152.1 5.5 %collective-permute-start.7 = (f32[17,16,256]{2,1,0:T(8,128)S(1)}, f32[17,16,256]{2,1,0:T(8,128)S(1)}, u32[]{:S(2)}, u32[]{:S(2)}) collective-permute-start(f32[17,16,256]{2,1,0:T(8,128)S(1)} %get-tuple-element.80), channel_id=1, source_target_pairs={{0,8},{8,0},{1,9},{9,1},{2,10},{10,2},{3,11},{11,3},{4,12},{12,4},... | collective-permute-start | bytes 835592 | tf_op jit(solution)/shard_map/ppermute | solution.py:399
  157.7 6.8 %collective-permute-start.8 = (f32[17,8,256]{2,1,0:T(8,128)S(1)}, f32[17,8,256]{2,1,0:T(8,128)S(1)}, u32[]{:S(2)}, u32[]{:S(2)}) collective-permute-start(f32[17,8,256]{2,1,0:T(8,128)S(1)} %get-tuple-element.82), channel_id=1, source_target_pairs={{0,256},{256,0},{1,257},{257,1},{2,258},{258,2},{3,259},{259,3},{4... | collective-permute-start | bytes 417800 | tf_op jit(solution)/shard_map/ppermute | solution.py:399
  165.2 18.1 %all-to-all-start.7 = ((f32[16,1,2176]{2,1,0:T(1,128)}), f32[16,1,2176]{2,1,0:T(1,128)S(1)}, u32[]{:S(2)}, u32[]{:S(2)}) async-start(f32[16,1,2176]{2,1,0:T(1,128)} %bitcast.12), calls=%async_computation.7 | async-start | bytes 278528 | tf_op jit(solution)/shard_map/all_to_all | solution.py:411
  176.6 5.3 %collective-permute-start.10 = (f32[2,32,256]{2,1,0:T(8,128)S(1)}, f32[2,32,256]{2,1,0:T(8,128)S(1)}, u32[]{:S(2)}, u32[]{:S(2)}) collective-permute-start(f32[2,32,256]{2,1,0:T(8,128)S(1)} %step_kernel.4.refs_2_), channel_id=1, source_target_pairs={{1,0},{2,1},{3,2},{7,3},{6,7},{5,6},{4,5},{9,8},{10,9},{11,10},{15... | collective-permute-start | bytes 196616 | tf_op jit(solution)/shard_map/ppermute | solution.py:405
  177.9 5.3 %collective-permute-start.9 = (f32[2,32,256]{2,1,0:T(8,128)S(1)}, f32[2,32,256]{2,1,0:T(8,128)S(1)}, u32[]{:S(2)}, u32[]{:S(2)}) collective-permute-start(f32[2,32,256]{2,1,0:T(8,128)S(1)} %step_kernel.4.refs_2_), channel_id=1, source_target_pairs={{0,1},{1,2},{2,3},{3,7},{7,6},{6,5},{5,4},{8,9},{9,10},{10,11},{11... | collective-permute-start | bytes 196616 | tf_op jit(solution)/shard_map/ppermute | solution.py:405
  183.9 21.8 %all-to-all-start.8 = ((f32[16,16,128]{2,1,0:T(8,128)}), f32[16,16,128]{2,1,0:T(8,128)S(1)}, u32[]{:S(2)}, u32[]{:S(2)}) async-start(f32[16,16,128]{2,1,0:T(8,128)} %get-tuple-element.87.refs_5_), calls=%async_computation.8 | async-start | bytes 262144 | tf_op jit(solution)/shard_map/all_to_all | solution.py:416
  191.4 10.5 %collective-permute-start.11 = (f32[2,64,256]{2,1,0:T(8,128)S(1)}, f32[2,64,256]{2,1,0:T(8,128)S(1)}, u32[]{:S(2)}, u32[]{:S(2)}) collective-permute-start(f32[2,64,256]{2,1,0:T(8,128)S(1)} %get-tuple-element.90), channel_id=1, source_target_pairs={{0,8},{8,16},{16,24},{24,32},{32,40},{40,48},{48,56},{56,64},{64,7... | collective-permute-start | bytes 393224 | tf_op jit(solution)/shard_map/ppermute | solution.py:395
  198.7 6.8 %collective-permute-start.12 = (f32[2,64,256]{2,1,0:T(8,128)S(1)}, f32[2,64,256]{2,1,0:T(8,128)S(1)}, u32[]{:S(2)}, u32[]{:S(2)}) collective-permute-start(f32[2,64,256]{2,1,0:T(8,128)S(1)} %get-tuple-element.91), channel_id=1, source_target_pairs={{8,0},{16,8},{24,16},{32,24},{40,32},{48,40},{56,48},{64,56},{72,6... | collective-permute-start | bytes 393224 | tf_op jit(solution)/shard_map/ppermute | solution.py:395
  245.1 5.5 %collective-permute-start.13 = (f32[17,16,256]{2,1,0:T(8,128)S(1)}, f32[17,16,256]{2,1,0:T(8,128)S(1)}, u32[]{:S(2)}, u32[]{:S(2)}) collective-permute-start(f32[17,16,256]{2,1,0:T(8,128)S(1)} %get-tuple-element.98), channel_id=1, source_target_pairs={{0,8},{8,0},{1,9},{9,1},{2,10},{10,2},{3,11},{11,3},{4,12},{12,4},... | collective-permute-start | bytes 835592 | tf_op jit(solution)/shard_map/ppermute | solution.py:399
  250.7 6.8 %collective-permute-start.14 = (f32[17,8,256]{2,1,0:T(8,128)S(1)}, f32[17,8,256]{2,1,0:T(8,128)S(1)}, u32[]{:S(2)}, u32[]{:S(2)}) collective-permute-start(f32[17,8,256]{2,1,0:T(8,128)S(1)} %get-tuple-element.100), channel_id=1, source_target_pairs={{0,256},{256,0},{1,257},{257,1},{2,258},{258,2},{3,259},{259,3},{4... | collective-permute-start | bytes 417800 | tf_op jit(solution)/shard_map/ppermute | solution.py:399
  258.2 18.1 %all-to-all-start.11 = ((f32[16,1,2176]{2,1,0:T(1,128)}), f32[16,1,2176]{2,1,0:T(1,128)S(1)}, u32[]{:S(2)}, u32[]{:S(2)}) async-start(f32[16,1,2176]{2,1,0:T(1,128)} %bitcast.16), calls=%async_computation.11 | async-start | bytes 278528 | tf_op jit(solution)/shard_map/all_to_all | solution.py:411
  269.6 5.3 %collective-permute-start.16 = (f32[2,32,256]{2,1,0:T(8,128)S(1)}, f32[2,32,256]{2,1,0:T(8,128)S(1)}, u32[]{:S(2)}, u32[]{:S(2)}) collective-permute-start(f32[2,32,256]{2,1,0:T(8,128)S(1)} %step_kernel.5.refs_2_), channel_id=1, source_target_pairs={{1,0},{2,1},{3,2},{7,3},{6,7},{5,6},{4,5},{9,8},{10,9},{11,10},{15... | collective-permute-start | bytes 196616 | tf_op jit(solution)/shard_map/ppermute | solution.py:405
  270.9 5.3 %collective-permute-start.15 = (f32[2,32,256]{2,1,0:T(8,128)S(1)}, f32[2,32,256]{2,1,0:T(8,128)S(1)}, u32[]{:S(2)}, u32[]{:S(2)}) collective-permute-start(f32[2,32,256]{2,1,0:T(8,128)S(1)} %step_kernel.5.refs_2_), channel_id=1, source_target_pairs={{0,1},{1,2},{2,3},{3,7},{7,6},{6,5},{5,4},{8,9},{9,10},{10,11},{11... | collective-permute-start | bytes 196616 | tf_op jit(solution)/shard_map/ppermute | solution.py:405
  276.9 19.2 %all-to-all-start.12 = ((f32[16,16,128]{2,1,0:T(8,128)}), f32[16,16,128]{2,1,0:T(8,128)S(1)}, u32[]{:S(2)}, u32[]{:S(2)}) async-start(f32[16,16,128]{2,1,0:T(8,128)} %get-tuple-element.104.refs_5_), calls=%async_computation.12 | async-start | bytes 262144 | tf_op jit(solution)/shard_map/all_to_all | solution.py:416
  284.4 10.5 %collective-permute-start.17 = (f32[2,64,256]{2,1,0:T(8,128)S(1)}, f32[2,64,256]{2,1,0:T(8,128)S(1)}, u32[]{:S(2)}, u32[]{:S(2)}) collective-permute-start(f32[2,64,256]{2,1,0:T(8,128)S(1)} %get-tuple-element.107), channel_id=1, source_target_pairs={{0,8},{8,16},{16,24},{24,32},{32,40},{40,48},{48,56},{56,64},{64,7... | collective-permute-start | bytes 393224 | tf_op jit(solution)/shard_map/ppermute | solution.py:395

commit v15 on v14

--- a/solution.py
+++ b/solution.py
@@ -525,7 +525,7 @@
             sums,
             shard,
             scalars=False,
-            after=(above, below),
+            after=(below,) if final else (above, below),
         )
         piece = exchange(shards, "z")
         part_band, to_right, *to_left = call(

time: 329 us -> 334 us (1.015)
    all_to_all x7, blocking collectives: 97.8 us -> 106 us  [exchange(): return lax.all_to_all(value, axes, 0, 0, tiled=True)]
    all_gather x3, blocking collectives: 31 us -> 26 us  [gather_pieces(): gathered = lax.all_gather(piece, ('xlo', 'core'))]
    ppermute x6, waiting for transfers between devices: 3.92 us -> 7.93 us  [beside_slab(): return lax.ppermute(value, MODE_AXES, pairs)]
  transfers between devices with their start and end apart: 25 -> 25, of which waited for: 17 -> 18; matrix products, arithmetic and copies ran while one was open for 0% -> 0% of each run, Pallas kernels for 1% -> 1%
where the time goes in v15:
time: 334 us; the launch traced here: 332 us
  starting transfers between devices  140 us (42%)
  blocking collectives  132 us (40%)
  waiting for transfers between devices  37.4 us (11%)
  Pallas kernels  18.9 us (6%)
    all_to_all x7, blocking collectives, exchange(): return lax.all_to_all(value, axes, 0, 0, tiled=True)  106 us
    all_to_all x3, starting transfers between devices, exchange_rings(): lax.all_to_all(value, 'z', 0, 0, tiled=True, axis_index_groups=groups)  40 us
    ppermute x6, starting transfers between devices, shift(): lax.ppermute(value, axes, [(i, i + steps) for i in range(first, last)])  31.4 us
    all_to_all x4, starting transfers between devices, exchange(): return lax.all_to_all(value, axes, 0, 0, tiled=True)  29.5 us
    all_gather x3, blocking collectives, gather_pieces(): gathered = lax.all_gather(piece, ('xlo', 'core'))  26 us
    ppermute x6, starting transfers between devices, other(): return lax.ppermute(value, axis, [(0, 1), (1, 0)])  25.8 us
    pallas_call x33, Pallas kernels, call(): pl.pallas_call(body, out_shape=[jax.ShapeDtypeStruct(shape, F32) for shap...  18.9 us
    ppermute x6, waiting for transfers between devices, other(): return lax.ppermute(value, axis, [(0, 1), (1, 0)])  14.5 us
  transfers between devices with their start and end apart: 25, of which 18 were waited for; matrix products, arithmetic and copies ran while one was open for 0% of the time, Pallas kernels for 1%

profile of v15, /device:TPU:1, one launch (start us, length us, event | category | flops | bytes accessed | tf_op | source)
XLA Modules:
  0.0 332.2 jit_solution(1517521573181696162)
XLA Ops:
  0.6 1.1 copy-done.3
  1.8 0.8 split_kernel.1._
  2.6 7.6 %all-to-all-start = ((f32[8,2,32,256]{3,2,1,0:T(8,128)}), f32[8,2,32,256]{3,2,1,0:T(8,128)S(1)}, u32[]{:S(2)}, u32[]{:S(2)}) async-start(f32[8,2,32,256]{3,2,1,0:T(8,128)} %split_kernel.1._), calls=%async_computation | async-start | bytes 1048576 | tf_op jit(solution)/shard_map/all_to_all | solution.py:416
  10.3 4.9 %collective-permute-start = (f32[2,64,256]{2,1,0:T(8,128)S(1)}, f32[2,64,256]{2,1,0:T(8,128)S(1)}, u32[]{:S(2)}, u32[]{:S(2)}) collective-permute-start(f32[2,64,256]{2,1,0:T(8,128)S(1)} %get-tuple-element.57), channel_id=1, source_target_pairs={{8,0},{16,8},{24,16},{32,24},{40,32},{48,40},{56,48},{64,56},{72,6... | collective-permute-start | bytes 393224 | tf_op jit(solution)/shard_map/ppermute | solution.py:395
  17.0 0.8 collective-permute-done.refs_2_
  17.8 1.3 all-to-all-done.refs_3_.refs_1_
  19.1 1.0 first_kernel.1
  20.1 15.1 %all_to_all.70.refs_0_ = f32[8,2,32,256]{3,2,1,0:T(8,128)S(1)} all-to-all(f32[8,2,32,256]{3,2,1,0:T(8,128)S(1)} %get-tuple-element.59), channel_id=1, replica_groups=mesh['xlo'=2,'z'=16,'core'=2,'xhi'=2,'y'=4] {'xhi','y'}, dimensions={0} | all-to-all | bytes 1048576 | tf_op jit(solution)/shard_map/all_to_all | solution.py:416
  35.2 1.4 ratio_kernel.3
  36.5 12.3 %all_to_all.71.refs_0_ = f32[8,2,32,256]{3,2,1,0:T(8,128)S(1)} all-to-all(f32[8,2,32,256]{3,2,1,0:T(8,128)S(1)} %ratio_kernel.3), channel_id=1, replica_groups=mesh['xlo'=2,'z'=16,'core'=2,'xhi'=2,'y'=4] {'xhi','y'}, dimensions={0} | all-to-all | bytes 1048576 | tf_op jit(solution)/shard_map/all_to_all | solution.py:416
  48.8 0.7 backward_kernel.3
  49.6 5.3 %collective-permute-start.1 = (f32[17,16,256]{2,1,0:T(8,128)S(1)}, f32[17,16,256]{2,1,0:T(8,128)S(1)}, u32[]{:S(2)}, u32[]{:S(2)}) collective-permute-start(f32[17,16,256]{2,1,0:T(8,128)S(1)} %get-tuple-element.63), channel_id=1, source_target_pairs={{0,8},{8,0},{1,9},{9,1},{2,10},{10,2},{3,11},{11,3},{4,12},{12,4},... | collective-permute-start | bytes 835592 | tf_op jit(solution)/shard_map/ppermute | solution.py:399
  54.9 1.2 collective-permute-done.1.refs_1_
  56.1 6.7 %collective-permute-start.2 = (f32[17,8,256]{2,1,0:T(8,128)S(1)}, f32[17,8,256]{2,1,0:T(8,128)S(1)}, u32[]{:S(2)}, u32[]{:S(2)}) collective-permute-start(f32[17,8,256]{2,1,0:T(8,128)S(1)} %get-tuple-element.65), channel_id=1, source_target_pairs={{0,256},{256,0},{1,257},{257,1},{2,258},{258,2},{3,259},{259,3},{4... | collective-permute-start | bytes 417800 | tf_op jit(solution)/shard_map/ppermute | solution.py:399
  63.4 3.2 collective-permute-done.2.refs_1_
  67.2 17.0 %all-to-all-start.3 = ((f32[16,1,2176]{2,1,0:T(1,128)}), f32[16,1,2176]{2,1,0:T(1,128)S(1)}, u32[]{:S(2)}, u32[]{:S(2)}) async-start(f32[16,1,2176]{2,1,0:T(1,128)} %bitcast.8), calls=%async_computation.3 | async-start | bytes 278528 | tf_op jit(solution)/shard_map/all_to_all | solution.py:411
  84.3 1.3 collective-permute-start.4
  85.5 4.0 %collective-permute-start.3 = (f32[2,32,256]{2,1,0:T(8,128)S(1)}, f32[2,32,256]{2,1,0:T(8,128)S(1)}, u32[]{:S(2)}, u32[]{:S(2)}) collective-permute-start(f32[2,32,256]{2,1,0:T(8,128)S(1)} %step_kernel.3.refs_2_), channel_id=1, source_target_pairs={{0,1},{1,2},{2,3},{3,7},{7,6},{6,5},{5,4},{8,9},{9,10},{10,11},{11... | collective-permute-start | bytes 196616 | tf_op jit(solution)/shard_map/ppermute | solution.py:405
  89.5 1.3 collective-permute-done.3.refs_2_.refs_1_
  91.5 7.2 %all-to-all-start.4 = ((f32[16,16,128]{2,1,0:T(8,128)}), f32[16,16,128]{2,1,0:T(8,128)S(1)}, u32[]{:S(2)}, u32[]{:S(2)}) async-start(f32[16,16,128]{2,1,0:T(8,128)} %get-tuple-element.69.refs_5_), calls=%async_computation.4 | async-start | bytes 262144 | tf_op jit(solution)/shard_map/all_to_all | solution.py:416
  99.0 7.3 %collective-permute-start.5 = (f32[2,64,256]{2,1,0:T(8,128)S(1)}, f32[2,64,256]{2,1,0:T(8,128)S(1)}, u32[]{:S(2)}, u32[]{:S(2)}) collective-permute-start(f32[2,64,256]{2,1,0:T(8,128)S(1)} %get-tuple-element.72), channel_id=1, source_target_pairs={{0,8},{8,16},{16,24},{24,32},{32,40},{40,48},{48,56},{56,64},{64,7... | collective-permute-start | bytes 393224 | tf_op jit(solution)/shard_map/ppermute | solution.py:395
  106.3 1.9 collective-permute-start.6
  108.2 1.3 collective-permute-done.5.refs_2_
  109.5 3.6 %collective-permute-done.6.refs_3_ = f32[2,64,256]{2,1,0:T(8,128)S(1)} collective-permute-done((f32[2,64,256]{2,1,0:T(8,128)S(1)}, f32[2,64,256]{2,1,0:T(8,128)S(1)}, u32[]{:S(2)}, u32[]{:S(2)}) %collective-permute-start.6) | collective-permute-done | bytes 131104 | tf_op jit(solution)/shard_map/ppermute | solution.py:395
  113.4 8.8 %all_gather.12 = f32[4,256,128]{2,1,0:T(8,128)S(1)} all-gather(f32[1,256,128]{2,1,0:T(8,128)S(1)} %bitcast.28), channel_id=1, replica_groups=mesh['xlo'=2,'z'=16,'core'=2,'xhi'=2,'y'=4] {'xlo','core'}, dimensions={0}, use_global_device_ids=true | all-gather | bytes 655360 | tf_op jit(solution)/shard_map/all_gather | solution.py:420
  122.2 1.0 next_kernel.2
  123.2 12.9 %all_to_all.72.refs_0_ = f32[8,2,32,256]{3,2,1,0:T(8,128)S(1)} all-to-all(f32[8,2,32,256]{3,2,1,0:T(8,128)S(1)} %get-tuple-element.77), channel_id=1, replica_groups=mesh['xlo'=2,'z'=16,'core'=2,'xhi'=2,'y'=4] {'xhi','y'}, dimensions={0} | all-to-all | bytes 1048576 | tf_op jit(solution)/shard_map/all_to_all | solution.py:416
  136.2 1.4 ratio_kernel.4
  137.6 13.8 %all_to_all.73.refs_0_ = f32[8,2,32,256]{3,2,1,0:T(8,128)S(1)} all-to-all(f32[8,2,32,256]{3,2,1,0:T(8,128)S(1)} %ratio_kernel.4), channel_id=1, replica_groups=mesh['xlo'=2,'z'=16,'core'=2,'xhi'=2,'y'=4] {'xhi','y'}, dimensions={0} | all-to-all | bytes 1048576 | tf_op jit(solution)/shard_map/all_to_all | solution.py:416
  151.4 0.7 backward_kernel.4
  152.1 4.4 %collective-permute-start.7 = (f32[17,16,256]{2,1,0:T(8,128)S(1)}, f32[17,16,256]{2,1,0:T(8,128)S(1)}, u32[]{:S(2)}, u32[]{:S(2)}) collective-permute-start(f32[17,16,256]{2,1,0:T(8,128)S(1)} %get-tuple-element.80), channel_id=1, source_target_pairs={{0,8},{8,0},{1,9},{9,1},{2,10},{10,2},{3,11},{11,3},{4,12},{12,4},... | collective-permute-start | bytes 835592 | tf_op jit(solution)/shard_map/ppermute | solution.py:399
  156.5 1.2 collective-permute-done.7.refs_1_
  157.7 2.8 collective-permute-start.8
  161.1 3.4 %collective-permute-done.8.refs_1_ = f32[17,8,256]{2,1,0:T(8,128)S(1)} collective-permute-done((f32[17,8,256]{2,1,0:T(8,128)S(1)}, f32[17,8,256]{2,1,0:T(8,128)S(1)}, u32[]{:S(2)}, u32[]{:S(2)}) %collective-permute-start.8) | collective-permute-done | bytes 139296 | tf_op jit(solution)/shard_map/ppermute | solution.py:399
  165.2 11.5 %all-to-all-start.7 = ((f32[16,1,2176]{2,1,0:T(1,128)}), f32[16,1,2176]{2,1,0:T(1,128)S(1)}, u32[]{:S(2)}, u32[]{:S(2)}) async-start(f32[16,1,2176]{2,1,0:T(1,128)} %bitcast.12), calls=%async_computation.7 | async-start | bytes 278528 | tf_op jit(solution)/shard_map/all_to_all | solution.py:411
  176.6 1.3 collective-permute-start.10
  177.9 4.0 %collective-permute-start.9 = (f32[2,32,256]{2,1,0:T(8,128)S(1)}, f32[2,32,256]{2,1,0:T(8,128)S(1)}, u32[]{:S(2)}, u32[]{:S(2)}) collective-permute-start(f32[2,32,256]{2,1,0:T(8,128)S(1)} %step_kernel.4.refs_2_), channel_id=1, source_target_pairs={{0,1},{1,2},{2,3},{3,7},{7,6},{6,5},{5,4},{8,9},{9,10},{10,11},{11... | collective-permute-start | bytes 196616 | tf_op jit(solution)/shard_map/ppermute | solution.py:405
  181.9 1.3 collective-permute-done.9.refs_2_.refs_1_
  183.9 7.2 %all-to-all-start.8 = ((f32[16,16,128]{2,1,0:T(8,128)}), f32[16,16,128]{2,1,0:T(8,128)S(1)}, u32[]{:S(2)}, u32[]{:S(2)}) async-start(f32[16,16,128]{2,1,0:T(8,128)} %get-tuple-element.87.refs_5_), calls=%async_computation.8 | async-start | bytes 262144 | tf_op jit(solution)/shard_map/all_to_all | solution.py:416
  191.4 7.3 %collective-permute-start.11 = (f32[2,64,256]{2,1,0:T(8,128)S(1)}, f32[2,64,256]{2,1,0:T(8,128)S(1)}, u32[]{:S(2)}, u32[]{:S(2)}) collective-permute-start(f32[2,64,256]{2,1,0:T(8,128)S(1)} %get-tuple-element.90), channel_id=1, source_target_pairs={{0,8},{8,16},{16,24},{24,32},{32,40},{40,48},{48,56},{56,64},{64,7... | collective-permute-start | bytes 393224 | tf_op jit(solution)/shard_map/ppermute | solution.py:395
  198.7 1.9 collective-permute-start.12
  200.6 1.3 collective-permute-done.11.refs_2_
  201.9 3.6 %collective-permute-done.12.refs_3_ = f32[2,64,256]{2,1,0:T(8,128)S(1)} collective-permute-done((f32[2,64,256]{2,1,0:T(8,128)S(1)}, f32[2,64,256]{2,1,0:T(8,128)S(1)}, u32[]{:S(2)}, u32[]{:S(2)}) %collective-permute-start.12) | collective-permute-done | bytes 131104 | tf_op jit(solution)/shard_map/ppermute | solution.py:395
  205.8 9.2 %all_gather.13 = f32[4,256,128]{2,1,0:T(8,128)S(1)} all-gather(f32[1,256,128]{2,1,0:T(8,128)S(1)} %bitcast.29), channel_id=1, replica_groups=mesh['xlo'=2,'z'=16,'core'=2,'xhi'=2,'y'=4] {'xlo','core'}, dimensions={0}, use_global_device_ids=true | all-gather | bytes 655360 | tf_op jit(solution)/shard_map/all_gather | solution.py:420
  215.0 1.0 next_kernel.3
  216.0 13.0 %all_to_all.74.refs_0_ = f32[8,2,32,256]{3,2,1,0:T(8,128)S(1)} all-to-all(f32[8,2,32,256]{3,2,1,0:T(8,128)S(1)} %get-tuple-element.95), channel_id=1, replica_groups=mesh['xlo'=2,'z'=16,'core'=2,'xhi'=2,'y'=4] {'xhi','y'}, dimensions={0} | all-to-all | bytes 1048576 | tf_op jit(solution)/shard_map/all_to_all | solution.py:416
  229.0 1.4 ratio_kernel.5
  230.4 14.0 %all_to_all.75.refs_0_ = f32[8,2,32,256]{3,2,1,0:T(8,128)S(1)} all-to-all(f32[8,2,32,256]{3,2,1,0:T(8,128)S(1)} %ratio_kernel.5), channel_id=1, replica_groups=mesh['xlo'=2,'z'=16,'core'=2,'xhi'=2,'y'=4] {'xhi','y'}, dimensions={0} | all-to-all | bytes 1048576 | tf_op jit(solution)/shard_map/all_to_all | solution.py:416
  245.1 4.4 %collective-permute-start.13 = (f32[17,16,256]{2,1,0:T(8,128)S(1)}, f32[17,16,256]{2,1,0:T(8,128)S(1)}, u32[]{:S(2)}, u32[]{:S(2)}) collective-permute-start(f32[17,16,256]{2,1,0:T(8,128)S(1)} %get-tuple-element.98), channel_id=1, source_target_pairs={{0,8},{8,0},{1,9},{9,1},{2,10},{10,2},{3,11},{11,3},{4,12},{12,4},... | collective-permute-start | bytes 835592 | tf_op jit(solution)/shard_map/ppermute | solution.py:399
  249.5 1.2 collective-permute-done.13.refs_1_
  250.7 2.2 collective-permute-start.14
  253.1 4.4 %collective-permute-done.14.refs_1_ = f32[17,8,256]{2,1,0:T(8,128)S(1)} collective-permute-done((f32[17,8,256]{2,1,0:T(8,128)S(1)}, f32[17,8,256]{2,1,0:T(8,128)S(1)}, u32[]{:S(2)}, u32[]{:S(2)}) %collective-permute-start.14) | collective-permute-done | bytes 139296 | tf_op jit(solution)/shard_map/ppermute | solution.py:399
  258.2 11.5 %all-to-all-start.11 = ((f32[16,1,2176]{2,1,0:T(1,128)}), f32[16,1,2176]{2,1,0:T(1,128)S(1)}, u32[]{:S(2)}, u32[]{:S(2)}) async-start(f32[16,1,2176]{2,1,0:T(1,128)} %bitcast.16), calls=%async_computation.11 | async-start | bytes 278528 | tf_op jit(solution)/shard_map/all_to_all | solution.py:411
  269.6 1.3 collective-permute-start.15
  270.9 4.0 %collective-permute-done.15.refs_2_.refs_3_ = f32[2,32,256]{2,1,0:T(8,128)S(1)} collective-permute-done((f32[2,32,256]{2,1,0:T(8,128)S(1)}, f32[2,32,256]{2,1,0:T(8,128)S(1)}, u32[]{:S(2)}, u32[]{:S(2)}) %collective-permute-start.15) | collective-permute-done | bytes 65568 | tf_op jit(solution)/shard_map/ppermute | solution.py:405
  274.9 1.0 all-to-all-done.11
  276.7 7.5 %all-to-all-start.12 = ((f32[16,16,128]{2,1,0:T(8,128)}), f32[16,16,128]{2,1,0:T(8,128)S(1)}, u32[]{:S(2)}, u32[]{:S(2)}) async-start(f32[16,16,128]{2,1,0:T(8,128)} %get-tuple-element.104.refs_5_), calls=%async_computation.12 | async-start | bytes 262144 | tf_op jit(solution)/shard_map/all_to_all | solution.py:416
  284.1 1.8 collective-permute-start.16
  286.0 1.3 collective-permute-done.16.refs_1_
  287.6 8.1 %collective-permute-start.17 = (f32[2,64,256]{2,1,0:T(8,128)S(1)}, f32[2,64,256]{2,1,0:T(8,128)S(1)}, u32[]{:S(2)}, u32[]{:S(2)}) collective-permute-start(f32[2,64,256]{2,1,0:T(8,128)S(1)} %get-tuple-element.107), channel_id=1, source_target_pairs={{0,8},{8,16},{16,24},{24,32},{32,40},{40,48},{48,56},{56,64},{64,7... | collective-permute-start | bytes 393224 | tf_op jit(solution)/shard_map/ppermute | solution.py:395
  295.7 2.1 collective-permute-done.17.refs_2_
  298.0 24.8 %all_to_all.76.refs_0_ = f32[8,320,128]{2,1,0:T(8,128)S(1)} all-to-all(f32[8,320,128]{2,1,0:T(8,128)S(1)} %tail_kernel.1), channel_id=1, replica_groups=mesh['xlo'=2,'z'=16,'core'=2,'xhi'=2,'y'=4] {'xhi','y'}, dimensions={0} | all-to-all | bytes 2621440 | tf_op jit(solution)/shard_map/all_to_all | solution.py:416
  322.9 8.0 %all-gather = f32[32,32,128]{2,1,0:T(8,128)S(1)} all-gather(f32[8,32,128]{2,1,0:T(8,128)S(1)} %slice.19), channel_id=2, replica_groups=mesh['xlo'=2,'z'=16,'core'=2,'xhi'=2,'y'=4] {'xlo','core'}, dimensions={0}, use_global_device_ids=true | all-gather | bytes 655360 | tf_op jit(solution)/shard_map/all_gather | solution.py:420
  330.9 1.3 last_kernel.1
  (58 shorter events, 8.8 us)
Async XLA Ops:
  0.6 9.6 %copy-start.2 = (f32[2,288,512]{2,1,0:T(8,128)S(1)}, f32[2,288,512]{2,1,0:T(8,128)}, u32[]{:S(2)}) copy-start(f32[2,288,512]{2,1,0:T(8,128)} %whole.1) | copy-start | bytes 3538948
  0.6 1.1 copy-start.3
  2.6 12.7 %copy-start.4 = (s32[1,3]{1,0:T(1,128)S(1)}, s32[1,3]{1,0:T(1,128)}, u32[]{:S(2)}) copy-start(s32[1,3]{1,0:T(1,128)} %param.14) | copy-start | bytes 40
  2.6 12.7 %copy-start.5 = (s32[1,3]{1,0:T(1,128)S(1)}, s32[1,3]{1,0:T(1,128)}, u32[]{:S(2)}) copy-start(s32[1,3]{1,0:T(1,128)} %param.12) | copy-start | bytes 40
  2.6 12.7 %copy-start.6 = (s32[1,3]{1,0:T(1,128)S(1)}, s32[1,3]{1,0:T(1,128)}, u32[]{:S(2)}) copy-start(s32[1,3]{1,0:T(1,128)} %param.11) | copy-start | bytes 40
  2.6 14.0 %copy-start.1 = (bf16[1,3,256,256]{3,2,1,0:T(8,128)(2,1)S(1)}, bf16[1,3,256,256]{3,2,1,0:T(8,128)(2,1)}, u32[]{:S(2)}) copy-start(bf16[1,3,256,256]{3,2,1,0:T(8,128)(2,1)} %refs_1_.5) | copy-start | bytes 1179652
  2.6 16.5 %all-to-all-start = ((f32[8,2,32,256]{3,2,1,0:T(8,128)}), f32[8,2,32,256]{3,2,1,0:T(8,128)S(1)}, u32[]{:S(2)}, u32[]{:S(2)}) async-start(f32[8,2,32,256]{3,2,1,0:T(8,128)} %split_kernel.1._), calls=%async_computation | async-start | bytes 1048576 | tf_op jit(solution)/shard_map/all_to_all | solution.py:416
  10.2 8.8 %copy-start = (bf16[3,2,256,256]{3,2,1,0:T(8,128)(2,1)S(1)}, bf16[3,2,256,256]{3,2,1,0:T(8,128)(2,1)}, u32[]{:S(2)}) copy-start(bf16[3,2,256,256]{3,2,1,0:T(8,128)(2,1)} %constant.35.clone.refs_4_.refs_3_.refs_2_) | copy-start | bytes 2359300
  10.3 7.5 %collective-permute-start = (f32[2,64,256]{2,1,0:T(8,128)S(1)}, f32[2,64,256]{2,1,0:T(8,128)S(1)}, u32[]{:S(2)}, u32[]{:S(2)}) collective-permute-start(f32[2,64,256]{2,1,0:T(8,128)S(1)} %get-tuple-element.57), channel_id=1, source_target_pairs={{8,0},{16,8},{24,16},{32,24},{40,32},{48,40},{56,48},{64,56},{72,6... | collective-permute-start | bytes 393224 | tf_op jit(solution)/shard_map/ppermute | solution.py:395
  49.6 6.5 %collective-permute-start.1 = (f32[17,16,256]{2,1,0:T(8,128)S(1)}, f32[17,16,256]{2,1,0:T(8,128)S(1)}, u32[]{:S(2)}, u32[]{:S(2)}) collective-permute-start(f32[17,16,256]{2,1,0:T(8,128)S(1)} %get-tuple-element.63), channel_id=1, source_target_pairs={{0,8},{8,0},{1,9},{9,1},{2,10},{10,2},{3,11},{11,3},{4,12},{12,4},... | collective-permute-start | bytes 835592 | tf_op jit(solution)/shard_map/ppermute | solution.py:399
  56.1 10.5 %collective-permute-start.2 = (f32[17,8,256]{2,1,0:T(8,128)S(1)}, f32[17,8,256]{2,1,0:T(8,128)S(1)}, u32[]{:S(2)}, u32[]{:S(2)}) collective-permute-start(f32[17,8,256]{2,1,0:T(8,128)S(1)} %get-tuple-element.65), channel_id=1, source_target_pairs={{0,256},{256,0},{1,257},{257,1},{2,258},{258,2},{3,259},{259,3},{4... | collective-permute-start | bytes 417800 | tf_op jit(solution)/shard_map/ppermute | solution.py:399
  67.2 23.6 %all-to-all-start.3 = ((f32[16,1,2176]{2,1,0:T(1,128)}), f32[16,1,2176]{2,1,0:T(1,128)S(1)}, u32[]{:S(2)}, u32[]{:S(2)}) async-start(f32[16,1,2176]{2,1,0:T(1,128)} %bitcast.8), calls=%async_computation.3 | async-start | bytes 278528 | tf_op jit(solution)/shard_map/all_to_all | solution.py:411
  84.3 5.3 %collective-permute-start.4 = (f32[2,32,256]{2,1,0:T(8,128)S(1)}, f32[2,32,256]{2,1,0:T(8,128)S(1)}, u32[]{:S(2)}, u32[]{:S(2)}) collective-permute-start(f32[2,32,256]{2,1,0:T(8,128)S(1)} %step_kernel.3.refs_2_), channel_id=1, source_target_pairs={{1,0},{2,1},{3,2},{7,3},{6,7},{5,6},{4,5},{9,8},{10,9},{11,10},{15... | collective-permute-start | bytes 196616 | tf_op jit(solution)/shard_map/ppermute | solution.py:405
  85.5 5.3 %collective-permute-start.3 = (f32[2,32,256]{2,1,0:T(8,128)S(1)}, f32[2,32,256]{2,1,0:T(8,128)S(1)}, u32[]{:S(2)}, u32[]{:S(2)}) collective-permute-start(f32[2,32,256]{2,1,0:T(8,128)S(1)} %step_kernel.3.refs_2_), channel_id=1, source_target_pairs={{0,1},{1,2},{2,3},{3,7},{7,6},{6,5},{5,4},{8,9},{9,10},{10,11},{11... | collective-permute-start | bytes 196616 | tf_op jit(solution)/shard_map/ppermute | solution.py:405
  91.5 21.8 %all-to-all-start.4 = ((f32[16,16,128]{2,1,0:T(8,128)}), f32[16,16,128]{2,1,0:T(8,128)S(1)}, u32[]{:S(2)}, u32[]{:S(2)}) async-start(f32[16,16,128]{2,1,0:T(8,128)} %get-tuple-element.69.refs_5_), calls=%async_computation.4 | async-start | bytes 262144 | tf_op jit(solution)/shard_map/all_to_all | solution.py:416
  99.0 10.5 %collective-permute-start.5 = (f32[2,64,256]{2,1,0:T(8,128)S(1)}, f32[2,64,256]{2,1,0:T(8,128)S(1)}, u32[]{:S(2)}, u32[]{:S(2)}) collective-permute-start(f32[2,64,256]{2,1,0:T(8,128)S(1)} %get-tuple-element.72), channel_id=1, source_target_pairs={{0,8},{8,16},{16,24},{24,32},{32,40},{40,48},{48,56},{56,64},{64,7... | collective-permute-start | bytes 393224 | tf_op jit(solution)/shard_map/ppermute | solution.py:395
  106.3 6.8 %collective-permute-start.6 = (f32[2,64,256]{2,1,0:T(8,128)S(1)}, f32[2,64,256]{2,1,0:T(8,128)S(1)}, u32[]{:S(2)}, u32[]{:S(2)}) collective-permute-start(f32[2,64,256]{2,1,0:T(8,128)S(1)} %get-tuple-element.73), channel_id=1, source_target_pairs={{8,0},{16,8},{24,16},{32,24},{40,32},{48,40},{56,48},{64,56},{72,6... | collective-permute-start | bytes 393224 | tf_op jit(solution)/shard_map/ppermute | solution.py:395
  152.1 5.5 %collective-permute-start.7 = (f32[17,16,256]{2,1,0:T(8,128)S(1)}, f32[17,16,256]{2,1,0:T(8,128)S(1)}, u32[]{:S(2)}, u32[]{:S(2)}) collective-permute-start(f32[17,16,256]{2,1,0:T(8,128)S(1)} %get-tuple-element.80), channel_id=1, source_target_pairs={{0,8},{8,0},{1,9},{9,1},{2,10},{10,2},{3,11},{11,3},{4,12},{12,4},... | collective-permute-start | bytes 835592 | tf_op jit(solution)/shard_map/ppermute | solution.py:399
  157.7 6.8 %collective-permute-start.8 = (f32[17,8,256]{2,1,0:T(8,128)S(1)}, f32[17,8,256]{2,1,0:T(8,128)S(1)}, u32[]{:S(2)}, u32[]{:S(2)}) collective-permute-start(f32[17,8,256]{2,1,0:T(8,128)S(1)} %get-tuple-element.82), channel_id=1, source_target_pairs={{0,256},{256,0},{1,257},{257,1},{2,258},{258,2},{3,259},{259,3},{4... | collective-permute-start | bytes 417800 | tf_op jit(solution)/shard_map/ppermute | solution.py:399
  165.2 18.1 %all-to-all-start.7 = ((f32[16,1,2176]{2,1,0:T(1,128)}), f32[16,1,2176]{2,1,0:T(1,128)S(1)}, u32[]{:S(2)}, u32[]{:S(2)}) async-start(f32[16,1,2176]{2,1,0:T(1,128)} %bitcast.12), calls=%async_computation.7 | async-start | bytes 278528 | tf_op jit(solution)/shard_map/all_to_all | solution.py:411
  176.6 5.3 %collective-permute-start.10 = (f32[2,32,256]{2,1,0:T(8,128)S(1)}, f32[2,32,256]{2,1,0:T(8,128)S(1)}, u32[]{:S(2)}, u32[]{:S(2)}) collective-permute-start(f32[2,32,256]{2,1,0:T(8,128)S(1)} %step_kernel.4.refs_2_), channel_id=1, source_target_pairs={{1,0},{2,1},{3,2},{7,3},{6,7},{5,6},{4,5},{9,8},{10,9},{11,10},{15... | collective-permute-start | bytes 196616 | tf_op jit(solution)/shard_map/ppermute | solution.py:405
  177.9 5.3 %collective-permute-start.9 = (f32[2,32,256]{2,1,0:T(8,128)S(1)}, f32[2,32,256]{2,1,0:T(8,128)S(1)}, u32[]{:S(2)}, u32[]{:S(2)}) collective-permute-start(f32[2,32,256]{2,1,0:T(8,128)S(1)} %step_kernel.4.refs_2_), channel_id=1, source_target_pairs={{0,1},{1,2},{2,3},{3,7},{7,6},{6,5},{5,4},{8,9},{9,10},{10,11},{11... | collective-permute-start | bytes 196616 | tf_op jit(solution)/shard_map/ppermute | solution.py:405
  183.9 21.8 %all-to-all-start.8 = ((f32[16,16,128]{2,1,0:T(8,128)}), f32[16,16,128]{2,1,0:T(8,128)S(1)}, u32[]{:S(2)}, u32[]{:S(2)}) async-start(f32[16,16,128]{2,1,0:T(8,128)} %get-tuple-element.87.refs_5_), calls=%async_computation.8 | async-start | bytes 262144 | tf_op jit(solution)/shard_map/all_to_all | solution.py:416
  191.4 10.5 %collective-permute-start.11 = (f32[2,64,256]{2,1,0:T(8,128)S(1)}, f32[2,64,256]{2,1,0:T(8,128)S(1)}, u32[]{:S(2)}, u32[]{:S(2)}) collective-permute-start(f32[2,64,256]{2,1,0:T(8,128)S(1)} %get-tuple-element.90), channel_id=1, source_target_pairs={{0,8},{8,16},{16,24},{24,32},{32,40},{40,48},{48,56},{56,64},{64,7... | collective-permute-start | bytes 393224 | tf_op jit(solution)/shard_map/ppermute | solution.py:395
  198.7 6.8 %collective-permute-start.12 = (f32[2,64,256]{2,1,0:T(8,128)S(1)}, f32[2,64,256]{2,1,0:T(8,128)S(1)}, u32[]{:S(2)}, u32[]{:S(2)}) collective-permute-start(f32[2,64,256]{2,1,0:T(8,128)S(1)} %get-tuple-element.91), channel_id=1, source_target_pairs={{8,0},{16,8},{24,16},{32,24},{40,32},{48,40},{56,48},{64,56},{72,6... | collective-permute-start | bytes 393224 | tf_op jit(solution)/shard_map/ppermute | solution.py:395
  245.1 5.5 %collective-permute-start.13 = (f32[17,16,256]{2,1,0:T(8,128)S(1)}, f32[17,16,256]{2,1,0:T(8,128)S(1)}, u32[]{:S(2)}, u32[]{:S(2)}) collective-permute-start(f32[17,16,256]{2,1,0:T(8,128)S(1)} %get-tuple-element.98), channel_id=1, source_target_pairs={{0,8},{8,0},{1,9},{9,1},{2,10},{10,2},{3,11},{11,3},{4,12},{12,4},... | collective-permute-start | bytes 835592 | tf_op jit(solution)/shard_map/ppermute | solution.py:399
  250.7 6.8 %collective-permute-start.14 = (f32[17,8,256]{2,1,0:T(8,128)S(1)}, f32[17,8,256]{2,1,0:T(8,128)S(1)}, u32[]{:S(2)}, u32[]{:S(2)}) collective-permute-start(f32[17,8,256]{2,1,0:T(8,128)S(1)} %get-tuple-element.100), channel_id=1, source_target_pairs={{0,256},{256,0},{1,257},{257,1},{2,258},{258,2},{3,259},{259,3},{4... | collective-permute-start | bytes 417800 | tf_op jit(solution)/shard_map/ppermute | solution.py:399
  258.2 17.8 %all-to-all-start.11 = ((f32[16,1,2176]{2,1,0:T(1,128)}), f32[16,1,2176]{2,1,0:T(1,128)S(1)}, u32[]{:S(2)}, u32[]{:S(2)}) async-start(f32[16,1,2176]{2,1,0:T(1,128)} %bitcast.16), calls=%async_computation.11 | async-start | bytes 278528 | tf_op jit(solution)/shard_map/all_to_all | solution.py:411
  269.6 5.3 %collective-permute-start.15 = (f32[2,32,256]{2,1,0:T(8,128)S(1)}, f32[2,32,256]{2,1,0:T(8,128)S(1)}, u32[]{:S(2)}, u32[]{:S(2)}) collective-permute-start(f32[2,32,256]{2,1,0:T(8,128)S(1)} %step_kernel.5.refs_2_), channel_id=1, source_target_pairs={{1,0},{2,1},{3,2},{7,3},{6,7},{5,6},{4,5},{9,8},{10,9},{11,10},{15... | collective-permute-start | bytes 196616 | tf_op jit(solution)/shard_map/ppermute | solution.py:405
  276.7 21.2 %all-to-all-start.12 = ((f32[16,16,128]{2,1,0:T(8,128)}), f32[16,16,128]{2,1,0:T(8,128)S(1)}, u32[]{:S(2)}, u32[]{:S(2)}) async-start(f32[16,16,128]{2,1,0:T(8,128)} %get-tuple-element.104.refs_5_), calls=%async_computation.12 | async-start | bytes 262144 | tf_op jit(solution)/shard_map/all_to_all | solution.py:416
  284.1 3.2 collective-permute-start.16
  287.6 10.2 %collective-permute-start.17 = (f32[2,64,256]{2,1,0:T(8,128)S(1)}, f32[2,64,256]{2,1,0:T(8,128)S(1)}, u32[]{:S(2)}, u32[]{:S(2)}) collective-permute-start(f32[2,64,256]{2,1,0:T(8,128)S(1)} %get-tuple-element.107), channel_id=1, source_target_pairs={{0,8},{8,16},{16,24},{24,32},{32,40},{40,48},{48,56},{56,64},{64,7... | collective-permute-start | bytes 393224 | tf_op jit(solution)/shard_map/ppermute | solution.py:395

commit v16 on v14

--- a/solution.py
+++ b/solution.py
@@ -308,7 +308,7 @@
             for part in range(2):
                 row = (half * 2 + part) * 8
                 rows = pl.ds(RINGS * half + 2 * place + part, 8, stride=2 * RINGS)
-                tail[place, row : row + 8] = piece[rows, :]
+                tail[place, row : row + 8] = pltpu.roll(piece[rows, :], RINGS // 4, 0)
         for part in range(2):
             for block in range(WIDTH // LANES):
                 row = 32 + (part * 4 + block) * OUT_ROWS
@@ -405,10 +405,13 @@
     return lax.ppermute(value, MODE_AXES, pairs)
 
 
+def exchange_far_first(value):
+    groups = [[(ring + RINGS // 2) % RINGS for ring in range(RINGS)]]
+    return lax.all_to_all(value, "z", 0, 0, tiled=True, axis_index_groups=groups)
+
+
 def exchange_rings(value):
-    groups = [[(ring + RINGS // 2) % RINGS for ring in range(RINGS)]]
-    value = value.reshape(RINGS, 1, MESSAGE * LANES)
-    value = lax.all_to_all(value, "z", 0, 0, tiled=True, axis_index_groups=groups)
+    value = exchange_far_first(value.reshape(RINGS, 1, MESSAGE * LANES))
     return value.reshape(RINGS * MESSAGE, LANES)
 
 
@@ -527,7 +530,7 @@
             scalars=False,
             after=(above, below),
         )
-        piece = exchange(shards, "z")
+        piece = exchange_far_first(shards) if final else exchange(shards, "z")
         part_band, to_right, *to_left = call(
             place_kernel,
             [band_shape, edge] if final else [band_shape, edge, edge],

time: 329 us -> 334 us (1.015)
  blocking collectives: 129 us -> 133 us
    all_to_all x3 -> x4, starting transfers between devices: 40 us -> 51.4 us  [exchange_far_first(): lax.all_to_all(value, 'z', 0, 0, tiled=True, axis_index_groups=groups)]
    all_to_all x7, blocking collectives: 97.8 us -> 107 us  [exchange(): return lax.all_to_all(value, axes, 0, 0, tiled=True)]
    all_to_all x4 -> x3, starting transfers between devices: 29.2 us -> 22 us  [exchange(): return lax.all_to_all(value, axes, 0, 0, tiled=True)]
    all_gather x3, blocking collectives: 31 us -> 25.8 us  [gather_pieces(): gathered = lax.all_gather(piece, ('xlo', 'core'))]
  transfers between devices with their start and end apart: 25 -> 25, of which waited for: 17 -> 16; matrix products, arithmetic and copies ran while one was open for 0% -> 0% of each run, Pallas kernels for 1% -> 1%
where the time goes in v16:
time: 334 us; the launch traced here: 332 us
  starting transfers between devices  144 us (43%)
  blocking collectives  133 us (40%)
  waiting for transfers between devices  33.1 us (10%)
  Pallas kernels  18.9 us (6%)
    all_to_all x7, blocking collectives, exchange(): return lax.all_to_all(value, axes, 0, 0, tiled=True)  107 us
    all_to_all x4, starting transfers between devices, exchange_far_first(): lax.all_to_all(value, 'z', 0, 0, tiled=True, axis_index_groups=groups)  51.4 us
    ppermute x6, starting transfers between devices, shift(): lax.ppermute(value, axes, [(i, i + steps) for i in range(first, last)])  28.8 us
    all_gather x3, blocking collectives, gather_pieces(): gathered = lax.all_gather(piece, ('xlo', 'core'))  25.8 us
    ppermute x6, starting transfers between devices, other(): return lax.ppermute(value, axis, [(0, 1), (1, 0)])  25.8 us
    all_to_all x3, starting transfers between devices, exchange(): return lax.all_to_all(value, axes, 0, 0, tiled=True)  22 us
    pallas_call x33, Pallas kernels, call(): pl.pallas_call(body, out_shape=[jax.ShapeDtypeStruct(shape, F32) for shap...  18.9 us
    ppermute x6, starting transfers between devices, beside_slab(): return lax.ppermute(value, MODE_AXES, pairs)  15.8 us
  transfers between devices with their start and end apart: 25, of which 16 were waited for; matrix products, arithmetic and copies ran while one was open for 0% of the time, Pallas kernels for 1%

profile of v16, /device:TPU:1, one launch (start us, length us, event | category | flops | bytes accessed | tf_op | source)
XLA Modules:
  0.0 332.1 jit_solution(14095400495112773736)
XLA Ops:
  0.6 1.1 copy-done.3
  1.8 0.8 split_kernel.1._
  2.6 7.6 %all-to-all-start = ((f32[8,2,32,256]{3,2,1,0:T(8,128)}), f32[8,2,32,256]{3,2,1,0:T(8,128)S(1)}, u32[]{:S(2)}, u32[]{:S(2)}) async-start(f32[8,2,32,256]{3,2,1,0:T(8,128)} %split_kernel.1._), calls=%async_computation | async-start | bytes 1048576 | tf_op jit(solution)/shard_map/all_to_all | solution.py:419
  10.3 4.9 %collective-permute-start = (f32[2,64,256]{2,1,0:T(8,128)S(1)}, f32[2,64,256]{2,1,0:T(8,128)S(1)}, u32[]{:S(2)}, u32[]{:S(2)}) collective-permute-start(f32[2,64,256]{2,1,0:T(8,128)S(1)} %get-tuple-element.57), channel_id=1, source_target_pairs={{8,0},{16,8},{24,16},{32,24},{40,32},{48,40},{56,48},{64,56},{72,6... | collective-permute-start | bytes 393224 | tf_op jit(solution)/shard_map/ppermute | solution.py:395
  17.0 0.8 collective-permute-done.refs_2_
  17.8 1.3 all-to-all-done.refs_3_.refs_1_
  19.1 1.0 first_kernel.1
  20.1 15.1 %all_to_all.70.refs_0_ = f32[8,2,32,256]{3,2,1,0:T(8,128)S(1)} all-to-all(f32[8,2,32,256]{3,2,1,0:T(8,128)S(1)} %get-tuple-element.59), channel_id=1, replica_groups=mesh['xlo'=2,'z'=16,'core'=2,'xhi'=2,'y'=4] {'xhi','y'}, dimensions={0} | all-to-all | bytes 1048576 | tf_op jit(solution)/shard_map/all_to_all | solution.py:419
  35.2 1.4 ratio_kernel.3
  36.5 12.3 %all_to_all.71.refs_0_ = f32[8,2,32,256]{3,2,1,0:T(8,128)S(1)} all-to-all(f32[8,2,32,256]{3,2,1,0:T(8,128)S(1)} %ratio_kernel.3), channel_id=1, replica_groups=mesh['xlo'=2,'z'=16,'core'=2,'xhi'=2,'y'=4] {'xhi','y'}, dimensions={0} | all-to-all | bytes 1048576 | tf_op jit(solution)/shard_map/all_to_all | solution.py:419
  48.8 0.7 backward_kernel.3
  49.6 5.3 %collective-permute-start.1 = (f32[17,16,256]{2,1,0:T(8,128)S(1)}, f32[17,16,256]{2,1,0:T(8,128)S(1)}, u32[]{:S(2)}, u32[]{:S(2)}) collective-permute-start(f32[17,16,256]{2,1,0:T(8,128)S(1)} %get-tuple-element.63), channel_id=1, source_target_pairs={{0,8},{8,0},{1,9},{9,1},{2,10},{10,2},{3,11},{11,3},{4,12},{12,4},... | collective-permute-start | bytes 835592 | tf_op jit(solution)/shard_map/ppermute | solution.py:399
  54.9 1.2 collective-permute-done.1.refs_1_
  56.1 6.7 %collective-permute-start.2 = (f32[17,8,256]{2,1,0:T(8,128)S(1)}, f32[17,8,256]{2,1,0:T(8,128)S(1)}, u32[]{:S(2)}, u32[]{:S(2)}) collective-permute-start(f32[17,8,256]{2,1,0:T(8,128)S(1)} %get-tuple-element.65), channel_id=1, source_target_pairs={{0,256},{256,0},{1,257},{257,1},{2,258},{258,2},{3,259},{259,3},{4... | collective-permute-start | bytes 417800 | tf_op jit(solution)/shard_map/ppermute | solution.py:399
  63.4 3.2 collective-permute-done.2.refs_1_
  67.2 17.0 %all-to-all-start.3 = ((f32[16,1,2176]{2,1,0:T(1,128)}), f32[16,1,2176]{2,1,0:T(1,128)S(1)}, u32[]{:S(2)}, u32[]{:S(2)}) async-start(f32[16,1,2176]{2,1,0:T(1,128)} %bitcast.8), calls=%async_computation.3 | async-start | bytes 278528 | tf_op jit(solution)/shard_map/all_to_all | solution.py:410
  84.3 1.3 collective-permute-start.4
  85.5 4.0 %collective-permute-start.3 = (f32[2,32,256]{2,1,0:T(8,128)S(1)}, f32[2,32,256]{2,1,0:T(8,128)S(1)}, u32[]{:S(2)}, u32[]{:S(2)}) collective-permute-start(f32[2,32,256]{2,1,0:T(8,128)S(1)} %step_kernel.3.refs_2_), channel_id=1, source_target_pairs={{0,1},{1,2},{2,3},{3,7},{7,6},{6,5},{5,4},{8,9},{9,10},{10,11},{11... | collective-permute-start | bytes 196616 | tf_op jit(solution)/shard_map/ppermute | solution.py:405
  89.5 1.3 collective-permute-done.3.refs_2_.refs_1_
  91.5 7.2 %all-to-all-start.4 = ((f32[16,16,128]{2,1,0:T(8,128)}), f32[16,16,128]{2,1,0:T(8,128)S(1)}, u32[]{:S(2)}, u32[]{:S(2)}) async-start(f32[16,16,128]{2,1,0:T(8,128)} %get-tuple-element.69.refs_5_), calls=%async_computation.4 | async-start | bytes 262144 | tf_op jit(solution)/shard_map/all_to_all | solution.py:419
  99.0 7.3 %collective-permute-start.5 = (f32[2,64,256]{2,1,0:T(8,128)S(1)}, f32[2,64,256]{2,1,0:T(8,128)S(1)}, u32[]{:S(2)}, u32[]{:S(2)}) collective-permute-start(f32[2,64,256]{2,1,0:T(8,128)S(1)} %get-tuple-element.72), channel_id=1, source_target_pairs={{0,8},{8,16},{16,24},{24,32},{32,40},{40,48},{48,56},{56,64},{64,7... | collective-permute-start | bytes 393224 | tf_op jit(solution)/shard_map/ppermute | solution.py:395
  106.3 1.9 collective-permute-start.6
  108.2 1.3 collective-permute-done.5.refs_2_
  109.5 3.6 %collective-permute-done.6.refs_3_ = f32[2,64,256]{2,1,0:T(8,128)S(1)} collective-permute-done((f32[2,64,256]{2,1,0:T(8,128)S(1)}, f32[2,64,256]{2,1,0:T(8,128)S(1)}, u32[]{:S(2)}, u32[]{:S(2)}) %collective-permute-start.6) | collective-permute-done | bytes 131104 | tf_op jit(solution)/shard_map/ppermute | solution.py:395
  113.4 8.8 %all_gather.12 = f32[4,256,128]{2,1,0:T(8,128)S(1)} all-gather(f32[1,256,128]{2,1,0:T(8,128)S(1)} %bitcast.28), channel_id=1, replica_groups=mesh['xlo'=2,'z'=16,'core'=2,'xhi'=2,'y'=4] {'xlo','core'}, dimensions={0}, use_global_device_ids=true | all-gather | bytes 655360 | tf_op jit(solution)/shard_map/all_gather | solution.py:423
  122.2 1.0 next_kernel.2
  123.2 12.9 %all_to_all.72.refs_0_ = f32[8,2,32,256]{3,2,1,0:T(8,128)S(1)} all-to-all(f32[8,2,32,256]{3,2,1,0:T(8,128)S(1)} %get-tuple-element.77), channel_id=1, replica_groups=mesh['xlo'=2,'z'=16,'core'=2,'xhi'=2,'y'=4] {'xhi','y'}, dimensions={0} | all-to-all | bytes 1048576 | tf_op jit(solution)/shard_map/all_to_all | solution.py:419
  136.2 1.4 ratio_kernel.4
  137.6 13.8 %all_to_all.73.refs_0_ = f32[8,2,32,256]{3,2,1,0:T(8,128)S(1)} all-to-all(f32[8,2,32,256]{3,2,1,0:T(8,128)S(1)} %ratio_kernel.4), channel_id=1, replica_groups=mesh['xlo'=2,'z'=16,'core'=2,'xhi'=2,'y'=4] {'xhi','y'}, dimensions={0} | all-to-all | bytes 1048576 | tf_op jit(solution)/shard_map/all_to_all | solution.py:419
  151.4 0.7 backward_kernel.4
  152.1 4.4 %collective-permute-start.7 = (f32[17,16,256]{2,1,0:T(8,128)S(1)}, f32[17,16,256]{2,1,0:T(8,128)S(1)}, u32[]{:S(2)}, u32[]{:S(2)}) collective-permute-start(f32[17,16,256]{2,1,0:T(8,128)S(1)} %get-tuple-element.80), channel_id=1, source_target_pairs={{0,8},{8,0},{1,9},{9,1},{2,10},{10,2},{3,11},{11,3},{4,12},{12,4},... | collective-permute-start | bytes 835592 | tf_op jit(solution)/shard_map/ppermute | solution.py:399
  156.5 1.2 collective-permute-done.7.refs_1_
  157.7 2.8 collective-permute-start.8
  161.1 3.4 %collective-permute-done.8.refs_1_ = f32[17,8,256]{2,1,0:T(8,128)S(1)} collective-permute-done((f32[17,8,256]{2,1,0:T(8,128)S(1)}, f32[17,8,256]{2,1,0:T(8,128)S(1)}, u32[]{:S(2)}, u32[]{:S(2)}) %collective-permute-start.8) | collective-permute-done | bytes 139296 | tf_op jit(solution)/shard_map/ppermute | solution.py:399
  165.2 11.5 %all-to-all-start.7 = ((f32[16,1,2176]{2,1,0:T(1,128)}), f32[16,1,2176]{2,1,0:T(1,128)S(1)}, u32[]{:S(2)}, u32[]{:S(2)}) async-start(f32[16,1,2176]{2,1,0:T(1,128)} %bitcast.12), calls=%async_computation.7 | async-start | bytes 278528 | tf_op jit(solution)/shard_map/all_to_all | solution.py:410
  176.6 1.3 collective-permute-start.10
  177.9 4.0 %collective-permute-start.9 = (f32[2,32,256]{2,1,0:T(8,128)S(1)}, f32[2,32,256]{2,1,0:T(8,128)S(1)}, u32[]{:S(2)}, u32[]{:S(2)}) collective-permute-start(f32[2,32,256]{2,1,0:T(8,128)S(1)} %step_kernel.4.refs_2_), channel_id=1, source_target_pairs={{0,1},{1,2},{2,3},{3,7},{7,6},{6,5},{5,4},{8,9},{9,10},{10,11},{11... | collective-permute-start | bytes 196616 | tf_op jit(solution)/shard_map/ppermute | solution.py:405
  181.9 1.3 collective-permute-done.9.refs_2_.refs_1_
  183.9 7.2 %all-to-all-start.8 = ((f32[16,16,128]{2,1,0:T(8,128)}), f32[16,16,128]{2,1,0:T(8,128)S(1)}, u32[]{:S(2)}, u32[]{:S(2)}) async-start(f32[16,16,128]{2,1,0:T(8,128)} %get-tuple-element.87.refs_5_), calls=%async_computation.8 | async-start | bytes 262144 | tf_op jit(solution)/shard_map/all_to_all | solution.py:419
  191.4 7.3 %collective-permute-start.11 = (f32[2,64,256]{2,1,0:T(8,128)S(1)}, f32[2,64,256]{2,1,0:T(8,128)S(1)}, u32[]{:S(2)}, u32[]{:S(2)}) collective-permute-start(f32[2,64,256]{2,1,0:T(8,128)S(1)} %get-tuple-element.90), channel_id=1, source_target_pairs={{0,8},{8,16},{16,24},{24,32},{32,40},{40,48},{48,56},{56,64},{64,7... | collective-permute-start | bytes 393224 | tf_op jit(solution)/shard_map/ppermute | solution.py:395
  198.7 1.9 collective-permute-start.12
  200.6 1.3 collective-permute-done.11.refs_2_
  201.9 3.6 %collective-permute-done.12.refs_3_ = f32[2,64,256]{2,1,0:T(8,128)S(1)} collective-permute-done((f32[2,64,256]{2,1,0:T(8,128)S(1)}, f32[2,64,256]{2,1,0:T(8,128)S(1)}, u32[]{:S(2)}, u32[]{:S(2)}) %collective-permute-start.12) | collective-permute-done | bytes 131104 | tf_op jit(solution)/shard_map/ppermute | solution.py:395
  205.8 9.2 %all_gather.13 = f32[4,256,128]{2,1,0:T(8,128)S(1)} all-gather(f32[1,256,128]{2,1,0:T(8,128)S(1)} %bitcast.29), channel_id=1, replica_groups=mesh['xlo'=2,'z'=16,'core'=2,'xhi'=2,'y'=4] {'xlo','core'}, dimensions={0}, use_global_device_ids=true | all-gather | bytes 655360 | tf_op jit(solution)/shard_map/all_gather | solution.py:423
  215.0 1.0 next_kernel.3
  216.0 13.0 %all_to_all.74.refs_0_ = f32[8,2,32,256]{3,2,1,0:T(8,128)S(1)} all-to-all(f32[8,2,32,256]{3,2,1,0:T(8,128)S(1)} %get-tuple-element.95), channel_id=1, replica_groups=mesh['xlo'=2,'z'=16,'core'=2,'xhi'=2,'y'=4] {'xhi','y'}, dimensions={0} | all-to-all | bytes 1048576 | tf_op jit(solution)/shard_map/all_to_all | solution.py:419
  229.0 1.4 ratio_kernel.5
  230.4 14.0 %all_to_all.75.refs_0_ = f32[8,2,32,256]{3,2,1,0:T(8,128)S(1)} all-to-all(f32[8,2,32,256]{3,2,1,0:T(8,128)S(1)} %ratio_kernel.5), channel_id=1, replica_groups=mesh['xlo'=2,'z'=16,'core'=2,'xhi'=2,'y'=4] {'xhi','y'}, dimensions={0} | all-to-all | bytes 1048576 | tf_op jit(solution)/shard_map/all_to_all | solution.py:419
  244.4 0.7 backward_kernel.5
  245.1 4.4 %collective-permute-start.13 = (f32[17,16,256]{2,1,0:T(8,128)S(1)}, f32[17,16,256]{2,1,0:T(8,128)S(1)}, u32[]{:S(2)}, u32[]{:S(2)}) collective-permute-start(f32[17,16,256]{2,1,0:T(8,128)S(1)} %get-tuple-element.98), channel_id=1, source_target_pairs={{0,8},{8,0},{1,9},{9,1},{2,10},{10,2},{3,11},{11,3},{4,12},{12,4},... | collective-permute-start | bytes 835592 | tf_op jit(solution)/shard_map/ppermute | solution.py:399
  249.5 1.2 collective-permute-done.13.refs_1_
  250.7 2.2 collective-permute-start.14
  253.1 4.4 %collective-permute-done.14.refs_1_ = f32[17,8,256]{2,1,0:T(8,128)S(1)} collective-permute-done((f32[17,8,256]{2,1,0:T(8,128)S(1)}, f32[17,8,256]{2,1,0:T(8,128)S(1)}, u32[]{:S(2)}, u32[]{:S(2)}) %collective-permute-start.14) | collective-permute-done | bytes 139296 | tf_op jit(solution)/shard_map/ppermute | solution.py:399
  258.2 11.5 %all-to-all-start.11 = ((f32[16,1,2176]{2,1,0:T(1,128)}), f32[16,1,2176]{2,1,0:T(1,128)S(1)}, u32[]{:S(2)}, u32[]{:S(2)}) async-start(f32[16,1,2176]{2,1,0:T(1,128)} %bitcast.16), calls=%async_computation.11 | async-start | bytes 278528 | tf_op jit(solution)/shard_map/all_to_all | solution.py:410
  269.6 1.3 collective-permute-start.16
  270.9 4.0 %collective-permute-start.15 = (f32[2,32,256]{2,1,0:T(8,128)S(1)}, f32[2,32,256]{2,1,0:T(8,128)S(1)}, u32[]{:S(2)}, u32[]{:S(2)}) collective-permute-start(f32[2,32,256]{2,1,0:T(8,128)S(1)} %step_kernel.5.refs_2_), channel_id=1, source_target_pairs={{0,1},{1,2},{2,3},{3,7},{7,6},{6,5},{5,4},{8,9},{9,10},{10,11},{11... | collective-permute-start | bytes 196616 | tf_op jit(solution)/shard_map/ppermute | solution.py:405
  274.9 1.3 collective-permute-done.15.refs_2_.refs_1_
  276.2 0.7 probe_kernel.5
  276.9 11.5 %all-to-all-start.12 = ((f32[16,16,128]{2,1,0:T(8,128)}), f32[16,16,128]{2,1,0:T(8,128)S(1)}, u32[]{:S(2)}, u32[]{:S(2)}) async-start(f32[16,16,128]{2,1,0:T(8,128)} %get-tuple-element.104.refs_5_), calls=%async_computation.12 | async-start | bytes 262144 | tf_op jit(solution)/shard_map/all_to_all | solution.py:410
  288.7 5.5 %collective-permute-start.17 = (f32[2,64,256]{2,1,0:T(8,128)S(1)}, f32[2,64,256]{2,1,0:T(8,128)S(1)}, u32[]{:S(2)}, u32[]{:S(2)}) collective-permute-start(f32[2,64,256]{2,1,0:T(8,128)S(1)} %get-tuple-element.107), channel_id=1, source_target_pairs={{0,8},{8,16},{16,24},{24,32},{32,40},{40,48},{48,56},{56,64},{64,7... | collective-permute-start | bytes 393224 | tf_op jit(solution)/shard_map/ppermute | solution.py:395
  294.2 2.7 collective-permute-done.17.refs_2_
  297.2 25.7 %all_to_all.76.refs_0_ = f32[8,320,128]{2,1,0:T(8,128)S(1)} all-to-all(f32[8,320,128]{2,1,0:T(8,128)S(1)} %tail_kernel.1), channel_id=1, replica_groups=mesh['xlo'=2,'z'=16,'core'=2,'xhi'=2,'y'=4] {'xhi','y'}, dimensions={0} | all-to-all | bytes 2621440 | tf_op jit(solution)/shard_map/all_to_all | solution.py:419
  323.0 7.8 %all-gather = f32[32,32,128]{2,1,0:T(8,128)S(1)} all-gather(f32[8,32,128]{2,1,0:T(8,128)S(1)} %slice.19), channel_id=2, replica_groups=mesh['xlo'=2,'z'=16,'core'=2,'xhi'=2,'y'=4] {'xlo','core'}, dimensions={0}, use_global_device_ids=true | all-gather | bytes 655360 | tf_op jit(solution)/shard_map/all_gather | solution.py:423
  330.8 1.3 last_kernel.1
  (58 shorter events, 7.4 us)
Async XLA Ops:
  0.6 9.6 %copy-start.2 = (f32[2,288,512]{2,1,0:T(8,128)S(1)}, f32[2,288,512]{2,1,0:T(8,128)}, u32[]{:S(2)}) copy-start(f32[2,288,512]{2,1,0:T(8,128)} %whole.1) | copy-start | bytes 3538948
  0.6 1.1 copy-start.3
  2.6 12.7 %copy-start.4 = (s32[1,3]{1,0:T(1,128)S(1)}, s32[1,3]{1,0:T(1,128)}, u32[]{:S(2)}) copy-start(s32[1,3]{1,0:T(1,128)} %param.14) | copy-start | bytes 40
  2.6 12.7 %copy-start.5 = (s32[1,3]{1,0:T(1,128)S(1)}, s32[1,3]{1,0:T(1,128)}, u32[]{:S(2)}) copy-start(s32[1,3]{1,0:T(1,128)} %param.12) | copy-start | bytes 40
  2.6 12.7 %copy-start.6 = (s32[1,3]{1,0:T(1,128)S(1)}, s32[1,3]{1,0:T(1,128)}, u32[]{:S(2)}) copy-start(s32[1,3]{1,0:T(1,128)} %param.11) | copy-start | bytes 40
  2.6 14.0 %copy-start.1 = (bf16[1,3,256,256]{3,2,1,0:T(8,128)(2,1)S(1)}, bf16[1,3,256,256]{3,2,1,0:T(8,128)(2,1)}, u32[]{:S(2)}) copy-start(bf16[1,3,256,256]{3,2,1,0:T(8,128)(2,1)} %refs_1_.5) | copy-start | bytes 1179652
  2.6 16.5 %all-to-all-start = ((f32[8,2,32,256]{3,2,1,0:T(8,128)}), f32[8,2,32,256]{3,2,1,0:T(8,128)S(1)}, u32[]{:S(2)}, u32[]{:S(2)}) async-start(f32[8,2,32,256]{3,2,1,0:T(8,128)} %split_kernel.1._), calls=%async_computation | async-start | bytes 1048576 | tf_op jit(solution)/shard_map/all_to_all | solution.py:419
  10.2 8.8 %copy-start = (bf16[3,2,256,256]{3,2,1,0:T(8,128)(2,1)S(1)}, bf16[3,2,256,256]{3,2,1,0:T(8,128)(2,1)}, u32[]{:S(2)}) copy-start(bf16[3,2,256,256]{3,2,1,0:T(8,128)(2,1)} %constant.35.clone.refs_4_.refs_3_.refs_2_) | copy-start | bytes 2359300
  10.3 7.5 %collective-permute-start = (f32[2,64,256]{2,1,0:T(8,128)S(1)}, f32[2,64,256]{2,1,0:T(8,128)S(1)}, u32[]{:S(2)}, u32[]{:S(2)}) collective-permute-start(f32[2,64,256]{2,1,0:T(8,128)S(1)} %get-tuple-element.57), channel_id=1, source_target_pairs={{8,0},{16,8},{24,16},{32,24},{40,32},{48,40},{56,48},{64,56},{72,6... | collective-permute-start | bytes 393224 | tf_op jit(solution)/shard_map/ppermute | solution.py:395
  49.6 6.5 %collective-permute-start.1 = (f32[17,16,256]{2,1,0:T(8,128)S(1)}, f32[17,16,256]{2,1,0:T(8,128)S(1)}, u32[]{:S(2)}, u32[]{:S(2)}) collective-permute-start(f32[17,16,256]{2,1,0:T(8,128)S(1)} %get-tuple-element.63), channel_id=1, source_target_pairs={{0,8},{8,0},{1,9},{9,1},{2,10},{10,2},{3,11},{11,3},{4,12},{12,4},... | collective-permute-start | bytes 835592 | tf_op jit(solution)/shard_map/ppermute | solution.py:399
  56.1 10.5 %collective-permute-start.2 = (f32[17,8,256]{2,1,0:T(8,128)S(1)}, f32[17,8,256]{2,1,0:T(8,128)S(1)}, u32[]{:S(2)}, u32[]{:S(2)}) collective-permute-start(f32[17,8,256]{2,1,0:T(8,128)S(1)} %get-tuple-element.65), channel_id=1, source_target_pairs={{0,256},{256,0},{1,257},{257,1},{2,258},{258,2},{3,259},{259,3},{4... | collective-permute-start | bytes 417800 | tf_op jit(solution)/shard_map/ppermute | solution.py:399
  67.2 23.6 %all-to-all-start.3 = ((f32[16,1,2176]{2,1,0:T(1,128)}), f32[16,1,2176]{2,1,0:T(1,128)S(1)}, u32[]{:S(2)}, u32[]{:S(2)}) async-start(f32[16,1,2176]{2,1,0:T(1,128)} %bitcast.8), calls=%async_computation.3 | async-start | bytes 278528 | tf_op jit(solution)/shard_map/all_to_all | solution.py:410
  84.3 5.3 %collective-permute-start.4 = (f32[2,32,256]{2,1,0:T(8,128)S(1)}, f32[2,32,256]{2,1,0:T(8,128)S(1)}, u32[]{:S(2)}, u32[]{:S(2)}) collective-permute-start(f32[2,32,256]{2,1,0:T(8,128)S(1)} %step_kernel.3.refs_2_), channel_id=1, source_target_pairs={{1,0},{2,1},{3,2},{7,3},{6,7},{5,6},{4,5},{9,8},{10,9},{11,10},{15... | collective-permute-start | bytes 196616 | tf_op jit(solution)/shard_map/ppermute | solution.py:405
  85.5 5.3 %collective-permute-start.3 = (f32[2,32,256]{2,1,0:T(8,128)S(1)}, f32[2,32,256]{2,1,0:T(8,128)S(1)}, u32[]{:S(2)}, u32[]{:S(2)}) collective-permute-start(f32[2,32,256]{2,1,0:T(8,128)S(1)} %step_kernel.3.refs_2_), channel_id=1, source_target_pairs={{0,1},{1,2},{2,3},{3,7},{7,6},{6,5},{5,4},{8,9},{9,10},{10,11},{11... | collective-permute-start | bytes 196616 | tf_op jit(solution)/shard_map/ppermute | solution.py:405
  91.5 21.8 %all-to-all-start.4 = ((f32[16,16,128]{2,1,0:T(8,128)}), f32[16,16,128]{2,1,0:T(8,128)S(1)}, u32[]{:S(2)}, u32[]{:S(2)}) async-start(f32[16,16,128]{2,1,0:T(8,128)} %get-tuple-element.69.refs_5_), calls=%async_computation.4 | async-start | bytes 262144 | tf_op jit(solution)/shard_map/all_to_all | solution.py:419
  99.0 10.5 %collective-permute-start.5 = (f32[2,64,256]{2,1,0:T(8,128)S(1)}, f32[2,64,256]{2,1,0:T(8,128)S(1)}, u32[]{:S(2)}, u32[]{:S(2)}) collective-permute-start(f32[2,64,256]{2,1,0:T(8,128)S(1)} %get-tuple-element.72), channel_id=1, source_target_pairs={{0,8},{8,16},{16,24},{24,32},{32,40},{40,48},{48,56},{56,64},{64,7... | collective-permute-start | bytes 393224 | tf_op jit(solution)/shard_map/ppermute | solution.py:395
  106.3 6.8 %collective-permute-start.6 = (f32[2,64,256]{2,1,0:T(8,128)S(1)}, f32[2,64,256]{2,1,0:T(8,128)S(1)}, u32[]{:S(2)}, u32[]{:S(2)}) collective-permute-start(f32[2,64,256]{2,1,0:T(8,128)S(1)} %get-tuple-element.73), channel_id=1, source_target_pairs={{8,0},{16,8},{24,16},{32,24},{40,32},{48,40},{56,48},{64,56},{72,6... | collective-permute-start | bytes 393224 | tf_op jit(solution)/shard_map/ppermute | solution.py:395
  152.1 5.5 %collective-permute-start.7 = (f32[17,16,256]{2,1,0:T(8,128)S(1)}, f32[17,16,256]{2,1,0:T(8,128)S(1)}, u32[]{:S(2)}, u32[]{:S(2)}) collective-permute-start(f32[17,16,256]{2,1,0:T(8,128)S(1)} %get-tuple-element.80), channel_id=1, source_target_pairs={{0,8},{8,0},{1,9},{9,1},{2,10},{10,2},{3,11},{11,3},{4,12},{12,4},... | collective-permute-start | bytes 835592 | tf_op jit(solution)/shard_map/ppermute | solution.py:399
  157.7 6.8 %collective-permute-start.8 = (f32[17,8,256]{2,1,0:T(8,128)S(1)}, f32[17,8,256]{2,1,0:T(8,128)S(1)}, u32[]{:S(2)}, u32[]{:S(2)}) collective-permute-start(f32[17,8,256]{2,1,0:T(8,128)S(1)} %get-tuple-element.82), channel_id=1, source_target_pairs={{0,256},{256,0},{1,257},{257,1},{2,258},{258,2},{3,259},{259,3},{4... | collective-permute-start | bytes 417800 | tf_op jit(solution)/shard_map/ppermute | solution.py:399
  165.2 18.1 %all-to-all-start.7 = ((f32[16,1,2176]{2,1,0:T(1,128)}), f32[16,1,2176]{2,1,0:T(1,128)S(1)}, u32[]{:S(2)}, u32[]{:S(2)}) async-start(f32[16,1,2176]{2,1,0:T(1,128)} %bitcast.12), calls=%async_computation.7 | async-start | bytes 278528 | tf_op jit(solution)/shard_map/all_to_all | solution.py:410
  176.6 5.3 %collective-permute-start.10 = (f32[2,32,256]{2,1,0:T(8,128)S(1)}, f32[2,32,256]{2,1,0:T(8,128)S(1)}, u32[]{:S(2)}, u32[]{:S(2)}) collective-permute-start(f32[2,32,256]{2,1,0:T(8,128)S(1)} %step_kernel.4.refs_2_), channel_id=1, source_target_pairs={{1,0},{2,1},{3,2},{7,3},{6,7},{5,6},{4,5},{9,8},{10,9},{11,10},{15... | collective-permute-start | bytes 196616 | tf_op jit(solution)/shard_map/ppermute | solution.py:405
  177.9 5.3 %collective-permute-start.9 = (f32[2,32,256]{2,1,0:T(8,128)S(1)}, f32[2,32,256]{2,1,0:T(8,128)S(1)}, u32[]{:S(2)}, u32[]{:S(2)}) collective-permute-start(f32[2,32,256]{2,1,0:T(8,128)S(1)} %step_kernel.4.refs_2_), channel_id=1, source_target_pairs={{0,1},{1,2},{2,3},{3,7},{7,6},{6,5},{5,4},{8,9},{9,10},{10,11},{11... | collective-permute-start | bytes 196616 | tf_op jit(solution)/shard_map/ppermute | solution.py:405
  183.9 21.8 %all-to-all-start.8 = ((f32[16,16,128]{2,1,0:T(8,128)}), f32[16,16,128]{2,1,0:T(8,128)S(1)}, u32[]{:S(2)}, u32[]{:S(2)}) async-start(f32[16,16,128]{2,1,0:T(8,128)} %get-tuple-element.87.refs_5_), calls=%async_computation.8 | async-start | bytes 262144 | tf_op jit(solution)/shard_map/all_to_all | solution.py:419
  191.4 10.5 %collective-permute-start.11 = (f32[2,64,256]{2,1,0:T(8,128)S(1)}, f32[2,64,256]{2,1,0:T(8,128)S(1)}, u32[]{:S(2)}, u32[]{:S(2)}) collective-permute-start(f32[2,64,256]{2,1,0:T(8,128)S(1)} %get-tuple-element.90), channel_id=1, source_target_pairs={{0,8},{8,16},{16,24},{24,32},{32,40},{40,48},{48,56},{56,64},{64,7... | collective-permute-start | bytes 393224 | tf_op jit(solution)/shard_map/ppermute | solution.py:395
  198.7 6.8 %collective-permute-start.12 = (f32[2,64,256]{2,1,0:T(8,128)S(1)}, f32[2,64,256]{2,1,0:T(8,128)S(1)}, u32[]{:S(2)}, u32[]{:S(2)}) collective-permute-start(f32[2,64,256]{2,1,0:T(8,128)S(1)} %get-tuple-element.91), channel_id=1, source_target_pairs={{8,0},{16,8},{24,16},{32,24},{40,32},{48,40},{56,48},{64,56},{72,6... | collective-permute-start | bytes 393224 | tf_op jit(solution)/shard_map/ppermute | solution.py:395
  245.1 5.5 %collective-permute-start.13 = (f32[17,16,256]{2,1,0:T(8,128)S(1)}, f32[17,16,256]{2,1,0:T(8,128)S(1)}, u32[]{:S(2)}, u32[]{:S(2)}) collective-permute-start(f32[17,16,256]{2,1,0:T(8,128)S(1)} %get-tuple-element.98), channel_id=1, source_target_pairs={{0,8},{8,0},{1,9},{9,1},{2,10},{10,2},{3,11},{11,3},{4,12},{12,4},... | collective-permute-start | bytes 835592 | tf_op jit(solution)/shard_map/ppermute | solution.py:399
  250.7 6.8 %collective-permute-start.14 = (f32[17,8,256]{2,1,0:T(8,128)S(1)}, f32[17,8,256]{2,1,0:T(8,128)S(1)}, u32[]{:S(2)}, u32[]{:S(2)}) collective-permute-start(f32[17,8,256]{2,1,0:T(8,128)S(1)} %get-tuple-element.100), channel_id=1, source_target_pairs={{0,256},{256,0},{1,257},{257,1},{2,258},{258,2},{3,259},{259,3},{4... | collective-permute-start | bytes 417800 | tf_op jit(solution)/shard_map/ppermute | solution.py:399
  258.2 18.1 %all-to-all-start.11 = ((f32[16,1,2176]{2,1,0:T(1,128)}), f32[16,1,2176]{2,1,0:T(1,128)S(1)}, u32[]{:S(2)}, u32[]{:S(2)}) async-start(f32[16,1,2176]{2,1,0:T(1,128)} %bitcast.16), calls=%async_computation.11 | async-start | bytes 278528 | tf_op jit(solution)/shard_map/all_to_all | solution.py:410
  269.6 5.3 %collective-permute-start.16 = (f32[2,32,256]{2,1,0:T(8,128)S(1)}, f32[2,32,256]{2,1,0:T(8,128)S(1)}, u32[]{:S(2)}, u32[]{:S(2)}) collective-permute-start(f32[2,32,256]{2,1,0:T(8,128)S(1)} %step_kernel.5.refs_2_), channel_id=1, source_target_pairs={{1,0},{2,1},{3,2},{7,3},{6,7},{5,6},{4,5},{9,8},{10,9},{11,10},{15... | collective-permute-start | bytes 196616 | tf_op jit(solution)/shard_map/ppermute | solution.py:405
  270.9 5.3 %collective-permute-start.15 = (f32[2,32,256]{2,1,0:T(8,128)S(1)}, f32[2,32,256]{2,1,0:T(8,128)S(1)}, u32[]{:S(2)}, u32[]{:S(2)}) collective-permute-start(f32[2,32,256]{2,1,0:T(8,128)S(1)} %step_kernel.5.refs_2_), channel_id=1, source_target_pairs={{0,1},{1,2},{2,3},{3,7},{7,6},{6,5},{5,4},{8,9},{9,10},{10,11},{11... | collective-permute-start | bytes 196616 | tf_op jit(solution)/shard_map/ppermute | solution.py:405
  276.9 20.2 %all-to-all-start.12 = ((f32[16,16,128]{2,1,0:T(8,128)}), f32[16,16,128]{2,1,0:T(8,128)S(1)}, u32[]{:S(2)}, u32[]{:S(2)}) async-start(f32[16,16,128]{2,1,0:T(8,128)} %get-tuple-element.104.refs_5_), calls=%async_computation.12 | async-start | bytes 262144 | tf_op jit(solution)/shard_map/all_to_all | solution.py:410
  288.7 8.3 %collective-permute-start.17 = (f32[2,64,256]{2,1,0:T(8,128)S(1)}, f32[2,64,256]{2,1,0:T(8,128)S(1)}, u32[]{:S(2)}, u32[]{:S(2)}) collective-permute-start(f32[2,64,256]{2,1,0:T(8,128)S(1)} %get-tuple-element.107), channel_id=1, source_target_pairs={{0,8},{8,16},{16,24},{24,32},{32,40},{40,48},{48,56},{56,64},{64,7... | collective-permute-start | bytes 393224 | tf_op jit(solution)/shard_map/ppermute | solution.py:395
